TPU v7x, 32 devices: a whole 2x2x4 slice. The times are simulated.
32 devices in a mesh: groups: 2 (over x), outp: 8 (over z, y), inp: 2 (over core).
Axes of the slice: x: 2, y: 2, z: 4, core: 2. Of those that a mesh axis runs over, the one named last changes fastest.
Arguments:
- inputs: bfloat16 [1024, 8192], P(('groups', 'outp'), 'inp'), parts along dimension 0, may hold values from -6 to 6
- cotangent: bfloat16 [1024, 28672], P(('groups', 'inp'), 'outp'), parts along dimension 0, may hold values from -6 to 6
- weight: bfloat16 [8192, 28672], P('inp', 'outp'), may hold values from -0.0625 to 0.0625
- in_sketch: bfloat16 [64, 8192], P(None, 'inp'), may hold values from -0.0625 to 0.0625
- out_sketch: bfloat16 [64, 28672], P(None, 'outp'), may hold values from -0.03125 to 0.03125
Outputs:
- outputs: bfloat16 [1024, 28672], P(('groups', 'inp'), 'outp'), parts along dimension 0
- input_grad: bfloat16 [1024, 8192], P(('groups', 'outp'), 'inp'), parts along dimension 0
- sketches: float32 [8, 4096], P('groups'), parts along dimension 0
There are 2 independent parts, one for each index of `groups`. A program takes and returns all parts, laid end to end along the dimension named above; an argument that names none is the same for every part. Nothing has to cross between parts.
All inputs are finite; a program needn't handle non-finite values.
Results may differ from a plain program's by a relative error of at most 0.001.
Values may be sent and summed in bfloat16 or wider, within the bound.
No kernel may reach another device: no remote copies, remote signals or barrier semaphores. Data moves between devices by JAX's collectives and lax.ppermute only.
A program may use at most 128 MiB of HBM per device.

v0:
```python
import jax
import jax.numpy as jnp
from jax import lax
from jax.sharding import PartitionSpec as P

LEN = 128


def contract_last(left_side, right_side):
    return lax.dot_general(
        left_side, right_side, (((1,), (1,)), ((), ())), preferred_element_type=jnp.float32
    )


def body(inputs, cotangent, weight, in_sketch, out_sketch):
    partial_out = jnp.dot(
        lax.all_gather(inputs, "outp", axis=0, tiled=True),
        weight,
        preferred_element_type=jnp.float32,
    )
    outputs = lax.psum_scatter(partial_out, "inp", scatter_dimension=0, tiled=True).astype(
        jnp.bfloat16
    )
    total_rows = cotangent.shape[0] * lax.axis_size("inp")
    grad_full = lax.all_gather(cotangent, "inp", axis=0, tiled=True)
    summed = lax.psum_scatter(
        contract_last(grad_full, weight), "outp", scatter_dimension=0, tiled=True
    )
    input_grad = summed.astype(jnp.bfloat16)
    left_own = contract_last(inputs, in_sketch)
    right_own = contract_last(cotangent, out_sketch)
    width = in_sketch.shape[0]
    left_own = lax.psum(left_own, "inp")
    left = lax.all_gather(left_own, "outp", axis=0, tiled=True)
    right_own = lax.psum(right_own, "outp")
    right = lax.all_gather(right_own, "inp", axis=0, tiled=True)
    examples = total_rows // LEN
    left = left.reshape(examples, LEN, width)
    right = right.reshape(examples, LEN, width)
    sketches = jnp.einsum("stj,stk->sjk", left, right, precision=lax.Precision.HIGHEST)
    sketches = (sketches * (1.0 / LEN**0.5)).reshape(examples, width * width)
    return (outputs, input_grad, sketches)


def solution(mesh):
    placed = (
        P(("groups", "outp"), "inp"),
        P(("groups", "inp"), "outp"),
        P("inp", "outp"),
        P(None, "inp"),
        P(None, "outp"),
    )
    return jax.shard_map(
        body,
        mesh=mesh,
        in_specs=placed,
        out_specs=(P(("groups", "inp"), "outp"), P(("groups", "outp"), "inp"), P("groups", None)),
        check_vma=False,
    )
```

profile of v0, /device:TPU:0, one launch (start us, length us, event | category | flops | bytes accessed | tf_op | source)
XLA Modules:
  0.0 352.3 jit_solution(4610931127628651581)
XLA Ops:
  7.2 0.0 all-gather.5.cloned.1.call-start
  7.2 0.7 all-gather.5.cloned.1.call-update
  7.9 0.0 all-gather.3.cloned.1.call-start
  8.0 0.7 all-gather.3.cloned.1.call-update
  8.7 0.0 all-reduce.2.cloned.1.call-start
  8.7 2.9 fusion.5
  11.6 0.0 reduce-scatter.5.cloned.1.call-start
  11.7 13.5 %all-gather.5.cloned.1.call-done = bf16[512,3584]{1,0:T(8,128)(2,1)} async-done(((bf16[256,3584]{1,0:T(8,128)(2,1)}), bf16[512,3584]{1,0:T(8,128)(2,1)}) %all-gather.5.cloned.1.call-update) | async-done | bytes 3670032 | tf_op jit(solution)/shard_map/all_gather | solution.py:25
  25.2 21.6 %fusion.3 = f32[512,4096]{1,0:T(8,128)} fusion(bf16[512,3584]{1,0:T(8,128)(2,1)} %all-gather.5.cloned.1.call-done, bf16[4096,3584]{1,0:T(8,128)(2,1)} %param.7), kind=kOutput, calls=%fused_computation.4 | convolution fusion | flops 15032385536 | bytes 41418752 | tf_op jit(solution)/shard_map/dot_general | solution.py:10
  46.8 0.0 reduce-scatter.3.cloned.1.call-start
  46.9 55.0 %all-gather.3.cloned.1.call-done = bf16[512,4096]{1,0:T(8,128)(2,1)} async-done(((bf16[64,4096]{1,0:T(8,128)(2,1)}), bf16[512,4096]{1,0:T(8,128)(2,1)}) %all-gather.3.cloned.1.call-update) | async-done | bytes 4194320 | tf_op jit(solution)/shard_map/all_gather | solution.py:17
  101.9 23.8 %fusion.2 = f32[512,3584]{1,0:T(8,128)} fusion(bf16[512,4096]{1,0:T(8,128)(2,1)} %all-gather.3.cloned.1.call-done, bf16[4096,3584]{1,0:T(8,128)(2,1)} %param.7), kind=kOutput, calls=%fused_computation.3 | convolution fusion | flops 15032385536 | bytes 40894464 | tf_op jit(solution)/shard_map/dot_general | solution.py:16
  125.8 1.0 copy-done.1
  126.8 0.3 fusion.4
  127.1 3.4 psum.14
  130.5 30.9 %all_gather.14 = f32[512,64]{1,0:T(8,128)S(1)} all-gather(f32[64,64]{1,0:T(8,128)S(1)} %psum.14), channel_id=1, replica_groups=mesh['groups'=2,'outp'=8,'inp'=2] {'outp'}, dimensions={0}, use_global_device_ids=true | all-gather | bytes 147456 | tf_op jit(solution)/shard_map/all_gather | solution.py:34
  161.4 11.4 %all-reduce.2.cloned.1.call-done = f32[256,64]{0,1:T(8,128)} async-done(((f32[256,64]{0,1:T(8,128)}), f32[256,64]{0,1:T(8,128)}) %all-reduce.2.cloned.1.call-update) | async-done | bytes 65552 | tf_op jit(solution)/shard_map/psum | solution.py:35
  172.8 2.3 all_gather.15
  175.0 0.6 convolution_multiply_fusion
  175.6 0.7 reshape.17
  176.4 148.9 %reduce-scatter.5.cloned.1.call-done = f32[64,4096]{1,0:T(8,128)} async-done(((f32[512,4096]{1,0:T(8,128)}), f32[64,4096]{1,0:T(8,128)}) %reduce-scatter.5.cloned.1.call-update) | async-done | bytes 1048592 | tf_op jit(solution)/shard_map/reduce_scatter | solution.py:26
  325.2 2.1 convert_element_type.7
  327.3 15.1 %reduce-scatter.3.cloned.1.call-done = f32[256,3584]{1,0:T(8,128)} async-done(((f32[512,3584]{1,0:T(8,128)}), f32[256,3584]{1,0:T(8,128)}) %reduce-scatter.3.cloned.1.call-update) | async-done | bytes 3670032 | tf_op jit(solution)/shard_map/reduce_scatter | solution.py:21
  342.4 3.4 convert_element_type.6
  (6 shorter events, 0.1 us)
Async XLA Ops:
  7.2 118.6 %copy-start = (bf16[64,4096]{1,0:T(8,128)(2,1)S(1)}, bf16[64,4096]{1,0:T(8,128)(2,1)}, u32[]{:S(2)}) copy-start(bf16[64,4096]{1,0:T(8,128)(2,1)} %param.8) | copy-start | bytes 1572868
  7.2 18.0 %all-gather.5.cloned.1.call-start = ((), (), s32[]{:S(2)}) async-start(), calls=%async_computation.4 | async-start | bytes 5505024 | tf_op jit(solution)/shard_map/all_gather | solution.py:25
  7.9 94.0 %all-gather.3.cloned.1.call-start = ((), (), s32[]{:S(2)}) async-start(), calls=%async_computation.2 | async-start | bytes 4718592 | tf_op jit(solution)/shard_map/all_gather | solution.py:17
  8.7 164.1 %all-reduce.2.cloned.1.call-start = ((), (), s32[]{:S(2)}) async-start(), calls=%async_computation.6 | async-start | bytes 131072 | tf_op jit(solution)/shard_map/psum | solution.py:35
  11.6 313.6 %reduce-scatter.5.cloned.1.call-start = ((), (), s32[]{:S(2)}) async-start(), calls=%async_computation.5 | async-start | bytes 9437184 | tf_op jit(solution)/shard_map/reduce_scatter | solution.py:26
  46.8 295.5 %reduce-scatter.3.cloned.1.call-start = ((), (), s32[]{:S(2)}) async-start(), calls=%async_computation.3 | async-start | bytes 11010048 | tf_op jit(solution)/shard_map/reduce_scatter | solution.py:21
  125.7 1.0 copy-start.1
Sparse Core Ops, SparseCore 0:
  9.6 15.5 all-gather.4
  27.3 74.5 all-gather.2
  105.9 66.7 all-reduce.1
  176.2 148.9 reduce-scatter.4
  327.5 14.8 reduce-scatter.2
where the time goes:
time: 353 us; the launch traced here: 352 us
  waiting for transfers between devices  245 us (69%)
  matrix products  49.2 us (14%)
  blocking collectives  36.5 us (10%)
  between operations  13.8 us (4%)
  other arithmetic  5.52 us (2%)
    reduce_scatter x1, waiting for transfers between devices, body(): lax.psum_scatter(contract_last(grad_full, weight), 'outp', scatter_dimens...  149 us
    all_gather x1, waiting for transfers between devices, body(): lax.all_gather(inputs, 'outp', axis=0, tiled=True)  55 us
    all_gather x1, blocking collectives, body(): left = lax.all_gather(left_own, 'outp', axis=0, tiled=True)  30.9 us
    dot_general x3, matrix products, contract_last(): lax.dot_general(left_side, right_side, (((1,), (1,)), ((), ())), preferre...  24.8 us
    dot_general x1, matrix products, body(): jnp.dot(lax.all_gather(inputs, 'outp', axis=0, tiled=True), weight, prefe...  23.8 us
    reduce_scatter x1, waiting for transfers between devices, body(): lax.psum_scatter(partial_out, 'inp', scatter_dimension=0, tiled=True)  15.1 us
    all_gather x1, waiting for transfers between devices, body(): grad_full = lax.all_gather(cotangent, 'inp', axis=0, tiled=True)  13.5 us
    psum x1, waiting for transfers between devices, body(): right_own = lax.psum(right_own, 'outp')  11.4 us
  transfers between devices with their start and end apart: 5, of which 5 were waited for; matrix products, arithmetic and copies ran while one was open for 15% of the time, Pallas kernels for 0%

commit v1 on v0

v1 whole, which is shorter than its diff:
```python
import jax
import jax.numpy as jnp
from jax import lax
from jax.sharding import PartitionSpec as P

LEN = 128
FWD_PIECES = 7


def contract_last(left_side, right_side):
    return lax.dot_general(
        left_side, right_side, (((1,), (1,)), ((), ())), preferred_element_type=jnp.float32
    )


def body(inputs, cotangent, weight, in_sketch, out_sketch):
    n = lax.axis_size("outp")
    rows, feats = inputs.shape
    half = feats // 2
    me = lax.axis_index("outp")
    core = lax.axis_index("inp")
    ring = [k for k in range(n) if k % 2 == 0] + [k for k in reversed(range(n)) if k % 2 == 1]
    place = [ring.index(k) for k in range(n)]
    ring_arr = jnp.array(ring, jnp.int32)
    p = jnp.array(place, jnp.int32)[me]
    up = [(ring[k], ring[(k + 1) % n]) for k in range(n)]
    down = [(ring[(k + 1) % n], ring[k]) for k in range(n)]
    swap = [(0, 1), (1, 0)]

    def slot(offset):
        owner = ring_arr[lax.rem(p + offset + 2 * n, n)]
        return lax.rem(owner - core * (n // 2) + n, n) * rows

    grad_other = lax.ppermute(cotangent, "inp", swap)

    buf = jnp.zeros((n * rows, feats), inputs.dtype)
    buf = lax.dynamic_update_slice(buf, inputs, (slot(0), 0))
    a, b = inputs[:, :half], inputs[:, half:]
    for s in range(1, n):
        a = lax.ppermute(a, "outp", up)
        b = lax.ppermute(b, "outp", down)
        buf = lax.dynamic_update_slice(buf, a, (slot(-s), 0))
        buf = lax.dynamic_update_slice(buf, b, (slot(s), half))

    grad = jnp.concatenate([cotangent, grad_other], axis=0)
    right = lax.psum(contract_last(grad, out_sketch), "outp")
    g_up = contract_last(grad, weight[:half])
    g_down = contract_last(grad, weight[half:])

    a = lax.dynamic_slice(g_up, (slot(-1), 0), (rows, half))
    b = lax.dynamic_slice(g_down, (slot(1), 0), (rows, half))
    for s in range(2, n + 1):
        a = lax.ppermute(a, "outp", up)
        b = lax.ppermute(b, "outp", down)
        a = a + lax.dynamic_slice(g_up, (slot(-s), 0), (rows, half))
        b = b + lax.dynamic_slice(g_down, (slot(s), 0), (rows, half))
    input_grad = jnp.concatenate([a, b], axis=1).astype(jnp.bfloat16)

    mine = n * rows // 2
    cols = weight.shape[1] // FWD_PIECES
    outs = []
    for k in range(FWD_PIECES):
        w = weight[:, k * cols : (k + 1) * cols]
        send = jnp.dot(buf[mine:], w, preferred_element_type=jnp.float32)
        got = lax.ppermute(send, "inp", swap)
        own = jnp.dot(buf[:mine], w, preferred_element_type=jnp.float32)
        outs.append((own + got).astype(jnp.bfloat16))
    outputs = jnp.concatenate(outs, axis=1)

    width = in_sketch.shape[0]
    left = contract_last(buf, in_sketch)
    examples = n * rows // LEN
    left = left.reshape(examples, LEN, width)
    right = right.reshape(examples, LEN, width)
    part = jnp.einsum("stj,stk->sjk", left, right, precision=lax.Precision.HIGHEST)
    got = lax.ppermute(part, "inp", swap)
    total = part + jnp.roll(got, examples // 2, axis=0)
    total = jnp.where(core == 0, total, jnp.roll(total, examples // 2, axis=0))
    sketches = (total * (1.0 / LEN**0.5)).reshape(examples, width * width)
    return (outputs, input_grad, sketches)


def solution(mesh):
    placed = (
        P(("groups", "outp"), "inp"),
        P(("groups", "inp"), "outp"),
        P("inp", "outp"),
        P(None, "inp"),
        P(None, "outp"),
    )
    return jax.shard_map(
        body,
        mesh=mesh,
        in_specs=placed,
        out_specs=(P(("groups", "inp"), "outp"), P(("groups", "outp"), "inp"), P("groups", None)),
        check_vma=False,
    )
```

time: 353 us -> 326 us (0.924)
  waiting for transfers between devices: 245 us -> 154 us
  blocking collectives: 36.5 us -> 0 us
  matrix products: 49.2 us -> 85.5 us
  starting transfers between devices: 0.2 us -> 31.3 us
  between operations: 13.8 us -> 36.7 us
  local copies, waits for them, and re-layouts: 1.76 us -> 12.7 us
    reduce_scatter x2 -> x0, waiting for transfers between devices: 164 us -> none  [the longest x1 149 us: body(): lax.psum_scatter(contract_last(grad_full, weight), 'outp', scatter_dimens...]
    ppermute x0 -> x37, waiting for transfers between devices: none -> 85.9 us  [the longest x14 65.9 us: body(): a = lax.ppermute(a, 'outp', up)]
    all_gather x2 -> x0, waiting for transfers between devices: 68.6 us -> none  [the longest x1 55 us: body(): lax.all_gather(inputs, 'outp', axis=0, tiled=True)]
    psum x1, waiting for transfers between devices: 11.4 us -> 68.4 us  [body(): right = lax.psum(contract_last(grad, out_sketch), 'outp')]
    all_gather x2 -> x0, blocking collectives: 33.1 us -> none  [the longest x1 30.9 us: body(): left = lax.all_gather(left_own, 'outp', axis=0, tiled=True)]
    dot_general x1 -> x14, matrix products: 23.8 us -> 56.8 us  [the longest x7 30.7 us: body(): send = jnp.dot(buf[mine:], w, preferred_element_type=jnp.float32)]
    ppermute x0 -> x37, starting transfers between devices: none -> 31.2 us  [the longest x14 22.9 us: body(): a = lax.ppermute(a, 'outp', up)]
    convert_element_type x2 -> x0, other arithmetic: 5.52 us -> none  [the longest x1 3.45 us: body(): lax.psum_scatter(partial_out, 'inp', scatter_dimension=0, tiled=True)]
  transfers between devices with their start and end apart: 5 -> 38, of which waited for: 5 -> 18; matrix products, arithmetic and copies ran while one was open for 15% -> 20% of each run, Pallas kernels for 0% -> 0%
where the time goes in v1:
time: 326 us; the launch traced here: 324 us
  waiting for transfers between devices  154 us (47%)
  matrix products  85.5 us (26%)
  between operations  36.7 us (11%)
  starting transfers between devices  31.3 us (10%)
  local copies, waits for them, and re-layouts  12.7 us (4%)
  other arithmetic  3.96 us (1%)
    psum x1, waiting for transfers between devices, body(): right = lax.psum(contract_last(grad, out_sketch), 'outp')  68.4 us
    ppermute x14, waiting for transfers between devices, body(): a = lax.ppermute(a, 'outp', up)  65.9 us
    dot_general x7, matrix products, body(): send = jnp.dot(buf[mine:], w, preferred_element_type=jnp.float32)  30.7 us
    dot_general x4, matrix products, contract_last(): lax.dot_general(left_side, right_side, (((1,), (1,)), ((), ())), preferre...  27.5 us
    dot_general x7, matrix products, body(): own = jnp.dot(buf[:mine], w, preferred_element_type=jnp.float32)  26.1 us
    ppermute x14, starting transfers between devices, body(): a = lax.ppermute(a, 'outp', up)  22.9 us
    ppermute x14, waiting for transfers between devices, body(): b = lax.ppermute(b, 'outp', down)  20 us
    ppermute x14, starting transfers between devices, body(): b = lax.ppermute(b, 'outp', down)  7.22 us
  transfers between devices with their start and end apart: 38, of which 18 were waited for; matrix products, arithmetic and copies ran while one was open for 20% of the time, Pallas kernels for 0%

profile of v1, /device:TPU:0, one launch (start us, length us, event | category | flops | bytes accessed | tf_op | source)
XLA Modules:
  0.0 324.4 jit_solution(8669393583790411014)
XLA Ops:
  43.3 6.8 %collective-permute-done.2 = bf16[64,2048]{1,0:T(8,128)(2,1)S(1)} collective-permute-done((bf16[64,2048]{1,0:T(8,128)(2,1)S(1)}, bf16[64,2048]{1,0:T(8,128)(2,1)S(1)}, u32[]{:S(2)}, u32[]{:S(2)}) %collective-permute-start.2) | collective-permute-done | bytes 262176 | tf_op jit(solution)/shard_map/ppermute | solution.py:40
  52.2 6.0 %collective-permute-done.4 = bf16[64,2048]{1,0:T(8,128)(2,1)S(1)} collective-permute-done((bf16[64,2048]{1,0:T(8,128)(2,1)S(1)}, bf16[64,2048]{1,0:T(8,128)(2,1)S(1)}, u32[]{:S(2)}, u32[]{:S(2)}) %collective-permute-start.4) | collective-permute-done | bytes 262176 | tf_op jit(solution)/shard_map/ppermute | solution.py:40
  60.3 5.1 %collective-permute-done.6 = bf16[64,2048]{1,0:T(8,128)(2,1)S(1)} collective-permute-done((bf16[64,2048]{1,0:T(8,128)(2,1)S(1)}, bf16[64,2048]{1,0:T(8,128)(2,1)S(1)}, u32[]{:S(2)}, u32[]{:S(2)}) %collective-permute-start.6) | collective-permute-done | bytes 262176 | tf_op jit(solution)/shard_map/ppermute | solution.py:40
  67.5 4.7 %collective-permute-done.8 = bf16[64,2048]{1,0:T(8,128)(2,1)S(1)} collective-permute-done((bf16[64,2048]{1,0:T(8,128)(2,1)S(1)}, bf16[64,2048]{1,0:T(8,128)(2,1)S(1)}, u32[]{:S(2)}, u32[]{:S(2)}) %collective-permute-start.8) | collective-permute-done | bytes 262176 | tf_op jit(solution)/shard_map/ppermute | solution.py:40
  74.3 5.8 %collective-permute-done.10 = bf16[64,2048]{1,0:T(8,128)(2,1)S(1)} collective-permute-done((bf16[64,2048]{1,0:T(8,128)(2,1)S(1)}, bf16[64,2048]{1,0:T(8,128)(2,1)S(1)}, u32[]{:S(2)}, u32[]{:S(2)}) %collective-permute-start.10) | collective-permute-done | bytes 262176 | tf_op jit(solution)/shard_map/ppermute | solution.py:40
  82.3 12.4 %fusion.2 = f32[512,2048]{1,0:T(8,128)} fusion(bf16[512,3584]{1,0:T(8,128)(2,1)S(1)} %constant_dynamic-update-slice_fusion, bf16[4096,3584]{1,0:T(8,128)(2,1)} %param.9), kind=kOutput, calls=%fused_computation.2 | convolution fusion | flops 7516192768 | bytes 22544384 | tf_op jit(solution)/shard_map/dot_general | solution.py:11
  94.7 12.4 %fusion = f32[512,2048]{1,0:T(8,128)} fusion(bf16[512,3584]{1,0:T(8,128)(2,1)S(1)} %constant_dynamic-update-slice_fusion, bf16[4096,3584]{1,0:T(8,128)(2,1)} %param.9), kind=kOutput, calls=%fused_computation | convolution fusion | flops 7516192768 | bytes 22544384 | tf_op jit(solution)/shard_map/dot_general | solution.py:11
  107.2 5.8 %fusion.28 = f32[256,512]{1,0:T(8,128)} fusion(bf16[4096,3584]{1,0:T(8,128)(2,1)} %param.9, bf16[512,4096]{1,0:T(8,128)(2,1)S(1)} %constant_dynamic-update-slice_fusion.10), kind=kOutput, calls=%fused_computation.28 | convolution fusion | flops 1073741824 | bytes 6815744 | tf_op jit(solution)/shard_map/dot_general | solution.py:64
  113.0 4.3 %fusion.24 = f32[256,512]{1,0:T(8,128)} fusion(bf16[4096,3584]{1,0:T(8,128)(2,1)} %param.9, bf16[512,4096]{1,0:T(8,128)(2,1)S(1)} %constant_dynamic-update-slice_fusion.10), kind=kOutput, calls=%fused_computation.24 | convolution fusion | flops 1073741824 | bytes 6815744 | tf_op jit(solution)/shard_map/dot_general | solution.py:64
  117.3 4.3 %fusion.20 = f32[256,512]{1,0:T(8,128)} fusion(bf16[4096,3584]{1,0:T(8,128)(2,1)} %param.9, bf16[512,4096]{1,0:T(8,128)(2,1)S(1)} %constant_dynamic-update-slice_fusion.10), kind=kOutput, calls=%fused_computation.20 | convolution fusion | flops 1073741824 | bytes 6815744 | tf_op jit(solution)/shard_map/dot_general | solution.py:64
  121.6 4.3 %fusion.16 = f32[256,512]{1,0:T(8,128)} fusion(bf16[4096,3584]{1,0:T(8,128)(2,1)} %param.9, bf16[512,4096]{1,0:T(8,128)(2,1)S(1)} %constant_dynamic-update-slice_fusion.10), kind=kOutput, calls=%fused_computation.16 | convolution fusion | flops 1073741824 | bytes 6815744 | tf_op jit(solution)/shard_map/dot_general | solution.py:64
  125.9 4.3 %fusion.12 = f32[256,512]{1,0:T(8,128)} fusion(bf16[4096,3584]{1,0:T(8,128)(2,1)} %param.9, bf16[512,4096]{1,0:T(8,128)(2,1)S(1)} %constant_dynamic-update-slice_fusion.10), kind=kOutput, calls=%fused_computation.12 | convolution fusion | flops 1073741824 | bytes 6815744 | tf_op jit(solution)/shard_map/dot_general | solution.py:64
  130.2 4.3 %fusion.8 = f32[256,512]{1,0:T(8,128)} fusion(bf16[4096,3584]{1,0:T(8,128)(2,1)} %param.9, bf16[512,4096]{1,0:T(8,128)(2,1)S(1)} %constant_dynamic-update-slice_fusion.10), kind=kOutput, calls=%fused_computation.8 | convolution fusion | flops 1073741824 | bytes 6815744 | tf_op jit(solution)/shard_map/dot_general | solution.py:64
  144.3 68.4 %all-reduce.2.cloned.1.call-done = f32[4,128,64]{1,2,0:T(8,128)} async-done(((f32[4,128,64]{1,2,0:T(8,128)}), f32[4,128,64]{1,2,0:T(8,128)}) %all-reduce.2.cloned.1.call-update) | async-done | bytes 131088 | tf_op jit(solution)/shard_map/psum | solution.py:46
  219.1 10.6 %collective-permute-done.29 = f32[64,2048]{1,0:T(8,128)S(1)} collective-permute-done((f32[64,2048]{1,0:T(8,128)S(1)}, f32[64,2048]{1,0:T(8,128)S(1)}, u32[]{:S(2)}, u32[]{:S(2)}) %collective-permute-start.29) | collective-permute-done | bytes 524320 | tf_op jit(solution)/shard_map/ppermute | solution.py:54
  231.8 4.4 %fusion.74 = bf16[256,3584]{1,0:T(8,128)(2,1)S(1)} fusion(f32[256,512]{1,0:T(8,128)} %collective-permute-done.14, bf16[4096,3584]{1,0:T(8,128)(2,1)} %param.9, bf16[512,4096]{1,0:T(8,128)(2,1)} %copy-done.1), kind=kOutput, calls=%fused_computation.46 | convolution fusion | flops 1074003968 | bytes 7077888 | tf_op jit(solution)/shard_map/dot_general | solution.py:66
  237.2 4.1 %fusion.77 = bf16[256,3584]{1,0:T(8,128)(2,1)S(1)} fusion(bf16[256,3584]{1,0:T(8,128)(2,1)S(1)} %fusion.74, f32[256,512]{1,0:T(8,128)} %collective-permute-done.15, bf16[4096,3584]{1,0:T(8,128)(2,1)} %param.9, bf16[512,4096]{1,0:T(8,128)(2,1)S(1)} %copy-done.2), kind=kOutput, calls=%fused_computation.47 | convolution fusion | flops 1074003968 | bytes 7077888 | tf_op jit(solution)/shard_map/dot_general | solution.py:66
  241.2 4.0 %collective-permute-done.23 = f32[64,2048]{1,0:T(8,128)S(1)} collective-permute-done((f32[64,2048]{1,0:T(8,128)S(1)}, f32[64,2048]{1,0:T(8,128)S(1)}, u32[]{:S(2)}, u32[]{:S(2)}) %collective-permute-start.23) | collective-permute-done | bytes 524320 | tf_op jit(solution)/shard_map/ppermute | solution.py:53
  245.3 5.2 %collective-permute-done.30 = f32[64,2048]{1,0:T(8,128)S(1)} collective-permute-done((f32[64,2048]{1,0:T(8,128)S(1)}, f32[64,2048]{1,0:T(8,128)S(1)}, u32[]{:S(2)}, u32[]{:S(2)}) %collective-permute-start.30) | collective-permute-done | bytes 524320 | tf_op jit(solution)/shard_map/ppermute | solution.py:54
  256.4 7.6 %collective-permute-done.24 = f32[64,2048]{1,0:T(8,128)S(1)} collective-permute-done((f32[64,2048]{1,0:T(8,128)S(1)}, f32[64,2048]{1,0:T(8,128)S(1)}, u32[]{:S(2)}, u32[]{:S(2)}) %collective-permute-start.24) | collective-permute-done | bytes 524320 | tf_op jit(solution)/shard_map/ppermute | solution.py:53
  270.7 7.8 %collective-permute-done.25 = f32[64,2048]{1,0:T(8,128)S(1)} collective-permute-done((f32[64,2048]{1,0:T(8,128)S(1)}, f32[64,2048]{1,0:T(8,128)S(1)}, u32[]{:S(2)}, u32[]{:S(2)}) %collective-permute-start.25) | collective-permute-done | bytes 524320 | tf_op jit(solution)/shard_map/ppermute | solution.py:53
  284.2 6.9 %collective-permute-done.26 = f32[64,2048]{1,0:T(8,128)S(1)} collective-permute-done((f32[64,2048]{1,0:T(8,128)S(1)}, f32[64,2048]{1,0:T(8,128)S(1)}, u32[]{:S(2)}, u32[]{:S(2)}) %collective-permute-start.26) | collective-permute-done | bytes 524320 | tf_op jit(solution)/shard_map/ppermute | solution.py:53
  296.8 5.9 %collective-permute-done.27 = f32[64,2048]{1,0:T(8,128)S(1)} collective-permute-done((f32[64,2048]{1,0:T(8,128)S(1)}, f32[64,2048]{1,0:T(8,128)S(1)}, u32[]{:S(2)}, u32[]{:S(2)}) %collective-permute-start.27) | collective-permute-done | bytes 524320 | tf_op jit(solution)/shard_map/ppermute | solution.py:53
  308.7 5.3 %collective-permute-done.28 = f32[64,2048]{1,0:T(8,128)S(1)} collective-permute-done((f32[64,2048]{1,0:T(8,128)S(1)}, f32[64,2048]{1,0:T(8,128)S(1)}, u32[]{:S(2)}, u32[]{:S(2)}) %collective-permute-start.28) | collective-permute-done | bytes 524320 | tf_op jit(solution)/shard_map/ppermute | solution.py:53
  (136 shorter events, 77.1 us)
Async XLA Ops:
  7.2 205.5 %all-reduce.2.cloned.1.call-start = ((), (), s32[]{:S(2)}) async-start(), calls=%async_computation | async-start | bytes 262144 | tf_op jit(solution)/shard_map/psum | solution.py:46
  9.1 32.0 %collective-permute-start = (bf16[64,2048]{1,0:T(8,128)(2,1)}, bf16[64,2048]{1,0:T(8,128)(2,1)S(1)}, u32[]{:S(2)}, u32[]{:S(2)}) collective-permute-start(bf16[64,2048]{1,0:T(8,128)(2,1)} %get-tuple-element.4), channel_id=1, source_target_pairs={{0,4},{4,8},{8,12},{12,14},{14,10},{10,6},{6,2},{2,0},{1,5},{5,9},... | collective-permute-start | bytes 786440 | tf_op jit(solution)/shard_map/ppermute | solution.py:40
  12.2 31.0 %collective-permute-start.1 = (bf16[64,2048]{1,0:T(8,128)(2,1)}, bf16[64,2048]{1,0:T(8,128)(2,1)S(1)}, u32[]{:S(2)}, u32[]{:S(2)}) collective-permute-start(bf16[64,2048]{1,0:T(8,128)(2,1)} %get-tuple-element.3), channel_id=1, source_target_pairs={{4,0},{8,4},{12,8},{14,12},{10,14},{6,10},{2,6},{0,2},{5,1},{9,5},... | collective-permute-start | bytes 786440 | tf_op jit(solution)/shard_map/ppermute | solution.py:41
  12.2 70.0 %collective-permute-start.21 = (bf16[256,3584]{1,0:T(8,128)(2,1)}, bf16[256,3584]{1,0:T(8,128)(2,1)S(1)}, u32[]{:S(2)}, u32[]{:S(2)}) collective-permute-start(bf16[256,3584]{1,0:T(8,128)(2,1)} %param.8), channel_id=1, source_target_pairs={{0,1},{1,0},{2,3},{3,2},{4,5},{5,4},{6,7},{7,6},{8,9},{9,8},{10,11... | collective-permute-start | bytes 5505032 | tf_op jit(solution)/shard_map/ppermute | solution.py:34
  80.1 27.1 %collective-permute-start.12 = (bf16[64,2048]{1,0:T(8,128)(2,1)S(1)}, bf16[64,2048]{1,0:T(8,128)(2,1)S(1)}, u32[]{:S(2)}, u32[]{:S(2)}) collective-permute-start(bf16[64,2048]{1,0:T(8,128)(2,1)S(1)} %collective-permute-done.10), channel_id=1, source_target_pairs={{0,4},{4,8},{8,12},{12,14},{14,10},{10,6},{6,2},{2,0},{1,5},{5,9},... | collective-permute-start | bytes 786440 | tf_op jit(solution)/shard_map/ppermute | solution.py:40
  81.9 25.3 %collective-permute-start.13 = (bf16[64,2048]{1,0:T(8,128)(2,1)S(1)}, bf16[64,2048]{1,0:T(8,128)(2,1)S(1)}, u32[]{:S(2)}, u32[]{:S(2)}) collective-permute-start(bf16[64,2048]{1,0:T(8,128)(2,1)S(1)} %collective-permute-done.11), channel_id=1, source_target_pairs={{4,0},{8,4},{12,8},{14,12},{10,14},{6,10},{2,6},{0,2},{5,1},{9,5},... | collective-permute-start | bytes 786440 | tf_op jit(solution)/shard_map/ppermute | solution.py:41
  142.4 75.3 %collective-permute-start.22 = (f32[64,2048]{1,0:T(8,128)S(1)}, f32[64,2048]{1,0:T(8,128)S(1)}, u32[]{:S(2)}, u32[]{:S(2)}) collective-permute-start(f32[64,2048]{1,0:T(8,128)S(1)} %constant_dynamic-slice_fusion.1), channel_id=1, source_target_pairs={{0,4},{4,8},{8,12},{12,14},{14,10},{10,6},{6,2},{2,0},{1,5},{5,9},... | collective-permute-start | bytes 1572872 | tf_op jit(solution)/shard_map/ppermute | solution.py:53
  215.1 14.6 %collective-permute-start.29 = (f32[64,2048]{1,0:T(8,128)S(1)}, f32[64,2048]{1,0:T(8,128)S(1)}, u32[]{:S(2)}, u32[]{:S(2)}) collective-permute-start(f32[64,2048]{1,0:T(8,128)S(1)} %constant_dynamic-slice_fusion), channel_id=1, source_target_pairs={{4,0},{8,4},{12,8},{14,12},{10,14},{6,10},{2,6},{0,2},{5,1},{9,5},... | collective-permute-start | bytes 1572872 | tf_op jit(solution)/shard_map/ppermute | solution.py:54
  216.2 14.7 %collective-permute-start.14 = (f32[256,512]{1,0:T(8,128)}, f32[256,512]{1,0:T(8,128)}, u32[]{:S(2)}, u32[]{:S(2)}) collective-permute-start(f32[256,512]{1,0:T(8,128)} %fusion.28), channel_id=1, source_target_pairs={{0,1},{1,0},{2,3},{3,2},{4,5},{5,4},{6,7},{7,6},{8,9},{9,8},{10,11... | collective-permute-start | bytes 1572872 | tf_op jit(solution)/shard_map/ppermute | solution.py:65
  216.4 19.9 %collective-permute-start.15 = (f32[256,512]{1,0:T(8,128)}, f32[256,512]{1,0:T(8,128)}, u32[]{:S(2)}, u32[]{:S(2)}) collective-permute-start(f32[256,512]{1,0:T(8,128)} %fusion.24), channel_id=1, source_target_pairs={{0,1},{1,0},{2,3},{3,2},{4,5},{5,4},{6,7},{7,6},{8,9},{9,8},{10,11... | collective-permute-start | bytes 1572872 | tf_op jit(solution)/shard_map/ppermute | solution.py:65
  216.7 35.1 %collective-permute-start.16 = (f32[256,512]{1,0:T(8,128)}, f32[256,512]{1,0:T(8,128)}, u32[]{:S(2)}, u32[]{:S(2)}) collective-permute-start(f32[256,512]{1,0:T(8,128)} %fusion.20), channel_id=1, source_target_pairs={{0,1},{1,0},{2,3},{3,2},{4,5},{5,4},{6,7},{7,6},{8,9},{9,8},{10,11... | collective-permute-start | bytes 1572872 | tf_op jit(solution)/shard_map/ppermute | solution.py:65
  217.7 48.6 %collective-permute-start.17 = (f32[256,512]{1,0:T(8,128)}, f32[256,512]{1,0:T(8,128)S(1)}, u32[]{:S(2)}, u32[]{:S(2)}) collective-permute-start(f32[256,512]{1,0:T(8,128)} %fusion.16), channel_id=1, source_target_pairs={{0,1},{1,0},{2,3},{3,2},{4,5},{5,4},{6,7},{7,6},{8,9},{9,8},{10,11... | collective-permute-start | bytes 1572872 | tf_op jit(solution)/shard_map/ppermute | solution.py:65
  229.7 51.0 %collective-permute-start.18 = (f32[256,512]{1,0:T(8,128)}, f32[256,512]{1,0:T(8,128)S(1)}, u32[]{:S(2)}, u32[]{:S(2)}) collective-permute-start(f32[256,512]{1,0:T(8,128)} %fusion.12), channel_id=1, source_target_pairs={{0,1},{1,0},{2,3},{3,2},{4,5},{5,4},{6,7},{7,6},{8,9},{9,8},{10,11... | collective-permute-start | bytes 1572872 | tf_op jit(solution)/shard_map/ppermute | solution.py:65
  230.8 14.4 %collective-permute-start.23 = (f32[64,2048]{1,0:T(8,128)S(1)}, f32[64,2048]{1,0:T(8,128)S(1)}, u32[]{:S(2)}, u32[]{:S(2)}) collective-permute-start(f32[64,2048]{1,0:T(8,128)S(1)} %dynamic-slice_add_fusion.11), channel_id=1, source_target_pairs={{0,4},{4,8},{8,12},{12,14},{14,10},{10,6},{6,2},{2,0},{1,5},{5,9},... | collective-permute-start | bytes 1572872 | tf_op jit(solution)/shard_map/ppermute | solution.py:53
  236.3 14.3 %collective-permute-start.30 = (f32[64,2048]{1,0:T(8,128)S(1)}, f32[64,2048]{1,0:T(8,128)S(1)}, u32[]{:S(2)}, u32[]{:S(2)}) collective-permute-start(f32[64,2048]{1,0:T(8,128)S(1)} %dynamic-slice_add_fusion.5), channel_id=1, source_target_pairs={{4,0},{8,4},{12,8},{14,12},{10,14},{6,10},{2,6},{0,2},{5,1},{9,5},... | collective-permute-start | bytes 1572872 | tf_op jit(solution)/shard_map/ppermute | solution.py:54
  245.2 48.1 %collective-permute-start.19 = (f32[256,512]{1,0:T(8,128)S(1)}, f32[256,512]{1,0:T(8,128)S(1)}, u32[]{:S(2)}, u32[]{:S(2)}) collective-permute-start(f32[256,512]{1,0:T(8,128)S(1)} %copy-done.8), channel_id=1, source_target_pairs={{0,1},{1,0},{2,3},{3,2},{4,5},{5,4},{6,7},{7,6},{8,9},{9,8},{10,11... | collective-permute-start | bytes 1572872 | tf_op jit(solution)/shard_map/ppermute | solution.py:65
  250.5 13.4 %collective-permute-start.24 = (f32[64,2048]{1,0:T(8,128)S(1)}, f32[64,2048]{1,0:T(8,128)S(1)}, u32[]{:S(2)}, u32[]{:S(2)}) collective-permute-start(f32[64,2048]{1,0:T(8,128)S(1)} %dynamic-slice_add_fusion.10), channel_id=1, source_target_pairs={{0,4},{4,8},{8,12},{12,14},{14,10},{10,6},{6,2},{2,0},{1,5},{5,9},... | collective-permute-start | bytes 1572872 | tf_op jit(solution)/shard_map/ppermute | solution.py:53
  251.7 13.3 %collective-permute-start.31 = (f32[64,2048]{1,0:T(8,128)S(1)}, f32[64,2048]{1,0:T(8,128)S(1)}, u32[]{:S(2)}, u32[]{:S(2)}) collective-permute-start(f32[64,2048]{1,0:T(8,128)S(1)} %dynamic-slice_add_fusion.4), channel_id=1, source_target_pairs={{4,0},{8,4},{12,8},{14,12},{10,14},{6,10},{2,6},{0,2},{5,1},{9,5},... | collective-permute-start | bytes 1572872 | tf_op jit(solution)/shard_map/ppermute | solution.py:54
  263.9 41.2 %collective-permute-start.20 = (f32[256,512]{1,0:T(8,128)S(1)}, f32[256,512]{1,0:T(8,128)S(1)}, u32[]{:S(2)}, u32[]{:S(2)}) collective-permute-start(f32[256,512]{1,0:T(8,128)S(1)} %fusion.4), channel_id=1, source_target_pairs={{0,1},{1,0},{2,3},{3,2},{4,5},{5,4},{6,7},{7,6},{8,9},{9,8},{10,11... | collective-permute-start | bytes 1572872 | tf_op jit(solution)/shard_map/ppermute | solution.py:65
  265.0 13.4 %collective-permute-start.25 = (f32[64,2048]{1,0:T(8,128)S(1)}, f32[64,2048]{1,0:T(8,128)S(1)}, u32[]{:S(2)}, u32[]{:S(2)}) collective-permute-start(f32[64,2048]{1,0:T(8,128)S(1)} %dynamic-slice_add_fusion.9), channel_id=1, source_target_pairs={{0,4},{4,8},{8,12},{12,14},{14,10},{10,6},{6,2},{2,0},{1,5},{5,9},... | collective-permute-start | bytes 1572872 | tf_op jit(solution)/shard_map/ppermute | solution.py:53
  266.4 13.4 %collective-permute-start.32 = (f32[64,2048]{1,0:T(8,128)S(1)}, f32[64,2048]{1,0:T(8,128)S(1)}, u32[]{:S(2)}, u32[]{:S(2)}) collective-permute-start(f32[64,2048]{1,0:T(8,128)S(1)} %dynamic-slice_add_fusion.3), channel_id=1, source_target_pairs={{4,0},{8,4},{12,8},{14,12},{10,14},{6,10},{2,6},{0,2},{5,1},{9,5},... | collective-permute-start | bytes 1572872 | tf_op jit(solution)/shard_map/ppermute | solution.py:54
  278.5 12.6 %collective-permute-start.26 = (f32[64,2048]{1,0:T(8,128)S(1)}, f32[64,2048]{1,0:T(8,128)S(1)}, u32[]{:S(2)}, u32[]{:S(2)}) collective-permute-start(f32[64,2048]{1,0:T(8,128)S(1)} %dynamic-slice_add_fusion.8), channel_id=1, source_target_pairs={{0,4},{4,8},{8,12},{12,14},{14,10},{10,6},{6,2},{2,0},{1,5},{5,9},... | collective-permute-start | bytes 1572872 | tf_op jit(solution)/shard_map/ppermute | solution.py:53
  279.8 12.6 %collective-permute-start.33 = (f32[64,2048]{1,0:T(8,128)S(1)}, f32[64,2048]{1,0:T(8,128)S(1)}, u32[]{:S(2)}, u32[]{:S(2)}) collective-permute-start(f32[64,2048]{1,0:T(8,128)S(1)} %dynamic-slice_add_fusion.2), channel_id=1, source_target_pairs={{4,0},{8,4},{12,8},{14,12},{10,14},{6,10},{2,6},{0,2},{5,1},{9,5},... | collective-permute-start | bytes 1572872 | tf_op jit(solution)/shard_map/ppermute | solution.py:54
  292.5 12.5 %collective-permute-start.34 = (f32[64,2048]{1,0:T(8,128)S(1)}, f32[64,2048]{1,0:T(8,128)S(1)}, u32[]{:S(2)}, u32[]{:S(2)}) collective-permute-start(f32[64,2048]{1,0:T(8,128)S(1)} %dynamic-slice_add_fusion.1), channel_id=1, source_target_pairs={{4,0},{8,4},{12,8},{14,12},{10,14},{6,10},{2,6},{0,2},{5,1},{9,5},... | collective-permute-start | bytes 1572872 | tf_op jit(solution)/shard_map/ppermute | solution.py:54
  (24 other events, 383.9 us)
Sparse Core Ops, SparseCore 0:
  141.5 71.1 all-reduce.1

commit v2 on v0

v2 whole, which is shorter than its diff:
```python
import functools

import jax
import jax.numpy as jnp
from jax import lax
from jax.experimental import pallas as pl
from jax.experimental.pallas import tpu as pltpu
from jax.sharding import PartitionSpec as P

LEN = 128
LANES = 128
BLK = 16
SPAN = 248.0
SHIFT = 124.0
Y_FIRST = 2048
F_TILE = 512
H_TILE = 512
MIB = 1 << 20


def pick(extent, cap):
    best = LANES
    for t in range(LANES, min(cap, extent) + 1, LANES):
        if extent % t == 0:
            best = t
    return best


def contract_last(a, b):
    return lax.dot_general(a, b, (((1,), (1,)), ((), ())), preferred_element_type=jnp.float32)


def params(mib):
    return pltpu.CompilerParams(vmem_limit_bytes=mib * MIB)


def cost(flops, nbytes):
    return pl.CostEstimate(flops=flops, bytes_accessed=nbytes, transcendentals=0)


def encode_rows(tiles, msg, at):
    top = jnp.max(jnp.abs(tiles[0]), axis=1, keepdims=True)
    for v in tiles[1:]:
        top = jnp.maximum(top, jnp.max(jnp.abs(v), axis=1, keepdims=True))
    scale = jnp.maximum(top * 1.004, 2.0**-110).astype(jnp.bfloat16).astype(jnp.float32)
    gain = SPAN / scale
    col = 0
    for v in tiles:
        w = jnp.exp2(jnp.abs(v) * gain - SHIFT)
        msg[at, col : col + v.shape[1]] = jnp.where(v < 0, -w, w).astype(jnp.bfloat16)
        col += v.shape[1]
    msg[at, col : col + LANES] = jnp.broadcast_to(scale, (BLK, LANES)).astype(jnp.bfloat16)


def decode_rows(msg, at, tile, count):
    scale = msg[at, tile * count : tile * count + LANES].astype(jnp.float32)[:, :1] * (1.0 / SPAN)
    out = []
    for t in range(count):
        w = msg[at, t * tile : (t + 1) * tile].astype(jnp.float32)
        a = (jnp.log2(jnp.maximum(jnp.abs(w), 2.0**-SHIFT)) + SHIFT) * scale
        out.append(jnp.where(w < 0, -a, a))
    return out


def backward(idx, own, oth, w, count, tile, first, sketch, rows, nz, y_first):
    half, hidden = own.shape
    zh = nz // 2
    grown = rows if y_first else 2 * rows
    width = count * tile

    def kernel(idx, own, oth, w, *rest):
        if y_first:
            sk, msg, keep, right, total = rest
        else:
            total, up, down = rest
        j = pl.program_id(0)
        z, y, core = idx[0], idx[1], idx[2]
        total[j, core] = contract_last(own[...], w[...])
        total[j, 1 - core] = contract_last(oth[...], w[...])
        if y_first:

            @pl.when(j == 0)
            def _():
                right[core] = contract_last(own[...], sk[...])
                right[1 - core] = contract_last(oth[...], sk[...])

            @pl.when(j == count - 1)
            def _():
                @pl.loop(0, nz * rows // BLK)
                def _(b):
                    zz, off = b // (rows // BLK), (b % (rows // BLK)) * BLK
                    base = (zz % zh) * 2 * rows + off
                    away = pl.ds(pl.multiple_of(base + (1 - y) * rows, BLK), BLK)
                    here = pl.ds(pl.multiple_of(base + y * rows, BLK), BLK)
                    at = pl.ds(pl.multiple_of(b * BLK, BLK), BLK)
                    encode_rows([total[t, zz // zh, away, :] for t in range(count)], msg, at)
                    for t in range(count):
                        keep[t, zz, pl.ds(pl.multiple_of(off, BLK), BLK), :] = total[
                            t, zz // zh, here, :
                        ]

        else:

            @pl.when(j == count - 1)
            def _():
                for msg, far in ((up, z + nz - 1), (down, z - nz + 1)):
                    zz = jnp.clip(far, 0, nz - 1)

                    @pl.loop(0, grown // BLK)
                    def _(b):
                        at = pl.ds(pl.multiple_of(b * BLK, BLK), BLK)
                        src = pl.ds(pl.multiple_of((zz % zh) * grown + b * BLK, BLK), BLK)
                        encode_rows([total[t, zz // zh, src, :] for t in range(count)], msg, at)

    once = pl.Buffered(1)
    whole = lambda *shape: pl.BlockSpec(shape, lambda j, s: (0,) * len(shape))
    in_specs = [
        pl.BlockSpec((half, hidden), lambda j, s: (0, 0), pipeline_mode=once),
        pl.BlockSpec((half, hidden), lambda j, s: (0, 0), pipeline_mode=once),
        pl.BlockSpec((tile, hidden), lambda j, s: (first + j, 0)),
    ]
    total_shape = (count, 2, half, tile)
    msg_shape = lambda r: jax.ShapeDtypeStruct((r, width + LANES), jnp.bfloat16)
    args = [idx, own, oth, w]
    if y_first:
        in_specs.append(whole(*sketch.shape))
        args.append(sketch)
        out_shape = [
            msg_shape(nz * rows),
            jax.ShapeDtypeStruct((count, nz, rows, tile), jnp.float32),
            jax.ShapeDtypeStruct((2, half, sketch.shape[0]), jnp.float32),
        ]
        scratch = [pltpu.VMEM(total_shape, jnp.float32)]
    else:
        out_shape = [
            jax.ShapeDtypeStruct(total_shape, jnp.float32),
            msg_shape(grown),
            msg_shape(grown),
        ]
        scratch = []
    return pl.pallas_call(
        kernel,
        out_shape=out_shape,
        grid_spec=pltpu.PrefetchScalarGridSpec(
            num_scalar_prefetch=1,
            grid=(count,),
            in_specs=in_specs,
            out_specs=[whole(*o.shape) for o in out_shape],
            scratch_shapes=scratch,
        ),
        compiler_params=params(40),
        cost_estimate=cost(4 * half * hidden * width, 2 * hidden * width + 16 * half * width),
        name="backward_y" if y_first else "backward_z",
    )(*args)


def local_call(kernel, idx, args, out_shape, name, specs=None, mib=16):
    whole = lambda shape: pl.BlockSpec(shape, lambda i, s: (0,) * len(shape))
    specs = specs or [whole(a.shape) for a in args]
    nbytes = sum(a.size * a.dtype.itemsize for a in args) + sum(
        o.size * o.dtype.itemsize for o in out_shape
    )
    return pl.pallas_call(
        kernel,
        out_shape=out_shape,
        grid_spec=pltpu.PrefetchScalarGridSpec(
            num_scalar_prefetch=1,
            grid=(1,),
            in_specs=specs,
            out_specs=[whole(o.shape) for o in out_shape],
        ),
        compiler_params=params(mib),
        cost_estimate=cost(0, nbytes),
        name=name,
    )(idx, *args)


def after_y(idx, keep, got):
    count, nz, rows, tile = keep.shape

    def kernel(idx, keep, got, total, up, down):
        z = idx[0]

        @pl.loop(0, nz * rows // BLK)
        def _(b):
            zz = b // (rows // BLK)
            off = pl.ds(pl.multiple_of((b % (rows // BLK)) * BLK, BLK), BLK)
            plus = decode_rows(got, pl.ds(pl.multiple_of(b * BLK, BLK), BLK), tile, count)
            for t in range(count):
                total[t, zz, off, :] = keep[t, zz, off, :] + plus[t]

        for msg, far in ((up, z + nz - 1), (down, z - nz + 1)):
            zz = jnp.clip(far, 0, nz - 1)

            @pl.loop(0, rows // BLK)
            def _(b):
                at = pl.ds(pl.multiple_of(b * BLK, BLK), BLK)
                encode_rows([total[t, zz, at, :] for t in range(count)], msg, at)

    msg = jax.ShapeDtypeStruct((rows, count * tile + LANES), jnp.bfloat16)
    out = [jax.ShapeDtypeStruct(keep.shape, jnp.float32), msg, msg]
    return local_call(kernel, idx, [keep, got], out, "after_y", mib=24)


def line_step(idx, total, up_got, down_got, reach):
    count, nz, rows, tile = total.shape

    def kernel(idx, up_total, down_total, up_got, down_got, up, down):
        for part, got, msg in ((up_total, up_got, up), (down_total, down_got, down)):

            @pl.loop(0, rows // BLK)
            def _(b):
                at = pl.ds(pl.multiple_of(b * BLK, BLK), BLK)
                plus = decode_rows(got, at, tile, count)
                encode_rows([part[t, 0, at, :] + plus[t] for t in range(count)], msg, at)

    def far(step):
        return pl.BlockSpec(
            (count, 1, rows, tile), lambda i, s: (0, jnp.clip(s[0] + step, 0, nz - 1), 0, 0)
        )

    full = pl.BlockSpec(up_got.shape, lambda i, s: (0, 0))
    msg = jax.ShapeDtypeStruct(up_got.shape, jnp.bfloat16)
    return local_call(
        kernel,
        idx,
        [total, total, up_got, down_got],
        [msg, msg],
        "line_step",
        specs=[far(reach), far(-reach), full, full],
    )


def line_end(idx, total, up_got, down_got, split):
    count, nz, rows, tile = total.shape
    width = count * tile
    mine = rows // 2 if split else rows

    def kernel(idx, part, up_got, down_got, *outs):
        y = idx[1]

        def summed(at):
            a = decode_rows(up_got, at, tile, count)
            b = decode_rows(down_got, at, tile, count)
            return [part[t, 0, at, :] + a[t] + b[t] for t in range(count)]

        @pl.loop(0, mine // BLK)
        def _(b):
            at = pl.ds(pl.multiple_of(b * BLK, BLK), BLK)
            if split:
                msg, keep = outs
                away = pl.ds(pl.multiple_of((1 - y) * mine + b * BLK, BLK), BLK)
                here = pl.ds(pl.multiple_of(y * mine + b * BLK, BLK), BLK)
                encode_rows(summed(away), msg, at)
                for t, v in enumerate(summed(here)):
                    keep[at, t * tile : (t + 1) * tile] = v
            else:
                for t, v in enumerate(summed(at)):
                    outs[0][at, t * tile : (t + 1) * tile] = v.astype(jnp.bfloat16)

    if split:
        out = [
            jax.ShapeDtypeStruct((mine, width + LANES), jnp.bfloat16),
            jax.ShapeDtypeStruct((mine, width), jnp.float32),
        ]
    else:
        out = [jax.ShapeDtypeStruct((mine, width), jnp.bfloat16)]
    own = pl.BlockSpec((count, 1, rows, tile), lambda i, s: (0, s[0], 0, 0))
    full = pl.BlockSpec(up_got.shape, lambda i, s: (0, 0))
    return local_call(
        kernel, idx, [total, up_got, down_got], out, "line_end", specs=[own, full, full]
    )


def finish_grad(idx, done, keep, got):
    rows, first = done.shape
    width = keep.shape[1]
    tile = pick(width, F_TILE)

    def kernel(idx, done, keep, got, out):
        out[:, :first] = done[...]

        @pl.loop(0, rows // BLK)
        def _(b):
            at = pl.ds(pl.multiple_of(b * BLK, BLK), BLK)
            for t, v in enumerate(decode_rows(got, at, tile, width // tile)):
                lo = t * tile
                out[at, first + lo : first + lo + tile] = (
                    keep[at, lo : lo + tile] + v
                ).astype(jnp.bfloat16)

    out = [jax.ShapeDtypeStruct((rows, first + width), jnp.bfloat16)]
    return local_call(kernel, idx, [done, keep, got], out, "finish_grad")[0]


def forward(idx, blocks, w, sketch):
    feats, hidden = w.shape
    part = [b.shape[0] // 2 for b in blocks]
    send_rows = sum(part)
    tile = pick(hidden, H_TILE)
    width = sketch.shape[0]

    def kernel(idx, *refs):
        k = 2 * len(blocks)
        xs = refs[:k]
        w, sk, send, keep, left, x = refs[k:]

        @pl.when(pl.program_id(0) == 0)
        def _():
            row = 0
            for ref in xs:
                x[row : row + ref.shape[0], :] = ref[...]
                row += ref.shape[0]
            left[...] = contract_last(x[...], sk[...])

        t = jnp.dot(x[...], w[...], preferred_element_type=jnp.float32)
        send[...] = t[:send_rows]
        keep[...] = t[send_rows:]

    once = pl.Buffered(1)
    specs = [
        pl.BlockSpec((r, feats), lambda j, s: (1 - s[2], 0), pipeline_mode=once) for r in part
    ] + [pl.BlockSpec((r, feats), lambda j, s: (s[2], 0), pipeline_mode=once) for r in part]
    specs += [
        pl.BlockSpec((feats, tile), lambda j, s: (0, j)),
        pl.BlockSpec((width, feats), lambda j, s: (0, 0), pipeline_mode=once),
    ]
    out = jax.ShapeDtypeStruct((send_rows, hidden), jnp.float32)
    column = pl.BlockSpec((send_rows, tile), lambda j, s: (0, j))
    return pl.pallas_call(
        kernel,
        out_shape=[out, out, jax.ShapeDtypeStruct((2 * send_rows, width), jnp.float32)],
        grid_spec=pltpu.PrefetchScalarGridSpec(
            num_scalar_prefetch=1,
            grid=(hidden // tile,),
            in_specs=specs,
            out_specs=[
                column,
                column,
                pl.BlockSpec((2 * send_rows, width), lambda j, s: (0, 0)),
            ],
            scratch_shapes=[pltpu.VMEM((2 * send_rows, feats), jnp.bfloat16)],
        ),
        compiler_params=params(32),
        cost_estimate=cost(
            4 * send_rows * feats * hidden, 2 * feats * hidden + 8 * send_rows * hidden
        ),
        name="forward",
    )(idx, *blocks, *blocks, w, sketch)


def places(rows, a_rows, nz):
    out = []
    zh, b_rows = nz // 2, rows - a_rows
    if a_rows:
        for same in (True, False):
            for zz in range(zh):
                out.append((0, ((0 if same else zh) + zz) * a_rows, zz, same, 0, a_rows))
    last = 1 if a_rows else 0
    for zz in range(zh):
        for same in (True, False):
            at = (2 * zz + (0 if same else 1)) * b_rows
            out.append((last, at, zz, same, a_rows, b_rows))
    return out


def combine(idx, pairs, rows, a_rows, nz):
    hidden = pairs[0][0].shape[1]
    tile = pick(hidden, H_TILE)
    half = nz * rows

    def kernel(idx, *refs):
        out = refs[-1]
        y = idx[1]
        for piece, at, zz, same, off, count in places(rows, a_rows, nz):
            yy = y if same else 1 - y
            keep, got = refs[2 * piece], refs[2 * piece + 1]
            to = pl.ds(pl.multiple_of(zz * 2 * rows + yy * rows + off, BLK), count)
            out[to, :] = (keep[at : at + count, :] + got[at : at + count, :]).astype(jnp.bfloat16)

    flat = [a for pair in pairs for a in pair]
    return pl.pallas_call(
        kernel,
        out_shape=jax.ShapeDtypeStruct((half, hidden), jnp.bfloat16),
        grid_spec=pltpu.PrefetchScalarGridSpec(
            num_scalar_prefetch=1,
            grid=(hidden // tile,),
            in_specs=[pl.BlockSpec((a.shape[0], tile), lambda j, s: (0, j)) for a in flat],
            out_specs=pl.BlockSpec((half, tile), lambda j, s: (0, j)),
        ),
        compiler_params=params(16),
        cost_estimate=cost(0, 10 * half * hidden),
        name="combine",
    )(idx, *flat)


def sketch_part(idx, lefts, right, rows, a_rows, nz):
    width = right.shape[1]
    tokens = right.shape[0]
    half = tokens // 2
    examples = tokens // LEN

    def kernel(idx, *refs):
        right, out, left = refs[-3:]
        y, core = idx[1], idx[2]
        for side in (0, 1):
            base = (1 - core if side == 0 else core) * half
            for piece, at, zz, same, off, count in places(rows, a_rows, nz):
                yy = y if same else 1 - y
                to = pl.ds(pl.multiple_of(base + zz * 2 * rows + yy * rows + off, 8), count)
                src = refs[piece]
                lo = side * (src.shape[0] // 2) + at
                left[to, :] = src[lo : lo + count, :]
        for e in range(examples):
            span = slice(e * LEN, (e + 1) * LEN)
            out[e] = lax.dot_general(
                left[span, :],
                right[span, :],
                (((0,), (0,)), ((), ())),
                precision=lax.Precision.HIGHEST,
                preferred_element_type=jnp.float32,
            )

    args = list(lefts) + [right]
    whole = lambda shape: pl.BlockSpec(shape, lambda i, s: (0,) * len(shape))
    return pl.pallas_call(
        kernel,
        out_shape=jax.ShapeDtypeStruct((examples, width, width), jnp.float32),
        grid_spec=pltpu.PrefetchScalarGridSpec(
            num_scalar_prefetch=1,
            grid=(1,),
            in_specs=[whole(a.shape) for a in args],
            out_specs=whole((examples, width, width)),
            scratch_shapes=[pltpu.VMEM((tokens, width), jnp.float32)],
        ),
        compiler_params=params(16),
        name="sketch_part",
    )(idx, *args)


def body(inputs, cotangent, weight, in_sketch, out_sketch):
    n = lax.axis_size("outp")
    nz = n // 2
    rows, feats = inputs.shape
    me = lax.axis_index("outp")
    idx = jnp.stack([me // 2, me % 2, lax.axis_index("inp")]).astype(jnp.int32)
    swap = [(0, 1), (1, 0)]
    across = [(d, d ^ 1) for d in range(n)]
    lines = [[2 * z + y for z in range(nz)] for y in range(2)]

    def up(reach):
        return [(2 * z + y, 2 * z + 2 + y) for z in range(nz - reach) for y in range(2)]

    def down(reach):
        return [(2 * z + y, 2 * z - 2 + y) for z in range(reach, nz) for y in range(2)]

    def along_z(x):
        return lax.all_gather(x, "outp", axis=0, tiled=True, axis_index_groups=lines)

    a_rows = rows // 2 if (rows // 2) % BLK == 0 else 0
    rest = inputs[a_rows:]
    rest = jnp.concatenate([rest, lax.ppermute(rest, "outp", across)], axis=0)
    grad_other = lax.ppermute(cotangent, "inp", swap)
    groups = []
    if a_rows:
        near = along_z(inputs[:a_rows])
        groups.append([near, lax.ppermute(near, "outp", across)])
    groups.append([along_z(rest)])

    tile = pick(min(Y_FIRST, feats - Y_FIRST), F_TILE)
    c1, c2 = Y_FIRST // tile, (feats - Y_FIRST) // tile
    back = functools.partial(
        backward, idx, cotangent, grad_other, weight, tile=tile, rows=rows, nz=nz
    )
    msg, keep, right = back(count=c1, first=0, sketch=out_sketch, y_first=True)
    got1 = lax.ppermute(msg, "outp", across)
    total2, u2, d2 = back(count=c2, first=c1, sketch=None, y_first=False)
    total2 = total2.reshape(c2, nz, 2 * rows, tile)

    k = 1
    while k < n:
        right = right + lax.ppermute(right, "outp", [(d, d ^ k) for d in range(n)])
        k *= 2

    total1 = None
    for reach in range(nz - 1, 0, -1):
        u2 = lax.ppermute(u2, "outp", up(reach))
        d2 = lax.ppermute(d2, "outp", down(reach))
        if total1 is None:
            total1, u1, d1 = after_y(idx, keep, got1)
        u1 = lax.ppermute(u1, "outp", up(reach))
        d1 = lax.ppermute(d1, "outp", down(reach))
        if reach > 1:
            u2, d2 = line_step(idx, total2, u2, d2, reach - 1)
            u1, d1 = line_step(idx, total1, u1, d1, reach - 1)
    msg2, keep2 = line_end(idx, total2, u2, d2, True)
    got2 = lax.ppermute(msg2, "outp", across)
    (done1,) = line_end(idx, total1, u1, d1, False)
    input_grad = finish_grad(idx, done1, keep2, got2)

    pairs, lefts = [], []
    for blocks in groups:
        send, own, left = forward(idx, blocks, weight, in_sketch)
        pairs.append((own, lax.ppermute(send, "inp", swap)))
        lefts.append(left)
    outputs = combine(idx, pairs, rows, a_rows, nz)
    width = in_sketch.shape[0]
    part = sketch_part(idx, lefts, right.reshape(n * rows, width), rows, a_rows, nz)
    part = (part + lax.ppermute(part, "inp", swap)) * (1.0 / LEN**0.5)
    sketches = part.reshape(n * rows // LEN, width * width)
    return (outputs, input_grad, sketches)


def solution(mesh):
    placed = (
        P(("groups", "outp"), "inp"),
        P(("groups", "inp"), "outp"),
        P("inp", "outp"),
        P(None, "inp"),
        P(None, "outp"),
    )
    return jax.shard_map(
        body,
        mesh=mesh,
        in_specs=placed,
        out_specs=(P(("groups", "inp"), "outp"), P(("groups", "outp"), "inp"), P("groups", None)),
        check_vma=False,
    )
```

time: 353 us -> 223 us (0.63)
  waiting for transfers between devices: 245 us -> 37.5 us
  Pallas kernels: 0 us -> 94.7 us
  starting transfers between devices: 0.2 us -> 63.8 us
  matrix products: 49.2 us -> 0 us
  blocking collectives: 36.5 us -> 0 us
  local copies, waits for them, and re-layouts: 1.76 us -> 8.52 us
    reduce_scatter x2 -> x0, waiting for transfers between devices: 164 us -> none  [the longest x1 149 us: body(): lax.psum_scatter(contract_last(grad_full, weight), 'outp', scatter_dimens...]
    pallas_call x0 -> x14, Pallas kernels: none -> 94.7 us  [the longest x2 32.6 us: forward(): pl.pallas_call(kernel, out_shape=[out, out, jax.ShapeDtypeStruct((2 * sen...]
    ppermute x0 -> x23, starting transfers between devices: none -> 63.8 us  [the longest x3 21.6 us: body(): right = right + lax.ppermute(right, 'outp', [(d, d ^ k) for d in range(n)])]
    dot_general x5 -> x0, matrix products: 49.2 us -> none  [the longest x3 24.8 us: contract_last(): lax.dot_general(left_side, right_side, (((1,), (1,)), ((), ())), preferre...]
    all_gather x2, waiting for transfers between devices: 68.6 us -> 20.7 us  [along_z(): lax.all_gather(x, 'outp', axis=0, tiled=True, axis_index_groups=lines)]
    all_gather x2 -> x0, blocking collectives: 33.1 us -> none  [the longest x1 30.9 us: body(): left = lax.all_gather(left_own, 'outp', axis=0, tiled=True)]
    ppermute x0 -> x23, waiting for transfers between devices: none -> 16.8 us  [the longest x1 6.9 us: body(): rest = jnp.concatenate([rest, lax.ppermute(rest, 'outp', across)], axis=0)]
    psum x1 -> x0, waiting for transfers between devices: 11.4 us -> none  [body(): right_own = lax.psum(right_own, 'outp')]
  transfers between devices with their start and end apart: 5 -> 25, of which waited for: 5 -> 6; matrix products, arithmetic and copies ran while one was open for 15% -> 2% of each run, Pallas kernels for 0% -> 40%
where the time goes in v2:
time: 223 us; the launch traced here: 222 us
  Pallas kernels  94.7 us (42%)
  starting transfers between devices  63.8 us (29%)
  waiting for transfers between devices  37.5 us (17%)
  between operations  14.4 us (6%)
  local copies, waits for them, and re-layouts  8.52 us (4%)
  other arithmetic  2.82 us (1%)
    pallas_call x2, Pallas kernels, forward(): pl.pallas_call(kernel, out_shape=[out, out, jax.ShapeDtypeStruct((2 * sen...  32.6 us
    pallas_call x2, Pallas kernels, backward(): pl.pallas_call(kernel, out_shape=out_shape, grid_spec=pltpu.PrefetchScala...  31.1 us
    pallas_call x8, Pallas kernels, local_call(): pl.pallas_call(kernel, out_shape=out_shape, grid_spec=pltpu.PrefetchScala...  24 us
    ppermute x3, starting transfers between devices, body(): right = right + lax.ppermute(right, 'outp', [(d, d ^ k) for d in range(n)])  21.6 us
    all_gather x2, waiting for transfers between devices, along_z(): lax.all_gather(x, 'outp', axis=0, tiled=True, axis_index_groups=lines)  20.7 us
    ppermute x3, starting transfers between devices, body(): u1 = lax.ppermute(u1, 'outp', up(reach))  20.4 us
    ppermute x3, starting transfers between devices, body(): u2 = lax.ppermute(u2, 'outp', up(reach))  8.43 us
    ppermute x1, waiting for transfers between devices, body(): rest = jnp.concatenate([rest, lax.ppermute(rest, 'outp', across)], axis=0)  6.9 us
  transfers between devices with their start and end apart: 25, of which 6 were waited for; matrix products, arithmetic and copies ran while one was open for 2% of the time, Pallas kernels for 40%

profile of v2, /device:TPU:0, one launch (start us, length us, event | category | flops | bytes accessed | tf_op | source)
XLA Modules:
  0.0 221.8 jit_solution(6635245405005694410)
XLA Ops:
  7.2 1.9 fusion
  9.7 2.6 %collective-permute-start.2 = (bf16[32,4096]{1,0:T(8,128)(2,1)S(1)}, bf16[32,4096]{1,0:T(8,128)(2,1)S(1)}, u32[]{:S(2)}, u32[]{:S(2)}) collective-permute-start(bf16[32,4096]{1,0:T(8,128)(2,1)S(1)} %get-tuple-element.53), channel_id=1, source_target_pairs={{0,2},{2,0},{4,6},{6,4},{8,10},{10,8},{12,14},{14,12},{1,3},{3,1},... | collective-permute-start | bytes 786440 | tf_op jit(solution)/shard_map/ppermute | solution.py:462
  12.3 6.9 %collective-permute-done.2 = bf16[32,4096]{1,0:T(8,128)(2,1)S(1)} collective-permute-done((bf16[32,4096]{1,0:T(8,128)(2,1)S(1)}, bf16[32,4096]{1,0:T(8,128)(2,1)S(1)}, u32[]{:S(2)}, u32[]{:S(2)}) %collective-permute-start.2) | collective-permute-done | bytes 262176 | tf_op jit(solution)/shard_map/ppermute | solution.py:462
  20.2 20.7 %all-gather.3.cloned.1.call-done.refs_0_.refs_2_ = bf16[128,4096]{1,0:T(8,128)(2,1)} async-done(((bf16[32,4096]{1,0:T(8,128)(2,1)}), bf16[128,4096]{1,0:T(8,128)(2,1)}) %all-gather.3.cloned.1.call-update) | async-done | bytes 1048592 | tf_op jit(solution)/shard_map/all_gather | solution.py:458
  42.3 16.3 %backward_y.1 = (bf16[256,2176]{1,0:T(8,128)(2,1)}, f32[4,4,64,512]{3,2,1,0:T(8,128)S(1)}, f32[2,256,64]{2,1,0:T(8,128)}) custom-call(s32[3]{0:T(128)S(1)} %pad_add_fusion.idx, bf16[256,3584]{1,0:T(8,128)(2,1)S(1)} %copy-done.3, bf16[256,3584]{1,0:T(8,128)(2,1)} %collective-permute-done.4.oth, bf16[4096,3584]{1,0:T(8,128)(2,1)} %w.3, ...), custom_call_target="tpu_custom_call" | custom-call | flops 7516192768 | bytes 23068672 | tf_op jit(solution)/shard_map/backward_y/pallas_call | solution.py:141
  62.1 14.7 %backward_z.1 = (f32[4,2,256,512]{3,2,1,0:T(8,128)S(1)}, bf16[128,2176]{1,0:T(8,128)(2,1)}, bf16[128,2176]{1,0:T(8,128)(2,1)}) custom-call(s32[3]{0:T(128)S(1)} %pad_add_fusion.idx, bf16[256,3584]{1,0:T(8,128)(2,1)S(1)} %copy-done.3, bf16[256,3584]{1,0:T(8,128)(2,1)} %collective-permute-done.4.oth, bf16[4096,3584]{1,0:T(8,128)(2,1)} %w.3), custom_call_target="tpu_custom_call" | custom-call | flops 7516192768 | bytes 23068672 | tf_op jit(solution)/shard_map/backward_z/pallas_call | solution.py:141
  76.8 4.2 %collective-permute-start.12 = (bf16[128,2176]{1,0:T(8,128)(2,1)}, bf16[128,2176]{1,0:T(8,128)(2,1)}, u32[]{:S(2)}, u32[]{:S(2)}) collective-permute-start(bf16[128,2176]{1,0:T(8,128)(2,1)} %get-tuple-element.42), channel_id=1, source_target_pairs={{0,4},{2,6},{1,5},{3,7},{16,20},{18,22},{17,21},{19,23}} | collective-permute-start | bytes 1671176 | tf_op jit(solution)/shard_map/ppermute | solution.py:487
  82.4 16.2 %forward.2 = (f32[128,3584]{1,0:T(8,128)}, f32[128,3584]{1,0:T(8,128)S(1)}, f32[256,64]{1,0:T(8,128)S(1)}) custom-call(s32[3]{0:T(128)S(1)} %pad_add_fusion.idx, bf16[128,4096]{1,0:T(8,128)(2,1)S(1)} %copy-done.4, bf16[128,4096]{1,0:T(8,128)(2,1)S(1)} %collective-permute-done.refs_1_.refs_3_, bf16[128,4096]{1,0:T(8,128)(2,1)S(1)} %copy-done.4, ...), custom_call_target="tpu_custom_call" | custom-call | flops 7516192768 | bytes 33030144 | tf_op jit(solution)/shard_map/forward/pallas_call | solution.py:330
  102.1 16.5 %forward.3 = (f32[128,3584]{1,0:T(8,128)}, f32[128,3584]{1,0:T(8,128)S(1)}, f32[256,64]{1,0:T(8,128)S(1)}) custom-call(s32[3]{0:T(128)S(1)} %pad_add_fusion.idx, bf16[256,4096]{1,0:T(8,128)(2,1)S(1)} %copy-done.2, bf16[256,4096]{1,0:T(8,128)(2,1)S(1)} %copy-done.2, bf16[4096,3584]{1,0:T(8,128)(2,1)} %w.3, bf16[64,4096]{1,0:T(8,128)(2,1)S(1)} %copy-done.5), custom_call_target="tpu_custom_call" | custom-call | flops 7516192768 | bytes 33030144 | tf_op jit(solution)/shard_map/forward/pallas_call | solution.py:330
  120.4 3.2 %after_y.1 = (f32[4,4,64,512]{3,2,1,0:T(8,128)S(1)}, bf16[64,2176]{1,0:T(8,128)(2,1)S(1)}, bf16[64,2176]{1,0:T(8,128)(2,1)S(1)}) custom-call(s32[3]{0:T(128)S(1)} %pad_add_fusion.idx, f32[4,4,64,512]{3,2,1,0:T(8,128)S(1)} %copy-done.7, bf16[256,2176]{1,0:T(8,128)(2,1)S(1)} %collective-permute-done.5.got), custom_call_target="tpu_custom_call" | custom-call | bytes 5865472 | tf_op jit(solution)/shard_map/after_y/pallas_call | solution.py:163
  123.7 3.9 %collective-permute-start.6 = (bf16[64,2176]{1,0:T(8,128)(2,1)S(1)}, bf16[64,2176]{1,0:T(8,128)(2,1)S(1)}, u32[]{:S(2)}, u32[]{:S(2)}) collective-permute-start(bf16[64,2176]{1,0:T(8,128)(2,1)S(1)} %get-tuple-element.35), channel_id=1, source_target_pairs={{0,4},{2,6},{1,5},{3,7},{16,20},{18,22},{17,21},{19,23}} | collective-permute-start | bytes 835592 | tf_op jit(solution)/shard_map/ppermute | solution.py:491
  127.6 5.4 %line_step.6 = (bf16[128,2176]{1,0:T(8,128)(2,1)S(1)}, bf16[128,2176]{1,0:T(8,128)(2,1)S(1)}) custom-call(s32[3]{0:T(128)S(1)} %pad_add_fusion.idx, f32[4,4,128,512]{3,2,1,0:T(8,128)S(1)} %bitcast.5, f32[4,4,128,512]{3,2,1,0:T(8,128)S(1)} %bitcast.6, bf16[128,2176]{1,0:T(8,128)(2,1)} %collective-permute-done.12.up_got, ...), custom_call_target="tpu_custom_call" | custom-call | bytes 10616832 | tf_op jit(solution)/shard_map/line_step/pallas_call | solution.py:163
  135.8 21.0 %collective-permute-start.21 = (f32[2,256,64]{2,1,0:T(8,128)S(1)}, f32[2,256,64]{2,1,0:T(8,128)S(1)}, u32[]{:S(2)}, u32[]{:S(2)}) collective-permute-start(f32[2,256,64]{2,1,0:T(8,128)S(1)} %add.19), channel_id=1, source_target_pairs={{0,8},{2,10},{4,12},{6,14},{8,0},{10,2},{12,4},{14,6},{1,9},{3,11}... | collective-permute-start | bytes 393224 | tf_op jit(solution)/shard_map/ppermute | solution.py:482
  156.8 2.4 %line_step.4 = (bf16[64,2176]{1,0:T(8,128)(2,1)S(1)}, bf16[64,2176]{1,0:T(8,128)(2,1)S(1)}) custom-call(s32[3]{0:T(128)S(1)} %pad_add_fusion.idx, f32[4,4,64,512]{3,2,1,0:T(8,128)S(1)} %get-tuple-element.34.up_total.down_total.part, f32[4,4,64,512]{3,2,1,0:T(8,128)S(1)} %get-tuple-element.34.up_total.down_total.part, ...), custom_call_target="tpu_custom_call" | custom-call | bytes 5308416 | tf_op jit(solution)/shard_map/line_step/pallas_call | solution.py:163
  160.9 4.3 %line_step.7 = (bf16[128,2176]{1,0:T(8,128)(2,1)S(1)}, bf16[128,2176]{1,0:T(8,128)(2,1)S(1)}) custom-call(s32[3]{0:T(128)S(1)} %pad_add_fusion.idx, f32[4,4,128,512]{3,2,1,0:T(8,128)S(1)} %bitcast.7, f32[4,4,128,512]{3,2,1,0:T(8,128)S(1)} %bitcast.8, bf16[128,2176]{1,0:T(8,128)(2,1)S(1)} %collective-permute-done.14.up_got, ...), custom_call_target="tpu_custom_call" | custom-call | bytes 10616832 | tf_op jit(solution)/shard_map/line_step/pallas_call | solution.py:163
  165.3 2.9 %collective-permute-start.16 = (bf16[128,2176]{1,0:T(8,128)(2,1)S(1)}, bf16[128,2176]{1,0:T(8,128)(2,1)S(1)}, u32[]{:S(2)}, u32[]{:S(2)}) collective-permute-start(bf16[128,2176]{1,0:T(8,128)(2,1)S(1)} %get-tuple-element.46), channel_id=1, source_target_pairs={{0,4},{2,6},{4,8},{6,10},{8,12},{10,14},{1,5},{3,7},{5,9},{7,11},{... | collective-permute-start | bytes 1671176 | tf_op jit(solution)/shard_map/ppermute | solution.py:487
  171.3 3.2 %line_step.5 = (bf16[64,2176]{1,0:T(8,128)(2,1)}, bf16[64,2176]{1,0:T(8,128)(2,1)}) custom-call(s32[3]{0:T(128)S(1)} %pad_add_fusion.idx, f32[4,4,64,512]{3,2,1,0:T(8,128)S(1)} %get-tuple-element.34.up_total.down_total.part, f32[4,4,64,512]{3,2,1,0:T(8,128)S(1)} %get-tuple-element.34.up_total.down_total.part, ...), custom_call_target="tpu_custom_call" | custom-call | bytes 5308416 | tf_op jit(solution)/shard_map/line_step/pallas_call | solution.py:163
  174.5 4.8 %collective-permute-done.16.up_got = bf16[128,2176]{1,0:T(8,128)(2,1)S(1)} collective-permute-done((bf16[128,2176]{1,0:T(8,128)(2,1)S(1)}, bf16[128,2176]{1,0:T(8,128)(2,1)S(1)}, u32[]{:S(2)}, u32[]{:S(2)}) %collective-permute-start.16) | collective-permute-done | bytes 557088 | tf_op jit(solution)/shard_map/ppermute | solution.py:487
  179.3 14.9 %collective-permute-start.10 = (bf16[64,2176]{1,0:T(8,128)(2,1)}, bf16[64,2176]{1,0:T(8,128)(2,1)S(1)}, u32[]{:S(2)}, u32[]{:S(2)}) collective-permute-start(bf16[64,2176]{1,0:T(8,128)(2,1)} %get-tuple-element.39), channel_id=1, source_target_pairs={{0,4},{2,6},{4,8},{6,10},{8,12},{10,14},{1,5},{3,7},{5,9},{7,11},{... | collective-permute-start | bytes 835592 | tf_op jit(solution)/shard_map/ppermute | solution.py:491
  195.5 2.5 %line_end.3 = (bf16[64,2176]{1,0:T(8,128)(2,1)}, f32[64,2048]{1,0:T(8,128)S(1)}) custom-call(s32[3]{0:T(128)S(1)} %pad_add_fusion.idx, f32[4,4,128,512]{3,2,1,0:T(8,128)S(1)} %bitcast.9, bf16[128,2176]{1,0:T(8,128)(2,1)S(1)} %collective-permute-done.16.up_got, bf16[128,2176]{1,0:T(8,128)(2,1)S(1)} %collective-permute-done.17.down_got), custom_call_target="tpu_custom_call" | custom-call | bytes 6111232 | tf_op jit(solution)/shard_map/line_end/pallas_call | solution.py:163
  199.2 1.6 reshape.17
  201.1 4.0 %collective-permute-done.11.down_got = bf16[64,2176]{1,0:T(8,128)(2,1)S(1)} collective-permute-done((bf16[64,2176]{1,0:T(8,128)(2,1)}, bf16[64,2176]{1,0:T(8,128)(2,1)S(1)}, u32[]{:S(2)}, u32[]{:S(2)}) %collective-permute-start.11) | collective-permute-done | bytes 278560 | tf_op jit(solution)/shard_map/ppermute | solution.py:492
  207.0 1.8 finish_grad.1
  208.8 6.1 %combine.1 = bf16[256,3584]{1,0:T(8,128)(2,1)} custom-call(s32[3]{0:T(128)S(1)} %pad_add_fusion.idx, f32[128,3584]{1,0:T(8,128)S(1)} %copy-done.9, f32[128,3584]{1,0:T(8,128)} %collective-permute-done.1.refs_1_, f32[128,3584]{1,0:T(8,128)S(1)} %copy-done.11, f32[128,3584]{1,0:T(8,128)} %collective-permute-done.3.refs_3_), custom_call_target="tpu_custom_call" | custom-call | bytes 9175040 | tf_op jit(solution)/shard_map/combine/pallas_call | solution.py:382
  (80 shorter events, 25.2 us)
Async XLA Ops:
  7.2 33.6 %all-gather.3.cloned.1.call-start = ((), (), s32[]{:S(2)}) async-start(), calls=%async_computation | async-start | bytes 1310720 | tf_op jit(solution)/shard_map/all_gather | solution.py:458
  9.2 91.4 %all-gather.5.cloned.1.call-start = ((), (), s32[]{:S(2)}) async-start(), calls=%async_computation.1 | async-start | bytes 2621440 | tf_op jit(solution)/shard_map/all_gather | solution.py:458
  9.2 33.1 %collective-permute-start.4 = (bf16[256,3584]{1,0:T(8,128)(2,1)}, bf16[256,3584]{1,0:T(8,128)(2,1)}, u32[]{:S(2)}, u32[]{:S(2)}) collective-permute-start(bf16[256,3584]{1,0:T(8,128)(2,1)} %own.3), channel_id=1, source_target_pairs={{0,1},{1,0},{2,3},{3,2},{4,5},{5,4},{6,7},{7,6},{8,9},{9,8},{10,11... | collective-permute-start | bytes 5505032 | tf_op jit(solution)/shard_map/ppermute | solution.py:463
  9.7 9.5 %collective-permute-start.2 = (bf16[32,4096]{1,0:T(8,128)(2,1)S(1)}, bf16[32,4096]{1,0:T(8,128)(2,1)S(1)}, u32[]{:S(2)}, u32[]{:S(2)}) collective-permute-start(bf16[32,4096]{1,0:T(8,128)(2,1)S(1)} %get-tuple-element.53), channel_id=1, source_target_pairs={{0,2},{2,0},{4,6},{6,4},{8,10},{10,8},{12,14},{14,12},{1,3},{3,1},... | collective-permute-start | bytes 786440 | tf_op jit(solution)/shard_map/ppermute | solution.py:462
  40.8 41.6 %collective-permute-start = (bf16[128,4096]{1,0:T(8,128)(2,1)}, bf16[128,4096]{1,0:T(8,128)(2,1)S(1)}, u32[]{:S(2)}, u32[]{:S(2)}) collective-permute-start(bf16[128,4096]{1,0:T(8,128)(2,1)} %all-gather.3.cloned.1.call-done.refs_0_.refs_2_), channel_id=1, source_target_pairs={{0,2},{2,0},{4,6},{6,4},{8,10},{10,8},{12,14},{14,12},{1,3},{3,1},... | collective-permute-start | bytes 3145736 | tf_op jit(solution)/shard_map/ppermute | solution.py:467
  60.0 58.6 %collective-permute-start.19 = (f32[2,256,64]{2,1,0:T(8,128)}, f32[2,256,64]{2,1,0:T(8,128)}, u32[]{:S(2)}, u32[]{:S(2)}) collective-permute-start(f32[2,256,64]{2,1,0:T(8,128)} %get-tuple-element.52), channel_id=1, source_target_pairs={{0,2},{2,0},{4,6},{6,4},{8,10},{10,8},{12,14},{14,12},{1,3},{3,1},... | collective-permute-start | bytes 393224 | tf_op jit(solution)/shard_map/ppermute | solution.py:482
  60.6 59.7 %collective-permute-start.5 = (bf16[256,2176]{1,0:T(8,128)(2,1)}, bf16[256,2176]{1,0:T(8,128)(2,1)S(1)}, u32[]{:S(2)}, u32[]{:S(2)}) collective-permute-start(bf16[256,2176]{1,0:T(8,128)(2,1)} %get-tuple-element.33), channel_id=1, source_target_pairs={{0,2},{2,0},{4,6},{6,4},{8,10},{10,8},{12,14},{14,12},{1,3},{3,1},... | collective-permute-start | bytes 3342344 | tf_op jit(solution)/shard_map/ppermute | solution.py:476
  76.8 46.8 %collective-permute-start.12 = (bf16[128,2176]{1,0:T(8,128)(2,1)}, bf16[128,2176]{1,0:T(8,128)(2,1)}, u32[]{:S(2)}, u32[]{:S(2)}) collective-permute-start(bf16[128,2176]{1,0:T(8,128)(2,1)} %get-tuple-element.42), channel_id=1, source_target_pairs={{0,4},{2,6},{1,5},{3,7},{16,20},{18,22},{17,21},{19,23}} | collective-permute-start | bytes 1671176 | tf_op jit(solution)/shard_map/ppermute | solution.py:487
  81.0 46.6 %collective-permute-start.13 = (bf16[128,2176]{1,0:T(8,128)(2,1)}, bf16[128,2176]{1,0:T(8,128)(2,1)}, u32[]{:S(2)}, u32[]{:S(2)}) collective-permute-start(bf16[128,2176]{1,0:T(8,128)(2,1)} %get-tuple-element.43), channel_id=1, source_target_pairs={{12,8},{14,10},{13,9},{15,11},{28,24},{30,26},{29,25},{31,27}} | collective-permute-start | bytes 1671176 | tf_op jit(solution)/shard_map/ppermute | solution.py:488
  100.5 108.2 %collective-permute-start.1 = (f32[128,3584]{1,0:T(8,128)}, f32[128,3584]{1,0:T(8,128)}, u32[]{:S(2)}, u32[]{:S(2)}) collective-permute-start(f32[128,3584]{1,0:T(8,128)} %get-tuple-element.29), channel_id=1, source_target_pairs={{0,1},{1,0},{2,3},{3,2},{4,5},{5,4},{6,7},{7,6},{8,9},{9,8},{10,11... | collective-permute-start | bytes 5505032 | tf_op jit(solution)/shard_map/ppermute | solution.py:504
  118.6 90.2 %collective-permute-start.3 = (f32[128,3584]{1,0:T(8,128)}, f32[128,3584]{1,0:T(8,128)}, u32[]{:S(2)}, u32[]{:S(2)}) collective-permute-start(f32[128,3584]{1,0:T(8,128)} %get-tuple-element.31), channel_id=1, source_target_pairs={{0,1},{1,0},{2,3},{3,2},{4,5},{5,4},{6,7},{7,6},{8,9},{9,8},{10,11... | collective-permute-start | bytes 5505032 | tf_op jit(solution)/shard_map/ppermute | solution.py:504
  120.3 14.1 %collective-permute-start.20 = (f32[2,256,64]{2,1,0:T(8,128)S(1)}, f32[2,256,64]{2,1,0:T(8,128)S(1)}, u32[]{:S(2)}, u32[]{:S(2)}) collective-permute-start(f32[2,256,64]{2,1,0:T(8,128)S(1)} %add.18), channel_id=1, source_target_pairs={{0,4},{2,6},{4,0},{6,2},{8,12},{10,14},{12,8},{14,10},{1,5},{3,7},... | collective-permute-start | bytes 393224 | tf_op jit(solution)/shard_map/ppermute | solution.py:482
  123.7 11.5 %collective-permute-start.6 = (bf16[64,2176]{1,0:T(8,128)(2,1)S(1)}, bf16[64,2176]{1,0:T(8,128)(2,1)S(1)}, u32[]{:S(2)}, u32[]{:S(2)}) collective-permute-start(bf16[64,2176]{1,0:T(8,128)(2,1)S(1)} %get-tuple-element.35), channel_id=1, source_target_pairs={{0,4},{2,6},{1,5},{3,7},{16,20},{18,22},{17,21},{19,23}} | collective-permute-start | bytes 835592 | tf_op jit(solution)/shard_map/ppermute | solution.py:491
  133.1 26.2 %collective-permute-start.14 = (bf16[128,2176]{1,0:T(8,128)(2,1)S(1)}, bf16[128,2176]{1,0:T(8,128)(2,1)S(1)}, u32[]{:S(2)}, u32[]{:S(2)}) collective-permute-start(bf16[128,2176]{1,0:T(8,128)(2,1)S(1)} %get-tuple-element.44), channel_id=1, source_target_pairs={{0,4},{2,6},{4,8},{6,10},{1,5},{3,7},{5,9},{7,11},{16,20},{18,22},... | collective-permute-start | bytes 1671176 | tf_op jit(solution)/shard_map/ppermute | solution.py:487
  134.4 26.5 %collective-permute-start.15 = (bf16[128,2176]{1,0:T(8,128)(2,1)S(1)}, bf16[128,2176]{1,0:T(8,128)(2,1)S(1)}, u32[]{:S(2)}, u32[]{:S(2)}) collective-permute-start(bf16[128,2176]{1,0:T(8,128)(2,1)S(1)} %get-tuple-element.45), channel_id=1, source_target_pairs={{8,4},{10,6},{12,8},{14,10},{9,5},{11,7},{13,9},{15,11},{24,20},{2... | collective-permute-start | bytes 1671176 | tf_op jit(solution)/shard_map/ppermute | solution.py:488
  135.8 32.4 %collective-permute-start.21 = (f32[2,256,64]{2,1,0:T(8,128)S(1)}, f32[2,256,64]{2,1,0:T(8,128)S(1)}, u32[]{:S(2)}, u32[]{:S(2)}) collective-permute-start(f32[2,256,64]{2,1,0:T(8,128)S(1)} %add.19), channel_id=1, source_target_pairs={{0,8},{2,10},{4,12},{6,14},{8,0},{10,2},{12,4},{14,6},{1,9},{3,11}... | collective-permute-start | bytes 393224 | tf_op jit(solution)/shard_map/ppermute | solution.py:482
  159.3 10.2 %collective-permute-start.8 = (bf16[64,2176]{1,0:T(8,128)(2,1)S(1)}, bf16[64,2176]{1,0:T(8,128)(2,1)S(1)}, u32[]{:S(2)}, u32[]{:S(2)}) collective-permute-start(bf16[64,2176]{1,0:T(8,128)(2,1)S(1)} %get-tuple-element.37), channel_id=1, source_target_pairs={{0,4},{2,6},{4,8},{6,10},{1,5},{3,7},{5,9},{7,11},{16,20},{18,22},... | collective-permute-start | bytes 835592 | tf_op jit(solution)/shard_map/ppermute | solution.py:491
  165.3 14.1 %collective-permute-start.16 = (bf16[128,2176]{1,0:T(8,128)(2,1)S(1)}, bf16[128,2176]{1,0:T(8,128)(2,1)S(1)}, u32[]{:S(2)}, u32[]{:S(2)}) collective-permute-start(bf16[128,2176]{1,0:T(8,128)(2,1)S(1)} %get-tuple-element.46), channel_id=1, source_target_pairs={{0,4},{2,6},{4,8},{6,10},{8,12},{10,14},{1,5},{3,7},{5,9},{7,11},{... | collective-permute-start | bytes 1671176 | tf_op jit(solution)/shard_map/ppermute | solution.py:487
  168.2 26.0 %collective-permute-start.17 = (bf16[128,2176]{1,0:T(8,128)(2,1)S(1)}, bf16[128,2176]{1,0:T(8,128)(2,1)S(1)}, u32[]{:S(2)}, u32[]{:S(2)}) collective-permute-start(bf16[128,2176]{1,0:T(8,128)(2,1)S(1)} %get-tuple-element.47), channel_id=1, source_target_pairs={{4,0},{6,2},{8,4},{10,6},{12,8},{14,10},{5,1},{7,3},{9,5},{11,7},{... | collective-permute-start | bytes 1671176 | tf_op jit(solution)/shard_map/ppermute | solution.py:488
  169.5 1.7 collective-permute-start.9
  171.2 26.8 %collective-permute-start.22 = (f32[4,64,64]{2,1,0:T(8,128)S(1)}, f32[4,64,64]{2,1,0:T(8,128)S(1)}, u32[]{:S(2)}, u32[]{:S(2)}) collective-permute-start(f32[4,64,64]{2,1,0:T(8,128)S(1)} %sketch_part.1), channel_id=1, source_target_pairs={{0,1},{1,0},{2,3},{3,2},{4,5},{5,4},{6,7},{7,6},{8,9},{9,8},{10,11... | collective-permute-start | bytes 196616 | tf_op jit(solution)/shard_map/ppermute | solution.py:509
  179.3 21.8 %collective-permute-start.10 = (bf16[64,2176]{1,0:T(8,128)(2,1)}, bf16[64,2176]{1,0:T(8,128)(2,1)S(1)}, u32[]{:S(2)}, u32[]{:S(2)}) collective-permute-start(bf16[64,2176]{1,0:T(8,128)(2,1)} %get-tuple-element.39), channel_id=1, source_target_pairs={{0,4},{2,6},{4,8},{6,10},{8,12},{10,14},{1,5},{3,7},{5,9},{7,11},{... | collective-permute-start | bytes 835592 | tf_op jit(solution)/shard_map/ppermute | solution.py:491
  194.2 10.9 %collective-permute-start.11 = (bf16[64,2176]{1,0:T(8,128)(2,1)}, bf16[64,2176]{1,0:T(8,128)(2,1)S(1)}, u32[]{:S(2)}, u32[]{:S(2)}) collective-permute-start(bf16[64,2176]{1,0:T(8,128)(2,1)} %get-tuple-element.40), channel_id=1, source_target_pairs={{4,0},{6,2},{8,4},{10,6},{12,8},{14,10},{5,1},{7,3},{9,5},{11,7},{... | collective-permute-start | bytes 835592 | tf_op jit(solution)/shard_map/ppermute | solution.py:492
  198.0 9.0 %collective-permute-start.18 = (bf16[64,2176]{1,0:T(8,128)(2,1)}, bf16[64,2176]{1,0:T(8,128)(2,1)S(1)}, u32[]{:S(2)}, u32[]{:S(2)}) collective-permute-start(bf16[64,2176]{1,0:T(8,128)(2,1)} %get-tuple-element.49), channel_id=1, source_target_pairs={{0,2},{2,0},{4,6},{6,4},{8,10},{10,8},{12,14},{14,12},{1,3},{3,1},... | collective-permute-start | bytes 835592 | tf_op jit(solution)/shard_map/ppermute | solution.py:497
  (16 other events, 217.0 us)
Sparse Core Ops, SparseCore 0:
  10.2 30.6 all-gather.2
  43.0 46.8 all-gather.4

commit v3 on v0

v3 whole, which is shorter than its diff:
```python
import jax
import jax.numpy as jnp
from jax import lax
from jax.experimental import pallas as pl
from jax.experimental.pallas import tpu as pltpu
from jax.sharding import PartitionSpec as P

LEN = 128
LANES = 128
BLK = 16
LN2 = 0.6931471805599453
SPAN = 248.0
SHIFT = 124.0
PIECES = 2
F_TILE = 512
H_TILE = 512
FWD_PIECES = 4
MIB = 1 << 20
ANY = pl.BlockSpec(memory_space=pl.ANY)


def pick(extent, cap):
    best = LANES
    for t in range(LANES, min(cap, extent) + 1, LANES):
        if extent % t == 0:
            best = t
    return best


def contract_last(a, b):
    return lax.dot_general(a, b, (((1,), (1,)), ((), ())), preferred_element_type=jnp.float32)


def whole(shape):
    return pl.BlockSpec(shape, lambda *_: (0,) * len(shape))


def call(kernel, idx, args, specs, out_shape, out_specs, name, grid, mib, work, after, scratch=()):
    token = jax.ShapeDtypeStruct((8, LANES), jnp.float32)
    n_args, n_after, n_out = len(args), len(after), len(out_shape)

    def with_token(idx, *refs):
        ins = refs[:n_args]
        outs = refs[n_args + n_after :]
        outs[n_out][...] = jnp.zeros((8, LANES), jnp.float32)
        kernel(idx, *ins, *outs[:n_out], *outs[n_out + 1 :])

    out = pl.pallas_call(
        with_token,
        out_shape=list(out_shape) + [token],
        grid_spec=pltpu.PrefetchScalarGridSpec(
            num_scalar_prefetch=1,
            grid=grid,
            in_specs=list(specs) + [ANY] * n_after,
            out_specs=list(out_specs) + [whole(token.shape)],
            scratch_shapes=list(scratch),
        ),
        compiler_params=pltpu.CompilerParams(vmem_limit_bytes=mib * MIB),
        cost_estimate=pl.CostEstimate(
            flops=work[0], bytes_accessed=work[1], transcendentals=0
        ),
        name=name,
    )(idx, *args, *after)
    return out[:-1], out[-1]


def encode_rows(tiles, msg, at):
    top = jnp.abs(tiles[0])
    for v in tiles[1:]:
        top = jnp.maximum(top, jnp.abs(v))
    top = jnp.max(top, axis=1, keepdims=True)
    scale = jnp.maximum(top * 1.004, 2.0**-110).astype(jnp.bfloat16).astype(jnp.float32)
    gain = SPAN / scale
    col = 0
    for v in tiles:
        w = jnp.exp2(jnp.abs(v) * gain - SHIFT)
        msg[at, col : col + v.shape[1]] = jnp.where(v < 0, -w, w).astype(jnp.bfloat16)
        col += v.shape[1]
    msg[at, col : col + LANES] = jnp.broadcast_to(scale, (BLK, LANES)).astype(jnp.bfloat16)


def decode_rows(msg, at, tile, count):
    scale = msg[at, tile * count : tile * count + LANES].astype(jnp.float32)[:, :1]
    scale = scale * (1.0 / (SPAN * LN2))
    out = []
    for t in range(count):
        w = msg[at, t * tile : (t + 1) * tile].astype(jnp.float32)
        a = (lax.log(jnp.maximum(jnp.abs(w), 2.0**-SHIFT)) + SHIFT * LN2) * scale
        out.append(jnp.where(w < 0, -a, a))
    return out


def with_bit(c, pos, value):
    low = c & ((1 << pos) - 1)
    return ((c >> pos) << (pos + 1)) + low + value * (1 << pos)


def rows_at(start):
    return pl.ds(pl.multiple_of(start, BLK), BLK)


def backward(idx, own, oth, w, sketch, count, tile, first, rows, bit, after):
    half, hidden = own.shape
    n = 2 * half // rows
    width = count * tile
    with_right = sketch is not None

    def kernel(idx, own, oth, w, *rest):
        if with_right:
            sk, msg, keep, right, x, total, sems = rest
        else:
            msg, keep, x, total, sems = rest
        j = pl.program_id(0)
        me, core = idx[0], idx[1]

        @pl.when(j == 0)
        def _():
            a = pltpu.make_async_copy(own, x.at[core], sems.at[0])
            b = pltpu.make_async_copy(oth, x.at[1 - core], sems.at[1])
            a.start()
            b.start()
            a.wait()
            b.wait()

        xs = x[...].reshape(2 * half, hidden)
        if with_right:

            @pl.when(j == 0)
            def _():
                right[...] = contract_last(xs, sk[...])

        total[j] = contract_last(xs, w[...]).reshape(n, rows, tile)

        @pl.when(j == count - 1)
        def _():
            mine = (me >> bit) & 1
            for c in range(n // 2):
                away, here = with_bit(c, bit, 1 - mine), with_bit(c, bit, mine)

                @pl.loop(0, rows // BLK)
                def _(b):
                    src = rows_at(b * BLK)
                    encode_rows(
                        [total[t, away, src, :] for t in range(count)],
                        msg,
                        rows_at(c * rows + b * BLK),
                    )
                    for t in range(count):
                        keep[t, c, src, :] = total[t, here, src, :]

    args = [own, oth, w]
    specs = [ANY, ANY, pl.BlockSpec((tile, hidden), lambda j, s: (first + j, 0))]
    out = [
        jax.ShapeDtypeStruct((n // 2 * rows, width + LANES), jnp.bfloat16),
        jax.ShapeDtypeStruct((count, n // 2, rows, tile), jnp.float32),
    ]
    if with_right:
        args.append(sketch)
        specs.append(whole(sketch.shape))
        out.append(jax.ShapeDtypeStruct((2 * half, sketch.shape[0]), jnp.float32))
    return call(
        kernel,
        idx,
        args,
        specs,
        out,
        [whole(o.shape) for o in out],
        "backward",
        (count,),
        40,
        (4 * half * hidden * width, 2 * hidden * width + 12 * half * width),
        after,
        [
            pltpu.VMEM((2, half, hidden), jnp.bfloat16),
            pltpu.VMEM((count, n, rows, tile), jnp.float32),
            pltpu.SemaphoreType.DMA((2,)),
        ],
    )


def fold(idx, keep, got, bit, pos, after):
    count, m, rows, tile = keep.shape

    def kernel(idx, keep, got, msg, rest):
        mine = (idx[0] >> bit) & 1
        for c in range(m // 2):
            away, here = with_bit(c, pos, 1 - mine), with_bit(c, pos, mine)

            @pl.loop(0, rows // BLK)
            def _(b):
                src = rows_at(b * BLK)
                plus = decode_rows(got, rows_at(away * rows + b * BLK), tile, count)
                encode_rows(
                    [keep[t, away, src, :] + plus[t] for t in range(count)],
                    msg,
                    rows_at(c * rows + b * BLK),
                )
                plus = decode_rows(got, rows_at(here * rows + b * BLK), tile, count)
                for t in range(count):
                    rest[t, c, src, :] = keep[t, here, src, :] + plus[t]

    out = [
        jax.ShapeDtypeStruct((m // 2 * rows, got.shape[1]), jnp.bfloat16),
        jax.ShapeDtypeStruct((count, m // 2, rows, tile), jnp.float32),
    ]
    return call(
        kernel,
        idx,
        [keep, got],
        [whole(keep.shape), whole(got.shape)],
        out,
        [whole(o.shape) for o in out],
        "fold",
        (1,),
        24,
        (0, 12 * keep.size),
        after,
    )


def finish(idx, keeps, gots, after):
    count, _, rows, tile = keeps[0].shape
    pieces = len(keeps)

    def kernel(idx, *refs):
        out = refs[-1]
        for p in range(pieces):

            @pl.loop(0, rows // BLK)
            def _(b):
                at = rows_at(b * BLK)
                plus = decode_rows(refs[pieces + p], at, tile, count)
                for t in range(count):
                    lo = (p * count + t) * tile
                    out[at, lo : lo + tile] = (refs[p][t, 0, at, :] + plus[t]).astype(
                        jnp.bfloat16
                    )

    args = list(keeps) + list(gots)
    out = [jax.ShapeDtypeStruct((rows, pieces * count * tile), jnp.bfloat16)]
    (grad,), _ = call(
        kernel,
        idx,
        args,
        [whole(a.shape) for a in args],
        out,
        [whole(out[0].shape)],
        "finish",
        (1,),
        16,
        (0, 16 * rows * count * tile),
        after,
    )
    return grad


def bit_reversed(r, bits):
    return sum(((r >> k) & 1) << (bits - 1 - k) for k in range(bits))


def join(idx, a, b, after):
    m = a.shape[0]

    def kernel(idx, a, b, out, sems):
        first = pltpu.make_async_copy(a, out.at[pl.ds(0, m)], sems.at[0])
        second = pltpu.make_async_copy(b, out.at[pl.ds(m, m)], sems.at[1])
        first.start()
        second.start()
        first.wait()
        second.wait()

    out = [jax.ShapeDtypeStruct((2 * m,) + a.shape[1:], a.dtype)]
    work = (0, 8 * a.size)
    dma = [pltpu.SemaphoreType.DMA((2,))]
    (joined,), token = call(
        kernel, idx, [a, b], [ANY, ANY], out, [ANY], "join", (1,), 8, work, after, dma
    )
    return joined, token


def add(idx, a, b, after):
    def kernel(idx, a, b, out):
        out[...] = a[...] + b[...]

    specs = [whole(a.shape)] * 2
    out = [jax.ShapeDtypeStruct(a.shape, a.dtype)]
    work = (a.size, 12 * a.size)
    (total,), token = call(
        kernel, idx, [a, b], specs, out, specs[:1], "add", (1,), 8, work, after
    )
    return total, token


def forward(idx, near, far, w, sketch, rows, first, count, tile, after):
    m, b_rows, feats = far[0].shape
    n = 2 * m
    a_rows = rows - b_rows
    half = n // 2 * rows
    bits = n.bit_length() - 1
    with_left = sketch is not None
    args = ([near] if a_rows else []) + [*far, w] + ([sketch] if with_left else [])
    specs = [ANY] * (3 if a_rows else 2) + [
        pl.BlockSpec((feats, tile), lambda j, s: (0, first + j))
    ]
    if with_left:
        specs.append(whole(sketch.shape))

    def kernel(idx, *refs):
        x, sems = refs[-2:]
        send, keep = refs[len(args) : len(args) + 2]
        *far, w = refs[1:4] if a_rows else refs[:3]
        me, core = idx[0], idx[1]

        def place(d):
            side = 1 - ((d // (n // 2)) ^ core)
            return side * half + (d % (n // 2)) * rows

        @pl.when(pl.program_id(0) == 0)
        def _():
            copies = []
            for r in range(n):
                to = pl.ds(pl.multiple_of(place(me ^ bit_reversed(r, bits)) + a_rows, BLK), b_rows)
                copies.append(pltpu.make_async_copy(far[r // m].at[r % m], x.at[to], sems.at[r]))
                if a_rows:
                    to = pl.ds(pl.multiple_of(place(jnp.int32(r)), BLK), a_rows)
                    copies.append(
                        pltpu.make_async_copy(
                            refs[0].at[pl.ds(r * a_rows, a_rows)], x.at[to], sems.at[n + r]
                        )
                    )
            for c in copies:
                c.start()
            for c in copies:
                c.wait()
            if with_left:
                refs[len(args) + 2][...] = contract_last(x[...], refs[len(args) - 1][...])

        t = jnp.dot(x[...], w[...], preferred_element_type=jnp.float32)
        send[...] = t[:half]
        keep[...] = t[half:]

    width = count * tile
    out = [jax.ShapeDtypeStruct((half, width), jnp.float32)] * 2
    out_specs = [pl.BlockSpec((half, tile), lambda j, s: (0, j))] * 2
    if with_left:
        out.append(jax.ShapeDtypeStruct((2 * half, sketch.shape[0]), jnp.float32))
        out_specs.append(whole(out[-1].shape))
    return call(
        kernel,
        idx,
        args,
        specs,
        out,
        out_specs,
        "forward",
        (count,),
        40,
        (4 * half * feats * width, 2 * feats * width + 8 * half * width),
        after,
        [pltpu.VMEM((2 * half, feats), jnp.bfloat16), pltpu.SemaphoreType.DMA((2 * n,))],
    )


def sketch_part(idx, left, right, after):
    tokens, width = right.shape
    half = tokens // 2
    examples = tokens // LEN

    def kernel(idx, left, right, out):
        core = idx[1]
        for e in range(examples):
            side = 1 - ((2 * e // examples) ^ core)
            at = pl.multiple_of(side * half + (e % (examples // 2)) * LEN, LEN)
            out[e] = lax.dot_general(
                left[pl.ds(at, LEN), :],
                right[e * LEN : (e + 1) * LEN, :],
                (((0,), (0,)), ((), ())),
                precision=lax.Precision.HIGHEST,
                preferred_element_type=jnp.float32,
            )

    out = [jax.ShapeDtypeStruct((examples, width, width), jnp.float32)]
    (part,), token = call(
        kernel,
        idx,
        [left, right],
        [whole(left.shape), whole(right.shape)],
        out,
        [whole(out[0].shape)],
        "sketch_part",
        (1,),
        16,
        (0, 8 * tokens * width),
        after,
    )
    return part, token


def body(inputs, cotangent, weight, in_sketch, out_sketch):
    n = lax.axis_size("outp")
    bits = n.bit_length() - 1
    rows, feats = inputs.shape
    hidden = weight.shape[1]
    idx = jnp.stack([lax.axis_index("outp"), lax.axis_index("inp")]).astype(jnp.int32)

    def partner(x, bit):
        return lax.ppermute(x, "outp", [(d, d ^ (1 << bit)) for d in range(n)])

    def swap(x):
        return lax.ppermute(x, "inp", [(0, 1), (1, 0)])

    a_rows = rows // 2 if (rows // 2) % BLK == 0 else 0
    near = None
    if a_rows:
        near = lax.all_gather(inputs[:a_rows], "outp", axis=0, tiled=True)
    far = inputs[a_rows:][None]
    grad_other = swap(cotangent)

    orders = [list(range(bits)), [1, 0] + list(range(2, bits))]
    tile = pick(feats // PIECES, F_TILE)
    count = feats // PIECES // tile
    msgs, keeps = [], []
    token = []
    far_bits = list(reversed(range(bits)))
    got = partner(far, far_bits.pop(0))
    for p in range(PIECES):
        outs, t = backward(
            idx,
            cotangent,
            grad_other,
            weight,
            out_sketch if p == 0 else None,
            count,
            tile,
            p * count,
            rows,
            orders[p][0],
            token,
        )
        token = [t]
        if p == 0:
            right = outs[2]
            right_got = partner(right, 0)
        msgs.append(partner(outs[0], orders[p][0]))
        keeps.append(outs[1])
        if far_bits:
            far, t = join(idx, far, got, token)
            token = [t]
            got = partner(far, far_bits.pop(0))
    while far_bits:
        far, t = join(idx, far, got, token)
        token = [t]
        got = partner(far, far_bits.pop(0))
    right_bits = list(range(1, bits))

    def right_step(after):
        total, t = add(idx, right, right_got, after)
        if right_bits:
            return total, partner(total, right_bits.pop(0)), [t]
        return total, None, [t]

    def folded(p, step, after):
        done, bit = orders[p][:step], orders[p][step]
        pos = sum(1 for k in range(bit) if k not in done)
        (msg, keeps[p]), t = fold(idx, keeps[p], msgs[p], bit, pos, after)
        msgs[p] = partner(msg, bit)
        return [t]

    h_tile = pick(hidden, H_TILE)
    tiles = hidden // h_tile
    ends = [-(-tiles * k // FWD_PIECES) for k in range(FWD_PIECES + 1)]
    folds = [(p, step) for step in range(1, bits) for p in range(PIECES)]
    columns = []
    right, right_got, token = right_step(token)
    token = folded(*folds.pop(0), token)
    for k in range(FWD_PIECES):
        if right_got is not None:
            right, right_got, token = right_step(token)
        outs, t = forward(
            idx,
            near,
            [far, got],
            weight,
            in_sketch if k == 0 else None,
            rows,
            ends[k],
            ends[k + 1] - ends[k],
            h_tile,
            token,
        )
        token = [t]
        if k == 0:
            left = outs[2]
        columns.append(outs[1] + swap(outs[0]))
        if folds:
            token = folded(*folds.pop(0), token)
    while right_got is not None:
        right, right_got, token = right_step(token)
    for p, step in folds:
        token = folded(p, step, token)
    part, t = sketch_part(idx, left, right, token)
    part = (part + swap(part)) * (1.0 / LEN**0.5)
    sketches = part.reshape(part.shape[0], -1)
    input_grad = finish(idx, keeps, msgs, [t])
    outputs = jnp.concatenate([c.astype(jnp.bfloat16) for c in columns], axis=1)
    return (outputs, input_grad, sketches)


def solution(mesh):
    placed = (
        P(("groups", "outp"), "inp"),
        P(("groups", "inp"), "outp"),
        P("inp", "outp"),
        P(None, "inp"),
        P(None, "outp"),
    )
    return jax.shard_map(
        body,
        mesh=mesh,
        in_specs=placed,
        out_specs=(P(("groups", "inp"), "outp"), P(("groups", "outp"), "inp"), P("groups", None)),
        check_vma=False,
    )
```

time: 353 us -> 207 us (0.59)
  waiting for transfers between devices: 245 us -> 73.4 us
  Pallas kernels: 0 us -> 80.3 us
  matrix products: 49.2 us -> 0 us
  blocking collectives: 36.5 us -> 0 us
  starting transfers between devices: 0.2 us -> 17.9 us
  local copies, waits for them, and re-layouts: 1.76 us -> 14.2 us
    reduce_scatter x2 -> x0, waiting for transfers between devices: 164 us -> none  [the longest x1 149 us: body(): lax.psum_scatter(contract_last(grad_full, weight), 'outp', scatter_dimens...]
    pallas_call x0 -> x17, Pallas kernels: none -> 80.3 us  [call(): pl.pallas_call(with_token, out_shape=list(out_shape) + [token], grid_spec...]
    ppermute x0 -> x18, waiting for transfers between devices: none -> 73.4 us  [the longest x12 73.4 us: partner(): return lax.ppermute(x, 'outp', [(d, d ^ 1 << bit) for d in range(n)])]
    all_gather x2 -> x1, waiting for transfers between devices: 68.6 us -> 0.01 us  [body(): near = lax.all_gather(inputs[:a_rows], 'outp', axis=0, tiled=True)]
    dot_general x5 -> x0, matrix products: 49.2 us -> none  [the longest x3 24.8 us: contract_last(): lax.dot_general(left_side, right_side, (((1,), (1,)), ((), ())), preferre...]
    all_gather x2 -> x0, blocking collectives: 33.1 us -> none  [the longest x1 30.9 us: body(): left = lax.all_gather(left_own, 'outp', axis=0, tiled=True)]
    ppermute x0 -> x18, starting transfers between devices: none -> 17.9 us  [the longest x12 16.3 us: partner(): return lax.ppermute(x, 'outp', [(d, d ^ 1 << bit) for d in range(n)])]
    psum x1 -> x0, waiting for transfers between devices: 11.4 us -> none  [body(): right_own = lax.psum(right_own, 'outp')]
  transfers between devices with their start and end apart: 5 -> 19, of which waited for: 5 -> 5; matrix products, arithmetic and copies ran while one was open for 15% -> 3% of each run, Pallas kernels for 0% -> 39%
where the time goes in v3:
time: 207 us; the launch traced here: 206 us
  Pallas kernels  80.3 us (39%)
  waiting for transfers between devices  73.4 us (35%)
  starting transfers between devices  17.9 us (9%)
  between operations  14.3 us (7%)
  local copies, waits for them, and re-layouts  14.2 us (7%)
  other arithmetic  5.95 us (3%)
    pallas_call x17, Pallas kernels, call(): pl.pallas_call(with_token, out_shape=list(out_shape) + [token], grid_spec...  80.3 us
    ppermute x12, waiting for transfers between devices, partner(): return lax.ppermute(x, 'outp', [(d, d ^ 1 << bit) for d in range(n)])  73.4 us
    ppermute x12, starting transfers between devices, partner(): return lax.ppermute(x, 'outp', [(d, d ^ 1 << bit) for d in range(n)])  16.3 us
    unnamed x40, local copies, waits for them, and re-layouts  11.7 us
    convert_element_type x4, other arithmetic, body(): outputs = jnp.concatenate([c.astype(jnp.bfloat16) for c in columns], axis=1)  4.51 us
  transfers between devices with their start and end apart: 19, of which 5 were waited for; matrix products, arithmetic and copies ran while one was open for 3% of the time, Pallas kernels for 39%

profile of v3, /device:TPU:0, one launch (start us, length us, event | category | flops | bytes accessed | tf_op | source)
XLA Modules:
  0.0 206.1 jit_solution(14643495894840535470)
XLA Ops:
  7.7 1.8 slice_bitcast_fusion
  9.5 3.7 %collective-permute-start = (bf16[1,32,4096]{2,1,0:T(8,128)(2,1)S(1)}, bf16[1,32,4096]{2,1,0:T(8,128)(2,1)S(1)}, u32[]{:S(2)}, u32[]{:S(2)}) collective-permute-start(bf16[1,32,4096]{2,1,0:T(8,128)(2,1)S(1)} %get-tuple-element.93.refs_0_), channel_id=1, source_target_pairs={{0,8},{2,10},{4,12},{6,14},{8,0},{10,2},{12,4},{14,6},{1,9},{3,11}... | collective-permute-start | bytes 786440 | tf_op jit(solution)/shard_map/ppermute | solution.py:407
  15.8 15.4 %backward.2 = (bf16[256,2176]{1,0:T(8,128)(2,1)S(1)}, f32[4,4,64,512]{3,2,1,0:T(8,128)S(1)}, f32[512,64]{1,0:T(8,128)S(1)}, f32[8,128]{1,0:T(8,128)S(1)}) custom-call(s32[2]{0:T(128)S(1)} %pad_add_fusion.idx, bf16[256,3584]{1,0:T(8,128)(2,1)S(1)} %copy-done.2, bf16[256,3584]{1,0:T(8,128)(2,1)S(1)} %collective-permute-done.1.refs_1_, ...), custom_call_target="tpu_custom_call" | custom-call | flops 7516192768 | bytes 20971520 | tf_op jit(solution)/shard_map/backward/pallas_call | solution.py:48
  31.8 1.6 collective-permute-start.2
  35.0 14.4 %backward.3 = (bf16[256,2176]{1,0:T(8,128)(2,1)}, f32[4,4,64,512]{3,2,1,0:T(8,128)S(1)}, f32[8,128]{1,0:T(8,128)S(1)}) custom-call(s32[2]{0:T(128)S(1)} %pad_add_fusion.idx, bf16[256,3584]{1,0:T(8,128)(2,1)S(1)} %copy-done.2, bf16[256,3584]{1,0:T(8,128)(2,1)S(1)} %collective-permute-done.1.refs_1_, bf16[4096,3584]{1,0:T(8,128)(2,1)} %refs_3_.9, ...), custom_call_target="tpu_custom_call" | custom-call | flops 7516192768 | bytes 20971520 | tf_op jit(solution)/shard_map/backward/pallas_call | solution.py:48
  49.4 3.4 %collective-permute-done.2.refs_1_ = bf16[2,32,4096]{2,1,0:T(8,128)(2,1)S(1)} collective-permute-done((bf16[2,32,4096]{2,1,0:T(8,128)(2,1)S(1)}, bf16[2,32,4096]{2,1,0:T(8,128)(2,1)S(1)}, u32[]{:S(2)}, u32[]{:S(2)}) %collective-permute-start.2) | collective-permute-done | bytes 524320 | tf_op jit(solution)/shard_map/ppermute | solution.py:407
  55.5 43.7 %collective-permute-done.4.refs_1_ = f32[512,64]{1,0:T(8,128)S(1)} collective-permute-done((f32[512,64]{1,0:T(8,128)S(1)}, f32[512,64]{1,0:T(8,128)S(1)}, u32[]{:S(2)}, u32[]{:S(2)}) %collective-permute-start.4) | collective-permute-done | bytes 131104 | tf_op jit(solution)/shard_map/ppermute | solution.py:407
  100.3 3.3 %fold.4 = (bf16[128,2176]{1,0:T(8,128)(2,1)}, f32[4,2,64,512]{3,2,1,0:T(8,128)S(1)}, f32[8,128]{1,0:T(8,128)S(1)}) custom-call(s32[2]{0:T(128)S(1)} %pad_add_fusion.idx, f32[4,4,64,512]{3,2,1,0:T(8,128)S(1)} %get-tuple-element.56.refs_0_, bf16[256,2176]{1,0:T(8,128)(2,1)S(1)} %collective-permute-done.6.refs_1_, f32[8,128]{1,0:T(8,128)S(1)} %get-tuple-element.58.refs_2_), custom_call_target="tpu_custom_call" | custom-call | bytes 6291456 | tf_op jit(solution)/shard_map/fold/pallas_call | solution.py:48
  104.5 2.6 %collective-permute-done.5.refs_1_ = f32[512,64]{1,0:T(8,128)S(1)} collective-permute-done((f32[512,64]{1,0:T(8,128)S(1)}, f32[512,64]{1,0:T(8,128)S(1)}, u32[]{:S(2)}, u32[]{:S(2)}) %collective-permute-start.5) | collective-permute-done | bytes 131104 | tf_op jit(solution)/shard_map/ppermute | solution.py:407
  107.7 1.7 collective-permute-start.8
  110.0 1.6 copy-done
  112.7 10.1 %forward.4 = (f32[256,1024]{1,0:T(8,128)}, f32[256,1024]{1,0:T(8,128)S(1)}, f32[512,64]{1,0:T(8,128)S(1)}, f32[8,128]{1,0:T(8,128)S(1)}) custom-call(s32[2]{0:T(128)S(1)} %pad_add_fusion.idx, bf16[256,4096]{1,0:T(8,128)(2,1)S(1)} %copy-done, bf16[4,32,4096]{2,1,0:T(8,128)(2,1)S(1)} %get-tuple-element.52.refs_1_, ...), custom_call_target="tpu_custom_call" | custom-call | flops 4294967296 | bytes 10485760 | tf_op jit(solution)/shard_map/forward/pallas_call | solution.py:48
  122.8 2.4 %fold.5 = (bf16[128,2176]{1,0:T(8,128)(2,1)S(1)}, f32[4,2,64,512]{3,2,1,0:T(8,128)S(1)}, f32[8,128]{1,0:T(8,128)S(1)}) custom-call(s32[2]{0:T(128)S(1)} %pad_add_fusion.idx, f32[4,4,64,512]{3,2,1,0:T(8,128)S(1)} %copy-done.4, bf16[256,2176]{1,0:T(8,128)(2,1)S(1)} %collective-permute-done.9.refs_1_, f32[8,128]{1,0:T(8,128)S(1)} %get-tuple-element.66.refs_2_), custom_call_target="tpu_custom_call" | custom-call | bytes 6291456 | tf_op jit(solution)/shard_map/fold/pallas_call | solution.py:48
  125.2 1.6 collective-permute-start.13
  126.8 1.5 add.32
  128.4 8.7 %forward.5 = (f32[256,1024]{1,0:T(8,128)}, f32[256,1024]{1,0:T(8,128)S(1)}, f32[8,128]{1,0:T(8,128)S(1)}) custom-call(s32[2]{0:T(128)S(1)} %pad_add_fusion.idx, bf16[256,4096]{1,0:T(8,128)(2,1)S(1)} %copy-done.1, bf16[4,32,4096]{2,1,0:T(8,128)(2,1)S(1)} %get-tuple-element.52.refs_1_, bf16[4,32,4096]{2,1,0:T(8,128)(2,1)S(1)} %collective-permute-done.3.refs_2_, ...), custom_call_target="tpu_custom_call" | custom-call | flops 4294967296 | bytes 10485760 | tf_op jit(solution)/shard_map/forward/pallas_call | solution.py:48
  137.6 2.5 %fold.6 = (bf16[64,2176]{1,0:T(8,128)(2,1)S(1)}, f32[4,1,64,512]{3,2,1,0:T(8,128)S(1)}, f32[8,128]{1,0:T(8,128)S(1)}) custom-call(s32[2]{0:T(128)S(1)} %pad_add_fusion.idx, f32[4,2,64,512]{3,2,1,0:T(8,128)S(1)} %copy-done.10, bf16[128,2176]{1,0:T(8,128)(2,1)} %collective-permute-done.11.refs_1_, f32[8,128]{1,0:T(8,128)S(1)} %get-tuple-element.73.refs_2_), custom_call_target="tpu_custom_call" | custom-call | bytes 3145728 | tf_op jit(solution)/shard_map/fold/pallas_call | solution.py:48
  140.9 8.7 %forward.6 = (f32[256,1024]{1,0:T(8,128)}, f32[256,1024]{1,0:T(8,128)S(1)}, f32[8,128]{1,0:T(8,128)S(1)}) custom-call(s32[2]{0:T(128)S(1)} %pad_add_fusion.idx, bf16[256,4096]{1,0:T(8,128)(2,1)S(1)} %copy-done.1, bf16[4,32,4096]{2,1,0:T(8,128)(2,1)S(1)} %get-tuple-element.52.refs_1_, bf16[4,32,4096]{2,1,0:T(8,128)(2,1)S(1)} %collective-permute-done.3.refs_2_, ...), custom_call_target="tpu_custom_call" | custom-call | flops 4294967296 | bytes 10485760 | tf_op jit(solution)/shard_map/forward/pallas_call | solution.py:48
  150.6 2.2 %fold.7 = (bf16[64,2176]{1,0:T(8,128)(2,1)}, f32[4,1,64,512]{3,2,1,0:T(8,128)S(1)}, f32[8,128]{1,0:T(8,128)S(1)}) custom-call(s32[2]{0:T(128)S(1)} %pad_add_fusion.idx, f32[4,2,64,512]{3,2,1,0:T(8,128)S(1)} %get-tuple-element.77.refs_0_, bf16[128,2176]{1,0:T(8,128)(2,1)S(1)} %collective-permute-done.13.refs_1_, f32[8,128]{1,0:T(8,128)S(1)} %get-tuple-element.79.refs_2_), custom_call_target="tpu_custom_call" | custom-call | bytes 3145728 | tf_op jit(solution)/shard_map/fold/pallas_call | solution.py:48
  153.6 5.7 %forward.7 = (f32[256,512]{1,0:T(8,128)S(1)}, f32[256,512]{1,0:T(8,128)S(1)}, f32[8,128]{1,0:T(8,128)S(1)}) custom-call(s32[2]{0:T(128)S(1)} %pad_add_fusion.idx, bf16[256,4096]{1,0:T(8,128)(2,1)S(1)} %copy-done.1, bf16[4,32,4096]{2,1,0:T(8,128)(2,1)S(1)} %get-tuple-element.52.refs_1_, bf16[4,32,4096]{2,1,0:T(8,128)(2,1)S(1)} %collective-permute-done.3.refs_2_, ...), custom_call_target="tpu_custom_call" | custom-call | flops 2147483648 | bytes 5242880 | tf_op jit(solution)/shard_map/forward/pallas_call | solution.py:48
  162.7 1.9 collective-permute-start.16
  165.3 18.6 %collective-permute-done.15.refs_2_ = bf16[64,2176]{1,0:T(8,128)(2,1)S(1)} collective-permute-done((bf16[64,2176]{1,0:T(8,128)(2,1)S(1)}, bf16[64,2176]{1,0:T(8,128)(2,1)S(1)}, u32[]{:S(2)}, u32[]{:S(2)}) %collective-permute-start.15) | collective-permute-done | bytes 278560 | tf_op jit(solution)/shard_map/ppermute | solution.py:407
  184.0 5.1 %collective-permute-done.16.refs_3_ = bf16[64,2176]{1,0:T(8,128)(2,1)S(1)} collective-permute-done((bf16[64,2176]{1,0:T(8,128)(2,1)}, bf16[64,2176]{1,0:T(8,128)(2,1)S(1)}, u32[]{:S(2)}, u32[]{:S(2)}) %collective-permute-start.16) | collective-permute-done | bytes 278560 | tf_op jit(solution)/shard_map/ppermute | solution.py:407
  191.2 2.1 %finish.1 = (bf16[64,4096]{1,0:T(8,128)(2,1)}, f32[8,128]{1,0:T(8,128)}) custom-call(s32[2]{0:T(128)S(1)} %pad_add_fusion.idx, f32[4,1,64,512]{3,2,1,0:T(8,128)S(1)} %copy-done.15, f32[4,1,64,512]{3,2,1,0:T(8,128)S(1)} %copy-done.17, bf16[64,2176]{1,0:T(8,128)(2,1)S(1)} %collective-permute-done.15.refs_2_, ...), custom_call_target="tpu_custom_call" | custom-call | bytes 2097152 | tf_op jit(solution)/shard_map/finish/pallas_call | solution.py:48
  (81 shorter events, 27.6 us)
Async XLA Ops:
  7.2 102.9 %all-gather.2.cloned.1.call-start = ((), (), s32[]{:S(2)}) async-start(), calls=%async_computation | async-start | bytes 2359296 | tf_op jit(solution)/shard_map/all_gather | solution.py:415
  7.2 6.1 %collective-permute-start.1 = (bf16[256,3584]{1,0:T(8,128)(2,1)}, bf16[256,3584]{1,0:T(8,128)(2,1)S(1)}, u32[]{:S(2)}, u32[]{:S(2)}) collective-permute-start(bf16[256,3584]{1,0:T(8,128)(2,1)} %refs_0_.3), channel_id=1, source_target_pairs={{0,1},{1,0},{2,3},{3,2},{4,5},{5,4},{6,7},{7,6},{8,9},{9,8},{10,11... | collective-permute-start | bytes 5505032 | tf_op jit(solution)/shard_map/ppermute | solution.py:410
  9.5 21.7 %collective-permute-start = (bf16[1,32,4096]{2,1,0:T(8,128)(2,1)S(1)}, bf16[1,32,4096]{2,1,0:T(8,128)(2,1)S(1)}, u32[]{:S(2)}, u32[]{:S(2)}) collective-permute-start(bf16[1,32,4096]{2,1,0:T(8,128)(2,1)S(1)} %get-tuple-element.93.refs_0_), channel_id=1, source_target_pairs={{0,8},{2,10},{4,12},{6,14},{8,0},{10,2},{12,4},{14,6},{1,9},{3,11}... | collective-permute-start | bytes 786440 | tf_op jit(solution)/shard_map/ppermute | solution.py:407
  31.8 21.0 %collective-permute-start.2 = (bf16[2,32,4096]{2,1,0:T(8,128)(2,1)S(1)}, bf16[2,32,4096]{2,1,0:T(8,128)(2,1)S(1)}, u32[]{:S(2)}, u32[]{:S(2)}) collective-permute-start(bf16[2,32,4096]{2,1,0:T(8,128)(2,1)S(1)} %get-tuple-element.49.refs_0_), channel_id=1, source_target_pairs={{0,4},{2,6},{4,0},{6,2},{8,12},{10,14},{12,8},{14,10},{1,5},{3,7},... | collective-permute-start | bytes 1572872 | tf_op jit(solution)/shard_map/ppermute | solution.py:407
  33.4 66.8 %collective-permute-start.6 = (bf16[256,2176]{1,0:T(8,128)(2,1)S(1)}, bf16[256,2176]{1,0:T(8,128)(2,1)S(1)}, u32[]{:S(2)}, u32[]{:S(2)}) collective-permute-start(bf16[256,2176]{1,0:T(8,128)(2,1)S(1)} %get-tuple-element.57), channel_id=1, source_target_pairs={{0,2},{2,0},{4,6},{6,4},{8,10},{10,8},{12,14},{14,12},{1,3},{3,1},... | collective-permute-start | bytes 3342344 | tf_op jit(solution)/shard_map/ppermute | solution.py:407
  49.4 54.2 %copy-start.3 = (f32[4,4,64,512]{3,2,1,0:T(8,128)}, f32[4,4,64,512]{3,2,1,0:T(8,128)S(1)}, u32[]{:S(2)}) copy-start(f32[4,4,64,512]{3,2,1,0:T(8,128)S(1)} %get-tuple-element.64.refs_0_) | copy-start | bytes 6291460
  53.4 56.6 %collective-permute-start.3 = (bf16[4,32,4096]{2,1,0:T(8,128)(2,1)S(1)}, bf16[4,32,4096]{2,1,0:T(8,128)(2,1)S(1)}, u32[]{:S(2)}, u32[]{:S(2)}) collective-permute-start(bf16[4,32,4096]{2,1,0:T(8,128)(2,1)S(1)} %get-tuple-element.52.refs_1_), channel_id=1, source_target_pairs={{0,2},{2,0},{4,6},{6,4},{8,10},{10,8},{12,14},{14,12},{1,3},{3,1},... | collective-permute-start | bytes 3145736 | tf_op jit(solution)/shard_map/ppermute | solution.py:407
  54.8 68.0 %collective-permute-start.9 = (bf16[256,2176]{1,0:T(8,128)(2,1)}, bf16[256,2176]{1,0:T(8,128)(2,1)S(1)}, u32[]{:S(2)}, u32[]{:S(2)}) collective-permute-start(bf16[256,2176]{1,0:T(8,128)(2,1)} %get-tuple-element.65), channel_id=1, source_target_pairs={{0,4},{2,6},{4,0},{6,2},{8,12},{10,14},{12,8},{14,10},{1,5},{3,7},... | collective-permute-start | bytes 3342344 | tf_op jit(solution)/shard_map/ppermute | solution.py:407
  54.8 44.4 %collective-permute-start.4 = (f32[512,64]{1,0:T(8,128)S(1)}, f32[512,64]{1,0:T(8,128)S(1)}, u32[]{:S(2)}, u32[]{:S(2)}) collective-permute-start(f32[512,64]{1,0:T(8,128)S(1)} %get-tuple-element.53.refs_0_), channel_id=1, source_target_pairs={{0,2},{2,0},{4,6},{6,4},{8,10},{10,8},{12,14},{14,12},{1,3},{3,1},... | collective-permute-start | bytes 393224 | tf_op jit(solution)/shard_map/ppermute | solution.py:407
  99.8 7.4 %collective-permute-start.5 = (f32[512,64]{1,0:T(8,128)S(1)}, f32[512,64]{1,0:T(8,128)S(1)}, u32[]{:S(2)}, u32[]{:S(2)}) collective-permute-start(f32[512,64]{1,0:T(8,128)S(1)} %get-tuple-element.55.refs_0_), channel_id=1, source_target_pairs={{0,4},{2,6},{4,0},{6,2},{8,12},{10,14},{12,8},{14,10},{1,5},{3,7},... | collective-permute-start | bytes 393224 | tf_op jit(solution)/shard_map/ppermute | solution.py:407
  107.7 19.1 %collective-permute-start.8 = (f32[512,64]{1,0:T(8,128)S(1)}, f32[512,64]{1,0:T(8,128)}, u32[]{:S(2)}, u32[]{:S(2)}) collective-permute-start(f32[512,64]{1,0:T(8,128)S(1)} %get-tuple-element.63.refs_0_), channel_id=1, source_target_pairs={{0,8},{2,10},{4,12},{6,14},{8,0},{10,2},{12,4},{14,6},{1,9},{3,11}... | collective-permute-start | bytes 393224 | tf_op jit(solution)/shard_map/ppermute | solution.py:407
  109.4 28.3 %collective-permute-start.11 = (bf16[128,2176]{1,0:T(8,128)(2,1)}, bf16[128,2176]{1,0:T(8,128)(2,1)}, u32[]{:S(2)}, u32[]{:S(2)}) collective-permute-start(bf16[128,2176]{1,0:T(8,128)(2,1)} %get-tuple-element.72), channel_id=1, source_target_pairs={{0,4},{2,6},{4,0},{6,2},{8,12},{10,14},{12,8},{14,10},{1,5},{3,7},... | collective-permute-start | bytes 1671176 | tf_op jit(solution)/shard_map/ppermute | solution.py:407
  112.7 10.1 %copy-start.4 = (f32[4,4,64,512]{3,2,1,0:T(8,128)S(1)}, f32[4,4,64,512]{3,2,1,0:T(8,128)}, u32[]{:S(2)}) copy-start(f32[4,4,64,512]{3,2,1,0:T(8,128)} %copy-done.3) | copy-start | bytes 6291460
  122.8 5.5 %copy-start.5 = (f32[256,1024]{1,0:T(8,128)}, f32[256,1024]{1,0:T(8,128)S(1)}, u32[]{:S(2)}) copy-start(f32[256,1024]{1,0:T(8,128)S(1)} %get-tuple-element.61) | copy-start | bytes 3145732
  125.2 25.4 %collective-permute-start.13 = (bf16[128,2176]{1,0:T(8,128)(2,1)S(1)}, bf16[128,2176]{1,0:T(8,128)(2,1)S(1)}, u32[]{:S(2)}, u32[]{:S(2)}) collective-permute-start(bf16[128,2176]{1,0:T(8,128)(2,1)S(1)} %get-tuple-element.78), channel_id=1, source_target_pairs={{0,2},{2,0},{4,6},{6,4},{8,10},{10,8},{12,14},{14,12},{1,3},{3,1},... | collective-permute-start | bytes 1671176 | tf_op jit(solution)/shard_map/ppermute | solution.py:407
  126.8 66.5 %collective-permute-start.7 = (f32[256,1024]{1,0:T(8,128)}, f32[256,1024]{1,0:T(8,128)}, u32[]{:S(2)}, u32[]{:S(2)}) collective-permute-start(f32[256,1024]{1,0:T(8,128)} %get-tuple-element.62), channel_id=1, source_target_pairs={{0,1},{1,0},{2,3},{3,2},{4,5},{5,4},{6,7},{7,6},{8,9},{9,8},{10,11... | collective-permute-start | bytes 3145736 | tf_op jit(solution)/shard_map/ppermute | solution.py:410
  128.4 9.3 %copy-start.10 = (f32[4,2,64,512]{3,2,1,0:T(8,128)S(1)}, f32[4,2,64,512]{3,2,1,0:T(8,128)}, u32[]{:S(2)}) copy-start(f32[4,2,64,512]{3,2,1,0:T(8,128)} %copy-done.9) | copy-start | bytes 3145732
  137.0 57.7 %collective-permute-start.10 = (f32[256,1024]{1,0:T(8,128)}, f32[256,1024]{1,0:T(8,128)}, u32[]{:S(2)}, u32[]{:S(2)}) collective-permute-start(f32[256,1024]{1,0:T(8,128)} %get-tuple-element.70), channel_id=1, source_target_pairs={{0,1},{1,0},{2,3},{3,2},{4,5},{5,4},{6,7},{7,6},{8,9},{9,8},{10,11... | collective-permute-start | bytes 3145736 | tf_op jit(solution)/shard_map/ppermute | solution.py:410
  150.6 45.7 %collective-permute-start.12 = (f32[256,1024]{1,0:T(8,128)}, f32[256,1024]{1,0:T(8,128)}, u32[]{:S(2)}, u32[]{:S(2)}) collective-permute-start(f32[256,1024]{1,0:T(8,128)} %get-tuple-element.76), channel_id=1, source_target_pairs={{0,1},{1,0},{2,3},{3,2},{4,5},{5,4},{6,7},{7,6},{8,9},{9,8},{10,11... | collective-permute-start | bytes 3145736 | tf_op jit(solution)/shard_map/ppermute | solution.py:410
  160.2 33.1 %copy-start.6 = (f32[256,1024]{1,0:T(8,128)S(1)}, f32[256,1024]{1,0:T(8,128)}, u32[]{:S(2)}) copy-start(f32[256,1024]{1,0:T(8,128)} %copy-done.5) | copy-start | bytes 3145732
  161.1 1.6 collective-permute-start.17
  161.6 22.3 %collective-permute-start.15 = (bf16[64,2176]{1,0:T(8,128)(2,1)S(1)}, bf16[64,2176]{1,0:T(8,128)(2,1)S(1)}, u32[]{:S(2)}, u32[]{:S(2)}) collective-permute-start(bf16[64,2176]{1,0:T(8,128)(2,1)S(1)} %get-tuple-element.85), channel_id=1, source_target_pairs={{0,8},{2,10},{4,12},{6,14},{8,0},{10,2},{12,4},{14,6},{1,9},{3,11}... | collective-permute-start | bytes 835592 | tf_op jit(solution)/shard_map/ppermute | solution.py:407
  162.7 26.4 %collective-permute-start.16 = (bf16[64,2176]{1,0:T(8,128)(2,1)}, bf16[64,2176]{1,0:T(8,128)(2,1)S(1)}, u32[]{:S(2)}, u32[]{:S(2)}) collective-permute-start(bf16[64,2176]{1,0:T(8,128)(2,1)} %get-tuple-element.86), channel_id=1, source_target_pairs={{0,8},{2,10},{4,12},{6,14},{8,0},{10,2},{12,4},{14,6},{1,9},{3,11}... | collective-permute-start | bytes 835592 | tf_op jit(solution)/shard_map/ppermute | solution.py:407
  184.0 13.8 %collective-permute-start.14 = (f32[256,512]{1,0:T(8,128)}, f32[256,512]{1,0:T(8,128)S(1)}, u32[]{:S(2)}, u32[]{:S(2)}) collective-permute-start(f32[256,512]{1,0:T(8,128)} %copy-done.19), channel_id=1, source_target_pairs={{0,1},{1,0},{2,3},{3,2},{4,5},{5,4},{6,7},{7,6},{8,9},{9,8},{10,11... | collective-permute-start | bytes 1572872 | tf_op jit(solution)/shard_map/ppermute | solution.py:410
  (15 other events, 22.8 us)
Sparse Core Ops, SparseCore 0:
  10.7 68.8 all-gather.1

commit v4 on v3

v4 whole, which is shorter than its diff:
```python
import jax
import jax.numpy as jnp
from jax import lax
from jax.experimental import pallas as pl
from jax.experimental.pallas import tpu as pltpu
from jax.sharding import PartitionSpec as P

LEN = 128
LANES = 128
BLK = 16
LN2 = 0.6931471805599453
SPAN = 248.0
SHIFT = 124.0
PIECES = 2
F_TILE = 512
H_TILE = 512
VMEM_MIB = {"backward": 32, "forward": 24}
MIB = 1 << 20
TIMES = {"fold": 0, "combine": 1 << 25, "sketch_part": 1 << 25}
ANY = pl.BlockSpec(memory_space=pl.ANY)


def pick(extent, cap):
    best = LANES
    for t in range(LANES, min(cap, extent) + 1, LANES):
        if extent % t == 0:
            best = t
    return best


def contract_last(a, b):
    return lax.dot_general(a, b, (((1,), (1,)), ((), ())), preferred_element_type=jnp.float32)


def whole(shape):
    return pl.BlockSpec(shape, lambda *_: (0,) * len(shape))


def call(
    kernel, idx, args, specs, out_shape, out_specs, name, grid, work, after, scratch=(), aliases=None
):
    token = jax.ShapeDtypeStruct((8, LANES), jnp.float32)
    n_args, n_after, n_out = len(args), len(after), len(out_shape)

    def with_token(idx, *refs):
        ins = refs[:n_args]
        outs = refs[n_args + n_after :]
        outs[n_out][...] = jnp.zeros((8, LANES), jnp.float32)
        kernel(idx, *ins, *outs[:n_out], *outs[n_out + 1 :])

    out = pl.pallas_call(
        with_token,
        out_shape=list(out_shape) + [token],
        grid_spec=pltpu.PrefetchScalarGridSpec(
            num_scalar_prefetch=1,
            grid=grid,
            in_specs=list(specs) + [ANY] * n_after,
            out_specs=list(out_specs) + [whole(token.shape)],
            scratch_shapes=list(scratch),
        ),
        compiler_params=pltpu.CompilerParams(vmem_limit_bytes=VMEM_MIB.get(name, 12) * MIB),
        cost_estimate=pl.CostEstimate(
            flops=TIMES.get(name, work[0]), bytes_accessed=work[1], transcendentals=0
        ),
        input_output_aliases=aliases or {},
        name=name,
    )(idx, *args, *after)
    return out[:-1], out[-1]


def encode_rows(tiles, msg, at):
    top = jnp.abs(tiles[0])
    for v in tiles[1:]:
        top = jnp.maximum(top, jnp.abs(v))
    top = jnp.max(top, axis=1, keepdims=True)
    scale = jnp.maximum(top * 1.004, 2.0**-110).astype(jnp.bfloat16).astype(jnp.float32)
    gain = SPAN / scale
    col = 0
    for v in tiles:
        w = jnp.exp2(jnp.abs(v) * gain - SHIFT)
        msg[at, col : col + v.shape[1]] = jnp.where(v < 0, -w, w).astype(jnp.bfloat16)
        col += v.shape[1]
    msg[at, col : col + LANES] = jnp.broadcast_to(scale, (BLK, LANES)).astype(jnp.bfloat16)


def decode_rows(msg, at, tile, count):
    scale = msg[at, tile * count : tile * count + LANES].astype(jnp.float32)[:, :1]
    scale = scale * (1.0 / (SPAN * LN2))
    out = []
    for t in range(count):
        w = msg[at, t * tile : (t + 1) * tile].astype(jnp.float32)
        a = (lax.log(jnp.maximum(jnp.abs(w), 2.0**-SHIFT)) + SHIFT * LN2) * scale
        out.append(jnp.where(w < 0, -a, a))
    return out


def with_bit(c, pos, value):
    low = c & ((1 << pos) - 1)
    return ((c >> pos) << (pos + 1)) + low + value * (1 << pos)


def rows_at(start):
    return pl.ds(pl.multiple_of(start, BLK), BLK)


def backward(idx, own, oth, w, count, tile, first, rows, bit, after):
    half, hidden = own.shape
    n = 2 * half // rows
    width = count * tile

    def kernel(idx, own, oth, w, msg, keep, x, total, sems):
        j = pl.program_id(0)
        me, core = idx[0], idx[1]

        @pl.when(j == 0)
        def _():
            a = pltpu.make_async_copy(own, x.at[core], sems.at[0])
            b = pltpu.make_async_copy(oth, x.at[1 - core], sems.at[1])
            a.start()
            b.start()
            a.wait()
            b.wait()

        xs = x[...].reshape(2 * half, hidden)
        total[j] = contract_last(xs, w[...]).reshape(n, rows, tile)

        @pl.when(j == count - 1)
        def _():
            mine = (me >> bit) & 1
            for c in range(n // 2):
                away, here = with_bit(c, bit, 1 - mine), with_bit(c, bit, mine)

                @pl.loop(0, rows // BLK)
                def _(b):
                    src = rows_at(b * BLK)
                    encode_rows(
                        [total[t, away, src, :] for t in range(count)],
                        msg,
                        rows_at(c * rows + b * BLK),
                    )
                    for t in range(count):
                        keep[t, c, src, :] = total[t, here, src, :]

    out = [
        jax.ShapeDtypeStruct((n // 2 * rows, width + LANES), jnp.bfloat16),
        jax.ShapeDtypeStruct((count, n // 2, rows, tile), jnp.float32),
    ]
    return call(
        kernel,
        idx,
        [own, oth, w],
        [ANY, ANY, pl.BlockSpec((tile, hidden), lambda j, s: (first + j, 0))],
        out,
        [whole(o.shape) for o in out],
        "backward",
        (count,),
        (4 * half * hidden * width, 2 * hidden * width + 12 * half * width),
        after,
        [
            pltpu.VMEM((2, half, hidden), jnp.bfloat16),
            pltpu.VMEM((count, n, rows, tile), jnp.float32),
            pltpu.SemaphoreType.DMA((2,)),
        ],
    )


def right_part(idx, own, oth, sketch):
    half, hidden = own.shape
    width = sketch.shape[0]

    def kernel(idx, own, oth, sk, out):
        core = idx[1]
        out[core] = contract_last(own[...], sk[...])
        out[1 - core] = contract_last(oth[...], sk[...])

    args = [own, oth, sketch]
    out = [jax.ShapeDtypeStruct((2, half, width), jnp.float32)]
    specs = [whole(a.shape) for a in args]
    work = (4 * half * hidden * width, 4 * half * hidden)
    (part,), token = call(
        kernel, idx, args, specs, out, [whole(out[0].shape)], "right", (1,), work, []
    )
    return part.reshape(2 * half, width), token


def fold(idx, keep, got, bit, pos, after):
    count, m, rows, tile = keep.shape

    def kernel(idx, keep, got, msg, rest):
        mine = (idx[0] >> bit) & 1
        for c in range(m // 2):
            away, here = with_bit(c, pos, 1 - mine), with_bit(c, pos, mine)

            @pl.loop(0, rows // BLK)
            def _(b):
                src = rows_at(b * BLK)
                plus = decode_rows(got, rows_at(away * rows + b * BLK), tile, count)
                encode_rows(
                    [keep[t, away, src, :] + plus[t] for t in range(count)],
                    msg,
                    rows_at(c * rows + b * BLK),
                )
                plus = decode_rows(got, rows_at(here * rows + b * BLK), tile, count)
                for t in range(count):
                    rest[t, c, src, :] = keep[t, here, src, :] + plus[t]

    out = [
        jax.ShapeDtypeStruct((m // 2 * rows, got.shape[1]), jnp.bfloat16),
        jax.ShapeDtypeStruct((count, m // 2, rows, tile), jnp.float32),
    ]
    return call(
        kernel,
        idx,
        [keep, got],
        [whole(keep.shape), whole(got.shape)],
        out,
        [whole(o.shape) for o in out],
        "fold",
        (1,),
        (0, 12 * keep.size),
        after,
    )


def finish(idx, keeps, gots, after):
    count, _, rows, tile = keeps[0].shape
    pieces = len(keeps)

    def kernel(idx, *refs):
        out = refs[-1]
        for p in range(pieces):

            @pl.loop(0, rows // BLK)
            def _(b):
                at = rows_at(b * BLK)
                plus = decode_rows(refs[pieces + p], at, tile, count)
                for t in range(count):
                    lo = (p * count + t) * tile
                    out[at, lo : lo + tile] = (refs[p][t, 0, at, :] + plus[t]).astype(
                        jnp.bfloat16
                    )

    args = list(keeps) + list(gots)
    out = [jax.ShapeDtypeStruct((rows, pieces * count * tile), jnp.bfloat16)]
    (grad,), _ = call(
        kernel,
        idx,
        args,
        [whole(a.shape) for a in args],
        out,
        [whole(out[0].shape)],
        "finish",
        (1,),
        (0, 16 * rows * count * tile),
        after,
    )
    return grad


def gate(idx, arrays, after):
    k = len(arrays)

    def kernel(idx, *refs):
        pass

    out, token = call(
        kernel,
        idx,
        arrays,
        [ANY] * k,
        [jax.ShapeDtypeStruct(a.shape, a.dtype) for a in arrays],
        [ANY] * k,
        "gate",
        (1,),
        (0, 0),
        after,
        aliases={1 + i: i for i in range(k)},
    )
    return list(out), [token]


def add(idx, a, b, after):
    def kernel(idx, a, b, out):
        out[...] = a[...] + b[...]

    specs = [whole(a.shape)] * 2
    out = [jax.ShapeDtypeStruct(a.shape, a.dtype)]
    work = (a.size, 12 * a.size)
    (total,), token = call(kernel, idx, [a, b], specs, out, specs[:1], "add", (1,), work, after)
    return total, [token]


def forward(idx, chunks, w, sketch, lo, hi, after):
    rows, feats = chunks[0][1].shape
    m = len(chunks)
    tile = pick(w.shape[1], H_TILE)
    hidden = (hi - lo) * tile
    part = m // 2 * rows

    def kernel(idx, *refs):
        w, sk, send, keep, left, x, sems = refs[m:]
        me, core = idx[0], idx[1]

        @pl.when(pl.program_id(0) == 0)
        def _():
            copies = []
            for i, (mask, _) in enumerate(chunks):
                d = me ^ mask
                side = 1 - ((d // m) ^ core)
                to = pl.ds(pl.multiple_of(side * part + (d % (m // 2)) * rows, BLK), rows)
                copies.append(pltpu.make_async_copy(refs[i], x.at[to], sems.at[i]))
            for c in copies:
                c.start()
            for c in copies:
                c.wait()
            left[...] = contract_last(x[...], sk[...])

        t = jnp.dot(x[...], w[...], preferred_element_type=jnp.float32)
        send[...] = t[:part]
        keep[...] = t[part:]

    out = [jax.ShapeDtypeStruct((part, hidden), jnp.float32)] * 2
    out.append(jax.ShapeDtypeStruct((2 * part, sketch.shape[0]), jnp.float32))
    column = pl.BlockSpec((part, tile), lambda j, s: (0, j))
    return call(
        kernel,
        idx,
        [c[1] for c in chunks] + [w, sketch],
        [ANY] * m + [pl.BlockSpec((feats, tile), lambda j, s: (0, lo + j)), whole(sketch.shape)],
        out,
        [column, column, whole(out[2].shape)],
        "forward",
        (hidden // tile,),
        (4 * part * feats * hidden, 2 * feats * hidden + 8 * part * hidden),
        after,
        [pltpu.VMEM((2 * part, feats), jnp.bfloat16), pltpu.SemaphoreType.DMA((m,))],
    )


def combine(idx, keep, got, lo, total, batch, bit, before, after):
    part, hidden = keep.shape
    tile = pick(total, H_TILE)
    block = pl.BlockSpec((part, tile), lambda j, s: (0, j))

    def kernel(idx, keep, got, *refs):
        refs[-1][...] = (keep[...] + got[...]).astype(jnp.bfloat16)

    (out,), token = call(
        kernel,
        idx,
        [keep, got] + before,
        [block, block] + [ANY] * len(before),
        [jax.ShapeDtypeStruct((2 * part, total), jnp.bfloat16)],
        [pl.BlockSpec((part, tile), lambda j, s: (((s[0] >> bit) & 1) ^ batch, lo + j))],
        "combine",
        (hidden // tile,),
        (0, 10 * part * hidden),
        after,
        aliases={3: 0} if before else None,
    )
    return out, [token]


def sketch_part(idx, lefts, right, bit, after):
    tokens, width = right.shape
    part = tokens // 4
    examples = part // LEN

    def kernel(idx, first, second, right, out):
        me, core = idx[0], idx[1]
        for batch, left in enumerate((first, second)):
            block = ((me >> bit) & 1) ^ batch
            for side in (0, 1):
                owner = 1 - (side ^ core)
                for e in range(examples):
                    at = (2 * owner + block) * examples + e
                    lo = side * part + e * LEN
                    out[at] = lax.dot_general(
                        left[lo : lo + LEN, :],
                        right[pl.ds(pl.multiple_of(at * LEN, LEN), LEN), :],
                        (((0,), (0,)), ((), ())),
                        precision=lax.Precision.HIGHEST,
                        preferred_element_type=jnp.float32,
                    )

    args = [*lefts, right]
    out = [jax.ShapeDtypeStruct((tokens // LEN, width, width), jnp.float32)]
    (sketch,), token = call(
        kernel,
        idx,
        args,
        [whole(a.shape) for a in args],
        out,
        [whole(out[0].shape)],
        "sketch_part",
        (1,),
        (0, 8 * tokens * width),
        after,
    )
    return sketch, [token]


def body(inputs, cotangent, weight, in_sketch, out_sketch):
    n = lax.axis_size("outp")
    bits = n.bit_length() - 1
    rows, feats = inputs.shape
    hidden = weight.shape[1]
    idx = jnp.stack([lax.axis_index("outp"), lax.axis_index("inp")]).astype(jnp.int32)

    def partner(x, bit):
        return lax.ppermute(x, "outp", [(d, d ^ (1 << bit)) for d in range(n)])

    def swap(x):
        return lax.ppermute(x, "inp", [(0, 1), (1, 0)])

    chunks = {0: inputs}

    def last_bit(mask):
        if mask.bit_count() == 2 and mask & 2:
            return 1
        return (mask & -mask).bit_length() - 1

    def wave(size):
        for mask in sorted(range(n), reverse=True):
            if mask.bit_count() == size:
                bit = last_bit(mask)
                chunks[mask] = partner(chunks[mask ^ (1 << bit)], bit)

    def hold(size, after):
        masks = [m for m in chunks if m.bit_count() == size]
        held, token = gate(idx, [chunks[m] for m in masks], after)
        chunks.update(zip(masks, held))
        return token

    grad_other = swap(cotangent)
    wave(1)
    right, t = right_part(idx, cotangent, grad_other, out_sketch)
    token = [t]
    right_got = partner(right, 0)

    orders = [list(range(bits)), [1, 0] + list(range(2, bits))]
    tile = pick(feats // PIECES, F_TILE)
    count = feats // PIECES // tile
    msgs, keeps = [], []
    for p in range(PIECES):
        outs, t = backward(
            idx, cotangent, grad_other, weight, count, tile, p * count, rows, orders[p][0], token
        )
        right, token = add(idx, right, right_got, [t])
        right_got = partner(right, 1 + p)
        token = hold(1 + p, token)
        wave(2 + p)
        msgs.append(partner(outs[0], orders[p][0]))
        keeps.append(outs[1])
    for k in range(1 + PIECES, bits):
        right, token = add(idx, right, right_got, token)
        right_got = partner(right, k)
        token = hold(k, token)
        wave(k + 1)

    def folded(p, step, after):
        done, bit = orders[p][:step], orders[p][step]
        pos = sum(1 for k in range(bit) if k not in done)
        (msg, keeps[p]), t = fold(idx, keeps[p], msgs[p], bit, pos, after)
        msgs[p] = partner(msg, bit)
        return [t]

    tiles = hidden // pick(hidden, H_TILE)

    def batch_forward(batch, lo, hi, after):
        masks = [m for m in range(n) if (m >> (bits - 2)) & 1 == batch]
        parts = [(m, chunks[m]) for m in masks]
        outs, t = forward(idx, parts, weight, in_sketch, lo, hi, after)
        return (outs[1], swap(outs[0]), lo, hidden, batch, bits - 2), outs[2], [t]

    cut = -(-tiles // 2)
    first, left1, token = batch_forward(0, 0, tiles, token)
    token = folded(0, 1, token)
    token = folded(1, 1, token)
    right, token = add(idx, right, right_got, token)
    second, left2, token = batch_forward(1, 0, cut, token)
    token = folded(0, 2, token)
    third, _, token = batch_forward(1, cut, tiles, token)
    token = folded(1, 2, token)
    for step in range(3, bits):
        for p in range(PIECES):
            token = folded(p, step, token)
    outputs, token = combine(idx, *first, [], token)
    part, token = sketch_part(idx, [left1, left2], right, bits - 2, token)
    outputs, token = combine(idx, *second, [outputs], token)
    outputs, token = combine(idx, *third, [outputs], token)
    part = (part + swap(part)) * (1.0 / LEN**0.5)
    sketches = part.reshape(part.shape[0], -1)
    input_grad = finish(idx, keeps, msgs, token)
    return (outputs, input_grad, sketches)


def solution(mesh):
    placed = (
        P(("groups", "outp"), "inp"),
        P(("groups", "inp"), "outp"),
        P("inp", "outp"),
        P(None, "inp"),
        P(None, "outp"),
    )
    return jax.shard_map(
        body,
        mesh=mesh,
        in_specs=placed,
        out_specs=(P(("groups", "inp"), "outp"), P(("groups", "outp"), "inp"), P("groups", None)),
        check_vma=False,
    )
```

time: 207 us -> 155 us (0.75)
  waiting for transfers between devices: 73.4 us -> 40.3 us
  between operations: 14.3 us -> 0.86 us
  local copies, waits for them, and re-layouts: 14.2 us -> 3.27 us
  starting transfers between devices: 17.9 us -> 26.3 us
  other arithmetic: 5.95 us -> 0.09 us
  Pallas kernels: 80.3 us -> 83.9 us
    ppermute x12 -> x16, waiting for transfers between devices: 73.4 us -> 40.3 us  [partner(): return lax.ppermute(x, 'outp', [(d, d ^ 1 << bit) for d in range(n)])]
    unnamed x40 -> x10, local copies, waits for them, and re-layouts: 11.7 us -> 2.53 us
    ppermute x12 -> x16, starting transfers between devices: 16.3 us -> 25 us  [partner(): return lax.ppermute(x, 'outp', [(d, d ^ 1 << bit) for d in range(n)])]
    convert_element_type x4 -> x0, other arithmetic: 4.51 us -> none  [body(): outputs = jnp.concatenate([c.astype(jnp.bfloat16) for c in columns], axis=1)]
    pallas_call x17 -> x20, Pallas kernels: 80.3 us -> 83.9 us  [call(): pl.pallas_call(with_token, out_shape=list(out_shape) + [token], grid_spec...]
  transfers between devices with their start and end apart: 19 -> 21, of which waited for: 5 -> 7; matrix products, arithmetic and copies ran while one was open for 3% -> 0% of each run, Pallas kernels for 39% -> 54%
where the time goes in v4:
time: 155 us
  Pallas kernels  83.9 us (54%)
  waiting for transfers between devices  40.3 us (26%)
  starting transfers between devices  26.3 us (17%)
  local copies, waits for them, and re-layouts  3.27 us (2%)
    pallas_call x20, Pallas kernels, call(): pl.pallas_call(with_token, out_shape=list(out_shape) + [token], grid_spec...  83.9 us
    ppermute x16, waiting for transfers between devices, partner(): return lax.ppermute(x, 'outp', [(d, d ^ 1 << bit) for d in range(n)])  40.3 us
    ppermute x16, starting transfers between devices, partner(): return lax.ppermute(x, 'outp', [(d, d ^ 1 << bit) for d in range(n)])  25 us
  transfers between devices with their start and end apart: 21, of which 7 were waited for; matrix products, arithmetic and copies ran while one was open for 0% of the time, Pallas kernels for 54%

profile of v4, /device:TPU:0, one launch (start us, length us, event | category | flops | bytes accessed | tf_op | source)
XLA Modules:
  0.0 154.7 jit_solution(1111084676145019037)
XLA Ops:
  1.1 3.7 %collective-permute-start = (bf16[64,4096]{1,0:T(8,128)(2,1)}, bf16[64,4096]{1,0:T(8,128)(2,1)S(1)}, u32[]{:S(2)}, u32[]{:S(2)}) collective-permute-start(bf16[64,4096]{1,0:T(8,128)(2,1)} %refs_0_.7), channel_id=1, source_target_pairs={{0,8},{2,10},{4,12},{6,14},{8,0},{10,2},{12,4},{14,6},{1,9},{3,11}... | collective-permute-start | bytes 1572872 | tf_op jit(solution)/shard_map/ppermute | solution.py:411
  4.8 1.6 %collective-permute-start.1 = (bf16[64,4096]{1,0:T(8,128)(2,1)}, bf16[64,4096]{1,0:T(8,128)(2,1)S(1)}, u32[]{:S(2)}, u32[]{:S(2)}) collective-permute-start(bf16[64,4096]{1,0:T(8,128)(2,1)} %refs_0_.7), channel_id=1, source_target_pairs={{0,4},{2,6},{4,0},{6,2},{8,12},{10,14},{12,8},{14,10},{1,5},{3,7},... | collective-permute-start | bytes 1572872 | tf_op jit(solution)/shard_map/ppermute | solution.py:411
  10.5 1.6 %right.1 = (f32[2,256,64]{2,1,0:T(8,128)S(1)}, f32[8,128]{1,0:T(8,128)S(1)}) custom-call(s32[2]{0:T(128)S(1)} %pad_add_fusion.idx, bf16[256,3584]{1,0:T(8,128)(2,1)S(1)} %copy-done, bf16[256,3584]{1,0:T(8,128)(2,1)S(1)} %collective-permute-done.3.refs_1_, bf16[64,3584]{1,0:T(8,128)(2,1)S(1)} %copy-done.4), custom_call_target="tpu_custom_call" | custom-call | flops 234881024 | bytes 3670016 | tf_op jit(solution)/shard_map/right/pallas_call | solution.py:51
  12.7 13.4 %backward.2 = (bf16[256,2176]{1,0:T(8,128)(2,1)S(1)}, f32[4,4,64,512]{3,2,1,0:T(8,128)S(1)}, f32[8,128]{1,0:T(8,128)S(1)}) custom-call(s32[2]{0:T(128)S(1)} %pad_add_fusion.idx, bf16[256,3584]{1,0:T(8,128)(2,1)S(1)} %copy-done.1, bf16[256,3584]{1,0:T(8,128)(2,1)S(1)} %collective-permute-done.3.refs_1_, bf16[4096,3584]{1,0:T(8,128)(2,1)} %refs_4_.5, ...), custom_call_target="tpu_custom_call" | custom-call | flops 7516192768 | bytes 20971520 | tf_op jit(solution)/shard_map/backward/pallas_call | solution.py:51
  26.1 1.6 %collective-permute-start.10 = (bf16[256,2176]{1,0:T(8,128)(2,1)S(1)}, bf16[256,2176]{1,0:T(8,128)(2,1)S(1)}, u32[]{:S(2)}, u32[]{:S(2)}) collective-permute-start(bf16[256,2176]{1,0:T(8,128)(2,1)S(1)} %get-tuple-element.71), channel_id=1, source_target_pairs={{0,2},{2,0},{4,6},{6,4},{8,10},{10,8},{12,14},{14,12},{1,3},{3,1},... | collective-permute-start | bytes 3342344 | tf_op jit(solution)/shard_map/ppermute | solution.py:411
  34.7 13.4 %backward.3 = (bf16[256,2176]{1,0:T(8,128)(2,1)S(1)}, f32[4,4,64,512]{3,2,1,0:T(8,128)S(1)}, f32[8,128]{1,0:T(8,128)S(1)}) custom-call(s32[2]{0:T(128)S(1)} %pad_add_fusion.idx, bf16[256,3584]{1,0:T(8,128)(2,1)S(1)} %copy-done.1, bf16[256,3584]{1,0:T(8,128)(2,1)S(1)} %collective-permute-done.3.refs_1_, bf16[4096,3584]{1,0:T(8,128)(2,1)} %refs_4_.5, ...), custom_call_target="tpu_custom_call" | custom-call | flops 7516192768 | bytes 20971520 | tf_op jit(solution)/shard_map/backward/pallas_call | solution.py:51
  48.1 2.0 %collective-permute-done.8.refs_1_ = f32[512,64]{1,0:T(8,128)S(1)} collective-permute-done((f32[512,64]{1,0:T(8,128)S(1)}, f32[512,64]{1,0:T(8,128)S(1)}, u32[]{:S(2)}, u32[]{:S(2)}) %collective-permute-start.8) | collective-permute-done | bytes 131104 | tf_op jit(solution)/shard_map/ppermute | solution.py:411
  52.2 11.0 %collective-permute-done.6.refs_1_ = bf16[64,4096]{1,0:T(8,128)(2,1)S(1)} collective-permute-done((bf16[64,4096]{1,0:T(8,128)(2,1)S(1)}, bf16[64,4096]{1,0:T(8,128)(2,1)S(1)}, u32[]{:S(2)}, u32[]{:S(2)}) %collective-permute-start.6) | collective-permute-done | bytes 524320 | tf_op jit(solution)/shard_map/ppermute | solution.py:411
  63.8 1.6 %collective-permute-start.9 = (bf16[64,4096]{1,0:T(8,128)(2,1)S(1)}, bf16[64,4096]{1,0:T(8,128)(2,1)S(1)}, u32[]{:S(2)}, u32[]{:S(2)}) collective-permute-start(bf16[64,4096]{1,0:T(8,128)(2,1)S(1)} %get-tuple-element.69.refs_2_), channel_id=1, source_target_pairs={{0,2},{2,0},{4,6},{6,4},{8,10},{10,8},{12,14},{14,12},{1,3},{3,1},... | collective-permute-start | bytes 1572872 | tf_op jit(solution)/shard_map/ppermute | solution.py:411
  65.3 15.5 %forward.3 = (f32[128,3584]{1,0:T(8,128)S(1)}, f32[128,3584]{1,0:T(8,128)S(1)}, f32[256,64]{1,0:T(8,128)S(1)}, f32[8,128]{1,0:T(8,128)S(1)}) custom-call(s32[2]{0:T(128)S(1)} %pad_add_fusion.idx, bf16[64,4096]{1,0:T(8,128)(2,1)S(1)} %copy-done.3, bf16[64,4096]{1,0:T(8,128)(2,1)S(1)} %get-tuple-element.63.refs_1_, ...), custom_call_target="tpu_custom_call" | custom-call | flops 7516192768 | bytes 33030144 | tf_op jit(solution)/shard_map/forward/pallas_call | solution.py:51
  80.9 2.4 %fold.4 = (bf16[128,2176]{1,0:T(8,128)(2,1)S(1)}, f32[4,2,64,512]{3,2,1,0:T(8,128)S(1)}, f32[8,128]{1,0:T(8,128)S(1)}) custom-call(s32[2]{0:T(128)S(1)} %pad_add_fusion.idx, f32[4,4,64,512]{3,2,1,0:T(8,128)S(1)} %get-tuple-element.70.refs_0_, bf16[256,2176]{1,0:T(8,128)(2,1)S(1)} %collective-permute-done.10.refs_1_, f32[8,128]{1,0:T(8,128)S(1)} %get-tuple-element.74.refs_2_), custom_call_target="tpu_custom_call" | custom-call | bytes 6291456 | tf_op jit(solution)/shard_map/fold/pallas_call | solution.py:51
  83.8 2.4 %collective-permute-start.12 = (f32[512,64]{1,0:T(8,128)S(1)}, f32[512,64]{1,0:T(8,128)S(1)}, u32[]{:S(2)}, u32[]{:S(2)}) collective-permute-start(f32[512,64]{1,0:T(8,128)S(1)} %get-tuple-element.77.refs_0_), channel_id=1, source_target_pairs={{0,8},{2,10},{4,12},{6,14},{8,0},{10,2},{12,4},{14,6},{1,9},{3,11}... | collective-permute-start | bytes 393224 | tf_op jit(solution)/shard_map/ppermute | solution.py:411
  86.2 2.4 %fold.5 = (bf16[128,2176]{1,0:T(8,128)(2,1)S(1)}, f32[4,2,64,512]{3,2,1,0:T(8,128)S(1)}, f32[8,128]{1,0:T(8,128)S(1)}) custom-call(s32[2]{0:T(128)S(1)} %pad_add_fusion.idx, f32[4,4,64,512]{3,2,1,0:T(8,128)S(1)} %get-tuple-element.78.refs_0_, bf16[256,2176]{1,0:T(8,128)(2,1)S(1)} %collective-permute-done.13.refs_1_, f32[8,128]{1,0:T(8,128)S(1)} %get-tuple-element.80.refs_2_), custom_call_target="tpu_custom_call" | custom-call | bytes 6291456 | tf_op jit(solution)/shard_map/fold/pallas_call | solution.py:51
  88.6 1.6 %collective-permute-start.17 = (bf16[128,2176]{1,0:T(8,128)(2,1)S(1)}, bf16[128,2176]{1,0:T(8,128)(2,1)S(1)}, u32[]{:S(2)}, u32[]{:S(2)}) collective-permute-start(bf16[128,2176]{1,0:T(8,128)(2,1)S(1)} %get-tuple-element.92), channel_id=1, source_target_pairs={{0,2},{2,0},{4,6},{6,4},{8,10},{10,8},{12,14},{14,12},{1,3},{3,1},... | collective-permute-start | bytes 1671176 | tf_op jit(solution)/shard_map/ppermute | solution.py:411
  90.2 11.8 %collective-permute-done.12.refs_1_ = f32[512,64]{1,0:T(8,128)S(1)} collective-permute-done((f32[512,64]{1,0:T(8,128)S(1)}, f32[512,64]{1,0:T(8,128)S(1)}, u32[]{:S(2)}, u32[]{:S(2)}) %collective-permute-start.12) | collective-permute-done | bytes 131104 | tf_op jit(solution)/shard_map/ppermute | solution.py:411
  102.5 9.9 %forward.4 = (f32[128,2048]{1,0:T(8,128)S(1)}, f32[128,2048]{1,0:T(8,128)S(1)}, f32[256,64]{1,0:T(8,128)S(1)}, f32[8,128]{1,0:T(8,128)S(1)}) custom-call(s32[2]{0:T(128)S(1)} %pad_add_fusion.idx, bf16[64,4096]{1,0:T(8,128)(2,1)S(1)} %get-tuple-element.61.refs_0_, bf16[64,4096]{1,0:T(8,128)(2,1)S(1)} %get-tuple-element.68.refs_1_, ...), custom_call_target="tpu_custom_call" | custom-call | flops 4294967296 | bytes 18874368 | tf_op jit(solution)/shard_map/forward/pallas_call | solution.py:51
  114.0 9.0 %forward.5 = (f32[128,1536]{1,0:T(8,128)S(1)}, f32[128,1536]{1,0:T(8,128)S(1)}, f32[256,64]{1,0:T(8,128)}, f32[8,128]{1,0:T(8,128)S(1)}) custom-call(s32[2]{0:T(128)S(1)} %pad_add_fusion.idx, bf16[64,4096]{1,0:T(8,128)(2,1)S(1)} %get-tuple-element.61.refs_0_, bf16[64,4096]{1,0:T(8,128)(2,1)S(1)} %get-tuple-element.68.refs_1_, ...), custom_call_target="tpu_custom_call" | custom-call | flops 3221225472 | bytes 14155776 | tf_op jit(solution)/shard_map/forward/pallas_call | solution.py:51
  123.6 3.4 %collective-permute-start.18 = (bf16[64,2176]{1,0:T(8,128)(2,1)S(1)}, bf16[64,2176]{1,0:T(8,128)(2,1)S(1)}, u32[]{:S(2)}, u32[]{:S(2)}) collective-permute-start(bf16[64,2176]{1,0:T(8,128)(2,1)S(1)} %get-tuple-element.106), channel_id=1, source_target_pairs={{0,8},{2,10},{4,12},{6,14},{8,0},{10,2},{12,4},{14,6},{1,9},{3,11}... | collective-permute-start | bytes 835592 | tf_op jit(solution)/shard_map/ppermute | solution.py:411
  128.5 3.4 %combine.3 = (bf16[256,3584]{1,0:T(8,128)(2,1)}, f32[8,128]{1,0:T(8,128)S(1)}) custom-call(s32[2]{0:T(128)S(1)} %pad_add_fusion.idx, f32[128,3584]{1,0:T(8,128)S(1)} %get-tuple-element.89.refs_0_, f32[128,3584]{1,0:T(8,128)S(1)} %collective-permute-done.16.refs_1_, f32[8,128]{1,0:T(8,128)S(1)} %get-tuple-element.94.refs_2_), custom_call_target="tpu_custom_call" | custom-call | flops 33554432 | bytes 4587520 | tf_op jit(solution)/shard_map/combine/pallas_call | solution.py:51
  133.0 2.1 %combine.4 = (bf16[256,3584]{1,0:T(8,128)(2,1)}, f32[8,128]{1,0:T(8,128)S(1)}) custom-call(s32[2]{0:T(128)S(1)} %pad_add_fusion.idx, f32[128,2048]{1,0:T(8,128)S(1)} %get-tuple-element.87.refs_0_, f32[128,2048]{1,0:T(8,128)S(1)} %collective-permute-done.15.refs_1_, bf16[256,3584]{1,0:T(8,128)(2,1)} %get-tuple-element.95.refs_2_, ...), custom_call_target="tpu_custom_call", output_to_operand_aliasing={{0}: (3, {})} | custom-call | flops 33554432 | bytes 2621440 | tf_op jit(solution)/shard_map/combine/pallas_call | solution.py:51
  135.1 2.0 %combine.5 = (bf16[256,3584]{1,0:T(8,128)(2,1)}, f32[8,128]{1,0:T(8,128)S(1)}) custom-call(s32[2]{0:T(128)S(1)} %pad_add_fusion.idx, f32[128,1536]{1,0:T(8,128)S(1)} %get-tuple-element.85.refs_0_, f32[128,1536]{1,0:T(8,128)S(1)} %collective-permute-done.14.refs_1_, bf16[256,3584]{1,0:T(8,128)(2,1)} %get-tuple-element.101.refs_2_, ...), custom_call_target="tpu_custom_call", output_to_operand_aliasing={{0}: (3, {})} | custom-call | flops 33554432 | bytes 1966080 | tf_op jit(solution)/shard_map/combine/pallas_call | solution.py:51
  137.1 9.3 %collective-permute-done.18.refs_2_ = bf16[64,2176]{1,0:T(8,128)(2,1)S(1)} collective-permute-done((bf16[64,2176]{1,0:T(8,128)(2,1)S(1)}, bf16[64,2176]{1,0:T(8,128)(2,1)S(1)}, u32[]{:S(2)}, u32[]{:S(2)}) %collective-permute-start.18) | collective-permute-done | bytes 278560 | tf_op jit(solution)/shard_map/ppermute | solution.py:411
  146.4 5.4 %collective-permute-done.19.refs_3_ = bf16[64,2176]{1,0:T(8,128)(2,1)S(1)} collective-permute-done((bf16[64,2176]{1,0:T(8,128)(2,1)S(1)}, bf16[64,2176]{1,0:T(8,128)(2,1)S(1)}, u32[]{:S(2)}, u32[]{:S(2)}) %collective-permute-start.19) | collective-permute-done | bytes 278560 | tf_op jit(solution)/shard_map/ppermute | solution.py:411
  151.8 2.1 %finish.1 = (bf16[64,4096]{1,0:T(8,128)(2,1)}, f32[8,128]{1,0:T(8,128)}) custom-call(s32[2]{0:T(128)S(1)} %pad_add_fusion.idx, f32[4,1,64,512]{3,2,1,0:T(8,128)S(1)} %get-tuple-element.104.refs_0_, f32[4,1,64,512]{3,2,1,0:T(8,128)S(1)} %get-tuple-element.105.refs_1_, bf16[64,2176]{1,0:T(8,128)(2,1)S(1)} %collective-permute-done.18.refs_2_, ...), custom_call_target="tpu_custom_call" | custom-call | bytes 2097152 | tf_op jit(solution)/shard_map/finish/pallas_call | solution.py:51
  (51 shorter events, 21.4 us)
Async XLA Ops:
  0.6 7.4 %collective-permute-start.3 = (bf16[256,3584]{1,0:T(8,128)(2,1)}, bf16[256,3584]{1,0:T(8,128)(2,1)S(1)}, u32[]{:S(2)}, u32[]{:S(2)}) collective-permute-start(bf16[256,3584]{1,0:T(8,128)(2,1)} %refs_0_.6), channel_id=1, source_target_pairs={{0,1},{1,0},{2,3},{3,2},{4,5},{5,4},{6,7},{7,6},{8,9},{9,8},{10,11... | collective-permute-start | bytes 5505032 | tf_op jit(solution)/shard_map/ppermute | solution.py:414
  1.1 27.7 %collective-permute-start = (bf16[64,4096]{1,0:T(8,128)(2,1)}, bf16[64,4096]{1,0:T(8,128)(2,1)S(1)}, u32[]{:S(2)}, u32[]{:S(2)}) collective-permute-start(bf16[64,4096]{1,0:T(8,128)(2,1)} %refs_0_.7), channel_id=1, source_target_pairs={{0,8},{2,10},{4,12},{6,14},{8,0},{10,2},{12,4},{14,6},{1,9},{3,11}... | collective-permute-start | bytes 1572872 | tf_op jit(solution)/shard_map/ppermute | solution.py:411
  4.8 24.3 %collective-permute-start.1 = (bf16[64,4096]{1,0:T(8,128)(2,1)}, bf16[64,4096]{1,0:T(8,128)(2,1)S(1)}, u32[]{:S(2)}, u32[]{:S(2)}) collective-permute-start(bf16[64,4096]{1,0:T(8,128)(2,1)} %refs_0_.7), channel_id=1, source_target_pairs={{0,4},{2,6},{4,0},{6,2},{8,12},{10,14},{12,8},{14,10},{1,5},{3,7},... | collective-permute-start | bytes 1572872 | tf_op jit(solution)/shard_map/ppermute | solution.py:411
  6.4 22.7 %collective-permute-start.2 = (bf16[64,4096]{1,0:T(8,128)(2,1)}, bf16[64,4096]{1,0:T(8,128)(2,1)S(1)}, u32[]{:S(2)}, u32[]{:S(2)}) collective-permute-start(bf16[64,4096]{1,0:T(8,128)(2,1)} %refs_0_.7), channel_id=1, source_target_pairs={{0,2},{2,0},{4,6},{6,4},{8,10},{10,8},{12,14},{14,12},{1,3},{3,1},... | collective-permute-start | bytes 1572872 | tf_op jit(solution)/shard_map/ppermute | solution.py:411
  10.5 2.2 %copy-start.1 = (bf16[256,3584]{1,0:T(8,128)(2,1)S(1)}, bf16[256,3584]{1,0:T(8,128)(2,1)}, u32[]{:S(2)}) copy-start(bf16[256,3584]{1,0:T(8,128)(2,1)} %refs_0_.6) | copy-start | bytes 5505028
  12.1 15.5 %collective-permute-start.4 = (f32[512,64]{1,0:T(8,128)S(1)}, f32[512,64]{1,0:T(8,128)S(1)}, u32[]{:S(2)}, u32[]{:S(2)}) collective-permute-start(f32[512,64]{1,0:T(8,128)S(1)} %bitcast.3), channel_id=1, source_target_pairs={{0,2},{2,0},{4,6},{6,4},{8,10},{10,8},{12,14},{14,12},{1,3},{3,1},... | collective-permute-start | bytes 393224 | tf_op jit(solution)/shard_map/ppermute | solution.py:411
  26.1 54.8 %collective-permute-start.10 = (bf16[256,2176]{1,0:T(8,128)(2,1)S(1)}, bf16[256,2176]{1,0:T(8,128)(2,1)S(1)}, u32[]{:S(2)}, u32[]{:S(2)}) collective-permute-start(bf16[256,2176]{1,0:T(8,128)(2,1)S(1)} %get-tuple-element.71), channel_id=1, source_target_pairs={{0,2},{2,0},{4,6},{6,4},{8,10},{10,8},{12,14},{14,12},{1,3},{3,1},... | collective-permute-start | bytes 3342344 | tf_op jit(solution)/shard_map/ppermute | solution.py:411
  29.6 22.6 %collective-permute-start.5 = (bf16[64,4096]{1,0:T(8,128)(2,1)S(1)}, bf16[64,4096]{1,0:T(8,128)(2,1)S(1)}, u32[]{:S(2)}, u32[]{:S(2)}) collective-permute-start(bf16[64,4096]{1,0:T(8,128)(2,1)S(1)} %get-tuple-element.62.refs_2_), channel_id=1, source_target_pairs={{0,4},{2,6},{4,0},{6,2},{8,12},{10,14},{12,8},{14,10},{1,5},{3,7},... | collective-permute-start | bytes 1572872 | tf_op jit(solution)/shard_map/ppermute | solution.py:411
  31.2 32.0 %collective-permute-start.6 = (bf16[64,4096]{1,0:T(8,128)(2,1)S(1)}, bf16[64,4096]{1,0:T(8,128)(2,1)S(1)}, u32[]{:S(2)}, u32[]{:S(2)}) collective-permute-start(bf16[64,4096]{1,0:T(8,128)(2,1)S(1)} %get-tuple-element.62.refs_2_), channel_id=1, source_target_pairs={{0,2},{2,0},{4,6},{6,4},{8,10},{10,8},{12,14},{14,12},{1,3},{3,1},... | collective-permute-start | bytes 1572872 | tf_op jit(solution)/shard_map/ppermute | solution.py:411
  32.7 17.4 %collective-permute-start.8 = (f32[512,64]{1,0:T(8,128)S(1)}, f32[512,64]{1,0:T(8,128)S(1)}, u32[]{:S(2)}, u32[]{:S(2)}) collective-permute-start(f32[512,64]{1,0:T(8,128)S(1)} %get-tuple-element.64.refs_0_), channel_id=1, source_target_pairs={{0,4},{2,6},{4,0},{6,2},{8,12},{10,14},{12,8},{14,10},{1,5},{3,7},... | collective-permute-start | bytes 393224 | tf_op jit(solution)/shard_map/ppermute | solution.py:411
  33.3 29.9 %collective-permute-start.7 = (bf16[64,4096]{1,0:T(8,128)(2,1)S(1)}, bf16[64,4096]{1,0:T(8,128)(2,1)S(1)}, u32[]{:S(2)}, u32[]{:S(2)}) collective-permute-start(bf16[64,4096]{1,0:T(8,128)(2,1)S(1)} %get-tuple-element.63.refs_1_), channel_id=1, source_target_pairs={{0,4},{2,6},{4,0},{6,2},{8,12},{10,14},{12,8},{14,10},{1,5},{3,7},... | collective-permute-start | bytes 1572872 | tf_op jit(solution)/shard_map/ppermute | solution.py:411
  48.1 17.2 %copy-start.2 = (bf16[64,4096]{1,0:T(8,128)(2,1)S(1)}, bf16[64,4096]{1,0:T(8,128)(2,1)}, u32[]{:S(2)}) copy-start(bf16[64,4096]{1,0:T(8,128)(2,1)} %refs_5_.5) | copy-start | bytes 1572868
  48.1 17.2 %copy-start.3 = (bf16[64,4096]{1,0:T(8,128)(2,1)S(1)}, bf16[64,4096]{1,0:T(8,128)(2,1)}, u32[]{:S(2)}) copy-start(bf16[64,4096]{1,0:T(8,128)(2,1)} %refs_0_.7) | copy-start | bytes 1572868
  50.2 36.0 %collective-permute-start.13 = (bf16[256,2176]{1,0:T(8,128)(2,1)S(1)}, bf16[256,2176]{1,0:T(8,128)(2,1)S(1)}, u32[]{:S(2)}, u32[]{:S(2)}) collective-permute-start(bf16[256,2176]{1,0:T(8,128)(2,1)S(1)} %get-tuple-element.79), channel_id=1, source_target_pairs={{0,4},{2,6},{4,0},{6,2},{8,12},{10,14},{12,8},{14,10},{1,5},{3,7},... | collective-permute-start | bytes 3342344 | tf_op jit(solution)/shard_map/ppermute | solution.py:411
  63.8 38.8 %collective-permute-start.9 = (bf16[64,4096]{1,0:T(8,128)(2,1)S(1)}, bf16[64,4096]{1,0:T(8,128)(2,1)S(1)}, u32[]{:S(2)}, u32[]{:S(2)}) collective-permute-start(bf16[64,4096]{1,0:T(8,128)(2,1)S(1)} %get-tuple-element.69.refs_2_), channel_id=1, source_target_pairs={{0,2},{2,0},{4,6},{6,4},{8,10},{10,8},{12,14},{14,12},{1,3},{3,1},... | collective-permute-start | bytes 1572872 | tf_op jit(solution)/shard_map/ppermute | solution.py:411
  80.8 47.7 %collective-permute-start.16 = (f32[128,3584]{1,0:T(8,128)S(1)}, f32[128,3584]{1,0:T(8,128)S(1)}, u32[]{:S(2)}, u32[]{:S(2)}) collective-permute-start(f32[128,3584]{1,0:T(8,128)S(1)} %get-tuple-element.90), channel_id=1, source_target_pairs={{0,1},{1,0},{2,3},{3,2},{4,5},{5,4},{6,7},{7,6},{8,9},{9,8},{10,11... | collective-permute-start | bytes 5505032 | tf_op jit(solution)/shard_map/ppermute | solution.py:414
  83.3 29.2 %collective-permute-start.11 = (bf16[128,2176]{1,0:T(8,128)(2,1)S(1)}, bf16[128,2176]{1,0:T(8,128)(2,1)S(1)}, u32[]{:S(2)}, u32[]{:S(2)}) collective-permute-start(bf16[128,2176]{1,0:T(8,128)(2,1)S(1)} %get-tuple-element.76), channel_id=1, source_target_pairs={{0,4},{2,6},{4,0},{6,2},{8,12},{10,14},{12,8},{14,10},{1,5},{3,7},... | collective-permute-start | bytes 1671176 | tf_op jit(solution)/shard_map/ppermute | solution.py:411
  83.8 18.2 %collective-permute-start.12 = (f32[512,64]{1,0:T(8,128)S(1)}, f32[512,64]{1,0:T(8,128)S(1)}, u32[]{:S(2)}, u32[]{:S(2)}) collective-permute-start(f32[512,64]{1,0:T(8,128)S(1)} %get-tuple-element.77.refs_0_), channel_id=1, source_target_pairs={{0,8},{2,10},{4,12},{6,14},{8,0},{10,2},{12,4},{14,6},{1,9},{3,11}... | collective-permute-start | bytes 393224 | tf_op jit(solution)/shard_map/ppermute | solution.py:411
  88.6 38.4 %collective-permute-start.17 = (bf16[128,2176]{1,0:T(8,128)(2,1)S(1)}, bf16[128,2176]{1,0:T(8,128)(2,1)S(1)}, u32[]{:S(2)}, u32[]{:S(2)}) collective-permute-start(bf16[128,2176]{1,0:T(8,128)(2,1)S(1)} %get-tuple-element.92), channel_id=1, source_target_pairs={{0,2},{2,0},{4,6},{6,4},{8,10},{10,8},{12,14},{14,12},{1,3},{3,1},... | collective-permute-start | bytes 1671176 | tf_op jit(solution)/shard_map/ppermute | solution.py:411
  112.4 20.5 %collective-permute-start.15 = (f32[128,2048]{1,0:T(8,128)S(1)}, f32[128,2048]{1,0:T(8,128)S(1)}, u32[]{:S(2)}, u32[]{:S(2)}) collective-permute-start(f32[128,2048]{1,0:T(8,128)S(1)} %get-tuple-element.88), channel_id=1, source_target_pairs={{0,1},{1,0},{2,3},{3,2},{4,5},{5,4},{6,7},{7,6},{8,9},{9,8},{10,11... | collective-permute-start | bytes 3145736 | tf_op jit(solution)/shard_map/ppermute | solution.py:414
  123.0 12.0 %collective-permute-start.14 = (f32[128,1536]{1,0:T(8,128)S(1)}, f32[128,1536]{1,0:T(8,128)S(1)}, u32[]{:S(2)}, u32[]{:S(2)}) collective-permute-start(f32[128,1536]{1,0:T(8,128)S(1)} %get-tuple-element.86), channel_id=1, source_target_pairs={{0,1},{1,0},{2,3},{3,2},{4,5},{5,4},{6,7},{7,6},{8,9},{9,8},{10,11... | collective-permute-start | bytes 2359304 | tf_op jit(solution)/shard_map/ppermute | solution.py:414
  123.6 22.8 %collective-permute-start.18 = (bf16[64,2176]{1,0:T(8,128)(2,1)S(1)}, bf16[64,2176]{1,0:T(8,128)(2,1)S(1)}, u32[]{:S(2)}, u32[]{:S(2)}) collective-permute-start(bf16[64,2176]{1,0:T(8,128)(2,1)S(1)} %get-tuple-element.106), channel_id=1, source_target_pairs={{0,8},{2,10},{4,12},{6,14},{8,0},{10,2},{12,4},{14,6},{1,9},{3,11}... | collective-permute-start | bytes 835592 | tf_op jit(solution)/shard_map/ppermute | solution.py:411
  128.5 23.3 %collective-permute-start.19 = (bf16[64,2176]{1,0:T(8,128)(2,1)S(1)}, bf16[64,2176]{1,0:T(8,128)(2,1)S(1)}, u32[]{:S(2)}, u32[]{:S(2)}) collective-permute-start(bf16[64,2176]{1,0:T(8,128)(2,1)S(1)} %get-tuple-element.107), channel_id=1, source_target_pairs={{0,8},{2,10},{4,12},{6,14},{8,0},{10,2},{12,4},{14,6},{1,9},{3,11}... | collective-permute-start | bytes 835592 | tf_op jit(solution)/shard_map/ppermute | solution.py:411
  132.9 21.0 %collective-permute-start.20 = (f32[4,64,64]{2,1,0:T(8,128)S(1)}, f32[4,64,64]{2,1,0:T(8,128)S(1)}, u32[]{:S(2)}, u32[]{:S(2)}) collective-permute-start(f32[4,64,64]{2,1,0:T(8,128)S(1)} %get-tuple-element.110), channel_id=1, source_target_pairs={{0,1},{1,0},{2,3},{3,2},{4,5},{5,4},{6,7},{7,6},{8,9},{9,8},{10,11... | collective-permute-start | bytes 196616 | tf_op jit(solution)/shard_map/ppermute | solution.py:414
  (2 other events, 2.5 us)

commit v5 on v4

--- a/solution.py
+++ b/solution.py
@@ -16,8 +16,9 @@
 H_TILE = 512
 VMEM_MIB = {"backward": 32, "forward": 24}
 MIB = 1 << 20
-TIMES = {"fold": 0, "combine": 1 << 25, "sketch_part": 1 << 25}
+TIMES = {"forward": 1 << 34, "fold": 0, "combine": 1 << 34, "sketch_part": 1 << 34}
 ANY = pl.BlockSpec(memory_space=pl.ANY)
+HBM = pl.BlockSpec(memory_space=pltpu.HBM)
 
 
 def pick(extent, cap):
@@ -58,7 +59,7 @@
             out_specs=list(out_specs) + [whole(token.shape)],
             scratch_shapes=list(scratch),
         ),
-        compiler_params=pltpu.CompilerParams(vmem_limit_bytes=VMEM_MIB.get(name, 12) * MIB),
+        compiler_params=pltpu.CompilerParams(vmem_limit_bytes=VMEM_MIB.get(name, 14) * MIB),
         cost_estimate=pl.CostEstimate(
             flops=TIMES.get(name, work[0]), bytes_accessed=work[1], transcendentals=0
         ),
@@ -103,12 +104,16 @@
     return pl.ds(pl.multiple_of(start, BLK), BLK)
 
 
-def backward(idx, own, oth, w, count, tile, first, rows, bit, after):
+def backward(idx, own, oth, w, sketch, count, tile, first, rows, bit, after):
     half, hidden = own.shape
     n = 2 * half // rows
     width = count * tile
 
-    def kernel(idx, own, oth, w, msg, keep, x, total, sems):
+    def kernel(idx, own, oth, w, *rest):
+        if sketch is None:
+            msg, keep, x, total, sems = rest
+        else:
+            sk, msg, keep, right, x, total, sems, sk_here = rest
         j = pl.program_id(0)
         me, core = idx[0], idx[1]
 
@@ -118,8 +123,14 @@
             b = pltpu.make_async_copy(oth, x.at[1 - core], sems.at[1])
             a.start()
             b.start()
+            if sketch is not None:
+                c = pltpu.make_async_copy(sk, sk_here, sems.at[2])
+                c.start()
+                c.wait()
             a.wait()
             b.wait()
+            if sketch is not None:
+                right[...] = contract_last(x[...].reshape(2 * half, hidden), sk_here[...])
 
         xs = x[...].reshape(2 * half, hidden)
         total[j] = contract_last(xs, w[...]).reshape(n, rows, tile)
@@ -145,42 +156,31 @@
         jax.ShapeDtypeStruct((n // 2 * rows, width + LANES), jnp.bfloat16),
         jax.ShapeDtypeStruct((count, n // 2, rows, tile), jnp.float32),
     ]
+    args = [own, oth, w]
+    specs = [HBM, ANY, pl.BlockSpec((tile, hidden), lambda j, s: (first + j, 0))]
+    scratch = [
+        pltpu.VMEM((2, half, hidden), jnp.bfloat16),
+        pltpu.VMEM((count, n, rows, tile), jnp.float32),
+        pltpu.SemaphoreType.DMA((3,)),
+    ]
+    if sketch is not None:
+        args.append(sketch)
+        specs.append(HBM)
+        out.append(jax.ShapeDtypeStruct((2 * half, sketch.shape[0]), jnp.float32))
+        scratch.append(pltpu.VMEM(sketch.shape, sketch.dtype))
     return call(
         kernel,
         idx,
-        [own, oth, w],
-        [ANY, ANY, pl.BlockSpec((tile, hidden), lambda j, s: (first + j, 0))],
+        args,
+        specs,
         out,
         [whole(o.shape) for o in out],
         "backward",
         (count,),
         (4 * half * hidden * width, 2 * hidden * width + 12 * half * width),
         after,
-        [
-            pltpu.VMEM((2, half, hidden), jnp.bfloat16),
-            pltpu.VMEM((count, n, rows, tile), jnp.float32),
-            pltpu.SemaphoreType.DMA((2,)),
-        ],
-    )
-
-
-def right_part(idx, own, oth, sketch):
-    half, hidden = own.shape
-    width = sketch.shape[0]
-
-    def kernel(idx, own, oth, sk, out):
-        core = idx[1]
-        out[core] = contract_last(own[...], sk[...])
-        out[1 - core] = contract_last(oth[...], sk[...])
-
-    args = [own, oth, sketch]
-    out = [jax.ShapeDtypeStruct((2, half, width), jnp.float32)]
-    specs = [whole(a.shape) for a in args]
-    work = (4 * half * hidden * width, 4 * half * hidden)
-    (part,), token = call(
-        kernel, idx, args, specs, out, [whole(out[0].shape)], "right", (1,), work, []
-    )
-    return part.reshape(2 * half, width), token
+        scratch,
+    )
 
 
 def fold(idx, keep, got, bit, pos, after):
@@ -307,7 +307,7 @@
             for i, (mask, _) in enumerate(chunks):
                 d = me ^ mask
                 side = 1 - ((d // m) ^ core)
-                to = pl.ds(pl.multiple_of(side * part + (d % (m // 2)) * rows, BLK), rows)
+                to = pl.ds(pl.multiple_of(side * part + ((d % m) >> 1) * rows, BLK), rows)
                 copies.append(pltpu.make_async_copy(refs[i], x.at[to], sems.at[i]))
             for c in copies:
                 c.start()
@@ -337,51 +337,70 @@
     )
 
 
-def combine(idx, keep, got, lo, total, batch, bit, before, after):
-    part, hidden = keep.shape
-    tile = pick(total, H_TILE)
-    block = pl.BlockSpec((part, tile), lambda j, s: (0, j))
+def combine(idx, keep, got, lo, total, batch, rows, before, after):
+    part, width = keep.shape
+    m = part // rows
 
     def kernel(idx, keep, got, *refs):
-        refs[-1][...] = (keep[...] + got[...]).astype(jnp.bfloat16)
+        out, x, sems = refs[-3:]
+        mine = (idx[0] & 1) ^ batch
+        x[...] = (keep[...] + got[...]).astype(jnp.bfloat16)
+        copies = []
+        for i in range(m):
+            to = pl.ds(pl.multiple_of((2 * i + mine) * rows, BLK), rows)
+            copies.append(
+                pltpu.make_async_copy(
+                    x.at[pl.ds(i * rows, rows)], out.at[to, pl.ds(lo, width)], sems.at[i]
+                )
+            )
+        for c in copies:
+            c.start()
+        for c in copies:
+            c.wait()
 
     (out,), token = call(
         kernel,
         idx,
         [keep, got] + before,
-        [block, block] + [ANY] * len(before),
+        [whole(keep.shape)] * 2 + [HBM] * len(before),
         [jax.ShapeDtypeStruct((2 * part, total), jnp.bfloat16)],
-        [pl.BlockSpec((part, tile), lambda j, s: (((s[0] >> bit) & 1) ^ batch, lo + j))],
+        [HBM],
         "combine",
-        (hidden // tile,),
-        (0, 10 * part * hidden),
-        after,
+        (1,),
+        (0, 10 * part * width),
+        after,
+        [pltpu.VMEM((part, width), jnp.bfloat16), pltpu.SemaphoreType.DMA((m,))],
         aliases={3: 0} if before else None,
     )
     return out, [token]
 
 
-def sketch_part(idx, lefts, right, bit, after):
+def sketch_part(idx, lefts, right, rows, after):
     tokens, width = right.shape
-    part = tokens // 4
-    examples = part // LEN
+    half = tokens // 2
+    part = half // 2
+    examples = half // LEN
 
     def kernel(idx, first, second, right, out):
         me, core = idx[0], idx[1]
-        for batch, left in enumerate((first, second)):
-            block = ((me >> bit) & 1) ^ batch
-            for side in (0, 1):
-                owner = 1 - (side ^ core)
-                for e in range(examples):
-                    at = (2 * owner + block) * examples + e
-                    lo = side * part + e * LEN
-                    out[at] = lax.dot_general(
-                        left[lo : lo + LEN, :],
-                        right[pl.ds(pl.multiple_of(at * LEN, LEN), LEN), :],
-                        (((0,), (0,)), ((), ())),
-                        precision=lax.Precision.HIGHEST,
-                        preferred_element_type=jnp.float32,
-                    )
+        for side in (0, 1):
+            owner = 1 - (side ^ core)
+            for e in range(examples):
+                total = jnp.zeros((width, width), jnp.float32)
+                for i in range(part // rows):
+                    if 2 * i * rows // LEN != e:
+                        continue
+                    for batch, left in enumerate((first, second)):
+                        at = owner * half + (2 * i + ((me & 1) ^ batch)) * rows
+                        lo = side * part + i * rows
+                        total += lax.dot_general(
+                            left[lo : lo + rows, :],
+                            right[pl.ds(pl.multiple_of(at, BLK), rows), :],
+                            (((0,), (0,)), ((), ())),
+                            precision=lax.Precision.HIGHEST,
+                            preferred_element_type=jnp.float32,
+                        )
+                out[owner * examples + e] = total
 
     args = [*lefts, right]
     out = [jax.ShapeDtypeStruct((tokens // LEN, width, width), jnp.float32)]
@@ -415,46 +434,65 @@
 
     chunks = {0: inputs}
 
-    def last_bit(mask):
-        if mask.bit_count() == 2 and mask & 2:
+    def wave_of(mask):
+        if mask & 1 and mask > 3:
+            return max(3, mask.bit_count())
+        return 2 if mask == 3 else mask.bit_count()
+
+    def step_of(mask):
+        if mask == 3:
             return 1
-        return (mask & -mask).bit_length() - 1
-
-    def wave(size):
-        for mask in sorted(range(n), reverse=True):
-            if mask.bit_count() == size:
-                bit = last_bit(mask)
+        return 0 if mask & 1 else (mask & -mask).bit_length() - 1
+
+    def wave(k):
+        for mask in sorted(range(1, n), reverse=True):
+            if wave_of(mask) == k:
+                bit = step_of(mask)
                 chunks[mask] = partner(chunks[mask ^ (1 << bit)], bit)
 
-    def hold(size, after):
-        masks = [m for m in chunks if m.bit_count() == size]
+    def hold(k, after):
+        masks = [m for m in range(1, n) if wave_of(m) == k]
         held, token = gate(idx, [chunks[m] for m in masks], after)
         chunks.update(zip(masks, held))
         return token
 
     grad_other = swap(cotangent)
     wave(1)
-    right, t = right_part(idx, cotangent, grad_other, out_sketch)
-    token = [t]
-    right_got = partner(right, 0)
 
     orders = [list(range(bits)), [1, 0] + list(range(2, bits))]
     tile = pick(feats // PIECES, F_TILE)
     count = feats // PIECES // tile
     msgs, keeps = [], []
+    token = []
     for p in range(PIECES):
         outs, t = backward(
-            idx, cotangent, grad_other, weight, count, tile, p * count, rows, orders[p][0], token
+            idx,
+            cotangent,
+            grad_other,
+            weight,
+            out_sketch if p == 0 else None,
+            count,
+            tile,
+            p * count,
+            rows,
+            orders[p][0],
+            token,
         )
-        right, token = add(idx, right, right_got, [t])
-        right_got = partner(right, 1 + p)
+        token = [t]
+        msgs.append(partner(outs[0], orders[p][0]))
+        keeps.append(outs[1])
+        if p == 0:
+            right = outs[2]
+        else:
+            right, token = add(idx, right, right_got, token)
+        right_got = partner(right, p)
         token = hold(1 + p, token)
         wave(2 + p)
-        msgs.append(partner(outs[0], orders[p][0]))
-        keeps.append(outs[1])
-    for k in range(1 + PIECES, bits):
+    for k in range(PIECES, bits - 1):
         right, token = add(idx, right, right_got, token)
         right_got = partner(right, k)
+    last = max(wave_of(m) for m in range(1, n))
+    for k in range(PIECES + 1, last):
         token = hold(k, token)
         wave(k + 1)
 
@@ -468,16 +506,18 @@
     tiles = hidden // pick(hidden, H_TILE)
 
     def batch_forward(batch, lo, hi, after):
-        masks = [m for m in range(n) if (m >> (bits - 2)) & 1 == batch]
-        parts = [(m, chunks[m]) for m in masks]
+        parts = [(m, chunks[m]) for m in range(n) if m & 1 == batch]
         outs, t = forward(idx, parts, weight, in_sketch, lo, hi, after)
-        return (outs[1], swap(outs[0]), lo, hidden, batch, bits - 2), outs[2], [t]
+        start = lo * (hidden // tiles)
+        return (outs[1], swap(outs[0]), start, hidden, batch, rows), outs[2], [t]
 
     cut = -(-tiles // 2)
+    token = folded(0, 1, token)
     first, left1, token = batch_forward(0, 0, tiles, token)
-    token = folded(0, 1, token)
+    token = hold(last, token)
     token = folded(1, 1, token)
     right, token = add(idx, right, right_got, token)
+    right_got = partner(right, bits - 1)
     second, left2, token = batch_forward(1, 0, cut, token)
     token = folded(0, 2, token)
     third, _, token = batch_forward(1, cut, tiles, token)
@@ -485,8 +525,9 @@
     for step in range(3, bits):
         for p in range(PIECES):
             token = folded(p, step, token)
-    outputs, token = combine(idx, *first, [], token)
-    part, token = sketch_part(idx, [left1, left2], right, bits - 2, token)
+    outputs, token = combine(idx, *first, [], token + [msgs[0]])
+    right, token = add(idx, right, right_got, token)
+    part, token = sketch_part(idx, [left1, left2], right, rows, token)
     outputs, token = combine(idx, *second, [outputs], token)
     outputs, token = combine(idx, *third, [outputs], token)
     part = (part + swap(part)) * (1.0 / LEN**0.5)

time: 155 us -> 149 us (0.961)
  starting transfers between devices: 26.3 us -> 19.6 us
  waiting for transfers between devices: 40.3 us -> 43.9 us
  Pallas kernels: 83.9 us -> 81 us
    ppermute x16, starting transfers between devices: 25 us -> 18.7 us  [partner(): return lax.ppermute(x, 'outp', [(d, d ^ 1 << bit) for d in range(n)])]
    ppermute x16, waiting for transfers between devices: 40.3 us -> 43.9 us  [partner(): return lax.ppermute(x, 'outp', [(d, d ^ 1 << bit) for d in range(n)])]
    pallas_call x20, Pallas kernels: 83.9 us -> 81 us  [call(): pl.pallas_call(with_token, out_shape=list(out_shape) + [token], grid_spec...]
  transfers between devices with their start and end apart: 21 -> 21, of which waited for: 7 -> 8; matrix products, arithmetic and copies ran while one was open for 0% -> 0% of each run, Pallas kernels for 54% -> 54%
where the time goes in v5:
time: 149 us
  Pallas kernels  81 us (54%)
  waiting for transfers between devices  43.9 us (29%)
  starting transfers between devices  19.6 us (13%)
  local copies, waits for them, and re-layouts  3.27 us (2%)
    pallas_call x20, Pallas kernels, call(): pl.pallas_call(with_token, out_shape=list(out_shape) + [token], grid_spec...  81 us
    ppermute x16, waiting for transfers between devices, partner(): return lax.ppermute(x, 'outp', [(d, d ^ 1 << bit) for d in range(n)])  43.9 us
    ppermute x16, starting transfers between devices, partner(): return lax.ppermute(x, 'outp', [(d, d ^ 1 << bit) for d in range(n)])  18.7 us
  transfers between devices with their start and end apart: 21, of which 8 were waited for; matrix products, arithmetic and copies ran while one was open for 0% of the time, Pallas kernels for 54%

profile of v5, /device:TPU:0, one launch (start us, length us, event | category | flops | bytes accessed | tf_op | source)
XLA Modules:
  0.0 148.8 jit_solution(7898724400939698119)
XLA Ops:
  1.1 2.6 %collective-permute-start = (bf16[64,4096]{1,0:T(8,128)(2,1)}, bf16[64,4096]{1,0:T(8,128)(2,1)S(1)}, u32[]{:S(2)}, u32[]{:S(2)}) collective-permute-start(bf16[64,4096]{1,0:T(8,128)(2,1)} %refs_0_.5), channel_id=1, source_target_pairs={{0,2},{2,0},{4,6},{6,4},{8,10},{10,8},{12,14},{14,12},{1,3},{3,1},... | collective-permute-start | bytes 1572872 | tf_op jit(solution)/shard_map/ppermute | solution.py:430
  3.7 1.6 %collective-permute-start.1 = (bf16[64,4096]{1,0:T(8,128)(2,1)}, bf16[64,4096]{1,0:T(8,128)(2,1)S(1)}, u32[]{:S(2)}, u32[]{:S(2)}) collective-permute-start(bf16[64,4096]{1,0:T(8,128)(2,1)} %refs_0_.5), channel_id=1, source_target_pairs={{0,4},{2,6},{4,0},{6,2},{8,12},{10,14},{12,8},{14,10},{1,5},{3,7},... | collective-permute-start | bytes 1572872 | tf_op jit(solution)/shard_map/ppermute | solution.py:430
  5.3 2.6 %collective-permute-start.2 = (bf16[64,4096]{1,0:T(8,128)(2,1)}, bf16[64,4096]{1,0:T(8,128)(2,1)S(1)}, u32[]{:S(2)}, u32[]{:S(2)}) collective-permute-start(bf16[64,4096]{1,0:T(8,128)(2,1)} %refs_0_.5), channel_id=1, source_target_pairs={{0,8},{2,10},{4,12},{6,14},{8,0},{10,2},{12,4},{14,6},{1,9},{3,11}... | collective-permute-start | bytes 1572872 | tf_op jit(solution)/shard_map/ppermute | solution.py:430
  8.0 1.5 %copy-done = bf16[256,3584]{1,0:T(8,128)(2,1)S(1)} copy-done((bf16[256,3584]{1,0:T(8,128)(2,1)S(1)}, bf16[256,3584]{1,0:T(8,128)(2,1)}, u32[]{:S(2)}) %copy-start) | copy-done | bytes 1835032
  10.5 14.7 %backward.2 = (bf16[256,2176]{1,0:T(8,128)(2,1)S(1)}, f32[4,4,64,512]{3,2,1,0:T(8,128)S(1)}, f32[512,64]{1,0:T(8,128)S(1)}, f32[8,128]{1,0:T(8,128)S(1)}) custom-call(s32[2]{0:T(128)S(1)} %pad_add_fusion.idx, bf16[256,3584]{1,0:T(8,128)(2,1)S(1)} %copy-done, bf16[256,3584]{1,0:T(8,128)(2,1)S(1)} %collective-permute-done.3.refs_1_, ...), custom_call_target="tpu_custom_call" | custom-call | flops 7516192768 | bytes 20971520 | tf_op jit(solution)/shard_map/backward/pallas_call | solution.py:52
  25.8 3.2 %collective-permute-done.1.refs_1_ = bf16[64,4096]{1,0:T(8,128)(2,1)S(1)} collective-permute-done((bf16[64,4096]{1,0:T(8,128)(2,1)}, bf16[64,4096]{1,0:T(8,128)(2,1)S(1)}, u32[]{:S(2)}, u32[]{:S(2)}) %collective-permute-start.1) | collective-permute-done | bytes 524320 | tf_op jit(solution)/shard_map/ppermute | solution.py:430
  29.1 2.4 %collective-permute-done.2.refs_2_ = bf16[64,4096]{1,0:T(8,128)(2,1)S(1)} collective-permute-done((bf16[64,4096]{1,0:T(8,128)(2,1)}, bf16[64,4096]{1,0:T(8,128)(2,1)S(1)}, u32[]{:S(2)}, u32[]{:S(2)}) %collective-permute-start.2) | collective-permute-done | bytes 524320 | tf_op jit(solution)/shard_map/ppermute | solution.py:430
  33.0 1.5 %collective-permute-start.6 = (f32[512,64]{1,0:T(8,128)S(1)}, f32[512,64]{1,0:T(8,128)S(1)}, u32[]{:S(2)}, u32[]{:S(2)}) collective-permute-start(f32[512,64]{1,0:T(8,128)S(1)} %get-tuple-element.61.refs_0_), channel_id=1, source_target_pairs={{0,2},{2,0},{4,6},{6,4},{8,10},{10,8},{12,14},{14,12},{1,3},{3,1},... | collective-permute-start | bytes 393224 | tf_op jit(solution)/shard_map/ppermute | solution.py:430
  34.5 1.6 %collective-permute-start.4 = (bf16[64,4096]{1,0:T(8,128)(2,1)S(1)}, bf16[64,4096]{1,0:T(8,128)(2,1)S(1)}, u32[]{:S(2)}, u32[]{:S(2)}) collective-permute-start(bf16[64,4096]{1,0:T(8,128)(2,1)S(1)} %get-tuple-element.59.refs_0_), channel_id=1, source_target_pairs={{0,4},{2,6},{4,0},{6,2},{8,12},{10,14},{12,8},{14,10},{1,5},{3,7},... | collective-permute-start | bytes 1572872 | tf_op jit(solution)/shard_map/ppermute | solution.py:430
  36.1 13.4 %backward.3 = (bf16[256,2176]{1,0:T(8,128)(2,1)S(1)}, f32[4,4,64,512]{3,2,1,0:T(8,128)S(1)}, f32[8,128]{1,0:T(8,128)S(1)}) custom-call(s32[2]{0:T(128)S(1)} %pad_add_fusion.idx, bf16[256,3584]{1,0:T(8,128)(2,1)S(1)} %copy-done, bf16[256,3584]{1,0:T(8,128)(2,1)S(1)} %collective-permute-done.3.refs_1_, bf16[4096,3584]{1,0:T(8,128)(2,1)} %refs_4_.5, ...), custom_call_target="tpu_custom_call" | custom-call | flops 7516192768 | bytes 20971520 | tf_op jit(solution)/shard_map/backward/pallas_call | solution.py:52
  49.5 18.8 %collective-permute-done.6.refs_1_ = f32[512,64]{1,0:T(8,128)S(1)} collective-permute-done((f32[512,64]{1,0:T(8,128)S(1)}, f32[512,64]{1,0:T(8,128)S(1)}, u32[]{:S(2)}, u32[]{:S(2)}) %collective-permute-start.6) | collective-permute-done | bytes 131104 | tf_op jit(solution)/shard_map/ppermute | solution.py:430
  69.3 1.6 %collective-permute-start.11 = (f32[512,64]{1,0:T(8,128)S(1)}, f32[512,64]{1,0:T(8,128)S(1)}, u32[]{:S(2)}, u32[]{:S(2)}) collective-permute-start(f32[512,64]{1,0:T(8,128)S(1)} %get-tuple-element.77.refs_0_), channel_id=1, source_target_pairs={{0,4},{2,6},{4,0},{6,2},{8,12},{10,14},{12,8},{14,10},{1,5},{3,7},... | collective-permute-start | bytes 393224 | tf_op jit(solution)/shard_map/ppermute | solution.py:430
  72.1 2.4 %fold.4 = (bf16[128,2176]{1,0:T(8,128)(2,1)S(1)}, f32[4,2,64,512]{3,2,1,0:T(8,128)S(1)}, f32[8,128]{1,0:T(8,128)S(1)}) custom-call(s32[2]{0:T(128)S(1)} %pad_add_fusion.idx, f32[4,4,64,512]{3,2,1,0:T(8,128)S(1)} %get-tuple-element.68.refs_0_, bf16[256,2176]{1,0:T(8,128)(2,1)S(1)} %collective-permute-done.9.refs_1_, f32[8,128]{1,0:T(8,128)S(1)} %get-tuple-element.70.refs_2_), custom_call_target="tpu_custom_call" | custom-call | bytes 6291456 | tf_op jit(solution)/shard_map/fold/pallas_call | solution.py:52
  75.8 15.5 %forward.3 = (f32[128,3584]{1,0:T(8,128)S(1)}, f32[128,3584]{1,0:T(8,128)S(1)}, f32[256,64]{1,0:T(8,128)S(1)}, f32[8,128]{1,0:T(8,128)S(1)}) custom-call(s32[2]{0:T(128)S(1)} %pad_add_fusion.idx, bf16[64,4096]{1,0:T(8,128)(2,1)S(1)} %copy-done.2, bf16[64,4096]{1,0:T(8,128)(2,1)S(1)} %get-tuple-element.67.refs_1_, ...), custom_call_target="tpu_custom_call" | custom-call | flops 17179869184 | bytes 33030144 | tf_op jit(solution)/shard_map/forward/pallas_call | solution.py:52
  91.8 3.9 %collective-permute-done.12.refs_1_ = bf16[256,2176]{1,0:T(8,128)(2,1)S(1)} collective-permute-done((bf16[256,2176]{1,0:T(8,128)(2,1)S(1)}, bf16[256,2176]{1,0:T(8,128)(2,1)S(1)}, u32[]{:S(2)}, u32[]{:S(2)}) %collective-permute-start.12) | collective-permute-done | bytes 1114144 | tf_op jit(solution)/shard_map/ppermute | solution.py:430
  95.7 2.4 %fold.5 = (bf16[128,2176]{1,0:T(8,128)(2,1)S(1)}, f32[4,2,64,512]{3,2,1,0:T(8,128)S(1)}, f32[8,128]{1,0:T(8,128)S(1)}) custom-call(s32[2]{0:T(128)S(1)} %pad_add_fusion.idx, f32[4,4,64,512]{3,2,1,0:T(8,128)S(1)} %get-tuple-element.78.refs_0_, bf16[256,2176]{1,0:T(8,128)(2,1)S(1)} %collective-permute-done.12.refs_1_, f32[8,128]{1,0:T(8,128)S(1)} %get-tuple-element.80.refs_2_), custom_call_target="tpu_custom_call" | custom-call | bytes 6291456 | tf_op jit(solution)/shard_map/fold/pallas_call | solution.py:52
  98.7 2.7 %collective-permute-done.11.refs_1_ = f32[512,64]{1,0:T(8,128)S(1)} collective-permute-done((f32[512,64]{1,0:T(8,128)S(1)}, f32[512,64]{1,0:T(8,128)S(1)}, u32[]{:S(2)}, u32[]{:S(2)}) %collective-permute-start.11) | collective-permute-done | bytes 131104 | tf_op jit(solution)/shard_map/ppermute | solution.py:430
  103.3 9.9 %forward.4 = (f32[128,2048]{1,0:T(8,128)S(1)}, f32[128,2048]{1,0:T(8,128)S(1)}, f32[256,64]{1,0:T(8,128)S(1)}, f32[8,128]{1,0:T(8,128)S(1)}) custom-call(s32[2]{0:T(128)S(1)} %pad_add_fusion.idx, bf16[64,4096]{1,0:T(8,128)(2,1)S(1)} %get-tuple-element.59.refs_0_, bf16[64,4096]{1,0:T(8,128)(2,1)S(1)} %get-tuple-element.65.refs_1_, ...), custom_call_target="tpu_custom_call" | custom-call | flops 17179869184 | bytes 18874368 | tf_op jit(solution)/shard_map/forward/pallas_call | solution.py:52
  113.2 3.4 %collective-permute-done.10.refs_1_ = bf16[128,2176]{1,0:T(8,128)(2,1)S(1)} collective-permute-done((bf16[128,2176]{1,0:T(8,128)(2,1)S(1)}, bf16[128,2176]{1,0:T(8,128)(2,1)S(1)}, u32[]{:S(2)}, u32[]{:S(2)}) %collective-permute-start.10) | collective-permute-done | bytes 557088 | tf_op jit(solution)/shard_map/ppermute | solution.py:430
  119.1 9.0 %forward.5 = (f32[128,1536]{1,0:T(8,128)S(1)}, f32[128,1536]{1,0:T(8,128)S(1)}, f32[256,64]{1,0:T(8,128)}, f32[8,128]{1,0:T(8,128)S(1)}) custom-call(s32[2]{0:T(128)S(1)} %pad_add_fusion.idx, bf16[64,4096]{1,0:T(8,128)(2,1)S(1)} %get-tuple-element.59.refs_0_, bf16[64,4096]{1,0:T(8,128)(2,1)S(1)} %get-tuple-element.65.refs_1_, ...), custom_call_target="tpu_custom_call" | custom-call | flops 17179869184 | bytes 14155776 | tf_op jit(solution)/shard_map/forward/pallas_call | solution.py:52
  129.7 1.7 %collective-permute-done.17.refs_3_.refs_2_ = bf16[64,2176]{1,0:T(8,128)(2,1)S(1)} collective-permute-done((bf16[64,2176]{1,0:T(8,128)(2,1)S(1)}, bf16[64,2176]{1,0:T(8,128)(2,1)S(1)}, u32[]{:S(2)}, u32[]{:S(2)}) %collective-permute-start.17) | collective-permute-done | bytes 278560 | tf_op jit(solution)/shard_map/ppermute | solution.py:430
  131.7 1.6 %combine.3 = (bf16[256,3584]{1,0:T(8,128)(2,1)}, f32[8,128]{1,0:T(8,128)S(1)}) custom-call(s32[2]{0:T(128)S(1)} %pad_add_fusion.idx, f32[128,3584]{1,0:T(8,128)S(1)} %get-tuple-element.89.refs_0_, f32[128,3584]{1,0:T(8,128)S(1)} %collective-permute-done.15.refs_1_, f32[8,128]{1,0:T(8,128)S(1)} %get-tuple-element.94.refs_2_, ...), custom_call_target="tpu_custom_call" | custom-call | flops 17179869184 | bytes 4587520 | tf_op jit(solution)/shard_map/combine/pallas_call | solution.py:52
  138.0 7.9 %collective-permute-done.19.refs_3_ = bf16[64,2176]{1,0:T(8,128)(2,1)S(1)} collective-permute-done((bf16[64,2176]{1,0:T(8,128)(2,1)S(1)}, bf16[64,2176]{1,0:T(8,128)(2,1)S(1)}, u32[]{:S(2)}, u32[]{:S(2)}) %collective-permute-start.19) | collective-permute-done | bytes 278560 | tf_op jit(solution)/shard_map/ppermute | solution.py:430
  145.9 2.1 %finish.1 = (bf16[64,4096]{1,0:T(8,128)(2,1)}, f32[8,128]{1,0:T(8,128)}) custom-call(s32[2]{0:T(128)S(1)} %pad_add_fusion.idx, f32[4,1,64,512]{3,2,1,0:T(8,128)S(1)} %get-tuple-element.107.refs_0_, f32[4,1,64,512]{3,2,1,0:T(8,128)S(1)} %get-tuple-element.108.refs_1_, bf16[64,2176]{1,0:T(8,128)(2,1)S(1)} %collective-permute-done.17.refs_3_.refs_2_, ...), custom_call_target="tpu_custom_call" | custom-call | bytes 2097152 | tf_op jit(solution)/shard_map/finish/pallas_call | solution.py:52
  (49 shorter events, 20.0 us)
Async XLA Ops:
  0.6 7.4 %collective-permute-start.3 = (bf16[256,3584]{1,0:T(8,128)(2,1)}, bf16[256,3584]{1,0:T(8,128)(2,1)S(1)}, u32[]{:S(2)}, u32[]{:S(2)}) collective-permute-start(bf16[256,3584]{1,0:T(8,128)(2,1)} %refs_0_.4), channel_id=1, source_target_pairs={{0,1},{1,0},{2,3},{3,2},{4,5},{5,4},{6,7},{7,6},{8,9},{9,8},{10,11... | collective-permute-start | bytes 5505032 | tf_op jit(solution)/shard_map/ppermute | solution.py:433
  1.1 24.7 %collective-permute-start = (bf16[64,4096]{1,0:T(8,128)(2,1)}, bf16[64,4096]{1,0:T(8,128)(2,1)S(1)}, u32[]{:S(2)}, u32[]{:S(2)}) collective-permute-start(bf16[64,4096]{1,0:T(8,128)(2,1)} %refs_0_.5), channel_id=1, source_target_pairs={{0,2},{2,0},{4,6},{6,4},{8,10},{10,8},{12,14},{14,12},{1,3},{3,1},... | collective-permute-start | bytes 1572872 | tf_op jit(solution)/shard_map/ppermute | solution.py:430
  3.7 25.3 %collective-permute-start.1 = (bf16[64,4096]{1,0:T(8,128)(2,1)}, bf16[64,4096]{1,0:T(8,128)(2,1)S(1)}, u32[]{:S(2)}, u32[]{:S(2)}) collective-permute-start(bf16[64,4096]{1,0:T(8,128)(2,1)} %refs_0_.5), channel_id=1, source_target_pairs={{0,4},{2,6},{4,0},{6,2},{8,12},{10,14},{12,8},{14,10},{1,5},{3,7},... | collective-permute-start | bytes 1572872 | tf_op jit(solution)/shard_map/ppermute | solution.py:430
  5.3 26.1 %collective-permute-start.2 = (bf16[64,4096]{1,0:T(8,128)(2,1)}, bf16[64,4096]{1,0:T(8,128)(2,1)S(1)}, u32[]{:S(2)}, u32[]{:S(2)}) collective-permute-start(bf16[64,4096]{1,0:T(8,128)(2,1)} %refs_0_.5), channel_id=1, source_target_pairs={{0,8},{2,10},{4,12},{6,14},{8,0},{10,2},{12,4},{14,6},{1,9},{3,11}... | collective-permute-start | bytes 1572872 | tf_op jit(solution)/shard_map/ppermute | solution.py:430
  8.0 1.5 %copy-start = (bf16[256,3584]{1,0:T(8,128)(2,1)S(1)}, bf16[256,3584]{1,0:T(8,128)(2,1)}, u32[]{:S(2)}) copy-start(bf16[256,3584]{1,0:T(8,128)(2,1)} %refs_0_.4) | copy-start | bytes 5505028
  25.2 46.8 %collective-permute-start.9 = (bf16[256,2176]{1,0:T(8,128)(2,1)S(1)}, bf16[256,2176]{1,0:T(8,128)(2,1)S(1)}, u32[]{:S(2)}, u32[]{:S(2)}) collective-permute-start(bf16[256,2176]{1,0:T(8,128)(2,1)S(1)} %get-tuple-element.69), channel_id=1, source_target_pairs={{0,2},{2,0},{4,6},{6,4},{8,10},{10,8},{12,14},{14,12},{1,3},{3,1},... | collective-permute-start | bytes 3342344 | tf_op jit(solution)/shard_map/ppermute | solution.py:430
  32.0 38.9 %collective-permute-start.5 = (bf16[64,4096]{1,0:T(8,128)(2,1)S(1)}, bf16[64,4096]{1,0:T(8,128)(2,1)S(1)}, u32[]{:S(2)}, u32[]{:S(2)}) collective-permute-start(bf16[64,4096]{1,0:T(8,128)(2,1)S(1)} %get-tuple-element.60.refs_2_), channel_id=1, source_target_pairs={{0,4},{2,6},{4,0},{6,2},{8,12},{10,14},{12,8},{14,10},{1,5},{3,7},... | collective-permute-start | bytes 1572872 | tf_op jit(solution)/shard_map/ppermute | solution.py:430
  32.5 58.8 %collective-permute-start.7 = (bf16[64,4096]{1,0:T(8,128)(2,1)S(1)}, bf16[64,4096]{1,0:T(8,128)(2,1)S(1)}, u32[]{:S(2)}, u32[]{:S(2)}) collective-permute-start(bf16[64,4096]{1,0:T(8,128)(2,1)S(1)} %get-tuple-element.60.refs_2_), channel_id=1, source_target_pairs={{0,2},{2,0},{4,6},{6,4},{8,10},{10,8},{12,14},{14,12},{1,3},{3,1},... | collective-permute-start | bytes 1572872 | tf_op jit(solution)/shard_map/ppermute | solution.py:430
  33.0 35.3 %collective-permute-start.6 = (f32[512,64]{1,0:T(8,128)S(1)}, f32[512,64]{1,0:T(8,128)S(1)}, u32[]{:S(2)}, u32[]{:S(2)}) collective-permute-start(f32[512,64]{1,0:T(8,128)S(1)} %get-tuple-element.61.refs_0_), channel_id=1, source_target_pairs={{0,2},{2,0},{4,6},{6,4},{8,10},{10,8},{12,14},{14,12},{1,3},{3,1},... | collective-permute-start | bytes 393224 | tf_op jit(solution)/shard_map/ppermute | solution.py:430
  34.5 34.8 %collective-permute-start.4 = (bf16[64,4096]{1,0:T(8,128)(2,1)S(1)}, bf16[64,4096]{1,0:T(8,128)(2,1)S(1)}, u32[]{:S(2)}, u32[]{:S(2)}) collective-permute-start(bf16[64,4096]{1,0:T(8,128)(2,1)S(1)} %get-tuple-element.59.refs_0_), channel_id=1, source_target_pairs={{0,4},{2,6},{4,0},{6,2},{8,12},{10,14},{12,8},{14,10},{1,5},{3,7},... | collective-permute-start | bytes 1572872 | tf_op jit(solution)/shard_map/ppermute | solution.py:430
  68.2 27.5 %collective-permute-start.12 = (bf16[256,2176]{1,0:T(8,128)(2,1)S(1)}, bf16[256,2176]{1,0:T(8,128)(2,1)S(1)}, u32[]{:S(2)}, u32[]{:S(2)}) collective-permute-start(bf16[256,2176]{1,0:T(8,128)(2,1)S(1)} %get-tuple-element.79), channel_id=1, source_target_pairs={{0,4},{2,6},{4,0},{6,2},{8,12},{10,14},{12,8},{14,10},{1,5},{3,7},... | collective-permute-start | bytes 3342344 | tf_op jit(solution)/shard_map/ppermute | solution.py:430
  69.3 32.1 %collective-permute-start.11 = (f32[512,64]{1,0:T(8,128)S(1)}, f32[512,64]{1,0:T(8,128)S(1)}, u32[]{:S(2)}, u32[]{:S(2)}) collective-permute-start(f32[512,64]{1,0:T(8,128)S(1)} %get-tuple-element.77.refs_0_), channel_id=1, source_target_pairs={{0,4},{2,6},{4,0},{6,2},{8,12},{10,14},{12,8},{14,10},{1,5},{3,7},... | collective-permute-start | bytes 393224 | tf_op jit(solution)/shard_map/ppermute | solution.py:430
  71.5 4.3 %copy-start.2 = (bf16[64,4096]{1,0:T(8,128)(2,1)S(1)}, bf16[64,4096]{1,0:T(8,128)(2,1)}, u32[]{:S(2)}) copy-start(bf16[64,4096]{1,0:T(8,128)(2,1)} %refs_0_.5) | copy-start | bytes 1572868
  71.5 4.3 %copy-start.3 = (bf16[64,4096]{1,0:T(8,128)(2,1)S(1)}, bf16[64,4096]{1,0:T(8,128)(2,1)}, u32[]{:S(2)}) copy-start(bf16[64,4096]{1,0:T(8,128)(2,1)} %refs_5_.5) | copy-start | bytes 1572868
  71.5 19.8 %collective-permute-start.8 = (bf16[64,4096]{1,0:T(8,128)(2,1)S(1)}, bf16[64,4096]{1,0:T(8,128)(2,1)S(1)}, u32[]{:S(2)}, u32[]{:S(2)}) collective-permute-start(bf16[64,4096]{1,0:T(8,128)(2,1)S(1)} %get-tuple-element.66.refs_3_), channel_id=1, source_target_pairs={{0,2},{2,0},{4,6},{6,4},{8,10},{10,8},{12,14},{14,12},{1,3},{3,1},... | collective-permute-start | bytes 1572872 | tf_op jit(solution)/shard_map/ppermute | solution.py:430
  74.5 42.1 %collective-permute-start.10 = (bf16[128,2176]{1,0:T(8,128)(2,1)S(1)}, bf16[128,2176]{1,0:T(8,128)(2,1)S(1)}, u32[]{:S(2)}, u32[]{:S(2)}) collective-permute-start(bf16[128,2176]{1,0:T(8,128)(2,1)S(1)} %get-tuple-element.76), channel_id=1, source_target_pairs={{0,4},{2,6},{4,0},{6,2},{8,12},{10,14},{12,8},{14,10},{1,5},{3,7},... | collective-permute-start | bytes 1671176 | tf_op jit(solution)/shard_map/ppermute | solution.py:430
  98.1 30.0 %collective-permute-start.16 = (bf16[128,2176]{1,0:T(8,128)(2,1)S(1)}, bf16[128,2176]{1,0:T(8,128)(2,1)S(1)}, u32[]{:S(2)}, u32[]{:S(2)}) collective-permute-start(bf16[128,2176]{1,0:T(8,128)(2,1)S(1)} %get-tuple-element.92), channel_id=1, source_target_pairs={{0,2},{2,0},{4,6},{6,4},{8,10},{10,8},{12,14},{14,12},{1,3},{3,1},... | collective-permute-start | bytes 1671176 | tf_op jit(solution)/shard_map/ppermute | solution.py:430
  98.7 33.0 %collective-permute-start.15 = (f32[128,3584]{1,0:T(8,128)S(1)}, f32[128,3584]{1,0:T(8,128)S(1)}, u32[]{:S(2)}, u32[]{:S(2)}) collective-permute-start(f32[128,3584]{1,0:T(8,128)S(1)} %get-tuple-element.90), channel_id=1, source_target_pairs={{0,1},{1,0},{2,3},{3,2},{4,5},{5,4},{6,7},{7,6},{8,9},{9,8},{10,11... | collective-permute-start | bytes 5505032 | tf_op jit(solution)/shard_map/ppermute | solution.py:433
  101.9 31.4 %collective-permute-start.18 = (f32[512,64]{1,0:T(8,128)S(1)}, f32[512,64]{1,0:T(8,128)S(1)}, u32[]{:S(2)}, u32[]{:S(2)}) collective-permute-start(f32[512,64]{1,0:T(8,128)S(1)} %get-tuple-element.99.refs_0_), channel_id=1, source_target_pairs={{0,8},{2,10},{4,12},{6,14},{8,0},{10,2},{12,4},{14,6},{1,9},{3,11}... | collective-permute-start | bytes 393224 | tf_op jit(solution)/shard_map/ppermute | solution.py:430
  113.2 22.0 %collective-permute-start.14 = (f32[128,2048]{1,0:T(8,128)S(1)}, f32[128,2048]{1,0:T(8,128)S(1)}, u32[]{:S(2)}, u32[]{:S(2)}) collective-permute-start(f32[128,2048]{1,0:T(8,128)S(1)} %get-tuple-element.88), channel_id=1, source_target_pairs={{0,1},{1,0},{2,3},{3,2},{4,5},{5,4},{6,7},{7,6},{8,9},{9,8},{10,11... | collective-permute-start | bytes 3145736 | tf_op jit(solution)/shard_map/ppermute | solution.py:433
  118.1 13.3 %collective-permute-start.17 = (bf16[64,2176]{1,0:T(8,128)(2,1)S(1)}, bf16[64,2176]{1,0:T(8,128)(2,1)S(1)}, u32[]{:S(2)}, u32[]{:S(2)}) collective-permute-start(bf16[64,2176]{1,0:T(8,128)(2,1)S(1)} %get-tuple-element.95), channel_id=1, source_target_pairs={{0,8},{2,10},{4,12},{6,14},{8,0},{10,2},{12,4},{14,6},{1,9},{3,11}... | collective-permute-start | bytes 835592 | tf_op jit(solution)/shard_map/ppermute | solution.py:430
  128.1 8.5 %collective-permute-start.13 = (f32[128,1536]{1,0:T(8,128)S(1)}, f32[128,1536]{1,0:T(8,128)S(1)}, u32[]{:S(2)}, u32[]{:S(2)}) collective-permute-start(f32[128,1536]{1,0:T(8,128)S(1)} %get-tuple-element.86), channel_id=1, source_target_pairs={{0,1},{1,0},{2,3},{3,2},{4,5},{5,4},{6,7},{7,6},{8,9},{9,8},{10,11... | collective-permute-start | bytes 2359304 | tf_op jit(solution)/shard_map/ppermute | solution.py:433
  131.4 14.5 %collective-permute-start.19 = (bf16[64,2176]{1,0:T(8,128)(2,1)S(1)}, bf16[64,2176]{1,0:T(8,128)(2,1)S(1)}, u32[]{:S(2)}, u32[]{:S(2)}) collective-permute-start(bf16[64,2176]{1,0:T(8,128)(2,1)S(1)} %get-tuple-element.109), channel_id=1, source_target_pairs={{0,8},{2,10},{4,12},{6,14},{8,0},{10,2},{12,4},{14,6},{1,9},{3,11}... | collective-permute-start | bytes 835592 | tf_op jit(solution)/shard_map/ppermute | solution.py:430
  134.9 13.1 %collective-permute-start.20 = (f32[4,64,64]{2,1,0:T(8,128)S(1)}, f32[4,64,64]{2,1,0:T(8,128)S(1)}, u32[]{:S(2)}, u32[]{:S(2)}) collective-permute-start(f32[4,64,64]{2,1,0:T(8,128)S(1)} %get-tuple-element.112), channel_id=1, source_target_pairs={{0,1},{1,0},{2,3},{3,2},{4,5},{5,4},{6,7},{7,6},{8,9},{9,8},{10,11... | collective-permute-start | bytes 196616 | tf_op jit(solution)/shard_map/ppermute | solution.py:433
  (1 other events, 1.0 us)

commit v6 on v5

--- a/solution.py
+++ b/solution.py
@@ -483,14 +483,9 @@
         keeps.append(outs[1])
         if p == 0:
             right = outs[2]
-        else:
-            right, token = add(idx, right, right_got, token)
-        right_got = partner(right, p)
+            right_got = partner(right, 0)
         token = hold(1 + p, token)
         wave(2 + p)
-    for k in range(PIECES, bits - 1):
-        right, token = add(idx, right, right_got, token)
-        right_got = partner(right, k)
     last = max(wave_of(m) for m in range(1, n))
     for k in range(PIECES + 1, last):
         token = hold(k, token)
@@ -517,9 +512,11 @@
     token = hold(last, token)
     token = folded(1, 1, token)
     right, token = add(idx, right, right_got, token)
-    right_got = partner(right, bits - 1)
+    right_got = partner(right, 1)
     second, left2, token = batch_forward(1, 0, cut, token)
     token = folded(0, 2, token)
+    right, token = add(idx, right, right_got, token)
+    right_got = partner(right, 2)
     third, _, token = batch_forward(1, cut, tiles, token)
     token = folded(1, 2, token)
     for step in range(3, bits):
@@ -527,6 +524,8 @@
             token = folded(p, step, token)
     outputs, token = combine(idx, *first, [], token + [msgs[0]])
     right, token = add(idx, right, right_got, token)
+    for k in range(3, bits):
+        right, token = add(idx, right, partner(right, k), token)
     part, token = sketch_part(idx, [left1, left2], right, rows, token)
     outputs, token = combine(idx, *second, [outputs], token)
     outputs, token = combine(idx, *third, [outputs], token)

time: 149 us -> 140 us (0.940)
  waiting for transfers between devices: 43.9 us -> 36 us
    ppermute x16, waiting for transfers between devices: 43.9 us -> 36 us  [partner(): return lax.ppermute(x, 'outp', [(d, d ^ 1 << bit) for d in range(n)])]
    ppermute x16, starting transfers between devices: 18.7 us -> 17.1 us  [partner(): return lax.ppermute(x, 'outp', [(d, d ^ 1 << bit) for d in range(n)])]
  transfers between devices with their start and end apart: 21 -> 21, of which waited for: 8 -> 8; matrix products, arithmetic and copies ran while one was open for 0% -> 0% of each run, Pallas kernels for 54% -> 58%
where the time goes in v6:
time: 140 us
  Pallas kernels  81.1 us (58%)
  waiting for transfers between devices  36 us (26%)
  starting transfers between devices  18.2 us (13%)
  local copies, waits for them, and re-layouts  3.27 us (2%)
    pallas_call x20, Pallas kernels, call(): pl.pallas_call(with_token, out_shape=list(out_shape) + [token], grid_spec...  81.1 us
    ppermute x16, waiting for transfers between devices, partner(): return lax.ppermute(x, 'outp', [(d, d ^ 1 << bit) for d in range(n)])  36 us
    ppermute x16, starting transfers between devices, partner(): return lax.ppermute(x, 'outp', [(d, d ^ 1 << bit) for d in range(n)])  17.1 us
  transfers between devices with their start and end apart: 21, of which 8 were waited for; matrix products, arithmetic and copies ran while one was open for 0% of the time, Pallas kernels for 58%

profile of v6, /device:TPU:0, one launch (start us, length us, event | category | flops | bytes accessed | tf_op | source)
XLA Modules:
  0.0 139.5 jit_solution(5142339047329043153)
XLA Ops:
  1.1 2.6 %collective-permute-start = (bf16[64,4096]{1,0:T(8,128)(2,1)}, bf16[64,4096]{1,0:T(8,128)(2,1)S(1)}, u32[]{:S(2)}, u32[]{:S(2)}) collective-permute-start(bf16[64,4096]{1,0:T(8,128)(2,1)} %refs_0_.5), channel_id=1, source_target_pairs={{0,2},{2,0},{4,6},{6,4},{8,10},{10,8},{12,14},{14,12},{1,3},{3,1},... | collective-permute-start | bytes 1572872 | tf_op jit(solution)/shard_map/ppermute | solution.py:430
  3.7 1.6 %collective-permute-start.1 = (bf16[64,4096]{1,0:T(8,128)(2,1)}, bf16[64,4096]{1,0:T(8,128)(2,1)S(1)}, u32[]{:S(2)}, u32[]{:S(2)}) collective-permute-start(bf16[64,4096]{1,0:T(8,128)(2,1)} %refs_0_.5), channel_id=1, source_target_pairs={{0,4},{2,6},{4,0},{6,2},{8,12},{10,14},{12,8},{14,10},{1,5},{3,7},... | collective-permute-start | bytes 1572872 | tf_op jit(solution)/shard_map/ppermute | solution.py:430
  5.3 2.6 %collective-permute-start.2 = (bf16[64,4096]{1,0:T(8,128)(2,1)}, bf16[64,4096]{1,0:T(8,128)(2,1)S(1)}, u32[]{:S(2)}, u32[]{:S(2)}) collective-permute-start(bf16[64,4096]{1,0:T(8,128)(2,1)} %refs_0_.5), channel_id=1, source_target_pairs={{0,8},{2,10},{4,12},{6,14},{8,0},{10,2},{12,4},{14,6},{1,9},{3,11}... | collective-permute-start | bytes 1572872 | tf_op jit(solution)/shard_map/ppermute | solution.py:430
  8.0 1.5 %copy-done = bf16[256,3584]{1,0:T(8,128)(2,1)S(1)} copy-done((bf16[256,3584]{1,0:T(8,128)(2,1)S(1)}, bf16[256,3584]{1,0:T(8,128)(2,1)}, u32[]{:S(2)}) %copy-start) | copy-done | bytes 1835032
  10.5 14.7 %backward.2 = (bf16[256,2176]{1,0:T(8,128)(2,1)S(1)}, f32[4,4,64,512]{3,2,1,0:T(8,128)S(1)}, f32[512,64]{1,0:T(8,128)S(1)}, f32[8,128]{1,0:T(8,128)S(1)}) custom-call(s32[2]{0:T(128)S(1)} %pad_add_fusion.idx, bf16[256,3584]{1,0:T(8,128)(2,1)S(1)} %copy-done, bf16[256,3584]{1,0:T(8,128)(2,1)S(1)} %collective-permute-done.3.refs_1_, ...), custom_call_target="tpu_custom_call" | custom-call | flops 7516192768 | bytes 20971520 | tf_op jit(solution)/shard_map/backward/pallas_call | solution.py:52
  25.8 3.2 %collective-permute-done.1.refs_1_ = bf16[64,4096]{1,0:T(8,128)(2,1)S(1)} collective-permute-done((bf16[64,4096]{1,0:T(8,128)(2,1)}, bf16[64,4096]{1,0:T(8,128)(2,1)S(1)}, u32[]{:S(2)}, u32[]{:S(2)}) %collective-permute-start.1) | collective-permute-done | bytes 524320 | tf_op jit(solution)/shard_map/ppermute | solution.py:430
  29.1 2.4 %collective-permute-done.2.refs_2_ = bf16[64,4096]{1,0:T(8,128)(2,1)S(1)} collective-permute-done((bf16[64,4096]{1,0:T(8,128)(2,1)}, bf16[64,4096]{1,0:T(8,128)(2,1)S(1)}, u32[]{:S(2)}, u32[]{:S(2)}) %collective-permute-start.2) | collective-permute-done | bytes 524320 | tf_op jit(solution)/shard_map/ppermute | solution.py:430
  33.0 1.6 %collective-permute-start.4 = (bf16[64,4096]{1,0:T(8,128)(2,1)S(1)}, bf16[64,4096]{1,0:T(8,128)(2,1)S(1)}, u32[]{:S(2)}, u32[]{:S(2)}) collective-permute-start(bf16[64,4096]{1,0:T(8,128)(2,1)S(1)} %get-tuple-element.59.refs_0_), channel_id=1, source_target_pairs={{0,4},{2,6},{4,0},{6,2},{8,12},{10,14},{12,8},{14,10},{1,5},{3,7},... | collective-permute-start | bytes 1572872 | tf_op jit(solution)/shard_map/ppermute | solution.py:430
  34.6 13.4 %backward.3 = (bf16[256,2176]{1,0:T(8,128)(2,1)S(1)}, f32[4,4,64,512]{3,2,1,0:T(8,128)S(1)}, f32[8,128]{1,0:T(8,128)S(1)}) custom-call(s32[2]{0:T(128)S(1)} %pad_add_fusion.idx, bf16[256,3584]{1,0:T(8,128)(2,1)S(1)} %copy-done, bf16[256,3584]{1,0:T(8,128)(2,1)S(1)} %collective-permute-done.3.refs_1_, bf16[4096,3584]{1,0:T(8,128)(2,1)} %refs_4_.5, ...), custom_call_target="tpu_custom_call" | custom-call | flops 7516192768 | bytes 20971520 | tf_op jit(solution)/shard_map/backward/pallas_call | solution.py:52
  48.5 9.7 %collective-permute-done.4.refs_0_ = bf16[64,4096]{1,0:T(8,128)(2,1)S(1)} collective-permute-done((bf16[64,4096]{1,0:T(8,128)(2,1)S(1)}, bf16[64,4096]{1,0:T(8,128)(2,1)S(1)}, u32[]{:S(2)}, u32[]{:S(2)}) %collective-permute-start.4) | collective-permute-done | bytes 524320 | tf_op jit(solution)/shard_map/ppermute | solution.py:430
  59.2 1.6 %collective-permute-start.7 = (bf16[64,4096]{1,0:T(8,128)(2,1)S(1)}, bf16[64,4096]{1,0:T(8,128)(2,1)S(1)}, u32[]{:S(2)}, u32[]{:S(2)}) collective-permute-start(bf16[64,4096]{1,0:T(8,128)(2,1)S(1)} %get-tuple-element.64.refs_3_), channel_id=1, source_target_pairs={{0,2},{2,0},{4,6},{6,4},{8,10},{10,8},{12,14},{14,12},{1,3},{3,1},... | collective-permute-start | bytes 1572872 | tf_op jit(solution)/shard_map/ppermute | solution.py:430
  60.8 2.4 %fold.4 = (bf16[128,2176]{1,0:T(8,128)(2,1)S(1)}, f32[4,2,64,512]{3,2,1,0:T(8,128)S(1)}, f32[8,128]{1,0:T(8,128)S(1)}) custom-call(s32[2]{0:T(128)S(1)} %pad_add_fusion.idx, f32[4,4,64,512]{3,2,1,0:T(8,128)S(1)} %get-tuple-element.66.refs_0_, bf16[256,2176]{1,0:T(8,128)(2,1)S(1)} %collective-permute-done.8.refs_1_, f32[8,128]{1,0:T(8,128)S(1)} %get-tuple-element.68.refs_2_), custom_call_target="tpu_custom_call" | custom-call | bytes 6291456 | tf_op jit(solution)/shard_map/fold/pallas_call | solution.py:52
  63.7 15.5 %forward.3 = (f32[128,3584]{1,0:T(8,128)S(1)}, f32[128,3584]{1,0:T(8,128)S(1)}, f32[256,64]{1,0:T(8,128)S(1)}, f32[8,128]{1,0:T(8,128)S(1)}) custom-call(s32[2]{0:T(128)S(1)} %pad_add_fusion.idx, bf16[64,4096]{1,0:T(8,128)(2,1)S(1)} %copy-done.2, bf16[64,4096]{1,0:T(8,128)(2,1)S(1)} %get-tuple-element.65.refs_1_, ...), custom_call_target="tpu_custom_call" | custom-call | flops 17179869184 | bytes 33030144 | tf_op jit(solution)/shard_map/forward/pallas_call | solution.py:52
  80.0 2.0 %collective-permute-done.10.refs_1_ = bf16[256,2176]{1,0:T(8,128)(2,1)S(1)} collective-permute-done((bf16[256,2176]{1,0:T(8,128)(2,1)S(1)}, bf16[256,2176]{1,0:T(8,128)(2,1)S(1)}, u32[]{:S(2)}, u32[]{:S(2)}) %collective-permute-start.10) | collective-permute-done | bytes 1114144 | tf_op jit(solution)/shard_map/ppermute | solution.py:430
  82.0 2.4 %fold.5 = (bf16[128,2176]{1,0:T(8,128)(2,1)S(1)}, f32[4,2,64,512]{3,2,1,0:T(8,128)S(1)}, f32[8,128]{1,0:T(8,128)S(1)}) custom-call(s32[2]{0:T(128)S(1)} %pad_add_fusion.idx, f32[4,4,64,512]{3,2,1,0:T(8,128)S(1)} %get-tuple-element.74.refs_0_, bf16[256,2176]{1,0:T(8,128)(2,1)S(1)} %collective-permute-done.10.refs_1_, f32[8,128]{1,0:T(8,128)S(1)} %get-tuple-element.76.refs_2_), custom_call_target="tpu_custom_call" | custom-call | bytes 6291456 | tf_op jit(solution)/shard_map/fold/pallas_call | solution.py:52
  86.0 9.9 %forward.4 = (f32[128,2048]{1,0:T(8,128)S(1)}, f32[128,2048]{1,0:T(8,128)S(1)}, f32[256,64]{1,0:T(8,128)S(1)}, f32[8,128]{1,0:T(8,128)S(1)}) custom-call(s32[2]{0:T(128)S(1)} %pad_add_fusion.idx, bf16[64,4096]{1,0:T(8,128)(2,1)S(1)} %get-tuple-element.59.refs_0_, bf16[64,4096]{1,0:T(8,128)(2,1)S(1)} %get-tuple-element.63.refs_1_, ...), custom_call_target="tpu_custom_call" | custom-call | flops 17179869184 | bytes 18874368 | tf_op jit(solution)/shard_map/forward/pallas_call | solution.py:52
  98.0 2.7 %collective-permute-start.17 = (bf16[64,2176]{1,0:T(8,128)(2,1)S(1)}, bf16[64,2176]{1,0:T(8,128)(2,1)S(1)}, u32[]{:S(2)}, u32[]{:S(2)}) collective-permute-start(bf16[64,2176]{1,0:T(8,128)(2,1)S(1)} %get-tuple-element.95), channel_id=1, source_target_pairs={{0,8},{2,10},{4,12},{6,14},{8,0},{10,2},{12,4},{14,6},{1,9},{3,11}... | collective-permute-start | bytes 835592 | tf_op jit(solution)/shard_map/ppermute | solution.py:430
  101.2 9.0 %forward.5 = (f32[128,1536]{1,0:T(8,128)S(1)}, f32[128,1536]{1,0:T(8,128)S(1)}, f32[256,64]{1,0:T(8,128)}, f32[8,128]{1,0:T(8,128)S(1)}) custom-call(s32[2]{0:T(128)S(1)} %pad_add_fusion.idx, bf16[64,4096]{1,0:T(8,128)(2,1)S(1)} %get-tuple-element.59.refs_0_, bf16[64,4096]{1,0:T(8,128)(2,1)S(1)} %get-tuple-element.63.refs_1_, ...), custom_call_target="tpu_custom_call" | custom-call | flops 17179869184 | bytes 14155776 | tf_op jit(solution)/shard_map/forward/pallas_call | solution.py:52
  110.6 1.5 %fold.7 = (bf16[64,2176]{1,0:T(8,128)(2,1)S(1)}, f32[4,1,64,512]{3,2,1,0:T(8,128)S(1)}, f32[8,128]{1,0:T(8,128)S(1)}) custom-call(s32[2]{0:T(128)S(1)} %pad_add_fusion.idx, f32[4,2,64,512]{3,2,1,0:T(8,128)S(1)} %get-tuple-element.91.refs_0_, bf16[128,2176]{1,0:T(8,128)(2,1)S(1)} %collective-permute-done.16.refs_1_, f32[8,128]{1,0:T(8,128)S(1)} %get-tuple-element.93.refs_2_), custom_call_target="tpu_custom_call" | custom-call | bytes 3145728 | tf_op jit(solution)/shard_map/fold/pallas_call | solution.py:52
  112.1 10.2 %collective-permute-done.17.refs_3_.refs_2_ = bf16[64,2176]{1,0:T(8,128)(2,1)S(1)} collective-permute-done((bf16[64,2176]{1,0:T(8,128)(2,1)S(1)}, bf16[64,2176]{1,0:T(8,128)(2,1)S(1)}, u32[]{:S(2)}, u32[]{:S(2)}) %collective-permute-start.17) | collective-permute-done | bytes 278560 | tf_op jit(solution)/shard_map/ppermute | solution.py:430
  122.3 1.6 %combine.3 = (bf16[256,3584]{1,0:T(8,128)(2,1)}, f32[8,128]{1,0:T(8,128)S(1)}) custom-call(s32[2]{0:T(128)S(1)} %pad_add_fusion.idx, f32[128,3584]{1,0:T(8,128)S(1)} %get-tuple-element.89.refs_0_, f32[128,3584]{1,0:T(8,128)S(1)} %collective-permute-done.15.refs_1_, f32[8,128]{1,0:T(8,128)S(1)} %get-tuple-element.94.refs_2_, ...), custom_call_target="tpu_custom_call" | custom-call | flops 17179869184 | bytes 4587520 | tf_op jit(solution)/shard_map/combine/pallas_call | solution.py:52
  124.0 7.0 %collective-permute-done.18.refs_1_ = f32[512,64]{1,0:T(8,128)S(1)} collective-permute-done((f32[512,64]{1,0:T(8,128)S(1)}, f32[512,64]{1,0:T(8,128)S(1)}, u32[]{:S(2)}, u32[]{:S(2)}) %collective-permute-start.18) | collective-permute-done | bytes 131104 | tf_op jit(solution)/shard_map/ppermute | solution.py:430
  132.5 1.5 %combine.4 = (bf16[256,3584]{1,0:T(8,128)(2,1)}, f32[8,128]{1,0:T(8,128)S(1)}) custom-call(s32[2]{0:T(128)S(1)} %pad_add_fusion.idx, f32[128,2048]{1,0:T(8,128)S(1)} %get-tuple-element.87.refs_0_, f32[128,2048]{1,0:T(8,128)S(1)} %collective-permute-done.14.refs_1_, bf16[256,3584]{1,0:T(8,128)(2,1)} %get-tuple-element.96.refs_2_, ...), custom_call_target="tpu_custom_call", output_to_operand_aliasing={{0}: (3, {})} | custom-call | flops 17179869184 | bytes 2621440 | tf_op jit(solution)/shard_map/combine/pallas_call | solution.py:52
  136.6 2.1 %finish.1 = (bf16[64,4096]{1,0:T(8,128)(2,1)}, f32[8,128]{1,0:T(8,128)}) custom-call(s32[2]{0:T(128)S(1)} %pad_add_fusion.idx, f32[4,1,64,512]{3,2,1,0:T(8,128)S(1)} %get-tuple-element.107.refs_0_, f32[4,1,64,512]{3,2,1,0:T(8,128)S(1)} %get-tuple-element.108.refs_1_, bf16[64,2176]{1,0:T(8,128)(2,1)S(1)} %collective-permute-done.17.refs_3_.refs_2_, ...), custom_call_target="tpu_custom_call" | custom-call | bytes 2097152 | tf_op jit(solution)/shard_map/finish/pallas_call | solution.py:52
  (49 shorter events, 16.1 us)
Async XLA Ops:
  0.6 7.4 %collective-permute-start.3 = (bf16[256,3584]{1,0:T(8,128)(2,1)}, bf16[256,3584]{1,0:T(8,128)(2,1)S(1)}, u32[]{:S(2)}, u32[]{:S(2)}) collective-permute-start(bf16[256,3584]{1,0:T(8,128)(2,1)} %refs_0_.4), channel_id=1, source_target_pairs={{0,1},{1,0},{2,3},{3,2},{4,5},{5,4},{6,7},{7,6},{8,9},{9,8},{10,11... | collective-permute-start | bytes 5505032 | tf_op jit(solution)/shard_map/ppermute | solution.py:433
  1.1 24.7 %collective-permute-start = (bf16[64,4096]{1,0:T(8,128)(2,1)}, bf16[64,4096]{1,0:T(8,128)(2,1)S(1)}, u32[]{:S(2)}, u32[]{:S(2)}) collective-permute-start(bf16[64,4096]{1,0:T(8,128)(2,1)} %refs_0_.5), channel_id=1, source_target_pairs={{0,2},{2,0},{4,6},{6,4},{8,10},{10,8},{12,14},{14,12},{1,3},{3,1},... | collective-permute-start | bytes 1572872 | tf_op jit(solution)/shard_map/ppermute | solution.py:430
  3.7 25.3 %collective-permute-start.1 = (bf16[64,4096]{1,0:T(8,128)(2,1)}, bf16[64,4096]{1,0:T(8,128)(2,1)S(1)}, u32[]{:S(2)}, u32[]{:S(2)}) collective-permute-start(bf16[64,4096]{1,0:T(8,128)(2,1)} %refs_0_.5), channel_id=1, source_target_pairs={{0,4},{2,6},{4,0},{6,2},{8,12},{10,14},{12,8},{14,10},{1,5},{3,7},... | collective-permute-start | bytes 1572872 | tf_op jit(solution)/shard_map/ppermute | solution.py:430
  5.3 26.1 %collective-permute-start.2 = (bf16[64,4096]{1,0:T(8,128)(2,1)}, bf16[64,4096]{1,0:T(8,128)(2,1)S(1)}, u32[]{:S(2)}, u32[]{:S(2)}) collective-permute-start(bf16[64,4096]{1,0:T(8,128)(2,1)} %refs_0_.5), channel_id=1, source_target_pairs={{0,8},{2,10},{4,12},{6,14},{8,0},{10,2},{12,4},{14,6},{1,9},{3,11}... | collective-permute-start | bytes 1572872 | tf_op jit(solution)/shard_map/ppermute | solution.py:430
  8.0 1.5 %copy-start = (bf16[256,3584]{1,0:T(8,128)(2,1)S(1)}, bf16[256,3584]{1,0:T(8,128)(2,1)}, u32[]{:S(2)}) copy-start(bf16[256,3584]{1,0:T(8,128)(2,1)} %refs_0_.4) | copy-start | bytes 5505028
  25.2 35.6 %collective-permute-start.8 = (bf16[256,2176]{1,0:T(8,128)(2,1)S(1)}, bf16[256,2176]{1,0:T(8,128)(2,1)S(1)}, u32[]{:S(2)}, u32[]{:S(2)}) collective-permute-start(bf16[256,2176]{1,0:T(8,128)(2,1)S(1)} %get-tuple-element.67), channel_id=1, source_target_pairs={{0,2},{2,0},{4,6},{6,4},{8,10},{10,8},{12,14},{14,12},{1,3},{3,1},... | collective-permute-start | bytes 3342344 | tf_op jit(solution)/shard_map/ppermute | solution.py:430
  32.0 26.7 %collective-permute-start.5 = (bf16[64,4096]{1,0:T(8,128)(2,1)S(1)}, bf16[64,4096]{1,0:T(8,128)(2,1)S(1)}, u32[]{:S(2)}, u32[]{:S(2)}) collective-permute-start(bf16[64,4096]{1,0:T(8,128)(2,1)S(1)} %get-tuple-element.60.refs_2_), channel_id=1, source_target_pairs={{0,4},{2,6},{4,0},{6,2},{8,12},{10,14},{12,8},{14,10},{1,5},{3,7},... | collective-permute-start | bytes 1572872 | tf_op jit(solution)/shard_map/ppermute | solution.py:430
  32.5 46.7 %collective-permute-start.6 = (bf16[64,4096]{1,0:T(8,128)(2,1)S(1)}, bf16[64,4096]{1,0:T(8,128)(2,1)S(1)}, u32[]{:S(2)}, u32[]{:S(2)}) collective-permute-start(bf16[64,4096]{1,0:T(8,128)(2,1)S(1)} %get-tuple-element.60.refs_2_), channel_id=1, source_target_pairs={{0,2},{2,0},{4,6},{6,4},{8,10},{10,8},{12,14},{14,12},{1,3},{3,1},... | collective-permute-start | bytes 1572872 | tf_op jit(solution)/shard_map/ppermute | solution.py:430
  33.0 25.2 %collective-permute-start.4 = (bf16[64,4096]{1,0:T(8,128)(2,1)S(1)}, bf16[64,4096]{1,0:T(8,128)(2,1)S(1)}, u32[]{:S(2)}, u32[]{:S(2)}) collective-permute-start(bf16[64,4096]{1,0:T(8,128)(2,1)S(1)} %get-tuple-element.59.refs_0_), channel_id=1, source_target_pairs={{0,4},{2,6},{4,0},{6,2},{8,12},{10,14},{12,8},{14,10},{1,5},{3,7},... | collective-permute-start | bytes 1572872 | tf_op jit(solution)/shard_map/ppermute | solution.py:430
  48.0 34.1 %collective-permute-start.10 = (bf16[256,2176]{1,0:T(8,128)(2,1)S(1)}, bf16[256,2176]{1,0:T(8,128)(2,1)S(1)}, u32[]{:S(2)}, u32[]{:S(2)}) collective-permute-start(bf16[256,2176]{1,0:T(8,128)(2,1)S(1)} %get-tuple-element.75), channel_id=1, source_target_pairs={{0,4},{2,6},{4,0},{6,2},{8,12},{10,14},{12,8},{14,10},{1,5},{3,7},... | collective-permute-start | bytes 3342344 | tf_op jit(solution)/shard_map/ppermute | solution.py:430
  58.2 26.3 %collective-permute-start.9 = (f32[512,64]{1,0:T(8,128)S(1)}, f32[512,64]{1,0:T(8,128)S(1)}, u32[]{:S(2)}, u32[]{:S(2)}) collective-permute-start(f32[512,64]{1,0:T(8,128)S(1)} %get-tuple-element.73.refs_0_), channel_id=1, source_target_pairs={{0,2},{2,0},{4,6},{6,4},{8,10},{10,8},{12,14},{14,12},{1,3},{3,1},... | collective-permute-start | bytes 393224 | tf_op jit(solution)/shard_map/ppermute | solution.py:430
  59.2 4.5 %copy-start.2 = (bf16[64,4096]{1,0:T(8,128)(2,1)S(1)}, bf16[64,4096]{1,0:T(8,128)(2,1)}, u32[]{:S(2)}) copy-start(bf16[64,4096]{1,0:T(8,128)(2,1)} %refs_0_.5) | copy-start | bytes 1572868
  59.2 4.5 %copy-start.3 = (bf16[64,4096]{1,0:T(8,128)(2,1)S(1)}, bf16[64,4096]{1,0:T(8,128)(2,1)}, u32[]{:S(2)}) copy-start(bf16[64,4096]{1,0:T(8,128)(2,1)} %refs_5_.5) | copy-start | bytes 1572868
  59.2 20.3 %collective-permute-start.7 = (bf16[64,4096]{1,0:T(8,128)(2,1)S(1)}, bf16[64,4096]{1,0:T(8,128)(2,1)S(1)}, u32[]{:S(2)}, u32[]{:S(2)}) collective-permute-start(bf16[64,4096]{1,0:T(8,128)(2,1)S(1)} %get-tuple-element.64.refs_3_), channel_id=1, source_target_pairs={{0,2},{2,0},{4,6},{6,4},{8,10},{10,8},{12,14},{14,12},{1,3},{3,1},... | collective-permute-start | bytes 1572872 | tf_op jit(solution)/shard_map/ppermute | solution.py:430
  63.2 33.3 %collective-permute-start.12 = (bf16[128,2176]{1,0:T(8,128)(2,1)S(1)}, bf16[128,2176]{1,0:T(8,128)(2,1)S(1)}, u32[]{:S(2)}, u32[]{:S(2)}) collective-permute-start(bf16[128,2176]{1,0:T(8,128)(2,1)S(1)} %get-tuple-element.80), channel_id=1, source_target_pairs={{0,4},{2,6},{4,0},{6,2},{8,12},{10,14},{12,8},{14,10},{1,5},{3,7},... | collective-permute-start | bytes 1671176 | tf_op jit(solution)/shard_map/ppermute | solution.py:430
  85.0 15.6 %collective-permute-start.11 = (f32[512,64]{1,0:T(8,128)S(1)}, f32[512,64]{1,0:T(8,128)S(1)}, u32[]{:S(2)}, u32[]{:S(2)}) collective-permute-start(f32[512,64]{1,0:T(8,128)S(1)} %get-tuple-element.78.refs_0_), channel_id=1, source_target_pairs={{0,4},{2,6},{4,0},{6,2},{8,12},{10,14},{12,8},{14,10},{1,5},{3,7},... | collective-permute-start | bytes 393224 | tf_op jit(solution)/shard_map/ppermute | solution.py:430
  85.5 25.1 %collective-permute-start.16 = (bf16[128,2176]{1,0:T(8,128)(2,1)S(1)}, bf16[128,2176]{1,0:T(8,128)(2,1)S(1)}, u32[]{:S(2)}, u32[]{:S(2)}) collective-permute-start(bf16[128,2176]{1,0:T(8,128)(2,1)S(1)} %get-tuple-element.92), channel_id=1, source_target_pairs={{0,2},{2,0},{4,6},{6,4},{8,10},{10,8},{12,14},{14,12},{1,3},{3,1},... | collective-permute-start | bytes 1671176 | tf_op jit(solution)/shard_map/ppermute | solution.py:430
  86.0 36.3 %collective-permute-start.15 = (f32[128,3584]{1,0:T(8,128)S(1)}, f32[128,3584]{1,0:T(8,128)S(1)}, u32[]{:S(2)}, u32[]{:S(2)}) collective-permute-start(f32[128,3584]{1,0:T(8,128)S(1)} %get-tuple-element.90), channel_id=1, source_target_pairs={{0,1},{1,0},{2,3},{3,2},{4,5},{5,4},{6,7},{7,6},{8,9},{9,8},{10,11... | collective-permute-start | bytes 5505032 | tf_op jit(solution)/shard_map/ppermute | solution.py:433
  95.9 36.6 %collective-permute-start.14 = (f32[128,2048]{1,0:T(8,128)S(1)}, f32[128,2048]{1,0:T(8,128)S(1)}, u32[]{:S(2)}, u32[]{:S(2)}) collective-permute-start(f32[128,2048]{1,0:T(8,128)S(1)} %get-tuple-element.88), channel_id=1, source_target_pairs={{0,1},{1,0},{2,3},{3,2},{4,5},{5,4},{6,7},{7,6},{8,9},{9,8},{10,11... | collective-permute-start | bytes 3145736 | tf_op jit(solution)/shard_map/ppermute | solution.py:433
  98.0 24.4 %collective-permute-start.17 = (bf16[64,2176]{1,0:T(8,128)(2,1)S(1)}, bf16[64,2176]{1,0:T(8,128)(2,1)S(1)}, u32[]{:S(2)}, u32[]{:S(2)}) collective-permute-start(bf16[64,2176]{1,0:T(8,128)(2,1)S(1)} %get-tuple-element.95), channel_id=1, source_target_pairs={{0,8},{2,10},{4,12},{6,14},{8,0},{10,2},{12,4},{14,6},{1,9},{3,11}... | collective-permute-start | bytes 835592 | tf_op jit(solution)/shard_map/ppermute | solution.py:430
  110.2 20.7 %collective-permute-start.18 = (f32[512,64]{1,0:T(8,128)S(1)}, f32[512,64]{1,0:T(8,128)S(1)}, u32[]{:S(2)}, u32[]{:S(2)}) collective-permute-start(f32[512,64]{1,0:T(8,128)S(1)} %get-tuple-element.99.refs_0_), channel_id=1, source_target_pairs={{0,8},{2,10},{4,12},{6,14},{8,0},{10,2},{12,4},{14,6},{1,9},{3,11}... | collective-permute-start | bytes 393224 | tf_op jit(solution)/shard_map/ppermute | solution.py:430
  110.6 23.4 %collective-permute-start.13 = (f32[128,1536]{1,0:T(8,128)S(1)}, f32[128,1536]{1,0:T(8,128)S(1)}, u32[]{:S(2)}, u32[]{:S(2)}) collective-permute-start(f32[128,1536]{1,0:T(8,128)S(1)} %get-tuple-element.86), channel_id=1, source_target_pairs={{0,1},{1,0},{2,3},{3,2},{4,5},{5,4},{6,7},{7,6},{8,9},{9,8},{10,11... | collective-permute-start | bytes 2359304 | tf_op jit(solution)/shard_map/ppermute | solution.py:433
  122.3 14.3 %collective-permute-start.19 = (bf16[64,2176]{1,0:T(8,128)(2,1)S(1)}, bf16[64,2176]{1,0:T(8,128)(2,1)S(1)}, u32[]{:S(2)}, u32[]{:S(2)}) collective-permute-start(bf16[64,2176]{1,0:T(8,128)(2,1)S(1)} %get-tuple-element.109), channel_id=1, source_target_pairs={{0,8},{2,10},{4,12},{6,14},{8,0},{10,2},{12,4},{14,6},{1,9},{3,11}... | collective-permute-start | bytes 835592 | tf_op jit(solution)/shard_map/ppermute | solution.py:430
  132.5 6.3 %collective-permute-start.20 = (f32[4,64,64]{2,1,0:T(8,128)S(1)}, f32[4,64,64]{2,1,0:T(8,128)S(1)}, u32[]{:S(2)}, u32[]{:S(2)}) collective-permute-start(f32[4,64,64]{2,1,0:T(8,128)S(1)} %get-tuple-element.112), channel_id=1, source_target_pairs={{0,1},{1,0},{2,3},{3,2},{4,5},{5,4},{6,7},{7,6},{8,9},{9,8},{10,11... | collective-permute-start | bytes 196616 | tf_op jit(solution)/shard_map/ppermute | solution.py:433
  (1 other events, 1.0 us)

commit v7 on v6

--- a/solution.py
+++ b/solution.py
@@ -16,7 +16,8 @@
 H_TILE = 512
 VMEM_MIB = {"backward": 32, "forward": 24}
 MIB = 1 << 20
-TIMES = {"forward": 1 << 34, "fold": 0, "combine": 1 << 34, "sketch_part": 1 << 34}
+RIGHT_ROWS = 32
+TIMES = {"backward": 19 * 10**9, "forward": 1 << 34, "fold": 0, "combine": 1 << 34, "sketch_part": 1 << 34}
 ANY = pl.BlockSpec(memory_space=pl.ANY)
 HBM = pl.BlockSpec(memory_space=pltpu.HBM)
 
@@ -95,6 +96,30 @@
     return out
 
 
+def put_right(value, msg):
+    base = msg.shape[0] - RIGHT_ROWS
+    for q in range(value.shape[0] // RIGHT_ROWS):
+        left_over = value[q * RIGHT_ROWS : (q + 1) * RIGHT_ROWS, :]
+        for k in range(3):
+            part = left_over.astype(jnp.bfloat16)
+            lo = (3 * q + k) * LANES
+            msg[base:, lo : lo + LANES] = part
+            left_over = left_over - part.astype(jnp.float32)
+
+
+def add_right(value, msg):
+    base = msg.shape[0] - RIGHT_ROWS
+    out = []
+    for q in range(value.shape[0] // RIGHT_ROWS):
+        lo = 3 * q * LANES
+        parts = [
+            msg[base:, lo + k * LANES : lo + (k + 1) * LANES].astype(jnp.float32) for k in range(3)
+        ]
+        got = parts[0] + (parts[1] + parts[2])
+        out.append(value[q * RIGHT_ROWS : (q + 1) * RIGHT_ROWS, :] + got)
+    return jnp.concatenate(out, axis=0)
+
+
 def with_bit(c, pos, value):
     low = c & ((1 << pos) - 1)
     return ((c >> pos) << (pos + 1)) + low + value * (1 << pos)
@@ -130,7 +155,13 @@
             a.wait()
             b.wait()
             if sketch is not None:
-                right[...] = contract_last(x[...].reshape(2 * half, hidden), sk_here[...])
+                low, high = jnp.zeros_like(sk_here[...]), sk_here[...]
+                first_block = jnp.concatenate([high, low], axis=0)
+                second_block = jnp.concatenate([low, high], axis=0)
+                right[...] = contract_last(x[core, : half // 2, :], first_block) + contract_last(
+                    x[core, half // 2 :, :], second_block
+                )
+                put_right(right[...], msg)
 
         xs = x[...].reshape(2 * half, hidden)
         total[j] = contract_last(xs, w[...]).reshape(n, rows, tile)
@@ -152,8 +183,9 @@
                     for t in range(count):
                         keep[t, c, src, :] = total[t, here, src, :]
 
+    extra = 0 if sketch is None else RIGHT_ROWS
     out = [
-        jax.ShapeDtypeStruct((n // 2 * rows, width + LANES), jnp.bfloat16),
+        jax.ShapeDtypeStruct((n // 2 * rows + extra, width + LANES), jnp.bfloat16),
         jax.ShapeDtypeStruct((count, n // 2, rows, tile), jnp.float32),
     ]
     args = [own, oth, w]
@@ -166,7 +198,7 @@
     if sketch is not None:
         args.append(sketch)
         specs.append(HBM)
-        out.append(jax.ShapeDtypeStruct((2 * half, sketch.shape[0]), jnp.float32))
+        out.append(jax.ShapeDtypeStruct((half // 2, 2 * sketch.shape[0]), jnp.float32))
         scratch.append(pltpu.VMEM(sketch.shape, sketch.dtype))
     return call(
         kernel,
@@ -183,10 +215,17 @@
     )
 
 
-def fold(idx, keep, got, bit, pos, after):
+def fold(idx, keep, got, right, bit, pos, after):
     count, m, rows, tile = keep.shape
-
-    def kernel(idx, keep, got, msg, rest):
+    extra = 0 if right is None else RIGHT_ROWS
+
+    def kernel(idx, keep, got, *refs):
+        if extra:
+            right, msg, rest, total = refs
+            total[...] = add_right(right[...], got)
+            put_right(total[...], msg)
+        else:
+            msg, rest = refs
         mine = (idx[0] >> bit) & 1
         for c in range(m // 2):
             away, here = with_bit(c, pos, 1 - mine), with_bit(c, pos, mine)
@@ -204,15 +243,16 @@
                 for t in range(count):
                     rest[t, c, src, :] = keep[t, here, src, :] + plus[t]
 
+    args = [keep, got] + ([right] if extra else [])
     out = [
-        jax.ShapeDtypeStruct((m // 2 * rows, got.shape[1]), jnp.bfloat16),
+        jax.ShapeDtypeStruct((m // 2 * rows + extra, got.shape[1]), jnp.bfloat16),
         jax.ShapeDtypeStruct((count, m // 2, rows, tile), jnp.float32),
-    ]
+    ] + ([jax.ShapeDtypeStruct(right.shape, jnp.float32)] if extra else [])
     return call(
         kernel,
         idx,
-        [keep, got],
-        [whole(keep.shape), whole(got.shape)],
+        args,
+        [whole(a.shape) for a in args],
         out,
         [whole(o.shape) for o in out],
         "fold",
@@ -279,14 +319,16 @@
     return list(out), [token]
 
 
-def add(idx, a, b, after):
-    def kernel(idx, a, b, out):
-        out[...] = a[...] + b[...]
-
-    specs = [whole(a.shape)] * 2
-    out = [jax.ShapeDtypeStruct(a.shape, a.dtype)]
-    work = (a.size, 12 * a.size)
-    (total,), token = call(kernel, idx, [a, b], specs, out, specs[:1], "add", (1,), work, after)
+def last_right(idx, right, got, after):
+    def kernel(idx, right, got, out):
+        out[...] = add_right(right[...], got)
+
+    out = [jax.ShapeDtypeStruct(right.shape, jnp.float32)]
+    specs = [whole(right.shape), whole(got.shape)]
+    work = (0, 2 * got.size)
+    (total,), token = call(
+        kernel, idx, [right, got], specs, out, specs[:1], "last_right", (1,), work, after
+    )
     return total, [token]
 
 
@@ -375,35 +417,38 @@
     return out, [token]
 
 
-def sketch_part(idx, lefts, right, rows, after):
-    tokens, width = right.shape
-    half = tokens // 2
+def sketch_part(idx, lefts, own, oth, rows, after):
+    packed, lanes = own.shape
+    width = lanes // 2
+    half = 2 * packed
     part = half // 2
     examples = half // LEN
 
-    def kernel(idx, first, second, right, out):
+    def kernel(idx, first, second, own, oth, out):
         me, core = idx[0], idx[1]
-        for side in (0, 1):
+        for side, right in ((0, oth), (1, own)):
             owner = 1 - (side ^ core)
             for e in range(examples):
                 total = jnp.zeros((width, width), jnp.float32)
                 for i in range(part // rows):
                     if 2 * i * rows // LEN != e:
                         continue
+                    block, start = divmod(2 * i * rows, packed)
                     for batch, left in enumerate((first, second)):
-                        at = owner * half + (2 * i + ((me & 1) ^ batch)) * rows
+                        at = start + ((me & 1) ^ batch) * rows
                         lo = side * part + i * rows
+                        both = right[pl.ds(pl.multiple_of(at, BLK), rows), :]
                         total += lax.dot_general(
                             left[lo : lo + rows, :],
-                            right[pl.ds(pl.multiple_of(at, BLK), rows), :],
+                            both[:, block * width : (block + 1) * width],
                             (((0,), (0,)), ((), ())),
                             precision=lax.Precision.HIGHEST,
                             preferred_element_type=jnp.float32,
                         )
                 out[owner * examples + e] = total
 
-    args = [*lefts, right]
-    out = [jax.ShapeDtypeStruct((tokens // LEN, width, width), jnp.float32)]
+    args = [*lefts, own, oth]
+    out = [jax.ShapeDtypeStruct((2 * examples, width, width), jnp.float32)]
     (sketch,), token = call(
         kernel,
         idx,
@@ -413,7 +458,7 @@
         [whole(out[0].shape)],
         "sketch_part",
         (1,),
-        (0, 8 * tokens * width),
+        (0, 16 * half * width),
         after,
     )
     return sketch, [token]
@@ -433,31 +478,23 @@
         return lax.ppermute(x, "inp", [(0, 1), (1, 0)])
 
     chunks = {0: inputs}
-
-    def wave_of(mask):
-        if mask & 1 and mask > 3:
-            return max(3, mask.bit_count())
-        return 2 if mask == 3 else mask.bit_count()
-
-    def step_of(mask):
-        if mask == 3:
-            return 1
-        return 0 if mask & 1 else (mask & -mask).bit_length() - 1
-
-    def wave(k):
-        for mask in sorted(range(1, n), reverse=True):
-            if wave_of(mask) == k:
-                bit = step_of(mask)
-                chunks[mask] = partner(chunks[mask ^ (1 << bit)], bit)
-
-    def hold(k, after):
-        masks = [m for m in range(1, n) if wave_of(m) == k]
+    evens = range(2, n, 2)
+
+    def wave(masks):
+        for mask in masks:
+            bit = (mask & -mask).bit_length() - 1
+            chunks[mask] = partner(chunks[mask ^ (1 << bit)], bit)
+
+    def along_z(k):
+        return [m for m in reversed(evens) if m.bit_count() == k]
+
+    def hold(masks, after):
         held, token = gate(idx, [chunks[m] for m in masks], after)
         chunks.update(zip(masks, held))
         return token
 
     grad_other = swap(cotangent)
-    wave(1)
+    wave(along_z(1) + [1])
 
     orders = [list(range(bits)), [1, 0] + list(range(2, bits))]
     tile = pick(feats // PIECES, F_TILE)
@@ -483,19 +520,24 @@
         keeps.append(outs[1])
         if p == 0:
             right = outs[2]
-            right_got = partner(right, 0)
-        token = hold(1 + p, token)
-        wave(2 + p)
-    last = max(wave_of(m) for m in range(1, n))
-    for k in range(PIECES + 1, last):
-        token = hold(k, token)
-        wave(k + 1)
+        if p == 0:
+            token = hold([1] + along_z(1), token)
+            wave(along_z(2))
+    for k in range(2, bits - 1):
+        token = hold(along_z(k), token)
+        wave(along_z(k + 1))
+    token = hold(list(evens), token)
+    wave([m + 1 for m in evens])
+
+    rights = [right] + [None] * (PIECES - 1)
 
     def folded(p, step, after):
         done, bit = orders[p][:step], orders[p][step]
         pos = sum(1 for k in range(bit) if k not in done)
-        (msg, keeps[p]), t = fold(idx, keeps[p], msgs[p], bit, pos, after)
-        msgs[p] = partner(msg, bit)
+        outs, t = fold(idx, keeps[p], msgs[p], rights[p], bit, pos, after)
+        msgs[p], keeps[p] = partner(outs[0], bit), outs[1]
+        if p == 0:
+            rights[p] = outs[2]
         return [t]
 
     tiles = hidden // pick(hidden, H_TILE)
@@ -509,29 +551,24 @@
     cut = -(-tiles // 2)
     token = folded(0, 1, token)
     first, left1, token = batch_forward(0, 0, tiles, token)
-    token = hold(last, token)
     token = folded(1, 1, token)
-    right, token = add(idx, right, right_got, token)
-    right_got = partner(right, 1)
+    token = folded(0, 2, token)
+    token = hold([m + 1 for m in evens], token)
     second, left2, token = batch_forward(1, 0, cut, token)
-    token = folded(0, 2, token)
-    right, token = add(idx, right, right_got, token)
-    right_got = partner(right, 2)
+    token = folded(1, 2, token)
     third, _, token = batch_forward(1, cut, tiles, token)
-    token = folded(1, 2, token)
     for step in range(3, bits):
         for p in range(PIECES):
             token = folded(p, step, token)
-    outputs, token = combine(idx, *first, [], token + [msgs[0]])
-    right, token = add(idx, right, right_got, token)
-    for k in range(3, bits):
-        right, token = add(idx, right, partner(right, k), token)
-    part, token = sketch_part(idx, [left1, left2], right, rows, token)
+    outputs, token = combine(idx, *first, [], token)
+    right, token = last_right(idx, rights[0], msgs[0], token)
+    right_got = swap(right)
     outputs, token = combine(idx, *second, [outputs], token)
     outputs, token = combine(idx, *third, [outputs], token)
+    part, token = sketch_part(idx, [left1, left2], right, right_got, rows, token)
+    input_grad = finish(idx, keeps, msgs, token)
     part = (part + swap(part)) * (1.0 / LEN**0.5)
     sketches = part.reshape(part.shape[0], -1)
-    input_grad = finish(idx, keeps, msgs, token)
     return (outputs, input_grad, sketches)
 
 

time: 140 us -> 130 us (0.929)
  waiting for transfers between devices: 36 us -> 23.7 us
  starting transfers between devices: 18.2 us -> 22.6 us
  Pallas kernels: 81.1 us -> 79.6 us
    ppermute x16 -> x13, waiting for transfers between devices: 36 us -> 22.7 us  [partner(): return lax.ppermute(x, 'outp', [(d, d ^ 1 << bit) for d in range(n)])]
    ppermute x16 -> x13, starting transfers between devices: 17.1 us -> 21.2 us  [partner(): return lax.ppermute(x, 'outp', [(d, d ^ 1 << bit) for d in range(n)])]
    pallas_call x20 -> x18, Pallas kernels: 81.1 us -> 79.6 us  [call(): pl.pallas_call(with_token, out_shape=list(out_shape) + [token], grid_spec...]
  transfers between devices with their start and end apart: 21 -> 19, of which waited for: 8 -> 6; matrix products, arithmetic and copies ran while one was open for 0% -> 0% of each run, Pallas kernels for 58% -> 61%
where the time goes in v7:
time: 130 us
  Pallas kernels  79.6 us (61%)
  waiting for transfers between devices  23.7 us (18%)
  starting transfers between devices  22.6 us (17%)
  local copies, waits for them, and re-layouts  3.27 us (3%)
    pallas_call x18, Pallas kernels, call(): pl.pallas_call(with_token, out_shape=list(out_shape) + [token], grid_spec...  79.6 us
    ppermute x13, waiting for transfers between devices, partner(): return lax.ppermute(x, 'outp', [(d, d ^ 1 << bit) for d in range(n)])  22.7 us
    ppermute x13, starting transfers between devices, partner(): return lax.ppermute(x, 'outp', [(d, d ^ 1 << bit) for d in range(n)])  21.2 us
  transfers between devices with their start and end apart: 19, of which 6 were waited for; matrix products, arithmetic and copies ran while one was open for 0% of the time, Pallas kernels for 61%

profile of v7, /device:TPU:0, one launch (start us, length us, event | category | flops | bytes accessed | tf_op | source)
XLA Modules:
  0.0 130.1 jit_solution(16507311669556851763)
XLA Ops:
  1.1 3.7 %collective-permute-start.1 = (bf16[64,4096]{1,0:T(8,128)(2,1)}, bf16[64,4096]{1,0:T(8,128)(2,1)S(1)}, u32[]{:S(2)}, u32[]{:S(2)}) collective-permute-start(bf16[64,4096]{1,0:T(8,128)(2,1)} %refs_0_.5), channel_id=1, source_target_pairs={{0,8},{2,10},{4,12},{6,14},{8,0},{10,2},{12,4},{14,6},{1,9},{3,11}... | collective-permute-start | bytes 1572872 | tf_op jit(solution)/shard_map/ppermute | solution.py:475
  4.8 1.5 %collective-permute-start = (bf16[64,4096]{1,0:T(8,128)(2,1)}, bf16[64,4096]{1,0:T(8,128)(2,1)S(1)}, u32[]{:S(2)}, u32[]{:S(2)}) collective-permute-start(bf16[64,4096]{1,0:T(8,128)(2,1)} %refs_0_.5), channel_id=1, source_target_pairs={{0,2},{2,0},{4,6},{6,4},{8,10},{10,8},{12,14},{14,12},{1,3},{3,1},... | collective-permute-start | bytes 1572872 | tf_op jit(solution)/shard_map/ppermute | solution.py:475
  6.3 1.6 %collective-permute-start.2 = (bf16[64,4096]{1,0:T(8,128)(2,1)}, bf16[64,4096]{1,0:T(8,128)(2,1)S(1)}, u32[]{:S(2)}, u32[]{:S(2)}) collective-permute-start(bf16[64,4096]{1,0:T(8,128)(2,1)} %refs_0_.5), channel_id=1, source_target_pairs={{0,4},{2,6},{4,0},{6,2},{8,12},{10,14},{12,8},{14,10},{1,5},{3,7},... | collective-permute-start | bytes 1572872 | tf_op jit(solution)/shard_map/ppermute | solution.py:475
  8.0 1.5 %copy-done = bf16[256,3584]{1,0:T(8,128)(2,1)S(1)} copy-done((bf16[256,3584]{1,0:T(8,128)(2,1)S(1)}, bf16[256,3584]{1,0:T(8,128)(2,1)}, u32[]{:S(2)}) %copy-start) | copy-done | bytes 1835032
  10.5 14.3 %backward.2 = (bf16[288,2176]{1,0:T(8,128)(2,1)S(1)}, f32[4,4,64,512]{3,2,1,0:T(8,128)S(1)}, f32[128,128]{1,0:T(8,128)S(1)}, f32[8,128]{1,0:T(8,128)S(1)}) custom-call(s32[2]{0:T(128)S(1)} %pad_add_fusion.idx, bf16[256,3584]{1,0:T(8,128)(2,1)S(1)} %copy-done, bf16[256,3584]{1,0:T(8,128)(2,1)S(1)} %collective-permute-done.3.refs_1_, ...), custom_call_target="tpu_custom_call" | custom-call | flops 19000000512 | bytes 20971520 | tf_op jit(solution)/shard_map/backward/pallas_call | solution.py:53
  24.8 4.1 %collective-permute-done.1.refs_1_ = bf16[64,4096]{1,0:T(8,128)(2,1)S(1)} collective-permute-done((bf16[64,4096]{1,0:T(8,128)(2,1)}, bf16[64,4096]{1,0:T(8,128)(2,1)S(1)}, u32[]{:S(2)}, u32[]{:S(2)}) %collective-permute-start.1) | collective-permute-done | bytes 524320 | tf_op jit(solution)/shard_map/ppermute | solution.py:475
  31.2 1.5 %collective-permute-start.8 = (bf16[288,2176]{1,0:T(8,128)(2,1)S(1)}, bf16[288,2176]{1,0:T(8,128)(2,1)S(1)}, u32[]{:S(2)}, u32[]{:S(2)}) collective-permute-start(bf16[288,2176]{1,0:T(8,128)(2,1)S(1)} %get-tuple-element.68), channel_id=1, source_target_pairs={{0,2},{2,0},{4,6},{6,4},{8,10},{10,8},{12,14},{14,12},{1,3},{3,1},... | collective-permute-start | bytes 3760136 | tf_op jit(solution)/shard_map/ppermute | solution.py:475
  32.7 13.4 %backward.3 = (bf16[256,2176]{1,0:T(8,128)(2,1)S(1)}, f32[4,4,64,512]{3,2,1,0:T(8,128)S(1)}, f32[8,128]{1,0:T(8,128)S(1)}) custom-call(s32[2]{0:T(128)S(1)} %pad_add_fusion.idx, bf16[256,3584]{1,0:T(8,128)(2,1)S(1)} %copy-done, bf16[256,3584]{1,0:T(8,128)(2,1)S(1)} %collective-permute-done.3.refs_1_, bf16[4096,3584]{1,0:T(8,128)(2,1)} %refs_4_.5, ...), custom_call_target="tpu_custom_call" | custom-call | flops 19000000512 | bytes 20971520 | tf_op jit(solution)/shard_map/backward/pallas_call | solution.py:53
  47.6 1.5 %collective-permute-start.5 = (bf16[64,4096]{1,0:T(8,128)(2,1)S(1)}, bf16[64,4096]{1,0:T(8,128)(2,1)S(1)}, u32[]{:S(2)}, u32[]{:S(2)}) collective-permute-start(bf16[64,4096]{1,0:T(8,128)(2,1)S(1)} %get-tuple-element.64.refs_1_), channel_id=1, source_target_pairs={{0,2},{2,0},{4,6},{6,4},{8,10},{10,8},{12,14},{14,12},{1,3},{3,1},... | collective-permute-start | bytes 1572872 | tf_op jit(solution)/shard_map/ppermute | solution.py:475
  51.1 10.6 %collective-permute-done.8.refs_1_ = bf16[288,2176]{1,0:T(8,128)(2,1)S(1)} collective-permute-done((bf16[288,2176]{1,0:T(8,128)(2,1)S(1)}, bf16[288,2176]{1,0:T(8,128)(2,1)S(1)}, u32[]{:S(2)}, u32[]{:S(2)}) %collective-permute-start.8) | collective-permute-done | bytes 1253408 | tf_op jit(solution)/shard_map/ppermute | solution.py:475
  61.7 2.4 %fold.4 = (bf16[160,2176]{1,0:T(8,128)(2,1)S(1)}, f32[4,2,64,512]{3,2,1,0:T(8,128)S(1)}, f32[128,128]{1,0:T(8,128)S(1)}, f32[8,128]{1,0:T(8,128)S(1)}) custom-call(s32[2]{0:T(128)S(1)} %pad_add_fusion.idx, f32[4,4,64,512]{3,2,1,0:T(8,128)S(1)} %get-tuple-element.67.refs_0_, bf16[288,2176]{1,0:T(8,128)(2,1)S(1)} %collective-permute-done.8.refs_1_, ...), custom_call_target="tpu_custom_call" | custom-call | bytes 6291456 | tf_op jit(solution)/shard_map/fold/pallas_call | solution.py:53
  64.1 1.8 %collective-permute-start.9 = (bf16[160,2176]{1,0:T(8,128)(2,1)S(1)}, bf16[160,2176]{1,0:T(8,128)(2,1)S(1)}, u32[]{:S(2)}, u32[]{:S(2)}) collective-permute-start(bf16[160,2176]{1,0:T(8,128)(2,1)S(1)} %get-tuple-element.72), channel_id=1, source_target_pairs={{0,4},{2,6},{4,0},{6,2},{8,12},{10,14},{12,8},{14,10},{1,5},{3,7},... | collective-permute-start | bytes 2088968 | tf_op jit(solution)/shard_map/ppermute | solution.py:475
  65.9 15.5 %forward.3 = (f32[128,3584]{1,0:T(8,128)S(1)}, f32[128,3584]{1,0:T(8,128)S(1)}, f32[256,64]{1,0:T(8,128)S(1)}, f32[8,128]{1,0:T(8,128)S(1)}) custom-call(s32[2]{0:T(128)S(1)} %pad_add_fusion.idx, bf16[64,4096]{1,0:T(8,128)(2,1)S(1)} %copy-done.1, bf16[64,4096]{1,0:T(8,128)(2,1)S(1)} %get-tuple-element.64.refs_1_, ...), custom_call_target="tpu_custom_call" | custom-call | flops 17179869184 | bytes 33030144 | tf_op jit(solution)/shard_map/forward/pallas_call | solution.py:53
  81.4 2.4 %fold.5 = (bf16[128,2176]{1,0:T(8,128)(2,1)S(1)}, f32[4,2,64,512]{3,2,1,0:T(8,128)S(1)}, f32[8,128]{1,0:T(8,128)S(1)}) custom-call(s32[2]{0:T(128)S(1)} %pad_add_fusion.idx, f32[4,4,64,512]{3,2,1,0:T(8,128)S(1)} %get-tuple-element.74.refs_0_, bf16[256,2176]{1,0:T(8,128)(2,1)S(1)} %collective-permute-done.10.refs_1_, f32[8,128]{1,0:T(8,128)S(1)} %get-tuple-element.77.refs_2_), custom_call_target="tpu_custom_call" | custom-call | bytes 6291456 | tf_op jit(solution)/shard_map/fold/pallas_call | solution.py:53
  84.4 2.2 %collective-permute-done.9.refs_1_ = bf16[160,2176]{1,0:T(8,128)(2,1)S(1)} collective-permute-done((bf16[160,2176]{1,0:T(8,128)(2,1)S(1)}, bf16[160,2176]{1,0:T(8,128)(2,1)S(1)}, u32[]{:S(2)}, u32[]{:S(2)}) %collective-permute-start.9) | collective-permute-done | bytes 696352 | tf_op jit(solution)/shard_map/ppermute | solution.py:475
  86.7 1.5 %fold.6 = (bf16[96,2176]{1,0:T(8,128)(2,1)S(1)}, f32[4,1,64,512]{3,2,1,0:T(8,128)S(1)}, f32[128,128]{1,0:T(8,128)S(1)}, f32[8,128]{1,0:T(8,128)S(1)}) custom-call(s32[2]{0:T(128)S(1)} %pad_add_fusion.idx, f32[4,2,64,512]{3,2,1,0:T(8,128)S(1)} %get-tuple-element.71.refs_0_, bf16[160,2176]{1,0:T(8,128)(2,1)S(1)} %collective-permute-done.9.refs_1_, ...), custom_call_target="tpu_custom_call" | custom-call | bytes 3145728 | tf_op jit(solution)/shard_map/fold/pallas_call | solution.py:53
  88.2 2.8 %collective-permute-start.15 = (bf16[96,2176]{1,0:T(8,128)(2,1)S(1)}, bf16[96,2176]{1,0:T(8,128)(2,1)S(1)}, u32[]{:S(2)}, u32[]{:S(2)}) collective-permute-start(bf16[96,2176]{1,0:T(8,128)(2,1)S(1)} %get-tuple-element.97), channel_id=1, source_target_pairs={{0,8},{2,10},{4,12},{6,14},{8,0},{10,2},{12,4},{14,6},{1,9},{3,11}... | collective-permute-start | bytes 1253384 | tf_op jit(solution)/shard_map/ppermute | solution.py:475
  91.0 4.4 %collective-permute-done.7.refs_2_ = bf16[64,4096]{1,0:T(8,128)(2,1)S(1)} collective-permute-done((bf16[64,4096]{1,0:T(8,128)(2,1)S(1)}, bf16[64,4096]{1,0:T(8,128)(2,1)S(1)}, u32[]{:S(2)}, u32[]{:S(2)}) %collective-permute-start.7) | collective-permute-done | bytes 524320 | tf_op jit(solution)/shard_map/ppermute | solution.py:475
  95.9 9.9 %forward.4 = (f32[128,2048]{1,0:T(8,128)S(1)}, f32[128,2048]{1,0:T(8,128)S(1)}, f32[256,64]{1,0:T(8,128)S(1)}, f32[8,128]{1,0:T(8,128)S(1)}) custom-call(s32[2]{0:T(128)S(1)} %pad_add_fusion.idx, bf16[64,4096]{1,0:T(8,128)(2,1)S(1)} %get-tuple-element.59.refs_0_, bf16[64,4096]{1,0:T(8,128)(2,1)S(1)} %get-tuple-element.80.refs_1_, ...), custom_call_target="tpu_custom_call" | custom-call | flops 17179869184 | bytes 18874368 | tf_op jit(solution)/shard_map/forward/pallas_call | solution.py:53
  105.8 1.5 %fold.7 = (bf16[64,2176]{1,0:T(8,128)(2,1)S(1)}, f32[4,1,64,512]{3,2,1,0:T(8,128)S(1)}, f32[8,128]{1,0:T(8,128)S(1)}) custom-call(s32[2]{0:T(128)S(1)} %pad_add_fusion.idx, f32[4,2,64,512]{3,2,1,0:T(8,128)S(1)} %get-tuple-element.83.refs_0_, bf16[128,2176]{1,0:T(8,128)(2,1)S(1)} %collective-permute-done.11.refs_1_, f32[8,128]{1,0:T(8,128)S(1)} %get-tuple-element.86.refs_2_), custom_call_target="tpu_custom_call" | custom-call | bytes 3145728 | tf_op jit(solution)/shard_map/fold/pallas_call | solution.py:53
  107.3 2.9 %collective-permute-start.16 = (bf16[64,2176]{1,0:T(8,128)(2,1)S(1)}, bf16[64,2176]{1,0:T(8,128)(2,1)S(1)}, u32[]{:S(2)}, u32[]{:S(2)}) collective-permute-start(bf16[64,2176]{1,0:T(8,128)(2,1)S(1)} %get-tuple-element.105), channel_id=1, source_target_pairs={{0,8},{2,10},{4,12},{6,14},{8,0},{10,2},{12,4},{14,6},{1,9},{3,11}... | collective-permute-start | bytes 835592 | tf_op jit(solution)/shard_map/ppermute | solution.py:475
  110.2 9.0 %forward.5 = (f32[128,1536]{1,0:T(8,128)S(1)}, f32[128,1536]{1,0:T(8,128)S(1)}, f32[256,64]{1,0:T(8,128)}, f32[8,128]{1,0:T(8,128)S(1)}) custom-call(s32[2]{0:T(128)S(1)} %pad_add_fusion.idx, bf16[64,4096]{1,0:T(8,128)(2,1)S(1)} %get-tuple-element.59.refs_0_, bf16[64,4096]{1,0:T(8,128)(2,1)S(1)} %get-tuple-element.80.refs_1_, ...), custom_call_target="tpu_custom_call" | custom-call | flops 17179869184 | bytes 14155776 | tf_op jit(solution)/shard_map/forward/pallas_call | solution.py:53
  119.8 1.6 %combine.3 = (bf16[256,3584]{1,0:T(8,128)(2,1)}, f32[8,128]{1,0:T(8,128)S(1)}) custom-call(s32[2]{0:T(128)S(1)} %pad_add_fusion.idx, f32[128,3584]{1,0:T(8,128)S(1)} %get-tuple-element.92.refs_0_, f32[128,3584]{1,0:T(8,128)S(1)} %collective-permute-done.14.refs_1_, f32[8,128]{1,0:T(8,128)S(1)} %get-tuple-element.94.refs_2_), custom_call_target="tpu_custom_call" | custom-call | flops 17179869184 | bytes 4587520 | tf_op jit(solution)/shard_map/combine/pallas_call | solution.py:53
  127.2 2.1 %finish.1 = (bf16[64,4096]{1,0:T(8,128)(2,1)}, f32[8,128]{1,0:T(8,128)}) custom-call(s32[2]{0:T(128)S(1)} %pad_add_fusion.idx, f32[4,1,64,512]{3,2,1,0:T(8,128)S(1)} %get-tuple-element.103.refs_0_, f32[4,1,64,512]{3,2,1,0:T(8,128)S(1)} %get-tuple-element.104.refs_1_, bf16[96,2176]{1,0:T(8,128)(2,1)S(1)} %collective-permute-done.15.refs_1_.refs_2_, ...), custom_call_target="tpu_custom_call" | custom-call | bytes 2097152 | tf_op jit(solution)/shard_map/finish/pallas_call | solution.py:53
  (43 shorter events, 15.6 us)
Async XLA Ops:
  0.6 7.4 %collective-permute-start.3 = (bf16[256,3584]{1,0:T(8,128)(2,1)}, bf16[256,3584]{1,0:T(8,128)(2,1)S(1)}, u32[]{:S(2)}, u32[]{:S(2)}) collective-permute-start(bf16[256,3584]{1,0:T(8,128)(2,1)} %refs_0_.4), channel_id=1, source_target_pairs={{0,1},{1,0},{2,3},{3,2},{4,5},{5,4},{6,7},{7,6},{8,9},{9,8},{10,11... | collective-permute-start | bytes 5505032 | tf_op jit(solution)/shard_map/ppermute | solution.py:478
  1.1 27.7 %collective-permute-start.1 = (bf16[64,4096]{1,0:T(8,128)(2,1)}, bf16[64,4096]{1,0:T(8,128)(2,1)S(1)}, u32[]{:S(2)}, u32[]{:S(2)}) collective-permute-start(bf16[64,4096]{1,0:T(8,128)(2,1)} %refs_0_.5), channel_id=1, source_target_pairs={{0,8},{2,10},{4,12},{6,14},{8,0},{10,2},{12,4},{14,6},{1,9},{3,11}... | collective-permute-start | bytes 1572872 | tf_op jit(solution)/shard_map/ppermute | solution.py:475
  4.8 24.1 %collective-permute-start = (bf16[64,4096]{1,0:T(8,128)(2,1)}, bf16[64,4096]{1,0:T(8,128)(2,1)S(1)}, u32[]{:S(2)}, u32[]{:S(2)}) collective-permute-start(bf16[64,4096]{1,0:T(8,128)(2,1)} %refs_0_.5), channel_id=1, source_target_pairs={{0,2},{2,0},{4,6},{6,4},{8,10},{10,8},{12,14},{14,12},{1,3},{3,1},... | collective-permute-start | bytes 1572872 | tf_op jit(solution)/shard_map/ppermute | solution.py:475
  6.3 24.0 %collective-permute-start.2 = (bf16[64,4096]{1,0:T(8,128)(2,1)}, bf16[64,4096]{1,0:T(8,128)(2,1)S(1)}, u32[]{:S(2)}, u32[]{:S(2)}) collective-permute-start(bf16[64,4096]{1,0:T(8,128)(2,1)} %refs_0_.5), channel_id=1, source_target_pairs={{0,4},{2,6},{4,0},{6,2},{8,12},{10,14},{12,8},{14,10},{1,5},{3,7},... | collective-permute-start | bytes 1572872 | tf_op jit(solution)/shard_map/ppermute | solution.py:475
  8.0 1.5 %copy-start = (bf16[256,3584]{1,0:T(8,128)(2,1)S(1)}, bf16[256,3584]{1,0:T(8,128)(2,1)}, u32[]{:S(2)}) copy-start(bf16[256,3584]{1,0:T(8,128)(2,1)} %refs_0_.4) | copy-start | bytes 5505028
  9.5 1.0 copy-start.3
  30.9 16.1 %collective-permute-start.4 = (bf16[64,4096]{1,0:T(8,128)(2,1)S(1)}, bf16[64,4096]{1,0:T(8,128)(2,1)S(1)}, u32[]{:S(2)}, u32[]{:S(2)}) collective-permute-start(bf16[64,4096]{1,0:T(8,128)(2,1)S(1)} %get-tuple-element.61.refs_1_), channel_id=1, source_target_pairs={{0,4},{2,6},{4,0},{6,2},{8,12},{10,14},{12,8},{14,10},{1,5},{3,7},... | collective-permute-start | bytes 1572872 | tf_op jit(solution)/shard_map/ppermute | solution.py:475
  31.2 30.5 %collective-permute-start.8 = (bf16[288,2176]{1,0:T(8,128)(2,1)S(1)}, bf16[288,2176]{1,0:T(8,128)(2,1)S(1)}, u32[]{:S(2)}, u32[]{:S(2)}) collective-permute-start(bf16[288,2176]{1,0:T(8,128)(2,1)S(1)} %get-tuple-element.68), channel_id=1, source_target_pairs={{0,2},{2,0},{4,6},{6,4},{8,10},{10,8},{12,14},{14,12},{1,3},{3,1},... | collective-permute-start | bytes 3760136 | tf_op jit(solution)/shard_map/ppermute | solution.py:475
  46.1 35.3 %collective-permute-start.10 = (bf16[256,2176]{1,0:T(8,128)(2,1)S(1)}, bf16[256,2176]{1,0:T(8,128)(2,1)S(1)}, u32[]{:S(2)}, u32[]{:S(2)}) collective-permute-start(bf16[256,2176]{1,0:T(8,128)(2,1)S(1)} %get-tuple-element.75), channel_id=1, source_target_pairs={{0,4},{2,6},{4,0},{6,2},{8,12},{10,14},{12,8},{14,10},{1,5},{3,7},... | collective-permute-start | bytes 3342344 | tf_op jit(solution)/shard_map/ppermute | solution.py:475
  47.5 18.4 %copy-start.1 = (bf16[64,4096]{1,0:T(8,128)(2,1)S(1)}, bf16[64,4096]{1,0:T(8,128)(2,1)}, u32[]{:S(2)}) copy-start(bf16[64,4096]{1,0:T(8,128)(2,1)} %refs_0_.5) | copy-start | bytes 1572868
  47.5 18.4 %copy-start.2 = (bf16[64,4096]{1,0:T(8,128)(2,1)S(1)}, bf16[64,4096]{1,0:T(8,128)(2,1)}, u32[]{:S(2)}) copy-start(bf16[64,4096]{1,0:T(8,128)(2,1)} %refs_5_.5) | copy-start | bytes 1572868
  47.6 40.6 %collective-permute-start.5 = (bf16[64,4096]{1,0:T(8,128)(2,1)S(1)}, bf16[64,4096]{1,0:T(8,128)(2,1)S(1)}, u32[]{:S(2)}, u32[]{:S(2)}) collective-permute-start(bf16[64,4096]{1,0:T(8,128)(2,1)S(1)} %get-tuple-element.64.refs_1_), channel_id=1, source_target_pairs={{0,2},{2,0},{4,6},{6,4},{8,10},{10,8},{12,14},{14,12},{1,3},{3,1},... | collective-permute-start | bytes 1572872 | tf_op jit(solution)/shard_map/ppermute | solution.py:475
  49.1 41.9 %collective-permute-start.6 = (bf16[64,4096]{1,0:T(8,128)(2,1)S(1)}, bf16[64,4096]{1,0:T(8,128)(2,1)S(1)}, u32[]{:S(2)}, u32[]{:S(2)}) collective-permute-start(bf16[64,4096]{1,0:T(8,128)(2,1)S(1)} %get-tuple-element.65.refs_2_), channel_id=1, source_target_pairs={{0,2},{2,0},{4,6},{6,4},{8,10},{10,8},{12,14},{14,12},{1,3},{3,1},... | collective-permute-start | bytes 1572872 | tf_op jit(solution)/shard_map/ppermute | solution.py:475
  49.6 45.7 %collective-permute-start.7 = (bf16[64,4096]{1,0:T(8,128)(2,1)S(1)}, bf16[64,4096]{1,0:T(8,128)(2,1)S(1)}, u32[]{:S(2)}, u32[]{:S(2)}) collective-permute-start(bf16[64,4096]{1,0:T(8,128)(2,1)S(1)} %get-tuple-element.66.refs_3_), channel_id=1, source_target_pairs={{0,2},{2,0},{4,6},{6,4},{8,10},{10,8},{12,14},{14,12},{1,3},{3,1},... | collective-permute-start | bytes 1572872 | tf_op jit(solution)/shard_map/ppermute | solution.py:475
  64.1 22.6 %collective-permute-start.9 = (bf16[160,2176]{1,0:T(8,128)(2,1)S(1)}, bf16[160,2176]{1,0:T(8,128)(2,1)S(1)}, u32[]{:S(2)}, u32[]{:S(2)}) collective-permute-start(bf16[160,2176]{1,0:T(8,128)(2,1)S(1)} %get-tuple-element.72), channel_id=1, source_target_pairs={{0,4},{2,6},{4,0},{6,2},{8,12},{10,14},{12,8},{14,10},{1,5},{3,7},... | collective-permute-start | bytes 2088968 | tf_op jit(solution)/shard_map/ppermute | solution.py:475
  83.8 22.0 %collective-permute-start.11 = (bf16[128,2176]{1,0:T(8,128)(2,1)S(1)}, bf16[128,2176]{1,0:T(8,128)(2,1)S(1)}, u32[]{:S(2)}, u32[]{:S(2)}) collective-permute-start(bf16[128,2176]{1,0:T(8,128)(2,1)S(1)} %get-tuple-element.84), channel_id=1, source_target_pairs={{0,2},{2,0},{4,6},{6,4},{8,10},{10,8},{12,14},{14,12},{1,3},{3,1},... | collective-permute-start | bytes 1671176 | tf_op jit(solution)/shard_map/ppermute | solution.py:475
  86.7 33.1 %collective-permute-start.14 = (f32[128,3584]{1,0:T(8,128)S(1)}, f32[128,3584]{1,0:T(8,128)S(1)}, u32[]{:S(2)}, u32[]{:S(2)}) collective-permute-start(f32[128,3584]{1,0:T(8,128)S(1)} %get-tuple-element.93), channel_id=1, source_target_pairs={{0,1},{1,0},{2,3},{3,2},{4,5},{5,4},{6,7},{7,6},{8,9},{9,8},{10,11... | collective-permute-start | bytes 5505032 | tf_op jit(solution)/shard_map/ppermute | solution.py:478
  88.2 33.3 %collective-permute-start.15 = (bf16[96,2176]{1,0:T(8,128)(2,1)S(1)}, bf16[96,2176]{1,0:T(8,128)(2,1)S(1)}, u32[]{:S(2)}, u32[]{:S(2)}) collective-permute-start(bf16[96,2176]{1,0:T(8,128)(2,1)S(1)} %get-tuple-element.97), channel_id=1, source_target_pairs={{0,8},{2,10},{4,12},{6,14},{8,0},{10,2},{12,4},{14,6},{1,9},{3,11}... | collective-permute-start | bytes 1253384 | tf_op jit(solution)/shard_map/ppermute | solution.py:475
  107.3 19.9 %collective-permute-start.16 = (bf16[64,2176]{1,0:T(8,128)(2,1)S(1)}, bf16[64,2176]{1,0:T(8,128)(2,1)S(1)}, u32[]{:S(2)}, u32[]{:S(2)}) collective-permute-start(bf16[64,2176]{1,0:T(8,128)(2,1)S(1)} %get-tuple-element.105), channel_id=1, source_target_pairs={{0,8},{2,10},{4,12},{6,14},{8,0},{10,2},{12,4},{14,6},{1,9},{3,11}... | collective-permute-start | bytes 835592 | tf_op jit(solution)/shard_map/ppermute | solution.py:475
  119.2 5.3 %collective-permute-start.12 = (f32[128,1536]{1,0:T(8,128)S(1)}, f32[128,1536]{1,0:T(8,128)S(1)}, u32[]{:S(2)}, u32[]{:S(2)}) collective-permute-start(f32[128,1536]{1,0:T(8,128)S(1)} %get-tuple-element.89), channel_id=1, source_target_pairs={{0,1},{1,0},{2,3},{3,2},{4,5},{5,4},{6,7},{7,6},{8,9},{9,8},{10,11... | collective-permute-start | bytes 2359304 | tf_op jit(solution)/shard_map/ppermute | solution.py:478
  119.3 3.8 %collective-permute-start.13 = (f32[128,2048]{1,0:T(8,128)S(1)}, f32[128,2048]{1,0:T(8,128)S(1)}, u32[]{:S(2)}, u32[]{:S(2)}) collective-permute-start(f32[128,2048]{1,0:T(8,128)S(1)} %get-tuple-element.91), channel_id=1, source_target_pairs={{0,1},{1,0},{2,3},{3,2},{4,5},{5,4},{6,7},{7,6},{8,9},{9,8},{10,11... | collective-permute-start | bytes 3145736 | tf_op jit(solution)/shard_map/ppermute | solution.py:478
  122.0 4.0 %collective-permute-start.17 = (f32[128,128]{1,0:T(8,128)S(1)}, f32[128,128]{1,0:T(8,128)S(1)}, u32[]{:S(2)}, u32[]{:S(2)}) collective-permute-start(f32[128,128]{1,0:T(8,128)S(1)} %get-tuple-element.108.refs_2_), channel_id=1, source_target_pairs={{0,1},{1,0},{2,3},{3,2},{4,5},{5,4},{6,7},{7,6},{8,9},{9,8},{10,11... | collective-permute-start | bytes 196616 | tf_op jit(solution)/shard_map/ppermute | solution.py:478
  127.0 2.3 %collective-permute-start.18 = (f32[4,64,64]{2,1,0:T(8,128)S(1)}, f32[4,64,64]{2,1,0:T(8,128)S(1)}, u32[]{:S(2)}, u32[]{:S(2)}) collective-permute-start(f32[4,64,64]{2,1,0:T(8,128)S(1)} %get-tuple-element.112), channel_id=1, source_target_pairs={{0,1},{1,0},{2,3},{3,2},{4,5},{5,4},{6,7},{7,6},{8,9},{9,8},{10,11... | collective-permute-start | bytes 196616 | tf_op jit(solution)/shard_map/ppermute | solution.py:478

commit v8 on v7

--- a/solution.py
+++ b/solution.py
@@ -17,7 +17,7 @@
 VMEM_MIB = {"backward": 32, "forward": 24}
 MIB = 1 << 20
 RIGHT_ROWS = 32
-TIMES = {"backward": 19 * 10**9, "forward": 1 << 34, "fold": 0, "combine": 1 << 34, "sketch_part": 1 << 34}
+TIMES = {"gate": 0, "backward_0": 19 * 10**9, "backward_4": 10 * 10**9, "forward": 1 << 34, "fold": 0, "combine": 1 << 34, "sketch_part": 1 << 34}
 ANY = pl.BlockSpec(memory_space=pl.ANY)
 HBM = pl.BlockSpec(memory_space=pltpu.HBM)
 
@@ -60,7 +60,7 @@
             out_specs=list(out_specs) + [whole(token.shape)],
             scratch_shapes=list(scratch),
         ),
-        compiler_params=pltpu.CompilerParams(vmem_limit_bytes=VMEM_MIB.get(name, 14) * MIB),
+        compiler_params=pltpu.CompilerParams(vmem_limit_bytes=VMEM_MIB.get(name.split("_")[0], 14) * MIB),
         cost_estimate=pl.CostEstimate(
             flops=TIMES.get(name, work[0]), bytes_accessed=work[1], transcendentals=0
         ),
@@ -207,7 +207,7 @@
         specs,
         out,
         [whole(o.shape) for o in out],
-        "backward",
+        f"backward_{first}",
         (count,),
         (4 * half * hidden * width, 2 * hidden * width + 12 * half * width),
         after,
@@ -556,11 +556,11 @@
     token = hold([m + 1 for m in evens], token)
     second, left2, token = batch_forward(1, 0, cut, token)
     token = folded(1, 2, token)
+    outputs, token = combine(idx, *first, [], token)
     third, _, token = batch_forward(1, cut, tiles, token)
     for step in range(3, bits):
         for p in range(PIECES):
             token = folded(p, step, token)
-    outputs, token = combine(idx, *first, [], token)
     right, token = last_right(idx, rights[0], msgs[0], token)
     right_got = swap(right)
     outputs, token = combine(idx, *second, [outputs], token)

time: 130 us -> 124 us (0.954)
  starting transfers between devices: 22.6 us -> 18.8 us
  waiting for transfers between devices: 23.7 us -> 21 us
    ppermute x13, starting transfers between devices: 21.2 us -> 17.2 us  [partner(): return lax.ppermute(x, 'outp', [(d, d ^ 1 << bit) for d in range(n)])]
    ppermute x13, waiting for transfers between devices: 22.7 us -> 20.5 us  [partner(): return lax.ppermute(x, 'outp', [(d, d ^ 1 << bit) for d in range(n)])]
  transfers between devices with their start and end apart: 19 -> 19, of which waited for: 6 -> 6; matrix products, arithmetic and copies ran while one was open for 0% -> 0% of each run, Pallas kernels for 61% -> 64%
where the time goes in v8:
time: 124 us
  Pallas kernels  79.5 us (64%)
  waiting for transfers between devices  21 us (17%)
  starting transfers between devices  18.8 us (15%)
  local copies, waits for them, and re-layouts  3.27 us (3%)
    pallas_call x18, Pallas kernels, call(): pl.pallas_call(with_token, out_shape=list(out_shape) + [token], grid_spec...  79.5 us
    ppermute x13, waiting for transfers between devices, partner(): return lax.ppermute(x, 'outp', [(d, d ^ 1 << bit) for d in range(n)])  20.5 us
    ppermute x13, starting transfers between devices, partner(): return lax.ppermute(x, 'outp', [(d, d ^ 1 << bit) for d in range(n)])  17.2 us
    unnamed x8, local copies, waits for them, and re-layouts  2.53 us
  transfers between devices with their start and end apart: 19, of which 6 were waited for; matrix products, arithmetic and copies ran while one was open for 0% of the time, Pallas kernels for 64%

profile of v8, /device:TPU:0, one launch (start us, length us, event | category | flops | bytes accessed | tf_op | source)
XLA Modules:
  0.0 123.5 jit_solution(1930379045372129186)
XLA Ops:
  1.1 3.7 %collective-permute-start.1 = (bf16[64,4096]{1,0:T(8,128)(2,1)}, bf16[64,4096]{1,0:T(8,128)(2,1)S(1)}, u32[]{:S(2)}, u32[]{:S(2)}) collective-permute-start(bf16[64,4096]{1,0:T(8,128)(2,1)} %refs_0_.5), channel_id=1, source_target_pairs={{0,8},{2,10},{4,12},{6,14},{8,0},{10,2},{12,4},{14,6},{1,9},{3,11}... | collective-permute-start | bytes 1572872 | tf_op jit(solution)/shard_map/ppermute | solution.py:475
  4.8 1.5 %collective-permute-start = (bf16[64,4096]{1,0:T(8,128)(2,1)}, bf16[64,4096]{1,0:T(8,128)(2,1)S(1)}, u32[]{:S(2)}, u32[]{:S(2)}) collective-permute-start(bf16[64,4096]{1,0:T(8,128)(2,1)} %refs_0_.5), channel_id=1, source_target_pairs={{0,2},{2,0},{4,6},{6,4},{8,10},{10,8},{12,14},{14,12},{1,3},{3,1},... | collective-permute-start | bytes 1572872 | tf_op jit(solution)/shard_map/ppermute | solution.py:475
  6.3 1.6 %collective-permute-start.2 = (bf16[64,4096]{1,0:T(8,128)(2,1)}, bf16[64,4096]{1,0:T(8,128)(2,1)S(1)}, u32[]{:S(2)}, u32[]{:S(2)}) collective-permute-start(bf16[64,4096]{1,0:T(8,128)(2,1)} %refs_0_.5), channel_id=1, source_target_pairs={{0,4},{2,6},{4,0},{6,2},{8,12},{10,14},{12,8},{14,10},{1,5},{3,7},... | collective-permute-start | bytes 1572872 | tf_op jit(solution)/shard_map/ppermute | solution.py:475
  8.0 1.5 %copy-done = bf16[256,3584]{1,0:T(8,128)(2,1)S(1)} copy-done((bf16[256,3584]{1,0:T(8,128)(2,1)S(1)}, bf16[256,3584]{1,0:T(8,128)(2,1)}, u32[]{:S(2)}) %copy-start) | copy-done | bytes 1835032
  10.5 14.3 %backward_0.1 = (bf16[288,2176]{1,0:T(8,128)(2,1)S(1)}, f32[4,4,64,512]{3,2,1,0:T(8,128)S(1)}, f32[128,128]{1,0:T(8,128)S(1)}, f32[8,128]{1,0:T(8,128)S(1)}) custom-call(s32[2]{0:T(128)S(1)} %pad_add_fusion.idx, bf16[256,3584]{1,0:T(8,128)(2,1)S(1)} %copy-done, bf16[256,3584]{1,0:T(8,128)(2,1)S(1)} %collective-permute-done.3.refs_1_, ...), custom_call_target="tpu_custom_call" | custom-call | flops 19000000512 | bytes 20971520 | tf_op jit(solution)/shard_map/backward_0/pallas_call | solution.py:53
  25.4 3.5 %collective-permute-done.1.refs_1_ = bf16[64,4096]{1,0:T(8,128)(2,1)S(1)} collective-permute-done((bf16[64,4096]{1,0:T(8,128)(2,1)}, bf16[64,4096]{1,0:T(8,128)(2,1)S(1)}, u32[]{:S(2)}, u32[]{:S(2)}) %collective-permute-start.1) | collective-permute-done | bytes 524320 | tf_op jit(solution)/shard_map/ppermute | solution.py:475
  28.9 1.4 %collective-permute-done.2.refs_2_ = bf16[64,4096]{1,0:T(8,128)(2,1)S(1)} collective-permute-done((bf16[64,4096]{1,0:T(8,128)(2,1)}, bf16[64,4096]{1,0:T(8,128)(2,1)S(1)}, u32[]{:S(2)}, u32[]{:S(2)}) %collective-permute-start.2) | collective-permute-done | bytes 524320 | tf_op jit(solution)/shard_map/ppermute | solution.py:475
  31.2 13.4 %backward_4.1 = (bf16[256,2176]{1,0:T(8,128)(2,1)S(1)}, f32[4,4,64,512]{3,2,1,0:T(8,128)S(1)}, f32[8,128]{1,0:T(8,128)S(1)}) custom-call(s32[2]{0:T(128)S(1)} %pad_add_fusion.idx, bf16[256,3584]{1,0:T(8,128)(2,1)S(1)} %copy-done, bf16[256,3584]{1,0:T(8,128)(2,1)S(1)} %collective-permute-done.3.refs_1_, bf16[4096,3584]{1,0:T(8,128)(2,1)} %refs_4_.5, ...), custom_call_target="tpu_custom_call" | custom-call | flops 10000000000 | bytes 20971520 | tf_op jit(solution)/shard_map/backward_4/pallas_call | solution.py:53
  44.6 1.8 %collective-permute-start.10 = (bf16[256,2176]{1,0:T(8,128)(2,1)S(1)}, bf16[256,2176]{1,0:T(8,128)(2,1)S(1)}, u32[]{:S(2)}, u32[]{:S(2)}) collective-permute-start(bf16[256,2176]{1,0:T(8,128)(2,1)S(1)} %get-tuple-element.75), channel_id=1, source_target_pairs={{0,4},{2,6},{4,0},{6,2},{8,12},{10,14},{12,8},{14,10},{1,5},{3,7},... | collective-permute-start | bytes 3342344 | tf_op jit(solution)/shard_map/ppermute | solution.py:475
  47.6 1.5 %collective-permute-start.6 = (bf16[64,4096]{1,0:T(8,128)(2,1)S(1)}, bf16[64,4096]{1,0:T(8,128)(2,1)S(1)}, u32[]{:S(2)}, u32[]{:S(2)}) collective-permute-start(bf16[64,4096]{1,0:T(8,128)(2,1)S(1)} %get-tuple-element.65.refs_2_), channel_id=1, source_target_pairs={{0,2},{2,0},{4,6},{6,4},{8,10},{10,8},{12,14},{14,12},{1,3},{3,1},... | collective-permute-start | bytes 1572872 | tf_op jit(solution)/shard_map/ppermute | solution.py:475
  49.6 5.7 %collective-permute-done.8.refs_1_ = bf16[288,2176]{1,0:T(8,128)(2,1)S(1)} collective-permute-done((bf16[288,2176]{1,0:T(8,128)(2,1)S(1)}, bf16[288,2176]{1,0:T(8,128)(2,1)S(1)}, u32[]{:S(2)}, u32[]{:S(2)}) %collective-permute-start.8) | collective-permute-done | bytes 1253408 | tf_op jit(solution)/shard_map/ppermute | solution.py:475
  55.3 2.4 %fold.4 = (bf16[160,2176]{1,0:T(8,128)(2,1)S(1)}, f32[4,2,64,512]{3,2,1,0:T(8,128)S(1)}, f32[128,128]{1,0:T(8,128)S(1)}, f32[8,128]{1,0:T(8,128)S(1)}) custom-call(s32[2]{0:T(128)S(1)} %pad_add_fusion.idx, f32[4,4,64,512]{3,2,1,0:T(8,128)S(1)} %get-tuple-element.67.refs_0_, bf16[288,2176]{1,0:T(8,128)(2,1)S(1)} %collective-permute-done.8.refs_1_, ...), custom_call_target="tpu_custom_call" | custom-call | bytes 6291456 | tf_op jit(solution)/shard_map/fold/pallas_call | solution.py:53
  58.3 15.5 %forward.3 = (f32[128,3584]{1,0:T(8,128)S(1)}, f32[128,3584]{1,0:T(8,128)S(1)}, f32[256,64]{1,0:T(8,128)S(1)}, f32[8,128]{1,0:T(8,128)S(1)}) custom-call(s32[2]{0:T(128)S(1)} %pad_add_fusion.idx, bf16[64,4096]{1,0:T(8,128)(2,1)S(1)} %copy-done.1, bf16[64,4096]{1,0:T(8,128)(2,1)S(1)} %get-tuple-element.64.refs_1_, ...), custom_call_target="tpu_custom_call" | custom-call | flops 17179869184 | bytes 33030144 | tf_op jit(solution)/shard_map/forward/pallas_call | solution.py:53
  73.8 2.4 %fold.5 = (bf16[128,2176]{1,0:T(8,128)(2,1)S(1)}, f32[4,2,64,512]{3,2,1,0:T(8,128)S(1)}, f32[8,128]{1,0:T(8,128)S(1)}) custom-call(s32[2]{0:T(128)S(1)} %pad_add_fusion.idx, f32[4,4,64,512]{3,2,1,0:T(8,128)S(1)} %get-tuple-element.74.refs_0_, bf16[256,2176]{1,0:T(8,128)(2,1)S(1)} %collective-permute-done.10.refs_1_, f32[8,128]{1,0:T(8,128)S(1)} %get-tuple-element.77.refs_2_), custom_call_target="tpu_custom_call" | custom-call | bytes 6291456 | tf_op jit(solution)/shard_map/fold/pallas_call | solution.py:53
  76.2 9.2 %collective-permute-done.9.refs_1_ = bf16[160,2176]{1,0:T(8,128)(2,1)S(1)} collective-permute-done((bf16[160,2176]{1,0:T(8,128)(2,1)S(1)}, bf16[160,2176]{1,0:T(8,128)(2,1)S(1)}, u32[]{:S(2)}, u32[]{:S(2)}) %collective-permute-start.9) | collective-permute-done | bytes 696352 | tf_op jit(solution)/shard_map/ppermute | solution.py:475
  85.4 1.5 %collective-permute-start.12 = (bf16[128,2176]{1,0:T(8,128)(2,1)S(1)}, bf16[128,2176]{1,0:T(8,128)(2,1)S(1)}, u32[]{:S(2)}, u32[]{:S(2)}) collective-permute-start(bf16[128,2176]{1,0:T(8,128)(2,1)S(1)} %get-tuple-element.86), channel_id=1, source_target_pairs={{0,2},{2,0},{4,6},{6,4},{8,10},{10,8},{12,14},{14,12},{1,3},{3,1},... | collective-permute-start | bytes 1671176 | tf_op jit(solution)/shard_map/ppermute | solution.py:475
  86.9 1.5 %fold.6 = (bf16[96,2176]{1,0:T(8,128)(2,1)S(1)}, f32[4,1,64,512]{3,2,1,0:T(8,128)S(1)}, f32[128,128]{1,0:T(8,128)S(1)}, f32[8,128]{1,0:T(8,128)S(1)}) custom-call(s32[2]{0:T(128)S(1)} %pad_add_fusion.idx, f32[4,2,64,512]{3,2,1,0:T(8,128)S(1)} %get-tuple-element.71.refs_0_, bf16[160,2176]{1,0:T(8,128)(2,1)S(1)} %collective-permute-done.9.refs_1_, ...), custom_call_target="tpu_custom_call" | custom-call | bytes 3145728 | tf_op jit(solution)/shard_map/fold/pallas_call | solution.py:53
  88.4 2.8 %collective-permute-start.15 = (bf16[96,2176]{1,0:T(8,128)(2,1)S(1)}, bf16[96,2176]{1,0:T(8,128)(2,1)S(1)}, u32[]{:S(2)}, u32[]{:S(2)}) collective-permute-start(bf16[96,2176]{1,0:T(8,128)(2,1)S(1)} %get-tuple-element.97), channel_id=1, source_target_pairs={{0,8},{2,10},{4,12},{6,14},{8,0},{10,2},{12,4},{14,6},{1,9},{3,11}... | collective-permute-start | bytes 1253384 | tf_op jit(solution)/shard_map/ppermute | solution.py:475
  91.8 9.9 %forward.4 = (f32[128,2048]{1,0:T(8,128)S(1)}, f32[128,2048]{1,0:T(8,128)S(1)}, f32[256,64]{1,0:T(8,128)S(1)}, f32[8,128]{1,0:T(8,128)S(1)}) custom-call(s32[2]{0:T(128)S(1)} %pad_add_fusion.idx, bf16[64,4096]{1,0:T(8,128)(2,1)S(1)} %get-tuple-element.59.refs_0_, bf16[64,4096]{1,0:T(8,128)(2,1)S(1)} %get-tuple-element.80.refs_1_, ...), custom_call_target="tpu_custom_call" | custom-call | flops 17179869184 | bytes 18874368 | tf_op jit(solution)/shard_map/forward/pallas_call | solution.py:53
  101.7 1.5 %fold.7 = (bf16[64,2176]{1,0:T(8,128)(2,1)S(1)}, f32[4,1,64,512]{3,2,1,0:T(8,128)S(1)}, f32[8,128]{1,0:T(8,128)S(1)}) custom-call(s32[2]{0:T(128)S(1)} %pad_add_fusion.idx, f32[4,2,64,512]{3,2,1,0:T(8,128)S(1)} %get-tuple-element.85.refs_0_, bf16[128,2176]{1,0:T(8,128)(2,1)S(1)} %collective-permute-done.12.refs_1_, f32[8,128]{1,0:T(8,128)S(1)} %get-tuple-element.88.refs_2_), custom_call_target="tpu_custom_call" | custom-call | bytes 3145728 | tf_op jit(solution)/shard_map/fold/pallas_call | solution.py:53
  103.4 1.6 %combine.3 = (bf16[256,3584]{1,0:T(8,128)(2,1)}, f32[8,128]{1,0:T(8,128)S(1)}) custom-call(s32[2]{0:T(128)S(1)} %pad_add_fusion.idx, f32[128,3584]{1,0:T(8,128)S(1)} %get-tuple-element.83.refs_0_, f32[128,3584]{1,0:T(8,128)S(1)} %collective-permute-done.11.refs_1_, f32[8,128]{1,0:T(8,128)S(1)} %get-tuple-element.89.refs_2_), custom_call_target="tpu_custom_call" | custom-call | flops 17179869184 | bytes 4587520 | tf_op jit(solution)/shard_map/combine/pallas_call | solution.py:53
  105.1 9.0 %forward.5 = (f32[128,1536]{1,0:T(8,128)S(1)}, f32[128,1536]{1,0:T(8,128)S(1)}, f32[256,64]{1,0:T(8,128)}, f32[8,128]{1,0:T(8,128)S(1)}) custom-call(s32[2]{0:T(128)S(1)} %pad_add_fusion.idx, bf16[64,4096]{1,0:T(8,128)(2,1)S(1)} %get-tuple-element.59.refs_0_, bf16[64,4096]{1,0:T(8,128)(2,1)S(1)} %get-tuple-element.80.refs_1_, ...), custom_call_target="tpu_custom_call" | custom-call | flops 17179869184 | bytes 14155776 | tf_op jit(solution)/shard_map/forward/pallas_call | solution.py:53
  115.9 1.4 %combine.4 = (bf16[256,3584]{1,0:T(8,128)(2,1)}, f32[8,128]{1,0:T(8,128)S(1)}) custom-call(s32[2]{0:T(128)S(1)} %pad_add_fusion.idx, f32[128,2048]{1,0:T(8,128)S(1)} %get-tuple-element.93.refs_0_, f32[128,2048]{1,0:T(8,128)S(1)} %collective-permute-done.14.refs_1_, bf16[256,3584]{1,0:T(8,128)(2,1)} %get-tuple-element.95.refs_2_, ...), custom_call_target="tpu_custom_call", output_to_operand_aliasing={{0}: (3, {})} | custom-call | flops 17179869184 | bytes 2621440 | tf_op jit(solution)/shard_map/combine/pallas_call | solution.py:53
  120.6 2.1 %finish.1 = (bf16[64,4096]{1,0:T(8,128)(2,1)}, f32[8,128]{1,0:T(8,128)}) custom-call(s32[2]{0:T(128)S(1)} %pad_add_fusion.idx, f32[4,1,64,512]{3,2,1,0:T(8,128)S(1)} %get-tuple-element.103.refs_0_, f32[4,1,64,512]{3,2,1,0:T(8,128)S(1)} %get-tuple-element.104.refs_1_, bf16[96,2176]{1,0:T(8,128)(2,1)S(1)} %collective-permute-done.15.refs_1_.refs_2_, ...), custom_call_target="tpu_custom_call" | custom-call | bytes 2097152 | tf_op jit(solution)/shard_map/finish/pallas_call | solution.py:53
  (43 shorter events, 12.0 us)
Async XLA Ops:
  0.6 7.4 %collective-permute-start.3 = (bf16[256,3584]{1,0:T(8,128)(2,1)}, bf16[256,3584]{1,0:T(8,128)(2,1)S(1)}, u32[]{:S(2)}, u32[]{:S(2)}) collective-permute-start(bf16[256,3584]{1,0:T(8,128)(2,1)} %refs_0_.4), channel_id=1, source_target_pairs={{0,1},{1,0},{2,3},{3,2},{4,5},{5,4},{6,7},{7,6},{8,9},{9,8},{10,11... | collective-permute-start | bytes 5505032 | tf_op jit(solution)/shard_map/ppermute | solution.py:478
  1.1 27.7 %collective-permute-start.1 = (bf16[64,4096]{1,0:T(8,128)(2,1)}, bf16[64,4096]{1,0:T(8,128)(2,1)S(1)}, u32[]{:S(2)}, u32[]{:S(2)}) collective-permute-start(bf16[64,4096]{1,0:T(8,128)(2,1)} %refs_0_.5), channel_id=1, source_target_pairs={{0,8},{2,10},{4,12},{6,14},{8,0},{10,2},{12,4},{14,6},{1,9},{3,11}... | collective-permute-start | bytes 1572872 | tf_op jit(solution)/shard_map/ppermute | solution.py:475
  4.8 24.1 %collective-permute-start = (bf16[64,4096]{1,0:T(8,128)(2,1)}, bf16[64,4096]{1,0:T(8,128)(2,1)S(1)}, u32[]{:S(2)}, u32[]{:S(2)}) collective-permute-start(bf16[64,4096]{1,0:T(8,128)(2,1)} %refs_0_.5), channel_id=1, source_target_pairs={{0,2},{2,0},{4,6},{6,4},{8,10},{10,8},{12,14},{14,12},{1,3},{3,1},... | collective-permute-start | bytes 1572872 | tf_op jit(solution)/shard_map/ppermute | solution.py:475
  6.3 24.0 %collective-permute-start.2 = (bf16[64,4096]{1,0:T(8,128)(2,1)}, bf16[64,4096]{1,0:T(8,128)(2,1)S(1)}, u32[]{:S(2)}, u32[]{:S(2)}) collective-permute-start(bf16[64,4096]{1,0:T(8,128)(2,1)} %refs_0_.5), channel_id=1, source_target_pairs={{0,4},{2,6},{4,0},{6,2},{8,12},{10,14},{12,8},{14,10},{1,5},{3,7},... | collective-permute-start | bytes 1572872 | tf_op jit(solution)/shard_map/ppermute | solution.py:475
  8.0 1.5 %copy-start = (bf16[256,3584]{1,0:T(8,128)(2,1)S(1)}, bf16[256,3584]{1,0:T(8,128)(2,1)}, u32[]{:S(2)}) copy-start(bf16[256,3584]{1,0:T(8,128)(2,1)} %refs_0_.4) | copy-start | bytes 5505028
  9.5 1.0 copy-start.3
  24.8 30.5 %collective-permute-start.8 = (bf16[288,2176]{1,0:T(8,128)(2,1)S(1)}, bf16[288,2176]{1,0:T(8,128)(2,1)S(1)}, u32[]{:S(2)}, u32[]{:S(2)}) collective-permute-start(bf16[288,2176]{1,0:T(8,128)(2,1)S(1)} %get-tuple-element.68), channel_id=1, source_target_pairs={{0,2},{2,0},{4,6},{6,4},{8,10},{10,8},{12,14},{14,12},{1,3},{3,1},... | collective-permute-start | bytes 3760136 | tf_op jit(solution)/shard_map/ppermute | solution.py:475
  30.9 15.5 %collective-permute-start.4 = (bf16[64,4096]{1,0:T(8,128)(2,1)S(1)}, bf16[64,4096]{1,0:T(8,128)(2,1)S(1)}, u32[]{:S(2)}, u32[]{:S(2)}) collective-permute-start(bf16[64,4096]{1,0:T(8,128)(2,1)S(1)} %get-tuple-element.61.refs_1_), channel_id=1, source_target_pairs={{0,4},{2,6},{4,0},{6,2},{8,12},{10,14},{12,8},{14,10},{1,5},{3,7},... | collective-permute-start | bytes 1572872 | tf_op jit(solution)/shard_map/ppermute | solution.py:475
  44.6 29.2 %collective-permute-start.10 = (bf16[256,2176]{1,0:T(8,128)(2,1)S(1)}, bf16[256,2176]{1,0:T(8,128)(2,1)S(1)}, u32[]{:S(2)}, u32[]{:S(2)}) collective-permute-start(bf16[256,2176]{1,0:T(8,128)(2,1)S(1)} %get-tuple-element.75), channel_id=1, source_target_pairs={{0,4},{2,6},{4,0},{6,2},{8,12},{10,14},{12,8},{14,10},{1,5},{3,7},... | collective-permute-start | bytes 3342344 | tf_op jit(solution)/shard_map/ppermute | solution.py:475
  47.0 11.3 %copy-start.1 = (bf16[64,4096]{1,0:T(8,128)(2,1)S(1)}, bf16[64,4096]{1,0:T(8,128)(2,1)}, u32[]{:S(2)}) copy-start(bf16[64,4096]{1,0:T(8,128)(2,1)} %refs_0_.5) | copy-start | bytes 1572868
  47.0 11.3 %copy-start.2 = (bf16[64,4096]{1,0:T(8,128)(2,1)S(1)}, bf16[64,4096]{1,0:T(8,128)(2,1)}, u32[]{:S(2)}) copy-start(bf16[64,4096]{1,0:T(8,128)(2,1)} %refs_5_.5) | copy-start | bytes 1572868
  47.0 41.5 %collective-permute-start.5 = (bf16[64,4096]{1,0:T(8,128)(2,1)S(1)}, bf16[64,4096]{1,0:T(8,128)(2,1)S(1)}, u32[]{:S(2)}, u32[]{:S(2)}) collective-permute-start(bf16[64,4096]{1,0:T(8,128)(2,1)S(1)} %get-tuple-element.64.refs_1_), channel_id=1, source_target_pairs={{0,2},{2,0},{4,6},{6,4},{8,10},{10,8},{12,14},{14,12},{1,3},{3,1},... | collective-permute-start | bytes 1572872 | tf_op jit(solution)/shard_map/ppermute | solution.py:475
  47.6 43.6 %collective-permute-start.6 = (bf16[64,4096]{1,0:T(8,128)(2,1)S(1)}, bf16[64,4096]{1,0:T(8,128)(2,1)S(1)}, u32[]{:S(2)}, u32[]{:S(2)}) collective-permute-start(bf16[64,4096]{1,0:T(8,128)(2,1)S(1)} %get-tuple-element.65.refs_2_), channel_id=1, source_target_pairs={{0,2},{2,0},{4,6},{6,4},{8,10},{10,8},{12,14},{14,12},{1,3},{3,1},... | collective-permute-start | bytes 1572872 | tf_op jit(solution)/shard_map/ppermute | solution.py:475
  49.1 42.2 %collective-permute-start.7 = (bf16[64,4096]{1,0:T(8,128)(2,1)S(1)}, bf16[64,4096]{1,0:T(8,128)(2,1)S(1)}, u32[]{:S(2)}, u32[]{:S(2)}) collective-permute-start(bf16[64,4096]{1,0:T(8,128)(2,1)S(1)} %get-tuple-element.66.refs_3_), channel_id=1, source_target_pairs={{0,2},{2,0},{4,6},{6,4},{8,10},{10,8},{12,14},{14,12},{1,3},{3,1},... | collective-permute-start | bytes 1572872 | tf_op jit(solution)/shard_map/ppermute | solution.py:475
  57.7 27.7 %collective-permute-start.9 = (bf16[160,2176]{1,0:T(8,128)(2,1)S(1)}, bf16[160,2176]{1,0:T(8,128)(2,1)S(1)}, u32[]{:S(2)}, u32[]{:S(2)}) collective-permute-start(bf16[160,2176]{1,0:T(8,128)(2,1)S(1)} %get-tuple-element.72), channel_id=1, source_target_pairs={{0,4},{2,6},{4,0},{6,2},{8,12},{10,14},{12,8},{14,10},{1,5},{3,7},... | collective-permute-start | bytes 2088968 | tf_op jit(solution)/shard_map/ppermute | solution.py:475
  73.7 29.7 %collective-permute-start.11 = (f32[128,3584]{1,0:T(8,128)S(1)}, f32[128,3584]{1,0:T(8,128)S(1)}, u32[]{:S(2)}, u32[]{:S(2)}) collective-permute-start(f32[128,3584]{1,0:T(8,128)S(1)} %get-tuple-element.84), channel_id=1, source_target_pairs={{0,1},{1,0},{2,3},{3,2},{4,5},{5,4},{6,7},{7,6},{8,9},{9,8},{10,11... | collective-permute-start | bytes 5505032 | tf_op jit(solution)/shard_map/ppermute | solution.py:478
  85.4 16.3 %collective-permute-start.12 = (bf16[128,2176]{1,0:T(8,128)(2,1)S(1)}, bf16[128,2176]{1,0:T(8,128)(2,1)S(1)}, u32[]{:S(2)}, u32[]{:S(2)}) collective-permute-start(bf16[128,2176]{1,0:T(8,128)(2,1)S(1)} %get-tuple-element.86), channel_id=1, source_target_pairs={{0,2},{2,0},{4,6},{6,4},{8,10},{10,8},{12,14},{14,12},{1,3},{3,1},... | collective-permute-start | bytes 1671176 | tf_op jit(solution)/shard_map/ppermute | solution.py:475
  88.4 26.3 %collective-permute-start.15 = (bf16[96,2176]{1,0:T(8,128)(2,1)S(1)}, bf16[96,2176]{1,0:T(8,128)(2,1)S(1)}, u32[]{:S(2)}, u32[]{:S(2)}) collective-permute-start(bf16[96,2176]{1,0:T(8,128)(2,1)S(1)} %get-tuple-element.97), channel_id=1, source_target_pairs={{0,8},{2,10},{4,12},{6,14},{8,0},{10,2},{12,4},{14,6},{1,9},{3,11}... | collective-permute-start | bytes 1253384 | tf_op jit(solution)/shard_map/ppermute | solution.py:475
  103.2 17.5 %collective-permute-start.16 = (bf16[64,2176]{1,0:T(8,128)(2,1)S(1)}, bf16[64,2176]{1,0:T(8,128)(2,1)S(1)}, u32[]{:S(2)}, u32[]{:S(2)}) collective-permute-start(bf16[64,2176]{1,0:T(8,128)(2,1)S(1)} %get-tuple-element.105), channel_id=1, source_target_pairs={{0,8},{2,10},{4,12},{6,14},{8,0},{10,2},{12,4},{14,6},{1,9},{3,11}... | collective-permute-start | bytes 835592 | tf_op jit(solution)/shard_map/ppermute | solution.py:475
  103.4 12.5 %collective-permute-start.14 = (f32[128,2048]{1,0:T(8,128)S(1)}, f32[128,2048]{1,0:T(8,128)S(1)}, u32[]{:S(2)}, u32[]{:S(2)}) collective-permute-start(f32[128,2048]{1,0:T(8,128)S(1)} %get-tuple-element.94), channel_id=1, source_target_pairs={{0,1},{1,0},{2,3},{3,2},{4,5},{5,4},{6,7},{7,6},{8,9},{9,8},{10,11... | collective-permute-start | bytes 3145736 | tf_op jit(solution)/shard_map/ppermute | solution.py:478
  115.3 3.9 %collective-permute-start.17 = (f32[128,128]{1,0:T(8,128)S(1)}, f32[128,128]{1,0:T(8,128)S(1)}, u32[]{:S(2)}, u32[]{:S(2)}) collective-permute-start(f32[128,128]{1,0:T(8,128)S(1)} %get-tuple-element.108.refs_2_), channel_id=1, source_target_pairs={{0,1},{1,0},{2,3},{3,2},{4,5},{5,4},{6,7},{7,6},{8,9},{9,8},{10,11... | collective-permute-start | bytes 196616 | tf_op jit(solution)/shard_map/ppermute | solution.py:478
  115.4 2.4 %collective-permute-start.13 = (f32[128,1536]{1,0:T(8,128)S(1)}, f32[128,1536]{1,0:T(8,128)S(1)}, u32[]{:S(2)}, u32[]{:S(2)}) collective-permute-start(f32[128,1536]{1,0:T(8,128)S(1)} %get-tuple-element.92), channel_id=1, source_target_pairs={{0,1},{1,0},{2,3},{3,2},{4,5},{5,4},{6,7},{7,6},{8,9},{9,8},{10,11... | collective-permute-start | bytes 2359304 | tf_op jit(solution)/shard_map/ppermute | solution.py:478
  120.2 2.6 %collective-permute-start.18 = (f32[4,64,64]{2,1,0:T(8,128)S(1)}, f32[4,64,64]{2,1,0:T(8,128)S(1)}, u32[]{:S(2)}, u32[]{:S(2)}) collective-permute-start(f32[4,64,64]{2,1,0:T(8,128)S(1)} %get-tuple-element.112), channel_id=1, source_target_pairs={{0,1},{1,0},{2,3},{3,2},{4,5},{5,4},{6,7},{7,6},{8,9},{9,8},{10,11... | collective-permute-start | bytes 196616 | tf_op jit(solution)/shard_map/ppermute | solution.py:478

commit v9 on v8

--- a/solution.py
+++ b/solution.py
@@ -16,7 +16,8 @@
 H_TILE = 512
 VMEM_MIB = {"backward": 32, "forward": 24}
 MIB = 1 << 20
-RIGHT_ROWS = 32
+RIGHT_ROWS = 16
+RIGHT_PARTS = 2
 TIMES = {"gate": 0, "backward_0": 19 * 10**9, "backward_4": 10 * 10**9, "forward": 1 << 34, "fold": 0, "combine": 1 << 34, "sketch_part": 1 << 34}
 ANY = pl.BlockSpec(memory_space=pl.ANY)
 HBM = pl.BlockSpec(memory_space=pltpu.HBM)
@@ -100,9 +101,9 @@
     base = msg.shape[0] - RIGHT_ROWS
     for q in range(value.shape[0] // RIGHT_ROWS):
         left_over = value[q * RIGHT_ROWS : (q + 1) * RIGHT_ROWS, :]
-        for k in range(3):
+        for k in range(RIGHT_PARTS):
             part = left_over.astype(jnp.bfloat16)
-            lo = (3 * q + k) * LANES
+            lo = (RIGHT_PARTS * q + k) * LANES
             msg[base:, lo : lo + LANES] = part
             left_over = left_over - part.astype(jnp.float32)
 
@@ -111,11 +112,12 @@
     base = msg.shape[0] - RIGHT_ROWS
     out = []
     for q in range(value.shape[0] // RIGHT_ROWS):
-        lo = 3 * q * LANES
+        lo = RIGHT_PARTS * q * LANES
         parts = [
-            msg[base:, lo + k * LANES : lo + (k + 1) * LANES].astype(jnp.float32) for k in range(3)
+            msg[base:, lo + k * LANES : lo + (k + 1) * LANES].astype(jnp.float32)
+            for k in range(RIGHT_PARTS)
         ]
-        got = parts[0] + (parts[1] + parts[2])
+        got = sum(parts)
         out.append(value[q * RIGHT_ROWS : (q + 1) * RIGHT_ROWS, :] + got)
     return jnp.concatenate(out, axis=0)
 
@@ -319,6 +321,37 @@
     return list(out), [token]
 
 
+def join(idx, arrays, after):
+    rows, width = arrays[0].shape
+    k = len(arrays)
+
+    def kernel(idx, *refs):
+        out, sems = refs[-2:]
+        copies = [
+            pltpu.make_async_copy(refs[i], out.at[pl.ds(i * rows, rows)], sems.at[i])
+            for i in range(k)
+        ]
+        for c in copies:
+            c.start()
+        for c in copies:
+            c.wait()
+
+    (out,), token = call(
+        kernel,
+        idx,
+        arrays,
+        [ANY] * k,
+        [jax.ShapeDtypeStruct((k * rows, width), arrays[0].dtype)],
+        [ANY],
+        "join",
+        (1,),
+        (0, 0),
+        after,
+        [pltpu.SemaphoreType.DMA((k,))],
+    )
+    return out, [token]
+
+
 def last_right(idx, right, got, after):
     def kernel(idx, right, got, out):
         out[...] = add_right(right[...], got)
@@ -332,8 +365,8 @@
     return total, [token]
 
 
-def forward(idx, chunks, w, sketch, lo, hi, after):
-    rows, feats = chunks[0][1].shape
+def forward(idx, chunks, rows, w, sketch, lo, hi, after):
+    feats = w.shape[0]
     m = len(chunks)
     tile = pick(w.shape[1], H_TILE)
     hidden = (hi - lo) * tile
@@ -346,11 +379,12 @@
         @pl.when(pl.program_id(0) == 0)
         def _():
             copies = []
-            for i, (mask, _) in enumerate(chunks):
+            for i, (mask, _, block) in enumerate(chunks):
                 d = me ^ mask
                 side = 1 - ((d // m) ^ core)
                 to = pl.ds(pl.multiple_of(side * part + ((d % m) >> 1) * rows, BLK), rows)
-                copies.append(pltpu.make_async_copy(refs[i], x.at[to], sems.at[i]))
+                src = refs[i].at[pl.ds(block * rows, rows)]
+                copies.append(pltpu.make_async_copy(src, x.at[to], sems.at[i]))
             for c in copies:
                 c.start()
             for c in copies:
@@ -477,16 +511,14 @@
     def swap(x):
         return lax.ppermute(x, "inp", [(0, 1), (1, 0)])
 
+    evens = list(range(2, n, 2))
+    far = n // 2
     chunks = {0: inputs}
-    evens = range(2, n, 2)
-
-    def wave(masks):
+
+    def fetch(masks):
         for mask in masks:
             bit = (mask & -mask).bit_length() - 1
             chunks[mask] = partner(chunks[mask ^ (1 << bit)], bit)
-
-    def along_z(k):
-        return [m for m in reversed(evens) if m.bit_count() == k]
 
     def hold(masks, after):
         held, token = gate(idx, [chunks[m] for m in masks], after)
@@ -494,7 +526,7 @@
         return token
 
     grad_other = swap(cotangent)
-    wave(along_z(1) + [1])
+    fetch([far, 1])
 
     orders = [list(range(bits)), [1, 0] + list(range(2, bits))]
     tile = pick(feats // PIECES, F_TILE)
@@ -521,13 +553,15 @@
         if p == 0:
             right = outs[2]
         if p == 0:
-            token = hold([1] + along_z(1), token)
-            wave(along_z(2))
-    for k in range(2, bits - 1):
-        token = hold(along_z(k), token)
-        wave(along_z(k + 1))
-    token = hold(list(evens), token)
-    wave([m + 1 for m in evens])
+            token = hold([far, 1], token)
+            fetch([m for m in evens if m != far and (m & ~far).bit_count() == 1][::-1])
+    ready = [m for m in evens if m in chunks]
+    while len(ready) < len(evens):
+        token = hold(ready, token)
+        fetch([m for m in evens if m not in chunks and m & (m - 1) in chunks])
+        ready = [m for m in evens if m in chunks]
+    crossed, token = join(idx, [chunks[m] for m in evens], token)
+    crossed = partner(crossed, 0)
 
     rights = [right] + [None] * (PIECES - 1)
 
@@ -543,8 +577,11 @@
     tiles = hidden // pick(hidden, H_TILE)
 
     def batch_forward(batch, lo, hi, after):
-        parts = [(m, chunks[m]) for m in range(n) if m & 1 == batch]
-        outs, t = forward(idx, parts, weight, in_sketch, lo, hi, after)
+        if batch:
+            parts = [(1, chunks[1], 0)] + [(m + 1, crossed, i) for i, m in enumerate(evens)]
+        else:
+            parts = [(m, chunks[m], 0) for m in [0] + evens]
+        outs, t = forward(idx, parts, rows, weight, in_sketch, lo, hi, after)
         start = lo * (hidden // tiles)
         return (outs[1], swap(outs[0]), start, hidden, batch, rows), outs[2], [t]
 
@@ -553,7 +590,7 @@
     first, left1, token = batch_forward(0, 0, tiles, token)
     token = folded(1, 1, token)
     token = folded(0, 2, token)
-    token = hold([m + 1 for m in evens], token)
+    (crossed,), token = gate(idx, [crossed], token)
     second, left2, token = batch_forward(1, 0, cut, token)
     token = folded(1, 2, token)
     outputs, token = combine(idx, *first, [], token)

time: 124 us -> 127 us (1.024)
  waiting for transfers between devices: 21 us -> 26.2 us
  starting transfers between devices: 18.8 us -> 15.9 us
    ppermute x13 -> x11, waiting for transfers between devices: 20.5 us -> 25.5 us  [partner(): return lax.ppermute(x, 'outp', [(d, d ^ 1 << bit) for d in range(n)])]
    ppermute x13 -> x11, starting transfers between devices: 17.2 us -> 14.4 us  [partner(): return lax.ppermute(x, 'outp', [(d, d ^ 1 << bit) for d in range(n)])]
  transfers between devices with their start and end apart: 19 -> 17, of which waited for: 6 -> 5; matrix products, arithmetic and copies ran while one was open for 0% -> 0% of each run, Pallas kernels for 64% -> 63%
where the time goes in v9:
time: 127 us; the launch traced here: 126 us
  Pallas kernels  79.9 us (63%)
  waiting for transfers between devices  26.2 us (21%)
  starting transfers between devices  15.9 us (13%)
  local copies, waits for them, and re-layouts  3.26 us (3%)
    pallas_call x18, Pallas kernels, call(): pl.pallas_call(with_token, out_shape=list(out_shape) + [token], grid_spec...  79.9 us
    ppermute x11, waiting for transfers between devices, partner(): return lax.ppermute(x, 'outp', [(d, d ^ 1 << bit) for d in range(n)])  25.5 us
    ppermute x11, starting transfers between devices, partner(): return lax.ppermute(x, 'outp', [(d, d ^ 1 << bit) for d in range(n)])  14.4 us
  transfers between devices with their start and end apart: 17, of which 5 were waited for; matrix products, arithmetic and copies ran while one was open for 0% of the time, Pallas kernels for 63%

profile of v9, /device:TPU:0, one launch (start us, length us, event | category | flops | bytes accessed | tf_op | source)
XLA Modules:
  0.0 126.1 jit_solution(8293288520238851828)
XLA Ops:
  1.1 2.6 %collective-permute-start.1 = (bf16[64,4096]{1,0:T(8,128)(2,1)}, bf16[64,4096]{1,0:T(8,128)(2,1)S(1)}, u32[]{:S(2)}, u32[]{:S(2)}) collective-permute-start(bf16[64,4096]{1,0:T(8,128)(2,1)} %refs_0_.5), channel_id=1, source_target_pairs={{0,2},{2,0},{4,6},{6,4},{8,10},{10,8},{12,14},{14,12},{1,3},{3,1},... | collective-permute-start | bytes 1572872 | tf_op jit(solution)/shard_map/ppermute | solution.py:509
  3.7 2.6 %collective-permute-start = (bf16[64,4096]{1,0:T(8,128)(2,1)}, bf16[64,4096]{1,0:T(8,128)(2,1)S(1)}, u32[]{:S(2)}, u32[]{:S(2)}) collective-permute-start(bf16[64,4096]{1,0:T(8,128)(2,1)} %refs_0_.5), channel_id=1, source_target_pairs={{0,8},{2,10},{4,12},{6,14},{8,0},{10,2},{12,4},{14,6},{1,9},{3,11}... | collective-permute-start | bytes 1572872 | tf_op jit(solution)/shard_map/ppermute | solution.py:509
  6.4 1.5 %copy-done = bf16[256,3584]{1,0:T(8,128)(2,1)S(1)} copy-done((bf16[256,3584]{1,0:T(8,128)(2,1)S(1)}, bf16[256,3584]{1,0:T(8,128)(2,1)}, u32[]{:S(2)}) %copy-start) | copy-done | bytes 1835032
  8.9 14.3 %backward_0.1 = (bf16[272,2176]{1,0:T(8,128)(2,1)S(1)}, f32[4,4,64,512]{3,2,1,0:T(8,128)S(1)}, f32[128,128]{1,0:T(8,128)S(1)}, f32[8,128]{1,0:T(8,128)S(1)}) custom-call(s32[2]{0:T(128)S(1)} %pad_add_fusion.idx, bf16[256,3584]{1,0:T(8,128)(2,1)S(1)} %copy-done, bf16[256,3584]{1,0:T(8,128)(2,1)S(1)} %collective-permute-done.2.refs_1_, ...), custom_call_target="tpu_custom_call" | custom-call | flops 19000000512 | bytes 20971520 | tf_op jit(solution)/shard_map/backward_0/pallas_call | solution.py:54
  24.5 1.6 %collective-permute-start.3 = (bf16[64,4096]{1,0:T(8,128)(2,1)S(1)}, bf16[64,4096]{1,0:T(8,128)(2,1)S(1)}, u32[]{:S(2)}, u32[]{:S(2)}) collective-permute-start(bf16[64,4096]{1,0:T(8,128)(2,1)S(1)} %copy-done.1), channel_id=1, source_target_pairs={{0,4},{2,6},{4,0},{6,2},{8,12},{10,14},{12,8},{14,10},{1,5},{3,7},... | collective-permute-start | bytes 1572872 | tf_op jit(solution)/shard_map/ppermute | solution.py:509
  26.1 4.1 %collective-permute-done.refs_0_ = bf16[64,4096]{1,0:T(8,128)(2,1)S(1)} collective-permute-done((bf16[64,4096]{1,0:T(8,128)(2,1)}, bf16[64,4096]{1,0:T(8,128)(2,1)S(1)}, u32[]{:S(2)}, u32[]{:S(2)}) %collective-permute-start) | collective-permute-done | bytes 524320 | tf_op jit(solution)/shard_map/ppermute | solution.py:509
  31.5 13.4 %backward_4.1 = (bf16[256,2176]{1,0:T(8,128)(2,1)S(1)}, f32[4,4,64,512]{3,2,1,0:T(8,128)S(1)}, f32[8,128]{1,0:T(8,128)S(1)}) custom-call(s32[2]{0:T(128)S(1)} %pad_add_fusion.idx, bf16[256,3584]{1,0:T(8,128)(2,1)S(1)} %copy-done, bf16[256,3584]{1,0:T(8,128)(2,1)S(1)} %collective-permute-done.2.refs_1_, bf16[4096,3584]{1,0:T(8,128)(2,1)} %refs_4_.5, ...), custom_call_target="tpu_custom_call" | custom-call | flops 10000000000 | bytes 20971520 | tf_op jit(solution)/shard_map/backward_4/pallas_call | solution.py:54
  44.9 1.4 %collective-permute-start.8 = (bf16[256,2176]{1,0:T(8,128)(2,1)S(1)}, bf16[256,2176]{1,0:T(8,128)(2,1)S(1)}, u32[]{:S(2)}, u32[]{:S(2)}) collective-permute-start(bf16[256,2176]{1,0:T(8,128)(2,1)S(1)} %get-tuple-element.67), channel_id=1, source_target_pairs={{0,4},{2,6},{4,0},{6,2},{8,12},{10,14},{12,8},{14,10},{1,5},{3,7},... | collective-permute-start | bytes 3342344 | tf_op jit(solution)/shard_map/ppermute | solution.py:509
  46.3 6.4 %collective-permute-done.4.refs_2_.refs_3_ = bf16[64,4096]{1,0:T(8,128)(2,1)S(1)} collective-permute-done((bf16[64,4096]{1,0:T(8,128)(2,1)S(1)}, bf16[64,4096]{1,0:T(8,128)(2,1)S(1)}, u32[]{:S(2)}, u32[]{:S(2)}) %collective-permute-start.4) | collective-permute-done | bytes 524320 | tf_op jit(solution)/shard_map/ppermute | solution.py:509
  53.9 2.4 %fold.4 = (bf16[144,2176]{1,0:T(8,128)(2,1)S(1)}, f32[4,2,64,512]{3,2,1,0:T(8,128)S(1)}, f32[128,128]{1,0:T(8,128)S(1)}, f32[8,128]{1,0:T(8,128)S(1)}) custom-call(s32[2]{0:T(128)S(1)} %pad_add_fusion.idx, f32[4,4,64,512]{3,2,1,0:T(8,128)S(1)} %get-tuple-element.59.refs_0_, bf16[272,2176]{1,0:T(8,128)(2,1)S(1)} %collective-permute-done.6.refs_1_, ...), custom_call_target="tpu_custom_call" | custom-call | bytes 6291456 | tf_op jit(solution)/shard_map/fold/pallas_call | solution.py:54
  56.4 15.5 %forward.3 = (f32[128,3584]{1,0:T(8,128)S(1)}, f32[128,3584]{1,0:T(8,128)S(1)}, f32[256,64]{1,0:T(8,128)S(1)}, f32[8,128]{1,0:T(8,128)S(1)}) custom-call(s32[2]{0:T(128)S(1)} %pad_add_fusion.idx, bf16[64,4096]{1,0:T(8,128)(2,1)S(1)} %copy-done.1, bf16[64,4096]{1,0:T(8,128)(2,1)S(1)} %collective-permute-done.3.refs_0_.refs_1_, ...), custom_call_target="tpu_custom_call" | custom-call | flops 17179869184 | bytes 33030144 | tf_op jit(solution)/shard_map/forward/pallas_call | solution.py:54
  72.0 4.6 %collective-permute-done.8.refs_1_ = bf16[256,2176]{1,0:T(8,128)(2,1)S(1)} collective-permute-done((bf16[256,2176]{1,0:T(8,128)(2,1)S(1)}, bf16[256,2176]{1,0:T(8,128)(2,1)S(1)}, u32[]{:S(2)}, u32[]{:S(2)}) %collective-permute-start.8) | collective-permute-done | bytes 1114144 | tf_op jit(solution)/shard_map/ppermute | solution.py:509
  76.5 2.4 %fold.5 = (bf16[128,2176]{1,0:T(8,128)(2,1)S(1)}, f32[4,2,64,512]{3,2,1,0:T(8,128)S(1)}, f32[8,128]{1,0:T(8,128)S(1)}) custom-call(s32[2]{0:T(128)S(1)} %pad_add_fusion.idx, f32[4,4,64,512]{3,2,1,0:T(8,128)S(1)} %get-tuple-element.66.refs_0_, bf16[256,2176]{1,0:T(8,128)(2,1)S(1)} %collective-permute-done.8.refs_1_, f32[8,128]{1,0:T(8,128)S(1)} %get-tuple-element.69.refs_2_), custom_call_target="tpu_custom_call" | custom-call | bytes 6291456 | tf_op jit(solution)/shard_map/fold/pallas_call | solution.py:54
  79.5 10.4 %collective-permute-done.7.refs_1_ = bf16[144,2176]{1,0:T(8,128)(2,1)S(1)} collective-permute-done((bf16[144,2176]{1,0:T(8,128)(2,1)S(1)}, bf16[144,2176]{1,0:T(8,128)(2,1)S(1)}, u32[]{:S(2)}, u32[]{:S(2)}) %collective-permute-start.7) | collective-permute-done | bytes 626720 | tf_op jit(solution)/shard_map/ppermute | solution.py:509
  89.9 1.5 %fold.6 = (bf16[80,2176]{1,0:T(8,128)(2,1)S(1)}, f32[4,1,64,512]{3,2,1,0:T(8,128)S(1)}, f32[128,128]{1,0:T(8,128)S(1)}, f32[8,128]{1,0:T(8,128)S(1)}) custom-call(s32[2]{0:T(128)S(1)} %pad_add_fusion.idx, f32[4,2,64,512]{3,2,1,0:T(8,128)S(1)} %get-tuple-element.63.refs_0_, bf16[144,2176]{1,0:T(8,128)(2,1)S(1)} %collective-permute-done.7.refs_1_, ...), custom_call_target="tpu_custom_call" | custom-call | bytes 3145728 | tf_op jit(solution)/shard_map/fold/pallas_call | solution.py:54
  91.4 1.6 %collective-permute-start.13 = (bf16[80,2176]{1,0:T(8,128)(2,1)S(1)}, bf16[80,2176]{1,0:T(8,128)(2,1)S(1)}, u32[]{:S(2)}, u32[]{:S(2)}) collective-permute-start(bf16[80,2176]{1,0:T(8,128)(2,1)S(1)} %get-tuple-element.87), channel_id=1, source_target_pairs={{0,8},{2,10},{4,12},{6,14},{8,0},{10,2},{12,4},{14,6},{1,9},{3,11}... | collective-permute-start | bytes 1044488 | tf_op jit(solution)/shard_map/ppermute | solution.py:509
  93.5 9.9 %forward.4 = (f32[128,2048]{1,0:T(8,128)S(1)}, f32[128,2048]{1,0:T(8,128)S(1)}, f32[256,64]{1,0:T(8,128)S(1)}, f32[8,128]{1,0:T(8,128)S(1)}) custom-call(s32[2]{0:T(128)S(1)} %pad_add_fusion.idx, bf16[64,4096]{1,0:T(8,128)(2,1)S(1)} %get-tuple-element.54.refs_0_, bf16[192,4096]{1,0:T(8,128)(2,1)S(1)} %get-tuple-element.72.refs_1_.refs_2_.refs_3_, ...), custom_call_target="tpu_custom_call" | custom-call | flops 17179869184 | bytes 18874368 | tf_op jit(solution)/shard_map/forward/pallas_call | solution.py:54
  103.4 1.5 %fold.7 = (bf16[64,2176]{1,0:T(8,128)(2,1)S(1)}, f32[4,1,64,512]{3,2,1,0:T(8,128)S(1)}, f32[8,128]{1,0:T(8,128)S(1)}) custom-call(s32[2]{0:T(128)S(1)} %pad_add_fusion.idx, f32[4,2,64,512]{3,2,1,0:T(8,128)S(1)} %get-tuple-element.75.refs_0_, bf16[128,2176]{1,0:T(8,128)(2,1)S(1)} %collective-permute-done.10.refs_1_, f32[8,128]{1,0:T(8,128)S(1)} %get-tuple-element.78.refs_2_), custom_call_target="tpu_custom_call" | custom-call | bytes 3145728 | tf_op jit(solution)/shard_map/fold/pallas_call | solution.py:54
  104.9 1.4 %collective-permute-start.14 = (bf16[64,2176]{1,0:T(8,128)(2,1)S(1)}, bf16[64,2176]{1,0:T(8,128)(2,1)S(1)}, u32[]{:S(2)}, u32[]{:S(2)}) collective-permute-start(bf16[64,2176]{1,0:T(8,128)(2,1)S(1)} %get-tuple-element.95), channel_id=1, source_target_pairs={{0,8},{2,10},{4,12},{6,14},{8,0},{10,2},{12,4},{14,6},{1,9},{3,11}... | collective-permute-start | bytes 835592 | tf_op jit(solution)/shard_map/ppermute | solution.py:509
  106.4 1.8 %combine.3 = (bf16[256,3584]{1,0:T(8,128)(2,1)}, f32[8,128]{1,0:T(8,128)S(1)}) custom-call(s32[2]{0:T(128)S(1)} %pad_add_fusion.idx, f32[128,3584]{1,0:T(8,128)S(1)} %get-tuple-element.73.refs_0_, f32[128,3584]{1,0:T(8,128)S(1)} %collective-permute-done.9.refs_1_, f32[8,128]{1,0:T(8,128)S(1)} %get-tuple-element.79.refs_2_), custom_call_target="tpu_custom_call" | custom-call | flops 17179869184 | bytes 4587520 | tf_op jit(solution)/shard_map/combine/pallas_call | solution.py:54
  108.2 9.0 %forward.5 = (f32[128,1536]{1,0:T(8,128)S(1)}, f32[128,1536]{1,0:T(8,128)S(1)}, f32[256,64]{1,0:T(8,128)}, f32[8,128]{1,0:T(8,128)S(1)}) custom-call(s32[2]{0:T(128)S(1)} %pad_add_fusion.idx, bf16[64,4096]{1,0:T(8,128)(2,1)S(1)} %get-tuple-element.54.refs_0_, bf16[192,4096]{1,0:T(8,128)(2,1)S(1)} %get-tuple-element.72.refs_1_.refs_2_.refs_3_, ...), custom_call_target="tpu_custom_call" | custom-call | flops 17179869184 | bytes 14155776 | tf_op jit(solution)/shard_map/forward/pallas_call | solution.py:54
  118.4 1.5 %combine.4 = (bf16[256,3584]{1,0:T(8,128)(2,1)}, f32[8,128]{1,0:T(8,128)S(1)}) custom-call(s32[2]{0:T(128)S(1)} %pad_add_fusion.idx, f32[128,2048]{1,0:T(8,128)S(1)} %get-tuple-element.83.refs_0_, f32[128,2048]{1,0:T(8,128)S(1)} %collective-permute-done.12.refs_1_, bf16[256,3584]{1,0:T(8,128)(2,1)} %get-tuple-element.85.refs_2_, ...), custom_call_target="tpu_custom_call", output_to_operand_aliasing={{0}: (3, {})} | custom-call | flops 17179869184 | bytes 2621440 | tf_op jit(solution)/shard_map/combine/pallas_call | solution.py:54
  120.6 1.4 %combine.5 = (bf16[256,3584]{1,0:T(8,128)(2,1)}, f32[8,128]{1,0:T(8,128)S(1)}) custom-call(s32[2]{0:T(128)S(1)} %pad_add_fusion.idx, f32[128,1536]{1,0:T(8,128)S(1)} %get-tuple-element.81.refs_0_, f32[128,1536]{1,0:T(8,128)S(1)} %collective-permute-done.11.refs_1_, bf16[256,3584]{1,0:T(8,128)(2,1)} %get-tuple-element.90.refs_2_, ...), custom_call_target="tpu_custom_call", output_to_operand_aliasing={{0}: (3, {})} | custom-call | flops 17179869184 | bytes 1966080 | tf_op jit(solution)/shard_map/combine/pallas_call | solution.py:54
  123.2 2.1 %finish.1 = (bf16[64,4096]{1,0:T(8,128)(2,1)}, f32[8,128]{1,0:T(8,128)}) custom-call(s32[2]{0:T(128)S(1)} %pad_add_fusion.idx, f32[4,1,64,512]{3,2,1,0:T(8,128)S(1)} %get-tuple-element.93.refs_0_, f32[4,1,64,512]{3,2,1,0:T(8,128)S(1)} %get-tuple-element.94.refs_1_, bf16[80,2176]{1,0:T(8,128)(2,1)S(1)} %collective-permute-done.13.refs_1_.refs_2_, ...), custom_call_target="tpu_custom_call" | custom-call | bytes 2097152 | tf_op jit(solution)/shard_map/finish/pallas_call | solution.py:54
  (39 shorter events, 10.5 us)
Async XLA Ops:
  0.6 5.8 %collective-permute-start.2 = (bf16[256,3584]{1,0:T(8,128)(2,1)}, bf16[256,3584]{1,0:T(8,128)(2,1)S(1)}, u32[]{:S(2)}, u32[]{:S(2)}) collective-permute-start(bf16[256,3584]{1,0:T(8,128)(2,1)} %refs_0_.4), channel_id=1, source_target_pairs={{0,1},{1,0},{2,3},{3,2},{4,5},{5,4},{6,7},{7,6},{8,9},{9,8},{10,11... | collective-permute-start | bytes 5505032 | tf_op jit(solution)/shard_map/ppermute | solution.py:512
  1.1 25.0 %collective-permute-start.1 = (bf16[64,4096]{1,0:T(8,128)(2,1)}, bf16[64,4096]{1,0:T(8,128)(2,1)S(1)}, u32[]{:S(2)}, u32[]{:S(2)}) collective-permute-start(bf16[64,4096]{1,0:T(8,128)(2,1)} %refs_0_.5), channel_id=1, source_target_pairs={{0,2},{2,0},{4,6},{6,4},{8,10},{10,8},{12,14},{14,12},{1,3},{3,1},... | collective-permute-start | bytes 1572872 | tf_op jit(solution)/shard_map/ppermute | solution.py:509
  3.7 26.5 %collective-permute-start = (bf16[64,4096]{1,0:T(8,128)(2,1)}, bf16[64,4096]{1,0:T(8,128)(2,1)S(1)}, u32[]{:S(2)}, u32[]{:S(2)}) collective-permute-start(bf16[64,4096]{1,0:T(8,128)(2,1)} %refs_0_.5), channel_id=1, source_target_pairs={{0,8},{2,10},{4,12},{6,14},{8,0},{10,2},{12,4},{14,6},{1,9},{3,11}... | collective-permute-start | bytes 1572872 | tf_op jit(solution)/shard_map/ppermute | solution.py:509
  6.4 1.5 %copy-start = (bf16[256,3584]{1,0:T(8,128)(2,1)S(1)}, bf16[256,3584]{1,0:T(8,128)(2,1)}, u32[]{:S(2)}) copy-start(bf16[256,3584]{1,0:T(8,128)(2,1)} %refs_0_.4) | copy-start | bytes 5505028
  7.9 1.0 copy-start.3
  8.9 15.6 %copy-start.1 = (bf16[64,4096]{1,0:T(8,128)(2,1)S(1)}, bf16[64,4096]{1,0:T(8,128)(2,1)}, u32[]{:S(2)}) copy-start(bf16[64,4096]{1,0:T(8,128)(2,1)} %refs_0_.5) | copy-start | bytes 1572868
  23.2 30.7 %collective-permute-start.6 = (bf16[272,2176]{1,0:T(8,128)(2,1)S(1)}, bf16[272,2176]{1,0:T(8,128)(2,1)S(1)}, u32[]{:S(2)}, u32[]{:S(2)}) collective-permute-start(bf16[272,2176]{1,0:T(8,128)(2,1)S(1)} %get-tuple-element.60), channel_id=1, source_target_pairs={{0,2},{2,0},{4,6},{6,4},{8,10},{10,8},{12,14},{14,12},{1,3},{3,1},... | collective-permute-start | bytes 3551240 | tf_op jit(solution)/shard_map/ppermute | solution.py:509
  24.5 21.8 %collective-permute-start.3 = (bf16[64,4096]{1,0:T(8,128)(2,1)S(1)}, bf16[64,4096]{1,0:T(8,128)(2,1)S(1)}, u32[]{:S(2)}, u32[]{:S(2)}) collective-permute-start(bf16[64,4096]{1,0:T(8,128)(2,1)S(1)} %copy-done.1), channel_id=1, source_target_pairs={{0,4},{2,6},{4,0},{6,2},{8,12},{10,14},{12,8},{14,10},{1,5},{3,7},... | collective-permute-start | bytes 1572872 | tf_op jit(solution)/shard_map/ppermute | solution.py:509
  30.8 21.9 %collective-permute-start.4 = (bf16[64,4096]{1,0:T(8,128)(2,1)S(1)}, bf16[64,4096]{1,0:T(8,128)(2,1)S(1)}, u32[]{:S(2)}, u32[]{:S(2)}) collective-permute-start(bf16[64,4096]{1,0:T(8,128)(2,1)S(1)} %get-tuple-element.55.refs_1_.refs_2_), channel_id=1, source_target_pairs={{0,4},{2,6},{4,0},{6,2},{8,12},{10,14},{12,8},{14,10},{1,5},{3,7},... | collective-permute-start | bytes 1572872 | tf_op jit(solution)/shard_map/ppermute | solution.py:509
  44.9 31.6 %collective-permute-start.8 = (bf16[256,2176]{1,0:T(8,128)(2,1)S(1)}, bf16[256,2176]{1,0:T(8,128)(2,1)S(1)}, u32[]{:S(2)}, u32[]{:S(2)}) collective-permute-start(bf16[256,2176]{1,0:T(8,128)(2,1)S(1)} %get-tuple-element.67), channel_id=1, source_target_pairs={{0,4},{2,6},{4,0},{6,2},{8,12},{10,14},{12,8},{14,10},{1,5},{3,7},... | collective-permute-start | bytes 3342344 | tf_op jit(solution)/shard_map/ppermute | solution.py:509
  53.3 3.0 %copy-start.2 = (bf16[64,4096]{1,0:T(8,128)(2,1)S(1)}, bf16[64,4096]{1,0:T(8,128)(2,1)}, u32[]{:S(2)}) copy-start(bf16[64,4096]{1,0:T(8,128)(2,1)} %refs_5_.5) | copy-start | bytes 1572868
  53.4 39.6 %collective-permute-start.5 = (bf16[192,4096]{1,0:T(8,128)(2,1)S(1)}, bf16[192,4096]{1,0:T(8,128)(2,1)S(1)}, u32[]{:S(2)}, u32[]{:S(2)}) collective-permute-start(bf16[192,4096]{1,0:T(8,128)(2,1)S(1)} %get-tuple-element.58), channel_id=1, source_target_pairs={{0,2},{2,0},{4,6},{6,4},{8,10},{10,8},{12,14},{14,12},{1,3},{3,1},... | collective-permute-start | bytes 4718600 | tf_op jit(solution)/shard_map/ppermute | solution.py:509
  56.3 33.6 %collective-permute-start.7 = (bf16[144,2176]{1,0:T(8,128)(2,1)S(1)}, bf16[144,2176]{1,0:T(8,128)(2,1)S(1)}, u32[]{:S(2)}, u32[]{:S(2)}) collective-permute-start(bf16[144,2176]{1,0:T(8,128)(2,1)S(1)} %get-tuple-element.64), channel_id=1, source_target_pairs={{0,4},{2,6},{4,0},{6,2},{8,12},{10,14},{12,8},{14,10},{1,5},{3,7},... | collective-permute-start | bytes 1880072 | tf_op jit(solution)/shard_map/ppermute | solution.py:509
  71.9 34.5 %collective-permute-start.9 = (f32[128,3584]{1,0:T(8,128)S(1)}, f32[128,3584]{1,0:T(8,128)S(1)}, u32[]{:S(2)}, u32[]{:S(2)}) collective-permute-start(f32[128,3584]{1,0:T(8,128)S(1)} %get-tuple-element.74), channel_id=1, source_target_pairs={{0,1},{1,0},{2,3},{3,2},{4,5},{5,4},{6,7},{7,6},{8,9},{9,8},{10,11... | collective-permute-start | bytes 5505032 | tf_op jit(solution)/shard_map/ppermute | solution.py:512
  78.9 24.5 %collective-permute-start.10 = (bf16[128,2176]{1,0:T(8,128)(2,1)S(1)}, bf16[128,2176]{1,0:T(8,128)(2,1)S(1)}, u32[]{:S(2)}, u32[]{:S(2)}) collective-permute-start(bf16[128,2176]{1,0:T(8,128)(2,1)S(1)} %get-tuple-element.76), channel_id=1, source_target_pairs={{0,2},{2,0},{4,6},{6,4},{8,10},{10,8},{12,14},{14,12},{1,3},{3,1},... | collective-permute-start | bytes 1671176 | tf_op jit(solution)/shard_map/ppermute | solution.py:509
  91.4 25.8 %collective-permute-start.13 = (bf16[80,2176]{1,0:T(8,128)(2,1)S(1)}, bf16[80,2176]{1,0:T(8,128)(2,1)S(1)}, u32[]{:S(2)}, u32[]{:S(2)}) collective-permute-start(bf16[80,2176]{1,0:T(8,128)(2,1)S(1)} %get-tuple-element.87), channel_id=1, source_target_pairs={{0,8},{2,10},{4,12},{6,14},{8,0},{10,2},{12,4},{14,6},{1,9},{3,11}... | collective-permute-start | bytes 1044488 | tf_op jit(solution)/shard_map/ppermute | solution.py:509
  104.9 18.3 %collective-permute-start.14 = (bf16[64,2176]{1,0:T(8,128)(2,1)S(1)}, bf16[64,2176]{1,0:T(8,128)(2,1)S(1)}, u32[]{:S(2)}, u32[]{:S(2)}) collective-permute-start(bf16[64,2176]{1,0:T(8,128)(2,1)S(1)} %get-tuple-element.95), channel_id=1, source_target_pairs={{0,8},{2,10},{4,12},{6,14},{8,0},{10,2},{12,4},{14,6},{1,9},{3,11}... | collective-permute-start | bytes 835592 | tf_op jit(solution)/shard_map/ppermute | solution.py:509
  106.4 12.1 %collective-permute-start.12 = (f32[128,2048]{1,0:T(8,128)S(1)}, f32[128,2048]{1,0:T(8,128)S(1)}, u32[]{:S(2)}, u32[]{:S(2)}) collective-permute-start(f32[128,2048]{1,0:T(8,128)S(1)} %get-tuple-element.84), channel_id=1, source_target_pairs={{0,1},{1,0},{2,3},{3,2},{4,5},{5,4},{6,7},{7,6},{8,9},{9,8},{10,11... | collective-permute-start | bytes 3145736 | tf_op jit(solution)/shard_map/ppermute | solution.py:512
  117.8 4.2 %collective-permute-start.15 = (f32[128,128]{1,0:T(8,128)S(1)}, f32[128,128]{1,0:T(8,128)S(1)}, u32[]{:S(2)}, u32[]{:S(2)}) collective-permute-start(f32[128,128]{1,0:T(8,128)S(1)} %get-tuple-element.98.refs_2_), channel_id=1, source_target_pairs={{0,1},{1,0},{2,3},{3,2},{4,5},{5,4},{6,7},{7,6},{8,9},{9,8},{10,11... | collective-permute-start | bytes 196616 | tf_op jit(solution)/shard_map/ppermute | solution.py:512
  118.3 2.3 %collective-permute-start.11 = (f32[128,1536]{1,0:T(8,128)S(1)}, f32[128,1536]{1,0:T(8,128)S(1)}, u32[]{:S(2)}, u32[]{:S(2)}) collective-permute-start(f32[128,1536]{1,0:T(8,128)S(1)} %get-tuple-element.82), channel_id=1, source_target_pairs={{0,1},{1,0},{2,3},{3,2},{4,5},{5,4},{6,7},{7,6},{8,9},{9,8},{10,11... | collective-permute-start | bytes 2359304 | tf_op jit(solution)/shard_map/ppermute | solution.py:512
  123.0 2.3 %collective-permute-start.16 = (f32[4,64,64]{2,1,0:T(8,128)S(1)}, f32[4,64,64]{2,1,0:T(8,128)S(1)}, u32[]{:S(2)}, u32[]{:S(2)}) collective-permute-start(f32[4,64,64]{2,1,0:T(8,128)S(1)} %get-tuple-element.102), channel_id=1, source_target_pairs={{0,1},{1,0},{2,3},{3,2},{4,5},{5,4},{6,7},{7,6},{8,9},{9,8},{10,11... | collective-permute-start | bytes 196616 | tf_op jit(solution)/shard_map/ppermute | solution.py:512

commit v10 on v9

--- a/solution.py
+++ b/solution.py
@@ -512,7 +512,6 @@
         return lax.ppermute(x, "inp", [(0, 1), (1, 0)])
 
     evens = list(range(2, n, 2))
-    far = n // 2
     chunks = {0: inputs}
 
     def fetch(masks):
@@ -526,7 +525,8 @@
         return token
 
     grad_other = swap(cotangent)
-    fetch([far, 1])
+    singles = [1 << k for k in reversed(range(bits))]
+    fetch(singles)
 
     orders = [list(range(bits)), [1, 0] + list(range(2, bits))]
     tile = pick(feats // PIECES, F_TILE)
@@ -553,8 +553,8 @@
         if p == 0:
             right = outs[2]
         if p == 0:
-            token = hold([far, 1], token)
-            fetch([m for m in evens if m != far and (m & ~far).bit_count() == 1][::-1])
+            token = hold(singles, token)
+            fetch([m for m in evens if m.bit_count() == 2])
     ready = [m for m in evens if m in chunks]
     while len(ready) < len(evens):
         token = hold(ready, token)
@@ -590,7 +590,6 @@
     first, left1, token = batch_forward(0, 0, tiles, token)
     token = folded(1, 1, token)
     token = folded(0, 2, token)
-    (crossed,), token = gate(idx, [crossed], token)
     second, left2, token = batch_forward(1, 0, cut, token)
     token = folded(1, 2, token)
     outputs, token = combine(idx, *first, [], token)

time: 127 us -> 121 us (0.953)
  waiting for transfers between devices: 26.2 us -> 19 us
  starting transfers between devices: 15.9 us -> 18.2 us
    ppermute x11, waiting for transfers between devices: 25.5 us -> 18.2 us  [partner(): return lax.ppermute(x, 'outp', [(d, d ^ 1 << bit) for d in range(n)])]
    ppermute x11, starting transfers between devices: 14.4 us -> 16.8 us  [partner(): return lax.ppermute(x, 'outp', [(d, d ^ 1 << bit) for d in range(n)])]
    pallas_call x18 -> x17, Pallas kernels: 79.9 us -> 79.3 us  [call(): pl.pallas_call(with_token, out_shape=list(out_shape) + [token], grid_spec...]
  transfers between devices with their start and end apart: 17 -> 17, of which waited for: 5 -> 6; matrix products, arithmetic and copies ran while one was open for 0% -> 0% of each run, Pallas kernels for 63% -> 66%
where the time goes in v10:
time: 121 us
  Pallas kernels  79.3 us (66%)
  waiting for transfers between devices  19 us (16%)
  starting transfers between devices  18.2 us (15%)
  local copies, waits for them, and re-layouts  3.27 us (3%)
    pallas_call x17, Pallas kernels, call(): pl.pallas_call(with_token, out_shape=list(out_shape) + [token], grid_spec...  79.3 us
    ppermute x11, waiting for transfers between devices, partner(): return lax.ppermute(x, 'outp', [(d, d ^ 1 << bit) for d in range(n)])  18.2 us
    ppermute x11, starting transfers between devices, partner(): return lax.ppermute(x, 'outp', [(d, d ^ 1 << bit) for d in range(n)])  16.8 us
    unnamed x8, local copies, waits for them, and re-layouts  2.53 us
  transfers between devices with their start and end apart: 17, of which 6 were waited for; matrix products, arithmetic and copies ran while one was open for 0% of the time, Pallas kernels for 66%

profile of v10, /device:TPU:0, one launch (start us, length us, event | category | flops | bytes accessed | tf_op | source)
XLA Modules:
  0.0 120.7 jit_solution(16886525312758122218)
XLA Ops:
  1.1 2.7 %collective-permute-start.1 = (bf16[64,4096]{1,0:T(8,128)(2,1)}, bf16[64,4096]{1,0:T(8,128)(2,1)S(1)}, u32[]{:S(2)}, u32[]{:S(2)}) collective-permute-start(bf16[64,4096]{1,0:T(8,128)(2,1)} %refs_0_.5), channel_id=1, source_target_pairs={{0,4},{2,6},{4,0},{6,2},{8,12},{10,14},{12,8},{14,10},{1,5},{3,7},... | collective-permute-start | bytes 1572872 | tf_op jit(solution)/shard_map/ppermute | solution.py:509
  3.8 2.6 %collective-permute-start = (bf16[64,4096]{1,0:T(8,128)(2,1)}, bf16[64,4096]{1,0:T(8,128)(2,1)S(1)}, u32[]{:S(2)}, u32[]{:S(2)}) collective-permute-start(bf16[64,4096]{1,0:T(8,128)(2,1)} %refs_0_.5), channel_id=1, source_target_pairs={{0,8},{2,10},{4,12},{6,14},{8,0},{10,2},{12,4},{14,6},{1,9},{3,11}... | collective-permute-start | bytes 1572872 | tf_op jit(solution)/shard_map/ppermute | solution.py:509
  6.4 1.5 %collective-permute-start.2 = (bf16[64,4096]{1,0:T(8,128)(2,1)}, bf16[64,4096]{1,0:T(8,128)(2,1)S(1)}, u32[]{:S(2)}, u32[]{:S(2)}) collective-permute-start(bf16[64,4096]{1,0:T(8,128)(2,1)} %refs_0_.5), channel_id=1, source_target_pairs={{0,2},{2,0},{4,6},{6,4},{8,10},{10,8},{12,14},{14,12},{1,3},{3,1},... | collective-permute-start | bytes 1572872 | tf_op jit(solution)/shard_map/ppermute | solution.py:509
  8.0 1.5 %copy-done = bf16[256,3584]{1,0:T(8,128)(2,1)S(1)} copy-done((bf16[256,3584]{1,0:T(8,128)(2,1)S(1)}, bf16[256,3584]{1,0:T(8,128)(2,1)}, u32[]{:S(2)}) %copy-start) | copy-done | bytes 1835032
  10.5 14.3 %backward_0.1 = (bf16[272,2176]{1,0:T(8,128)(2,1)S(1)}, f32[4,4,64,512]{3,2,1,0:T(8,128)S(1)}, f32[128,128]{1,0:T(8,128)S(1)}, f32[8,128]{1,0:T(8,128)S(1)}) custom-call(s32[2]{0:T(128)S(1)} %pad_add_fusion.idx, bf16[256,3584]{1,0:T(8,128)(2,1)S(1)} %copy-done, bf16[256,3584]{1,0:T(8,128)(2,1)S(1)} %collective-permute-done.3.refs_1_, ...), custom_call_target="tpu_custom_call" | custom-call | flops 19000000512 | bytes 20971520 | tf_op jit(solution)/shard_map/backward_0/pallas_call | solution.py:54
  25.4 2.3 %collective-permute-done.1.refs_1_ = bf16[64,4096]{1,0:T(8,128)(2,1)S(1)} collective-permute-done((bf16[64,4096]{1,0:T(8,128)(2,1)}, bf16[64,4096]{1,0:T(8,128)(2,1)S(1)}, u32[]{:S(2)}, u32[]{:S(2)}) %collective-permute-start.1) | collective-permute-done | bytes 524320 | tf_op jit(solution)/shard_map/ppermute | solution.py:509
  27.6 2.6 %collective-permute-done.refs_0_ = bf16[64,4096]{1,0:T(8,128)(2,1)S(1)} collective-permute-done((bf16[64,4096]{1,0:T(8,128)(2,1)}, bf16[64,4096]{1,0:T(8,128)(2,1)S(1)}, u32[]{:S(2)}, u32[]{:S(2)}) %collective-permute-start) | collective-permute-done | bytes 524320 | tf_op jit(solution)/shard_map/ppermute | solution.py:509
  31.3 13.4 %backward_4.1 = (bf16[256,2176]{1,0:T(8,128)(2,1)S(1)}, f32[4,4,64,512]{3,2,1,0:T(8,128)S(1)}, f32[8,128]{1,0:T(8,128)S(1)}) custom-call(s32[2]{0:T(128)S(1)} %pad_add_fusion.idx, bf16[256,3584]{1,0:T(8,128)(2,1)S(1)} %copy-done, bf16[256,3584]{1,0:T(8,128)(2,1)S(1)} %collective-permute-done.3.refs_1_, bf16[4096,3584]{1,0:T(8,128)(2,1)} %refs_4_.5, ...), custom_call_target="tpu_custom_call" | custom-call | flops 10000000000 | bytes 20971520 | tf_op jit(solution)/shard_map/backward_4/pallas_call | solution.py:54
  44.6 1.7 %collective-permute-start.8 = (bf16[256,2176]{1,0:T(8,128)(2,1)S(1)}, bf16[256,2176]{1,0:T(8,128)(2,1)S(1)}, u32[]{:S(2)}, u32[]{:S(2)}) collective-permute-start(bf16[256,2176]{1,0:T(8,128)(2,1)S(1)} %get-tuple-element.67), channel_id=1, source_target_pairs={{0,4},{2,6},{4,0},{6,2},{8,12},{10,14},{12,8},{14,10},{1,5},{3,7},... | collective-permute-start | bytes 3342344 | tf_op jit(solution)/shard_map/ppermute | solution.py:509
  47.0 1.6 %collective-permute-start.5 = (bf16[192,4096]{1,0:T(8,128)(2,1)S(1)}, bf16[192,4096]{1,0:T(8,128)(2,1)S(1)}, u32[]{:S(2)}, u32[]{:S(2)}) collective-permute-start(bf16[192,4096]{1,0:T(8,128)(2,1)S(1)} %get-tuple-element.58), channel_id=1, source_target_pairs={{0,2},{2,0},{4,6},{6,4},{8,10},{10,8},{12,14},{14,12},{1,3},{3,1},... | collective-permute-start | bytes 4718600 | tf_op jit(solution)/shard_map/ppermute | solution.py:509
  48.6 5.2 %collective-permute-done.6.refs_1_ = bf16[272,2176]{1,0:T(8,128)(2,1)S(1)} collective-permute-done((bf16[272,2176]{1,0:T(8,128)(2,1)S(1)}, bf16[272,2176]{1,0:T(8,128)(2,1)S(1)}, u32[]{:S(2)}, u32[]{:S(2)}) %collective-permute-start.6) | collective-permute-done | bytes 1183776 | tf_op jit(solution)/shard_map/ppermute | solution.py:509
  53.8 2.4 %fold.4 = (bf16[144,2176]{1,0:T(8,128)(2,1)S(1)}, f32[4,2,64,512]{3,2,1,0:T(8,128)S(1)}, f32[128,128]{1,0:T(8,128)S(1)}, f32[8,128]{1,0:T(8,128)S(1)}) custom-call(s32[2]{0:T(128)S(1)} %pad_add_fusion.idx, f32[4,4,64,512]{3,2,1,0:T(8,128)S(1)} %get-tuple-element.59.refs_0_, bf16[272,2176]{1,0:T(8,128)(2,1)S(1)} %collective-permute-done.6.refs_1_, ...), custom_call_target="tpu_custom_call" | custom-call | bytes 6291456 | tf_op jit(solution)/shard_map/fold/pallas_call | solution.py:54
  56.8 15.5 %forward.3 = (f32[128,3584]{1,0:T(8,128)S(1)}, f32[128,3584]{1,0:T(8,128)S(1)}, f32[256,64]{1,0:T(8,128)S(1)}, f32[8,128]{1,0:T(8,128)S(1)}) custom-call(s32[2]{0:T(128)S(1)} %pad_add_fusion.idx, bf16[64,4096]{1,0:T(8,128)(2,1)S(1)} %copy-done.1, bf16[64,4096]{1,0:T(8,128)(2,1)S(1)} %get-tuple-element.54.refs_0_.refs_1_, ...), custom_call_target="tpu_custom_call" | custom-call | flops 17179869184 | bytes 33030144 | tf_op jit(solution)/shard_map/forward/pallas_call | solution.py:54
  72.3 2.4 %fold.5 = (bf16[128,2176]{1,0:T(8,128)(2,1)S(1)}, f32[4,2,64,512]{3,2,1,0:T(8,128)S(1)}, f32[8,128]{1,0:T(8,128)S(1)}) custom-call(s32[2]{0:T(128)S(1)} %pad_add_fusion.idx, f32[4,4,64,512]{3,2,1,0:T(8,128)S(1)} %get-tuple-element.66.refs_0_, bf16[256,2176]{1,0:T(8,128)(2,1)S(1)} %collective-permute-done.8.refs_1_, f32[8,128]{1,0:T(8,128)S(1)} %get-tuple-element.68.refs_2_), custom_call_target="tpu_custom_call" | custom-call | bytes 6291456 | tf_op jit(solution)/shard_map/fold/pallas_call | solution.py:54
  74.7 1.5 %collective-permute-start.9 = (bf16[128,2176]{1,0:T(8,128)(2,1)S(1)}, bf16[128,2176]{1,0:T(8,128)(2,1)S(1)}, u32[]{:S(2)}, u32[]{:S(2)}) collective-permute-start(bf16[128,2176]{1,0:T(8,128)(2,1)S(1)} %get-tuple-element.70), channel_id=1, source_target_pairs={{0,2},{2,0},{4,6},{6,4},{8,10},{10,8},{12,14},{14,12},{1,3},{3,1},... | collective-permute-start | bytes 1671176 | tf_op jit(solution)/shard_map/ppermute | solution.py:509
  76.2 7.7 %collective-permute-done.10.refs_1_ = bf16[144,2176]{1,0:T(8,128)(2,1)S(1)} collective-permute-done((bf16[144,2176]{1,0:T(8,128)(2,1)S(1)}, bf16[144,2176]{1,0:T(8,128)(2,1)S(1)}, u32[]{:S(2)}, u32[]{:S(2)}) %collective-permute-start.10) | collective-permute-done | bytes 626720 | tf_op jit(solution)/shard_map/ppermute | solution.py:509
  83.9 1.5 %fold.6 = (bf16[80,2176]{1,0:T(8,128)(2,1)S(1)}, f32[4,1,64,512]{3,2,1,0:T(8,128)S(1)}, f32[128,128]{1,0:T(8,128)S(1)}, f32[8,128]{1,0:T(8,128)S(1)}) custom-call(s32[2]{0:T(128)S(1)} %pad_add_fusion.idx, f32[4,2,64,512]{3,2,1,0:T(8,128)S(1)} %get-tuple-element.71.refs_0_, bf16[144,2176]{1,0:T(8,128)(2,1)S(1)} %collective-permute-done.10.refs_1_, ...), custom_call_target="tpu_custom_call" | custom-call | bytes 3145728 | tf_op jit(solution)/shard_map/fold/pallas_call | solution.py:54
  85.4 2.4 %collective-permute-start.13 = (bf16[80,2176]{1,0:T(8,128)(2,1)S(1)}, bf16[80,2176]{1,0:T(8,128)(2,1)S(1)}, u32[]{:S(2)}, u32[]{:S(2)}) collective-permute-start(bf16[80,2176]{1,0:T(8,128)(2,1)S(1)} %get-tuple-element.85), channel_id=1, source_target_pairs={{0,8},{2,10},{4,12},{6,14},{8,0},{10,2},{12,4},{14,6},{1,9},{3,11}... | collective-permute-start | bytes 1044488 | tf_op jit(solution)/shard_map/ppermute | solution.py:509
  87.8 9.9 %forward.4 = (f32[128,2048]{1,0:T(8,128)S(1)}, f32[128,2048]{1,0:T(8,128)S(1)}, f32[256,64]{1,0:T(8,128)S(1)}, f32[8,128]{1,0:T(8,128)S(1)}) custom-call(s32[2]{0:T(128)S(1)} %pad_add_fusion.idx, bf16[64,4096]{1,0:T(8,128)(2,1)S(1)} %get-tuple-element.53.refs_0_, bf16[192,4096]{1,0:T(8,128)(2,1)S(1)} %collective-permute-done.5.refs_1_.refs_2_.refs_3_, ...), custom_call_target="tpu_custom_call" | custom-call | flops 17179869184 | bytes 18874368 | tf_op jit(solution)/shard_map/forward/pallas_call | solution.py:54
  98.1 1.5 %fold.7 = (bf16[64,2176]{1,0:T(8,128)(2,1)S(1)}, f32[4,1,64,512]{3,2,1,0:T(8,128)S(1)}, f32[8,128]{1,0:T(8,128)S(1)}) custom-call(s32[2]{0:T(128)S(1)} %pad_add_fusion.idx, f32[4,2,64,512]{3,2,1,0:T(8,128)S(1)} %get-tuple-element.69.refs_0_, bf16[128,2176]{1,0:T(8,128)(2,1)S(1)} %collective-permute-done.9.refs_1_, f32[8,128]{1,0:T(8,128)S(1)} %get-tuple-element.76.refs_2_), custom_call_target="tpu_custom_call" | custom-call | bytes 3145728 | tf_op jit(solution)/shard_map/fold/pallas_call | solution.py:54
  100.9 1.8 %combine.3 = (bf16[256,3584]{1,0:T(8,128)(2,1)}, f32[8,128]{1,0:T(8,128)S(1)}) custom-call(s32[2]{0:T(128)S(1)} %pad_add_fusion.idx, f32[128,3584]{1,0:T(8,128)S(1)} %get-tuple-element.64.refs_0_, f32[128,3584]{1,0:T(8,128)S(1)} %collective-permute-done.7.refs_1_, f32[8,128]{1,0:T(8,128)S(1)} %get-tuple-element.77.refs_2_), custom_call_target="tpu_custom_call" | custom-call | flops 17179869184 | bytes 4587520 | tf_op jit(solution)/shard_map/combine/pallas_call | solution.py:54
  102.7 9.0 %forward.5 = (f32[128,1536]{1,0:T(8,128)S(1)}, f32[128,1536]{1,0:T(8,128)S(1)}, f32[256,64]{1,0:T(8,128)}, f32[8,128]{1,0:T(8,128)S(1)}) custom-call(s32[2]{0:T(128)S(1)} %pad_add_fusion.idx, bf16[64,4096]{1,0:T(8,128)(2,1)S(1)} %get-tuple-element.53.refs_0_, bf16[192,4096]{1,0:T(8,128)(2,1)S(1)} %collective-permute-done.5.refs_1_.refs_2_.refs_3_, ...), custom_call_target="tpu_custom_call" | custom-call | flops 17179869184 | bytes 14155776 | tf_op jit(solution)/shard_map/forward/pallas_call | solution.py:54
  112.9 1.4 %combine.4 = (bf16[256,3584]{1,0:T(8,128)(2,1)}, f32[8,128]{1,0:T(8,128)S(1)}) custom-call(s32[2]{0:T(128)S(1)} %pad_add_fusion.idx, f32[128,2048]{1,0:T(8,128)S(1)} %get-tuple-element.81.refs_0_, f32[128,2048]{1,0:T(8,128)S(1)} %collective-permute-done.12.refs_1_, bf16[256,3584]{1,0:T(8,128)(2,1)} %get-tuple-element.83.refs_2_, ...), custom_call_target="tpu_custom_call", output_to_operand_aliasing={{0}: (3, {})} | custom-call | flops 17179869184 | bytes 2621440 | tf_op jit(solution)/shard_map/combine/pallas_call | solution.py:54
  117.8 2.1 %finish.1 = (bf16[64,4096]{1,0:T(8,128)(2,1)}, f32[8,128]{1,0:T(8,128)}) custom-call(s32[2]{0:T(128)S(1)} %pad_add_fusion.idx, f32[4,1,64,512]{3,2,1,0:T(8,128)S(1)} %get-tuple-element.91.refs_0_, f32[4,1,64,512]{3,2,1,0:T(8,128)S(1)} %get-tuple-element.92.refs_1_, bf16[80,2176]{1,0:T(8,128)(2,1)S(1)} %collective-permute-done.13.refs_1_.refs_2_, ...), custom_call_target="tpu_custom_call" | custom-call | bytes 2097152 | tf_op jit(solution)/shard_map/finish/pallas_call | solution.py:54
  (38 shorter events, 11.6 us)
Async XLA Ops:
  0.6 7.4 %collective-permute-start.3 = (bf16[256,3584]{1,0:T(8,128)(2,1)}, bf16[256,3584]{1,0:T(8,128)(2,1)S(1)}, u32[]{:S(2)}, u32[]{:S(2)}) collective-permute-start(bf16[256,3584]{1,0:T(8,128)(2,1)} %refs_0_.4), channel_id=1, source_target_pairs={{0,1},{1,0},{2,3},{3,2},{4,5},{5,4},{6,7},{7,6},{8,9},{9,8},{10,11... | collective-permute-start | bytes 5505032 | tf_op jit(solution)/shard_map/ppermute | solution.py:512
  1.1 26.5 %collective-permute-start.1 = (bf16[64,4096]{1,0:T(8,128)(2,1)}, bf16[64,4096]{1,0:T(8,128)(2,1)S(1)}, u32[]{:S(2)}, u32[]{:S(2)}) collective-permute-start(bf16[64,4096]{1,0:T(8,128)(2,1)} %refs_0_.5), channel_id=1, source_target_pairs={{0,4},{2,6},{4,0},{6,2},{8,12},{10,14},{12,8},{14,10},{1,5},{3,7},... | collective-permute-start | bytes 1572872 | tf_op jit(solution)/shard_map/ppermute | solution.py:509
  3.8 26.4 %collective-permute-start = (bf16[64,4096]{1,0:T(8,128)(2,1)}, bf16[64,4096]{1,0:T(8,128)(2,1)S(1)}, u32[]{:S(2)}, u32[]{:S(2)}) collective-permute-start(bf16[64,4096]{1,0:T(8,128)(2,1)} %refs_0_.5), channel_id=1, source_target_pairs={{0,8},{2,10},{4,12},{6,14},{8,0},{10,2},{12,4},{14,6},{1,9},{3,11}... | collective-permute-start | bytes 1572872 | tf_op jit(solution)/shard_map/ppermute | solution.py:509
  6.4 23.8 %collective-permute-start.2 = (bf16[64,4096]{1,0:T(8,128)(2,1)}, bf16[64,4096]{1,0:T(8,128)(2,1)S(1)}, u32[]{:S(2)}, u32[]{:S(2)}) collective-permute-start(bf16[64,4096]{1,0:T(8,128)(2,1)} %refs_0_.5), channel_id=1, source_target_pairs={{0,2},{2,0},{4,6},{6,4},{8,10},{10,8},{12,14},{14,12},{1,3},{3,1},... | collective-permute-start | bytes 1572872 | tf_op jit(solution)/shard_map/ppermute | solution.py:509
  8.0 1.5 %copy-start = (bf16[256,3584]{1,0:T(8,128)(2,1)S(1)}, bf16[256,3584]{1,0:T(8,128)(2,1)}, u32[]{:S(2)}) copy-start(bf16[256,3584]{1,0:T(8,128)(2,1)} %refs_0_.4) | copy-start | bytes 5505028
  9.5 1.0 copy-start.3
  24.8 29.0 %collective-permute-start.6 = (bf16[272,2176]{1,0:T(8,128)(2,1)S(1)}, bf16[272,2176]{1,0:T(8,128)(2,1)S(1)}, u32[]{:S(2)}, u32[]{:S(2)}) collective-permute-start(bf16[272,2176]{1,0:T(8,128)(2,1)S(1)} %get-tuple-element.60), channel_id=1, source_target_pairs={{0,2},{2,0},{4,6},{6,4},{8,10},{10,8},{12,14},{14,12},{1,3},{3,1},... | collective-permute-start | bytes 3551240 | tf_op jit(solution)/shard_map/ppermute | solution.py:509
  30.8 15.5 %collective-permute-start.4 = (bf16[64,4096]{1,0:T(8,128)(2,1)S(1)}, bf16[64,4096]{1,0:T(8,128)(2,1)S(1)}, u32[]{:S(2)}, u32[]{:S(2)}) collective-permute-start(bf16[64,4096]{1,0:T(8,128)(2,1)S(1)} %get-tuple-element.55.refs_1_.refs_2_), channel_id=1, source_target_pairs={{0,4},{2,6},{4,0},{6,2},{8,12},{10,14},{12,8},{14,10},{1,5},{3,7},... | collective-permute-start | bytes 1572872 | tf_op jit(solution)/shard_map/ppermute | solution.py:509
  44.6 27.7 %collective-permute-start.8 = (bf16[256,2176]{1,0:T(8,128)(2,1)S(1)}, bf16[256,2176]{1,0:T(8,128)(2,1)S(1)}, u32[]{:S(2)}, u32[]{:S(2)}) collective-permute-start(bf16[256,2176]{1,0:T(8,128)(2,1)S(1)} %get-tuple-element.67), channel_id=1, source_target_pairs={{0,4},{2,6},{4,0},{6,2},{8,12},{10,14},{12,8},{14,10},{1,5},{3,7},... | collective-permute-start | bytes 3342344 | tf_op jit(solution)/shard_map/ppermute | solution.py:509
  47.0 9.8 %copy-start.1 = (bf16[64,4096]{1,0:T(8,128)(2,1)S(1)}, bf16[64,4096]{1,0:T(8,128)(2,1)}, u32[]{:S(2)}) copy-start(bf16[64,4096]{1,0:T(8,128)(2,1)} %refs_0_.5) | copy-start | bytes 1572868
  47.0 9.8 %copy-start.2 = (bf16[64,4096]{1,0:T(8,128)(2,1)S(1)}, bf16[64,4096]{1,0:T(8,128)(2,1)}, u32[]{:S(2)}) copy-start(bf16[64,4096]{1,0:T(8,128)(2,1)} %refs_5_.5) | copy-start | bytes 1572868
  47.0 40.8 %collective-permute-start.5 = (bf16[192,4096]{1,0:T(8,128)(2,1)S(1)}, bf16[192,4096]{1,0:T(8,128)(2,1)S(1)}, u32[]{:S(2)}, u32[]{:S(2)}) collective-permute-start(bf16[192,4096]{1,0:T(8,128)(2,1)S(1)} %get-tuple-element.58), channel_id=1, source_target_pairs={{0,2},{2,0},{4,6},{6,4},{8,10},{10,8},{12,14},{14,12},{1,3},{3,1},... | collective-permute-start | bytes 4718600 | tf_op jit(solution)/shard_map/ppermute | solution.py:509
  56.3 27.7 %collective-permute-start.10 = (bf16[144,2176]{1,0:T(8,128)(2,1)S(1)}, bf16[144,2176]{1,0:T(8,128)(2,1)S(1)}, u32[]{:S(2)}, u32[]{:S(2)}) collective-permute-start(bf16[144,2176]{1,0:T(8,128)(2,1)S(1)} %get-tuple-element.72), channel_id=1, source_target_pairs={{0,4},{2,6},{4,0},{6,2},{8,12},{10,14},{12,8},{14,10},{1,5},{3,7},... | collective-permute-start | bytes 1880072 | tf_op jit(solution)/shard_map/ppermute | solution.py:509
  72.2 28.6 %collective-permute-start.7 = (f32[128,3584]{1,0:T(8,128)S(1)}, f32[128,3584]{1,0:T(8,128)S(1)}, u32[]{:S(2)}, u32[]{:S(2)}) collective-permute-start(f32[128,3584]{1,0:T(8,128)S(1)} %get-tuple-element.65), channel_id=1, source_target_pairs={{0,1},{1,0},{2,3},{3,2},{4,5},{5,4},{6,7},{7,6},{8,9},{9,8},{10,11... | collective-permute-start | bytes 5505032 | tf_op jit(solution)/shard_map/ppermute | solution.py:512
  74.7 23.3 %collective-permute-start.9 = (bf16[128,2176]{1,0:T(8,128)(2,1)S(1)}, bf16[128,2176]{1,0:T(8,128)(2,1)S(1)}, u32[]{:S(2)}, u32[]{:S(2)}) collective-permute-start(bf16[128,2176]{1,0:T(8,128)(2,1)S(1)} %get-tuple-element.70), channel_id=1, source_target_pairs={{0,2},{2,0},{4,6},{6,4},{8,10},{10,8},{12,14},{14,12},{1,3},{3,1},... | collective-permute-start | bytes 1671176 | tf_op jit(solution)/shard_map/ppermute | solution.py:509
  85.4 26.3 %collective-permute-start.13 = (bf16[80,2176]{1,0:T(8,128)(2,1)S(1)}, bf16[80,2176]{1,0:T(8,128)(2,1)S(1)}, u32[]{:S(2)}, u32[]{:S(2)}) collective-permute-start(bf16[80,2176]{1,0:T(8,128)(2,1)S(1)} %get-tuple-element.85), channel_id=1, source_target_pairs={{0,8},{2,10},{4,12},{6,14},{8,0},{10,2},{12,4},{14,6},{1,9},{3,11}... | collective-permute-start | bytes 1044488 | tf_op jit(solution)/shard_map/ppermute | solution.py:509
  99.5 18.3 %collective-permute-start.14 = (bf16[64,2176]{1,0:T(8,128)(2,1)S(1)}, bf16[64,2176]{1,0:T(8,128)(2,1)S(1)}, u32[]{:S(2)}, u32[]{:S(2)}) collective-permute-start(bf16[64,2176]{1,0:T(8,128)(2,1)S(1)} %get-tuple-element.93), channel_id=1, source_target_pairs={{0,8},{2,10},{4,12},{6,14},{8,0},{10,2},{12,4},{14,6},{1,9},{3,11}... | collective-permute-start | bytes 835592 | tf_op jit(solution)/shard_map/ppermute | solution.py:509
  100.9 12.1 %collective-permute-start.12 = (f32[128,2048]{1,0:T(8,128)S(1)}, f32[128,2048]{1,0:T(8,128)S(1)}, u32[]{:S(2)}, u32[]{:S(2)}) collective-permute-start(f32[128,2048]{1,0:T(8,128)S(1)} %get-tuple-element.82), channel_id=1, source_target_pairs={{0,1},{1,0},{2,3},{3,2},{4,5},{5,4},{6,7},{7,6},{8,9},{9,8},{10,11... | collective-permute-start | bytes 3145736 | tf_op jit(solution)/shard_map/ppermute | solution.py:512
  112.3 4.3 %collective-permute-start.15 = (f32[128,128]{1,0:T(8,128)S(1)}, f32[128,128]{1,0:T(8,128)S(1)}, u32[]{:S(2)}, u32[]{:S(2)}) collective-permute-start(f32[128,128]{1,0:T(8,128)S(1)} %get-tuple-element.96.refs_2_), channel_id=1, source_target_pairs={{0,1},{1,0},{2,3},{3,2},{4,5},{5,4},{6,7},{7,6},{8,9},{9,8},{10,11... | collective-permute-start | bytes 196616 | tf_op jit(solution)/shard_map/ppermute | solution.py:512
  112.8 2.3 %collective-permute-start.11 = (f32[128,1536]{1,0:T(8,128)S(1)}, f32[128,1536]{1,0:T(8,128)S(1)}, u32[]{:S(2)}, u32[]{:S(2)}) collective-permute-start(f32[128,1536]{1,0:T(8,128)S(1)} %get-tuple-element.80), channel_id=1, source_target_pairs={{0,1},{1,0},{2,3},{3,2},{4,5},{5,4},{6,7},{7,6},{8,9},{9,8},{10,11... | collective-permute-start | bytes 2359304 | tf_op jit(solution)/shard_map/ppermute | solution.py:512
  117.6 2.3 %collective-permute-start.16 = (f32[4,64,64]{2,1,0:T(8,128)S(1)}, f32[4,64,64]{2,1,0:T(8,128)S(1)}, u32[]{:S(2)}, u32[]{:S(2)}) collective-permute-start(f32[4,64,64]{2,1,0:T(8,128)S(1)} %get-tuple-element.100), channel_id=1, source_target_pairs={{0,1},{1,0},{2,3},{3,2},{4,5},{5,4},{6,7},{7,6},{8,9},{9,8},{10,11... | collective-permute-start | bytes 196616 | tf_op jit(solution)/shard_map/ppermute | solution.py:512

commit v11 on v10

--- a/solution.py
+++ b/solution.py
@@ -14,8 +14,9 @@
 PIECES = 2
 F_TILE = 512
 H_TILE = 512
-VMEM_MIB = {"backward": 32, "forward": 24}
+VMEM_MIB = {"backward": 36, "forward": 28}
 MIB = 1 << 20
+SLOTS = 3
 RIGHT_ROWS = 16
 RIGHT_PARTS = 2
 TIMES = {"gate": 0, "backward_0": 19 * 10**9, "backward_4": 10 * 10**9, "forward": 1 << 34, "fold": 0, "combine": 1 << 34, "sketch_part": 1 << 34}
@@ -138,52 +139,62 @@
 
     def kernel(idx, own, oth, w, *rest):
         if sketch is None:
-            msg, keep, x, total, sems = rest
+            msg, keep, x, total, sems, tiles = rest
         else:
-            sk, msg, keep, right, x, total, sems, sk_here = rest
-        j = pl.program_id(0)
+            sk, msg, keep, right, x, total, sems, tiles, sk_here = rest
         me, core = idx[0], idx[1]
 
-        @pl.when(j == 0)
-        def _():
-            a = pltpu.make_async_copy(own, x.at[core], sems.at[0])
-            b = pltpu.make_async_copy(oth, x.at[1 - core], sems.at[1])
-            a.start()
-            b.start()
-            if sketch is not None:
-                c = pltpu.make_async_copy(sk, sk_here, sems.at[2])
-                c.start()
-                c.wait()
-            a.wait()
-            b.wait()
-            if sketch is not None:
-                low, high = jnp.zeros_like(sk_here[...]), sk_here[...]
-                first_block = jnp.concatenate([high, low], axis=0)
-                second_block = jnp.concatenate([low, high], axis=0)
-                right[...] = contract_last(x[core, : half // 2, :], first_block) + contract_last(
-                    x[core, half // 2 :, :], second_block
+        def fetch(j):
+            at = pl.ds(pl.multiple_of((first + j) * tile, tile), tile)
+            slot = lax.rem(j, SLOTS)
+            return pltpu.make_async_copy(w.at[at], tiles.at[slot], sems.at[3 + slot])
+
+        copies = [
+            pltpu.make_async_copy(own, x.at[core], sems.at[0]),
+            pltpu.make_async_copy(oth, x.at[1 - core], sems.at[1]),
+        ]
+        if sketch is not None:
+            copies.append(pltpu.make_async_copy(sk, sk_here, sems.at[2]))
+        for c in copies:
+            c.start()
+        for j in range(min(SLOTS - 1, count)):
+            fetch(jnp.int32(j)).start()
+        for c in copies:
+            c.wait()
+        if sketch is not None:
+            low, high = jnp.zeros_like(sk_here[...]), sk_here[...]
+            first_block = jnp.concatenate([high, low], axis=0)
+            second_block = jnp.concatenate([low, high], axis=0)
+            right[...] = contract_last(x[core, : half // 2, :], first_block) + contract_last(
+                x[core, half // 2 :, :], second_block
+            )
+            put_right(right[...], msg)
+
+        @pl.loop(0, count)
+        def _(j):
+            fetch(j).wait()
+
+            @pl.when(j + SLOTS - 1 < count)
+            def _():
+                fetch(j + SLOTS - 1).start()
+
+            xs = x[...].reshape(2 * half, hidden)
+            total[j] = contract_last(xs, tiles[lax.rem(j, SLOTS)]).reshape(n, rows, tile)
+
+        mine = (me >> bit) & 1
+        for c in range(n // 2):
+            away, here = with_bit(c, bit, 1 - mine), with_bit(c, bit, mine)
+
+            @pl.loop(0, rows // BLK)
+            def _(b):
+                src = rows_at(b * BLK)
+                encode_rows(
+                    [total[t, away, src, :] for t in range(count)],
+                    msg,
+                    rows_at(c * rows + b * BLK),
                 )
-                put_right(right[...], msg)
-
-        xs = x[...].reshape(2 * half, hidden)
-        total[j] = contract_last(xs, w[...]).reshape(n, rows, tile)
-
-        @pl.when(j == count - 1)
-        def _():
-            mine = (me >> bit) & 1
-            for c in range(n // 2):
-                away, here = with_bit(c, bit, 1 - mine), with_bit(c, bit, mine)
-
-                @pl.loop(0, rows // BLK)
-                def _(b):
-                    src = rows_at(b * BLK)
-                    encode_rows(
-                        [total[t, away, src, :] for t in range(count)],
-                        msg,
-                        rows_at(c * rows + b * BLK),
-                    )
-                    for t in range(count):
-                        keep[t, c, src, :] = total[t, here, src, :]
+                for t in range(count):
+                    keep[t, c, src, :] = total[t, here, src, :]
 
     extra = 0 if sketch is None else RIGHT_ROWS
     out = [
@@ -191,11 +202,12 @@
         jax.ShapeDtypeStruct((count, n // 2, rows, tile), jnp.float32),
     ]
     args = [own, oth, w]
-    specs = [HBM, ANY, pl.BlockSpec((tile, hidden), lambda j, s: (first + j, 0))]
+    specs = [HBM, ANY, HBM]
     scratch = [
         pltpu.VMEM((2, half, hidden), jnp.bfloat16),
         pltpu.VMEM((count, n, rows, tile), jnp.float32),
-        pltpu.SemaphoreType.DMA((3,)),
+        pltpu.SemaphoreType.DMA((3 + SLOTS,)),
+        pltpu.VMEM((SLOTS, tile, hidden), w.dtype),
     ]
     if sketch is not None:
         args.append(sketch)
@@ -210,7 +222,7 @@
         out,
         [whole(o.shape) for o in out],
         f"backward_{first}",
-        (count,),
+        (1,),
         (4 * half * hidden * width, 2 * hidden * width + 12 * half * width),
         after,
         scratch,
@@ -372,44 +384,94 @@
     hidden = (hi - lo) * tile
     part = m // 2 * rows
 
+    count = hi - lo
+
     def kernel(idx, *refs):
-        w, sk, send, keep, left, x, sems = refs[m:]
+        if sketch is None:
+            w, send, keep, x, sems, tiles, outs, out_sems = refs[m:]
+        else:
+            w, sk, send, keep, left, x, sems, tiles, outs, out_sems = refs[m:]
         me, core = idx[0], idx[1]
 
-        @pl.when(pl.program_id(0) == 0)
-        def _():
-            copies = []
-            for i, (mask, _, block) in enumerate(chunks):
-                d = me ^ mask
-                side = 1 - ((d // m) ^ core)
-                to = pl.ds(pl.multiple_of(side * part + ((d % m) >> 1) * rows, BLK), rows)
-                src = refs[i].at[pl.ds(block * rows, rows)]
-                copies.append(pltpu.make_async_copy(src, x.at[to], sems.at[i]))
-            for c in copies:
+        def fetch(j):
+            at = pl.ds(pl.multiple_of((lo + j) * tile, tile), tile)
+            slot = lax.rem(j, SLOTS)
+            return pltpu.make_async_copy(w.at[:, at], tiles.at[slot], sems.at[m + slot])
+
+        def give(j):
+            at = pl.ds(pl.multiple_of(j * tile, tile), tile)
+            slot = lax.rem(j, 2)
+            return [
+                pltpu.make_async_copy(outs.at[slot, side], ref.at[:, at], out_sems.at[slot, side])
+                for side, ref in enumerate((send, keep))
+            ]
+
+        copies = []
+        for i, (mask, _, block) in enumerate(chunks):
+            d = me ^ mask
+            side = 1 - ((d // m) ^ core)
+            to = pl.ds(pl.multiple_of(side * part + ((d % m) >> 1) * rows, BLK), rows)
+            src = refs[i].at[pl.ds(block * rows, rows)]
+            copies.append(pltpu.make_async_copy(src, x.at[to], sems.at[i]))
+        for c in copies:
+            c.start()
+        for j in range(min(SLOTS - 1, count)):
+            fetch(jnp.int32(j)).start()
+        for c in copies:
+            c.wait()
+        if sketch is not None:
+            left[...] = contract_last(x[...], sk[...])
+
+        @pl.loop(0, count)
+        def _(j):
+            fetch(j).wait()
+
+            @pl.when(j + SLOTS - 1 < count)
+            def _():
+                fetch(j + SLOTS - 1).start()
+
+            t = jnp.dot(x[...], tiles[lax.rem(j, SLOTS)], preferred_element_type=jnp.float32)
+
+            @pl.when(j >= 2)
+            def _():
+                for c in give(j - 2):
+                    c.wait()
+
+            outs[lax.rem(j, 2)] = t.reshape(2, part, tile)
+            for c in give(j):
                 c.start()
-            for c in copies:
+
+        for j in range(max(0, count - 2), count):
+            for c in give(jnp.int32(j)):
                 c.wait()
-            left[...] = contract_last(x[...], sk[...])
-
-        t = jnp.dot(x[...], w[...], preferred_element_type=jnp.float32)
-        send[...] = t[:part]
-        keep[...] = t[part:]
-
+
+    args = [c[1] for c in chunks] + [w]
+    specs = [ANY] * m + [HBM]
     out = [jax.ShapeDtypeStruct((part, hidden), jnp.float32)] * 2
-    out.append(jax.ShapeDtypeStruct((2 * part, sketch.shape[0]), jnp.float32))
-    column = pl.BlockSpec((part, tile), lambda j, s: (0, j))
+    out_specs = [ANY, ANY]
+    if sketch is not None:
+        args.append(sketch)
+        specs.append(whole(sketch.shape))
+        out.append(jax.ShapeDtypeStruct((2 * part, sketch.shape[0]), jnp.float32))
+        out_specs.append(whole(out[2].shape))
     return call(
         kernel,
         idx,
-        [c[1] for c in chunks] + [w, sketch],
-        [ANY] * m + [pl.BlockSpec((feats, tile), lambda j, s: (0, lo + j)), whole(sketch.shape)],
+        args,
+        specs,
         out,
-        [column, column, whole(out[2].shape)],
+        out_specs,
         "forward",
-        (hidden // tile,),
+        (1,),
         (4 * part * feats * hidden, 2 * feats * hidden + 8 * part * hidden),
         after,
-        [pltpu.VMEM((2 * part, feats), jnp.bfloat16), pltpu.SemaphoreType.DMA((m,))],
+        [
+            pltpu.VMEM((2 * part, feats), jnp.bfloat16),
+            pltpu.SemaphoreType.DMA((m + SLOTS,)),
+            pltpu.VMEM((SLOTS, feats, tile), w.dtype),
+            pltpu.VMEM((2, 2, part, tile), jnp.float32),
+            pltpu.SemaphoreType.DMA((2, 2)),
+        ],
     )
 
 
@@ -581,9 +643,9 @@
             parts = [(1, chunks[1], 0)] + [(m + 1, crossed, i) for i, m in enumerate(evens)]
         else:
             parts = [(m, chunks[m], 0) for m in [0] + evens]
-        outs, t = forward(idx, parts, rows, weight, in_sketch, lo, hi, after)
+        outs, t = forward(idx, parts, rows, weight, None if lo else in_sketch, lo, hi, after)
         start = lo * (hidden // tiles)
-        return (outs[1], swap(outs[0]), start, hidden, batch, rows), outs[2], [t]
+        return (outs[1], swap(outs[0]), start, hidden, batch, rows), outs[-1], [t]
 
     cut = -(-tiles // 2)
     token = folded(0, 1, token)

time: 121 us -> 118 us (0.975)
  Pallas kernels: 79.3 us -> 72.1 us
  waiting for transfers between devices: 19 us -> 23.4 us
    pallas_call x17, Pallas kernels: 79.3 us -> 72.1 us  [call(): pl.pallas_call(with_token, out_shape=list(out_shape) + [token], grid_spec...]
    ppermute x11, waiting for transfers between devices: 18.2 us -> 22.7 us  [partner(): return lax.ppermute(x, 'outp', [(d, d ^ 1 << bit) for d in range(n)])]
  transfers between devices with their start and end apart: 17 -> 17, of which waited for: 6 -> 7; matrix products, arithmetic and copies ran while one was open for 0% -> 0% of each run, Pallas kernels for 66% -> 61%
where the time goes in v11:
time: 118 us
  Pallas kernels  72.1 us (61%)
  waiting for transfers between devices  23.4 us (20%)
  starting transfers between devices  18.3 us (16%)
  local copies, waits for them, and re-layouts  3.27 us (3%)
    pallas_call x17, Pallas kernels, call(): pl.pallas_call(with_token, out_shape=list(out_shape) + [token], grid_spec...  72.1 us
    ppermute x11, waiting for transfers between devices, partner(): return lax.ppermute(x, 'outp', [(d, d ^ 1 << bit) for d in range(n)])  22.7 us
    ppermute x11, starting transfers between devices, partner(): return lax.ppermute(x, 'outp', [(d, d ^ 1 << bit) for d in range(n)])  16.9 us
    unnamed x8, local copies, waits for them, and re-layouts  2.53 us
  transfers between devices with their start and end apart: 17, of which 7 were waited for; matrix products, arithmetic and copies ran while one was open for 0% of the time, Pallas kernels for 61%

profile of v11, /device:TPU:0, one launch (start us, length us, event | category | flops | bytes accessed | tf_op | source)
XLA Modules:
  0.0 118.1 jit_solution(3213203566411391024)
XLA Ops:
  1.1 2.7 %collective-permute-start.1 = (bf16[64,4096]{1,0:T(8,128)(2,1)}, bf16[64,4096]{1,0:T(8,128)(2,1)S(1)}, u32[]{:S(2)}, u32[]{:S(2)}) collective-permute-start(bf16[64,4096]{1,0:T(8,128)(2,1)} %refs_0_.5), channel_id=1, source_target_pairs={{0,4},{2,6},{4,0},{6,2},{8,12},{10,14},{12,8},{14,10},{1,5},{3,7},... | collective-permute-start | bytes 1572872 | tf_op jit(solution)/shard_map/ppermute | solution.py:571
  3.8 2.6 %collective-permute-start = (bf16[64,4096]{1,0:T(8,128)(2,1)}, bf16[64,4096]{1,0:T(8,128)(2,1)S(1)}, u32[]{:S(2)}, u32[]{:S(2)}) collective-permute-start(bf16[64,4096]{1,0:T(8,128)(2,1)} %refs_0_.5), channel_id=1, source_target_pairs={{0,8},{2,10},{4,12},{6,14},{8,0},{10,2},{12,4},{14,6},{1,9},{3,11}... | collective-permute-start | bytes 1572872 | tf_op jit(solution)/shard_map/ppermute | solution.py:571
  6.4 1.5 %collective-permute-start.2 = (bf16[64,4096]{1,0:T(8,128)(2,1)}, bf16[64,4096]{1,0:T(8,128)(2,1)S(1)}, u32[]{:S(2)}, u32[]{:S(2)}) collective-permute-start(bf16[64,4096]{1,0:T(8,128)(2,1)} %refs_0_.5), channel_id=1, source_target_pairs={{0,2},{2,0},{4,6},{6,4},{8,10},{10,8},{12,14},{14,12},{1,3},{3,1},... | collective-permute-start | bytes 1572872 | tf_op jit(solution)/shard_map/ppermute | solution.py:571
  8.0 1.5 %copy-done = bf16[256,3584]{1,0:T(8,128)(2,1)S(1)} copy-done((bf16[256,3584]{1,0:T(8,128)(2,1)S(1)}, bf16[256,3584]{1,0:T(8,128)(2,1)}, u32[]{:S(2)}) %copy-start) | copy-done | bytes 1835032
  10.5 13.6 %backward_0.1 = (bf16[272,2176]{1,0:T(8,128)(2,1)S(1)}, f32[4,4,64,512]{3,2,1,0:T(8,128)S(1)}, f32[128,128]{1,0:T(8,128)S(1)}, f32[8,128]{1,0:T(8,128)S(1)}) custom-call(s32[2]{0:T(128)S(1)} %pad_add_fusion.idx, bf16[256,3584]{1,0:T(8,128)(2,1)S(1)} %copy-done, bf16[256,3584]{1,0:T(8,128)(2,1)S(1)} %collective-permute-done.3.refs_1_, ...), custom_call_target="tpu_custom_call" | custom-call | flops 19000000512 | bytes 20971520 | tf_op jit(solution)/shard_map/backward_0/pallas_call | solution.py:55
  24.7 2.9 %collective-permute-done.1.refs_1_ = bf16[64,4096]{1,0:T(8,128)(2,1)S(1)} collective-permute-done((bf16[64,4096]{1,0:T(8,128)(2,1)}, bf16[64,4096]{1,0:T(8,128)(2,1)S(1)}, u32[]{:S(2)}, u32[]{:S(2)}) %collective-permute-start.1) | collective-permute-done | bytes 524320 | tf_op jit(solution)/shard_map/ppermute | solution.py:571
  27.6 2.6 %collective-permute-done.refs_0_ = bf16[64,4096]{1,0:T(8,128)(2,1)S(1)} collective-permute-done((bf16[64,4096]{1,0:T(8,128)(2,1)}, bf16[64,4096]{1,0:T(8,128)(2,1)S(1)}, u32[]{:S(2)}, u32[]{:S(2)}) %collective-permute-start) | collective-permute-done | bytes 524320 | tf_op jit(solution)/shard_map/ppermute | solution.py:571
  31.3 13.4 %backward_4.1 = (bf16[256,2176]{1,0:T(8,128)(2,1)S(1)}, f32[4,4,64,512]{3,2,1,0:T(8,128)S(1)}, f32[8,128]{1,0:T(8,128)S(1)}) custom-call(s32[2]{0:T(128)S(1)} %pad_add_fusion.idx, bf16[256,3584]{1,0:T(8,128)(2,1)S(1)} %copy-done, bf16[256,3584]{1,0:T(8,128)(2,1)S(1)} %collective-permute-done.3.refs_1_, bf16[4096,3584]{1,0:T(8,128)(2,1)} %refs_4_.5, ...), custom_call_target="tpu_custom_call" | custom-call | flops 10000000000 | bytes 20971520 | tf_op jit(solution)/shard_map/backward_4/pallas_call | solution.py:55
  44.6 1.7 %collective-permute-start.8 = (bf16[256,2176]{1,0:T(8,128)(2,1)S(1)}, bf16[256,2176]{1,0:T(8,128)(2,1)S(1)}, u32[]{:S(2)}, u32[]{:S(2)}) collective-permute-start(bf16[256,2176]{1,0:T(8,128)(2,1)S(1)} %get-tuple-element.67), channel_id=1, source_target_pairs={{0,4},{2,6},{4,0},{6,2},{8,12},{10,14},{12,8},{14,10},{1,5},{3,7},... | collective-permute-start | bytes 3342344 | tf_op jit(solution)/shard_map/ppermute | solution.py:571
  47.0 1.6 %collective-permute-start.5 = (bf16[192,4096]{1,0:T(8,128)(2,1)S(1)}, bf16[192,4096]{1,0:T(8,128)(2,1)S(1)}, u32[]{:S(2)}, u32[]{:S(2)}) collective-permute-start(bf16[192,4096]{1,0:T(8,128)(2,1)S(1)} %get-tuple-element.58), channel_id=1, source_target_pairs={{0,2},{2,0},{4,6},{6,4},{8,10},{10,8},{12,14},{14,12},{1,3},{3,1},... | collective-permute-start | bytes 4718600 | tf_op jit(solution)/shard_map/ppermute | solution.py:571
  48.6 4.6 %collective-permute-done.6.refs_1_ = bf16[272,2176]{1,0:T(8,128)(2,1)S(1)} collective-permute-done((bf16[272,2176]{1,0:T(8,128)(2,1)S(1)}, bf16[272,2176]{1,0:T(8,128)(2,1)S(1)}, u32[]{:S(2)}, u32[]{:S(2)}) %collective-permute-start.6) | collective-permute-done | bytes 1183776 | tf_op jit(solution)/shard_map/ppermute | solution.py:571
  53.2 2.4 %fold.4 = (bf16[144,2176]{1,0:T(8,128)(2,1)S(1)}, f32[4,2,64,512]{3,2,1,0:T(8,128)S(1)}, f32[128,128]{1,0:T(8,128)S(1)}, f32[8,128]{1,0:T(8,128)S(1)}) custom-call(s32[2]{0:T(128)S(1)} %pad_add_fusion.idx, f32[4,4,64,512]{3,2,1,0:T(8,128)S(1)} %get-tuple-element.59.refs_0_, bf16[272,2176]{1,0:T(8,128)(2,1)S(1)} %collective-permute-done.6.refs_1_, ...), custom_call_target="tpu_custom_call" | custom-call | bytes 6291456 | tf_op jit(solution)/shard_map/fold/pallas_call | solution.py:55
  56.1 12.4 %forward.3 = (f32[128,3584]{1,0:T(8,128)S(1)}, f32[128,3584]{1,0:T(8,128)S(1)}, f32[256,64]{1,0:T(8,128)S(1)}, f32[8,128]{1,0:T(8,128)S(1)}) custom-call(s32[2]{0:T(128)S(1)} %pad_add_fusion.idx, bf16[64,4096]{1,0:T(8,128)(2,1)S(1)} %copy-done.1, bf16[64,4096]{1,0:T(8,128)(2,1)S(1)} %get-tuple-element.54.refs_0_.refs_1_, ...), custom_call_target="tpu_custom_call" | custom-call | flops 17179869184 | bytes 33030144 | tf_op jit(solution)/shard_map/forward/pallas_call | solution.py:55
  68.6 3.6 %collective-permute-done.8.refs_1_ = bf16[256,2176]{1,0:T(8,128)(2,1)S(1)} collective-permute-done((bf16[256,2176]{1,0:T(8,128)(2,1)S(1)}, bf16[256,2176]{1,0:T(8,128)(2,1)S(1)}, u32[]{:S(2)}, u32[]{:S(2)}) %collective-permute-start.8) | collective-permute-done | bytes 1114144 | tf_op jit(solution)/shard_map/ppermute | solution.py:571
  72.2 2.4 %fold.5 = (bf16[128,2176]{1,0:T(8,128)(2,1)S(1)}, f32[4,2,64,512]{3,2,1,0:T(8,128)S(1)}, f32[8,128]{1,0:T(8,128)S(1)}) custom-call(s32[2]{0:T(128)S(1)} %pad_add_fusion.idx, f32[4,4,64,512]{3,2,1,0:T(8,128)S(1)} %get-tuple-element.66.refs_0_, bf16[256,2176]{1,0:T(8,128)(2,1)S(1)} %collective-permute-done.8.refs_1_, f32[8,128]{1,0:T(8,128)S(1)} %get-tuple-element.68.refs_2_), custom_call_target="tpu_custom_call" | custom-call | bytes 6291456 | tf_op jit(solution)/shard_map/fold/pallas_call | solution.py:55
  74.6 1.6 %collective-permute-start.9 = (bf16[128,2176]{1,0:T(8,128)(2,1)S(1)}, bf16[128,2176]{1,0:T(8,128)(2,1)S(1)}, u32[]{:S(2)}, u32[]{:S(2)}) collective-permute-start(bf16[128,2176]{1,0:T(8,128)(2,1)S(1)} %get-tuple-element.70), channel_id=1, source_target_pairs={{0,2},{2,0},{4,6},{6,4},{8,10},{10,8},{12,14},{14,12},{1,3},{3,1},... | collective-permute-start | bytes 1671176 | tf_op jit(solution)/shard_map/ppermute | solution.py:571
  76.2 7.7 %collective-permute-done.10.refs_1_ = bf16[144,2176]{1,0:T(8,128)(2,1)S(1)} collective-permute-done((bf16[144,2176]{1,0:T(8,128)(2,1)S(1)}, bf16[144,2176]{1,0:T(8,128)(2,1)S(1)}, u32[]{:S(2)}, u32[]{:S(2)}) %collective-permute-start.10) | collective-permute-done | bytes 626720 | tf_op jit(solution)/shard_map/ppermute | solution.py:571
  83.9 1.5 %fold.6 = (bf16[80,2176]{1,0:T(8,128)(2,1)S(1)}, f32[4,1,64,512]{3,2,1,0:T(8,128)S(1)}, f32[128,128]{1,0:T(8,128)S(1)}, f32[8,128]{1,0:T(8,128)S(1)}) custom-call(s32[2]{0:T(128)S(1)} %pad_add_fusion.idx, f32[4,2,64,512]{3,2,1,0:T(8,128)S(1)} %get-tuple-element.71.refs_0_, bf16[144,2176]{1,0:T(8,128)(2,1)S(1)} %collective-permute-done.10.refs_1_, ...), custom_call_target="tpu_custom_call" | custom-call | bytes 3145728 | tf_op jit(solution)/shard_map/fold/pallas_call | solution.py:55
  85.4 2.4 %collective-permute-start.13 = (bf16[80,2176]{1,0:T(8,128)(2,1)S(1)}, bf16[80,2176]{1,0:T(8,128)(2,1)S(1)}, u32[]{:S(2)}, u32[]{:S(2)}) collective-permute-start(bf16[80,2176]{1,0:T(8,128)(2,1)S(1)} %get-tuple-element.85), channel_id=1, source_target_pairs={{0,8},{2,10},{4,12},{6,14},{8,0},{10,2},{12,4},{14,6},{1,9},{3,11}... | collective-permute-start | bytes 1044488 | tf_op jit(solution)/shard_map/ppermute | solution.py:571
  87.8 8.4 %forward.4 = (f32[128,2048]{1,0:T(8,128)S(1)}, f32[128,2048]{1,0:T(8,128)S(1)}, f32[256,64]{1,0:T(8,128)S(1)}, f32[8,128]{1,0:T(8,128)S(1)}) custom-call(s32[2]{0:T(128)S(1)} %pad_add_fusion.idx, bf16[64,4096]{1,0:T(8,128)(2,1)S(1)} %get-tuple-element.53.refs_0_, bf16[192,4096]{1,0:T(8,128)(2,1)S(1)} %collective-permute-done.5.refs_1_.refs_2_.refs_3_, ...), custom_call_target="tpu_custom_call" | custom-call | flops 17179869184 | bytes 18874368 | tf_op jit(solution)/shard_map/forward/pallas_call | solution.py:55
  97.4 1.5 %fold.7 = (bf16[64,2176]{1,0:T(8,128)(2,1)S(1)}, f32[4,1,64,512]{3,2,1,0:T(8,128)S(1)}, f32[8,128]{1,0:T(8,128)S(1)}) custom-call(s32[2]{0:T(128)S(1)} %pad_add_fusion.idx, f32[4,2,64,512]{3,2,1,0:T(8,128)S(1)} %get-tuple-element.69.refs_0_, bf16[128,2176]{1,0:T(8,128)(2,1)S(1)} %collective-permute-done.9.refs_1_, f32[8,128]{1,0:T(8,128)S(1)} %get-tuple-element.76.refs_2_), custom_call_target="tpu_custom_call" | custom-call | bytes 3145728 | tf_op jit(solution)/shard_map/fold/pallas_call | solution.py:55
  100.3 1.8 %combine.3 = (bf16[256,3584]{1,0:T(8,128)(2,1)}, f32[8,128]{1,0:T(8,128)S(1)}) custom-call(s32[2]{0:T(128)S(1)} %pad_add_fusion.idx, f32[128,3584]{1,0:T(8,128)S(1)} %get-tuple-element.64.refs_0_, f32[128,3584]{1,0:T(8,128)S(1)} %collective-permute-done.7.refs_1_, f32[8,128]{1,0:T(8,128)S(1)} %get-tuple-element.77.refs_2_), custom_call_target="tpu_custom_call" | custom-call | flops 17179869184 | bytes 4587520 | tf_op jit(solution)/shard_map/combine/pallas_call | solution.py:55
  102.0 7.0 %forward.5 = (f32[128,1536]{1,0:T(8,128)S(1)}, f32[128,1536]{1,0:T(8,128)S(1)}, f32[8,128]{1,0:T(8,128)S(1)}) custom-call(s32[2]{0:T(128)S(1)} %pad_add_fusion.idx, bf16[64,4096]{1,0:T(8,128)(2,1)S(1)} %get-tuple-element.53.refs_0_, bf16[192,4096]{1,0:T(8,128)(2,1)S(1)} %collective-permute-done.5.refs_1_.refs_2_.refs_3_, ...), custom_call_target="tpu_custom_call" | custom-call | flops 17179869184 | bytes 14155776 | tf_op jit(solution)/shard_map/forward/pallas_call | solution.py:55
  115.2 2.1 %finish.1 = (bf16[64,4096]{1,0:T(8,128)(2,1)}, f32[8,128]{1,0:T(8,128)}) custom-call(s32[2]{0:T(128)S(1)} %pad_add_fusion.idx, f32[4,1,64,512]{3,2,1,0:T(8,128)S(1)} %get-tuple-element.91.refs_0_, f32[4,1,64,512]{3,2,1,0:T(8,128)S(1)} %get-tuple-element.92.refs_1_, bf16[80,2176]{1,0:T(8,128)(2,1)S(1)} %collective-permute-done.13.refs_1_.refs_2_, ...), custom_call_target="tpu_custom_call" | custom-call | bytes 2097152 | tf_op jit(solution)/shard_map/finish/pallas_call | solution.py:55
  (38 shorter events, 13.9 us)
Async XLA Ops:
  0.6 7.4 %collective-permute-start.3 = (bf16[256,3584]{1,0:T(8,128)(2,1)}, bf16[256,3584]{1,0:T(8,128)(2,1)S(1)}, u32[]{:S(2)}, u32[]{:S(2)}) collective-permute-start(bf16[256,3584]{1,0:T(8,128)(2,1)} %refs_0_.4), channel_id=1, source_target_pairs={{0,1},{1,0},{2,3},{3,2},{4,5},{5,4},{6,7},{7,6},{8,9},{9,8},{10,11... | collective-permute-start | bytes 5505032 | tf_op jit(solution)/shard_map/ppermute | solution.py:574
  1.1 26.5 %collective-permute-start.1 = (bf16[64,4096]{1,0:T(8,128)(2,1)}, bf16[64,4096]{1,0:T(8,128)(2,1)S(1)}, u32[]{:S(2)}, u32[]{:S(2)}) collective-permute-start(bf16[64,4096]{1,0:T(8,128)(2,1)} %refs_0_.5), channel_id=1, source_target_pairs={{0,4},{2,6},{4,0},{6,2},{8,12},{10,14},{12,8},{14,10},{1,5},{3,7},... | collective-permute-start | bytes 1572872 | tf_op jit(solution)/shard_map/ppermute | solution.py:571
  3.8 26.4 %collective-permute-start = (bf16[64,4096]{1,0:T(8,128)(2,1)}, bf16[64,4096]{1,0:T(8,128)(2,1)S(1)}, u32[]{:S(2)}, u32[]{:S(2)}) collective-permute-start(bf16[64,4096]{1,0:T(8,128)(2,1)} %refs_0_.5), channel_id=1, source_target_pairs={{0,8},{2,10},{4,12},{6,14},{8,0},{10,2},{12,4},{14,6},{1,9},{3,11}... | collective-permute-start | bytes 1572872 | tf_op jit(solution)/shard_map/ppermute | solution.py:571
  6.4 23.8 %collective-permute-start.2 = (bf16[64,4096]{1,0:T(8,128)(2,1)}, bf16[64,4096]{1,0:T(8,128)(2,1)S(1)}, u32[]{:S(2)}, u32[]{:S(2)}) collective-permute-start(bf16[64,4096]{1,0:T(8,128)(2,1)} %refs_0_.5), channel_id=1, source_target_pairs={{0,2},{2,0},{4,6},{6,4},{8,10},{10,8},{12,14},{14,12},{1,3},{3,1},... | collective-permute-start | bytes 1572872 | tf_op jit(solution)/shard_map/ppermute | solution.py:571
  8.0 1.5 %copy-start = (bf16[256,3584]{1,0:T(8,128)(2,1)S(1)}, bf16[256,3584]{1,0:T(8,128)(2,1)}, u32[]{:S(2)}) copy-start(bf16[256,3584]{1,0:T(8,128)(2,1)} %refs_0_.4) | copy-start | bytes 5505028
  9.5 1.0 copy-start.3
  24.2 29.0 %collective-permute-start.6 = (bf16[272,2176]{1,0:T(8,128)(2,1)S(1)}, bf16[272,2176]{1,0:T(8,128)(2,1)S(1)}, u32[]{:S(2)}, u32[]{:S(2)}) collective-permute-start(bf16[272,2176]{1,0:T(8,128)(2,1)S(1)} %get-tuple-element.60), channel_id=1, source_target_pairs={{0,2},{2,0},{4,6},{6,4},{8,10},{10,8},{12,14},{14,12},{1,3},{3,1},... | collective-permute-start | bytes 3551240 | tf_op jit(solution)/shard_map/ppermute | solution.py:571
  30.8 15.5 %collective-permute-start.4 = (bf16[64,4096]{1,0:T(8,128)(2,1)S(1)}, bf16[64,4096]{1,0:T(8,128)(2,1)S(1)}, u32[]{:S(2)}, u32[]{:S(2)}) collective-permute-start(bf16[64,4096]{1,0:T(8,128)(2,1)S(1)} %get-tuple-element.55.refs_1_.refs_2_), channel_id=1, source_target_pairs={{0,4},{2,6},{4,0},{6,2},{8,12},{10,14},{12,8},{14,10},{1,5},{3,7},... | collective-permute-start | bytes 1572872 | tf_op jit(solution)/shard_map/ppermute | solution.py:571
  44.6 27.6 %collective-permute-start.8 = (bf16[256,2176]{1,0:T(8,128)(2,1)S(1)}, bf16[256,2176]{1,0:T(8,128)(2,1)S(1)}, u32[]{:S(2)}, u32[]{:S(2)}) collective-permute-start(bf16[256,2176]{1,0:T(8,128)(2,1)S(1)} %get-tuple-element.67), channel_id=1, source_target_pairs={{0,4},{2,6},{4,0},{6,2},{8,12},{10,14},{12,8},{14,10},{1,5},{3,7},... | collective-permute-start | bytes 3342344 | tf_op jit(solution)/shard_map/ppermute | solution.py:571
  47.0 9.2 %copy-start.1 = (bf16[64,4096]{1,0:T(8,128)(2,1)S(1)}, bf16[64,4096]{1,0:T(8,128)(2,1)}, u32[]{:S(2)}) copy-start(bf16[64,4096]{1,0:T(8,128)(2,1)} %refs_0_.5) | copy-start | bytes 1572868
  47.0 9.1 %copy-start.2 = (bf16[64,4096]{1,0:T(8,128)(2,1)S(1)}, bf16[64,4096]{1,0:T(8,128)(2,1)}, u32[]{:S(2)}) copy-start(bf16[64,4096]{1,0:T(8,128)(2,1)} %refs_5_.3) | copy-start | bytes 1572868
  47.0 40.8 %collective-permute-start.5 = (bf16[192,4096]{1,0:T(8,128)(2,1)S(1)}, bf16[192,4096]{1,0:T(8,128)(2,1)S(1)}, u32[]{:S(2)}, u32[]{:S(2)}) collective-permute-start(bf16[192,4096]{1,0:T(8,128)(2,1)S(1)} %get-tuple-element.58), channel_id=1, source_target_pairs={{0,2},{2,0},{4,6},{6,4},{8,10},{10,8},{12,14},{14,12},{1,3},{3,1},... | collective-permute-start | bytes 4718600 | tf_op jit(solution)/shard_map/ppermute | solution.py:571
  55.6 28.3 %collective-permute-start.10 = (bf16[144,2176]{1,0:T(8,128)(2,1)S(1)}, bf16[144,2176]{1,0:T(8,128)(2,1)S(1)}, u32[]{:S(2)}, u32[]{:S(2)}) collective-permute-start(bf16[144,2176]{1,0:T(8,128)(2,1)S(1)} %get-tuple-element.72), channel_id=1, source_target_pairs={{0,4},{2,6},{4,0},{6,2},{8,12},{10,14},{12,8},{14,10},{1,5},{3,7},... | collective-permute-start | bytes 1880072 | tf_op jit(solution)/shard_map/ppermute | solution.py:571
  68.5 31.7 %collective-permute-start.7 = (f32[128,3584]{1,0:T(8,128)S(1)}, f32[128,3584]{1,0:T(8,128)S(1)}, u32[]{:S(2)}, u32[]{:S(2)}) collective-permute-start(f32[128,3584]{1,0:T(8,128)S(1)} %get-tuple-element.65), channel_id=1, source_target_pairs={{0,1},{1,0},{2,3},{3,2},{4,5},{5,4},{6,7},{7,6},{8,9},{9,8},{10,11... | collective-permute-start | bytes 5505032 | tf_op jit(solution)/shard_map/ppermute | solution.py:574
  74.6 22.8 %collective-permute-start.9 = (bf16[128,2176]{1,0:T(8,128)(2,1)S(1)}, bf16[128,2176]{1,0:T(8,128)(2,1)S(1)}, u32[]{:S(2)}, u32[]{:S(2)}) collective-permute-start(bf16[128,2176]{1,0:T(8,128)(2,1)S(1)} %get-tuple-element.70), channel_id=1, source_target_pairs={{0,2},{2,0},{4,6},{6,4},{8,10},{10,8},{12,14},{14,12},{1,3},{3,1},... | collective-permute-start | bytes 1671176 | tf_op jit(solution)/shard_map/ppermute | solution.py:571
  85.4 23.7 %collective-permute-start.13 = (bf16[80,2176]{1,0:T(8,128)(2,1)S(1)}, bf16[80,2176]{1,0:T(8,128)(2,1)S(1)}, u32[]{:S(2)}, u32[]{:S(2)}) collective-permute-start(bf16[80,2176]{1,0:T(8,128)(2,1)S(1)} %get-tuple-element.85), channel_id=1, source_target_pairs={{0,8},{2,10},{4,12},{6,14},{8,0},{10,2},{12,4},{14,6},{1,9},{3,11}... | collective-permute-start | bytes 1044488 | tf_op jit(solution)/shard_map/ppermute | solution.py:571
  98.9 16.3 %collective-permute-start.14 = (bf16[64,2176]{1,0:T(8,128)(2,1)S(1)}, bf16[64,2176]{1,0:T(8,128)(2,1)S(1)}, u32[]{:S(2)}, u32[]{:S(2)}) collective-permute-start(bf16[64,2176]{1,0:T(8,128)(2,1)S(1)} %get-tuple-element.93), channel_id=1, source_target_pairs={{0,8},{2,10},{4,12},{6,14},{8,0},{10,2},{12,4},{14,6},{1,9},{3,11}... | collective-permute-start | bytes 835592 | tf_op jit(solution)/shard_map/ppermute | solution.py:571
  100.2 10.1 %collective-permute-start.12 = (f32[128,2048]{1,0:T(8,128)S(1)}, f32[128,2048]{1,0:T(8,128)S(1)}, u32[]{:S(2)}, u32[]{:S(2)}) collective-permute-start(f32[128,2048]{1,0:T(8,128)S(1)} %get-tuple-element.82), channel_id=1, source_target_pairs={{0,1},{1,0},{2,3},{3,2},{4,5},{5,4},{6,7},{7,6},{8,9},{9,8},{10,11... | collective-permute-start | bytes 3145736 | tf_op jit(solution)/shard_map/ppermute | solution.py:574
  109.7 4.3 %collective-permute-start.15 = (f32[128,128]{1,0:T(8,128)S(1)}, f32[128,128]{1,0:T(8,128)S(1)}, u32[]{:S(2)}, u32[]{:S(2)}) collective-permute-start(f32[128,128]{1,0:T(8,128)S(1)} %get-tuple-element.96.refs_2_), channel_id=1, source_target_pairs={{0,1},{1,0},{2,3},{3,2},{4,5},{5,4},{6,7},{7,6},{8,9},{9,8},{10,11... | collective-permute-start | bytes 196616 | tf_op jit(solution)/shard_map/ppermute | solution.py:574
  110.2 2.3 %collective-permute-start.11 = (f32[128,1536]{1,0:T(8,128)S(1)}, f32[128,1536]{1,0:T(8,128)S(1)}, u32[]{:S(2)}, u32[]{:S(2)}) collective-permute-start(f32[128,1536]{1,0:T(8,128)S(1)} %get-tuple-element.80), channel_id=1, source_target_pairs={{0,1},{1,0},{2,3},{3,2},{4,5},{5,4},{6,7},{7,6},{8,9},{9,8},{10,11... | collective-permute-start | bytes 2359304 | tf_op jit(solution)/shard_map/ppermute | solution.py:574
  115.0 2.3 %collective-permute-start.16 = (f32[4,64,64]{2,1,0:T(8,128)S(1)}, f32[4,64,64]{2,1,0:T(8,128)S(1)}, u32[]{:S(2)}, u32[]{:S(2)}) collective-permute-start(f32[4,64,64]{2,1,0:T(8,128)S(1)} %get-tuple-element.100), channel_id=1, source_target_pairs={{0,1},{1,0},{2,3},{3,2},{4,5},{5,4},{6,7},{7,6},{8,9},{9,8},{10,11... | collective-permute-start | bytes 196616 | tf_op jit(solution)/shard_map/ppermute | solution.py:574

commit v12 on v11

--- a/solution.py
+++ b/solution.py
@@ -478,36 +478,54 @@
 def combine(idx, keep, got, lo, total, batch, rows, before, after):
     part, width = keep.shape
     m = part // rows
+    slices = max(k for k in (1, 2, 4) if width % (k * LANES) == 0)
+    span = width // slices
 
     def kernel(idx, keep, got, *refs):
-        out, x, sems = refs[-3:]
+        out, a, b, x, in_sems, out_sems = refs[-6:]
         mine = (idx[0] & 1) ^ batch
-        x[...] = (keep[...] + got[...]).astype(jnp.bfloat16)
-        copies = []
-        for i in range(m):
-            to = pl.ds(pl.multiple_of((2 * i + mine) * rows, BLK), rows)
-            copies.append(
-                pltpu.make_async_copy(
-                    x.at[pl.ds(i * rows, rows)], out.at[to, pl.ds(lo, width)], sems.at[i]
-                )
+        loads, stores = [], []
+        for k in range(slices):
+            cols = pl.ds(k * span, span)
+            loads.append(
+                [
+                    pltpu.make_async_copy(keep.at[:, cols], a.at[k], in_sems.at[k, 0]),
+                    pltpu.make_async_copy(got.at[:, cols], b.at[k], in_sems.at[k, 1]),
+                ]
             )
-        for c in copies:
-            c.start()
-        for c in copies:
+            for c in loads[k]:
+                c.start()
+        for k in range(slices):
+            for c in loads[k]:
+                c.wait()
+            x[k] = (a[k] + b[k]).astype(jnp.bfloat16)
+            for i in range(m):
+                to = pl.ds(pl.multiple_of((2 * i + mine) * rows, BLK), rows)
+                dst = out.at[to, pl.ds(lo + k * span, span)]
+                src = x.at[k, pl.ds(i * rows, rows)]
+                stores.append(pltpu.make_async_copy(src, dst, out_sems.at[k, i]))
+                stores[-1].start()
+        for c in stores:
             c.wait()
 
     (out,), token = call(
         kernel,
         idx,
         [keep, got] + before,
-        [whole(keep.shape)] * 2 + [HBM] * len(before),
+        [ANY] * 2 + [HBM] * len(before),
         [jax.ShapeDtypeStruct((2 * part, total), jnp.bfloat16)],
         [HBM],
         "combine",
         (1,),
         (0, 10 * part * width),
         after,
-        [pltpu.VMEM((part, width), jnp.bfloat16), pltpu.SemaphoreType.DMA((m,))],
+        [
+            pltpu.VMEM((slices, part, span), jnp.float32),
+            pltpu.VMEM((slices, part, span), jnp.float32),
+            pltpu.VMEM((slices, part, span), jnp.bfloat16),
+            pltpu.SemaphoreType.DMA((slices, 2)),
+            pltpu.SemaphoreType.DMA((slices, m)),
+        ],
         aliases={3: 0} if before else None,
     )
     return out, [token]
@@ -655,15 +673,15 @@
     second, left2, token = batch_forward(1, 0, cut, token)
     token = folded(1, 2, token)
     outputs, token = combine(idx, *first, [], token)
+    right, token = last_right(idx, rights[0], msgs[0], token)
+    right_got = swap(right)
     third, _, token = batch_forward(1, cut, tiles, token)
     for step in range(3, bits):
         for p in range(PIECES):
             token = folded(p, step, token)
-    right, token = last_right(idx, rights[0], msgs[0], token)
-    right_got = swap(right)
+    part, token = sketch_part(idx, [left1, left2], right, right_got, rows, token)
     outputs, token = combine(idx, *second, [outputs], token)
     outputs, token = combine(idx, *third, [outputs], token)
-    part, token = sketch_part(idx, [left1, left2], right, right_got, rows, token)
     input_grad = finish(idx, keeps, msgs, token)
     part = (part + swap(part)) * (1.0 / LEN**0.5)
     sketches = part.reshape(part.shape[0], -1)

time: 118 us -> 126 us (1.068)
  waiting for transfers between devices: 23.4 us -> 27.8 us
  Pallas kernels: 72.1 us -> 74.2 us
    ppermute x11, waiting for transfers between devices: 22.7 us -> 27.8 us  [partner(): return lax.ppermute(x, 'outp', [(d, d ^ 1 << bit) for d in range(n)])]
    pallas_call x17, Pallas kernels: 72.1 us -> 74.2 us  [call(): pl.pallas_call(with_token, out_shape=list(out_shape) + [token], grid_spec...]
    unnamed x8 -> x12, local copies, waits for them, and re-layouts: 2.53 us -> 3.67 us
  transfers between devices with their start and end apart: 17 -> 17, of which waited for: 7 -> 7; matrix products, arithmetic and copies ran while one was open for 0% -> 1% of each run, Pallas kernels for 61% -> 57%
where the time goes in v12:
time: 126 us
  Pallas kernels  74.2 us (59%)
  waiting for transfers between devices  27.8 us (22%)
  starting transfers between devices  18.3 us (15%)
  local copies, waits for them, and re-layouts  4.4 us (3%)
    pallas_call x17, Pallas kernels, call(): pl.pallas_call(with_token, out_shape=list(out_shape) + [token], grid_spec...  74.2 us
    ppermute x11, waiting for transfers between devices, partner(): return lax.ppermute(x, 'outp', [(d, d ^ 1 << bit) for d in range(n)])  27.8 us
    ppermute x11, starting transfers between devices, partner(): return lax.ppermute(x, 'outp', [(d, d ^ 1 << bit) for d in range(n)])  17 us
    unnamed x12, local copies, waits for them, and re-layouts  3.67 us
  transfers between devices with their start and end apart: 17, of which 7 were waited for; matrix products, arithmetic and copies ran while one was open for 1% of the time, Pallas kernels for 57%

profile of v12, /device:TPU:0, one launch (start us, length us, event | category | flops | bytes accessed | tf_op | source)
XLA Modules:
  0.0 125.7 jit_solution(13720711289665586073)
XLA Ops:
  1.1 2.7 %collective-permute-start.1 = (bf16[64,4096]{1,0:T(8,128)(2,1)}, bf16[64,4096]{1,0:T(8,128)(2,1)S(1)}, u32[]{:S(2)}, u32[]{:S(2)}) collective-permute-start(bf16[64,4096]{1,0:T(8,128)(2,1)} %refs_0_.5), channel_id=1, source_target_pairs={{0,4},{2,6},{4,0},{6,2},{8,12},{10,14},{12,8},{14,10},{1,5},{3,7},... | collective-permute-start | bytes 1572872 | tf_op jit(solution)/shard_map/ppermute | solution.py:589
  3.8 2.6 %collective-permute-start = (bf16[64,4096]{1,0:T(8,128)(2,1)}, bf16[64,4096]{1,0:T(8,128)(2,1)S(1)}, u32[]{:S(2)}, u32[]{:S(2)}) collective-permute-start(bf16[64,4096]{1,0:T(8,128)(2,1)} %refs_0_.5), channel_id=1, source_target_pairs={{0,8},{2,10},{4,12},{6,14},{8,0},{10,2},{12,4},{14,6},{1,9},{3,11}... | collective-permute-start | bytes 1572872 | tf_op jit(solution)/shard_map/ppermute | solution.py:589
  6.4 1.5 %collective-permute-start.2 = (bf16[64,4096]{1,0:T(8,128)(2,1)}, bf16[64,4096]{1,0:T(8,128)(2,1)S(1)}, u32[]{:S(2)}, u32[]{:S(2)}) collective-permute-start(bf16[64,4096]{1,0:T(8,128)(2,1)} %refs_0_.5), channel_id=1, source_target_pairs={{0,2},{2,0},{4,6},{6,4},{8,10},{10,8},{12,14},{14,12},{1,3},{3,1},... | collective-permute-start | bytes 1572872 | tf_op jit(solution)/shard_map/ppermute | solution.py:589
  10.5 13.9 %backward_0.1 = (bf16[272,2176]{1,0:T(8,128)(2,1)S(1)}, f32[4,4,64,512]{3,2,1,0:T(8,128)S(1)}, f32[128,128]{1,0:T(8,128)S(1)}, f32[8,128]{1,0:T(8,128)S(1)}) custom-call(s32[2]{0:T(128)S(1)} %pad_add_fusion.idx, bf16[256,3584]{1,0:T(8,128)(2,1)S(1)} %copy-done, bf16[256,3584]{1,0:T(8,128)(2,1)} %collective-permute-done.3.refs_1_, ...), custom_call_target="tpu_custom_call" | custom-call | flops 19000000512 | bytes 20971520 | tf_op jit(solution)/shard_map/backward_0/pallas_call | solution.py:55
  25.0 2.7 %collective-permute-done.1.refs_1_ = bf16[64,4096]{1,0:T(8,128)(2,1)S(1)} collective-permute-done((bf16[64,4096]{1,0:T(8,128)(2,1)}, bf16[64,4096]{1,0:T(8,128)(2,1)S(1)}, u32[]{:S(2)}, u32[]{:S(2)}) %collective-permute-start.1) | collective-permute-done | bytes 524320 | tf_op jit(solution)/shard_map/ppermute | solution.py:589
  27.6 2.6 %collective-permute-done.refs_0_ = bf16[64,4096]{1,0:T(8,128)(2,1)S(1)} collective-permute-done((bf16[64,4096]{1,0:T(8,128)(2,1)}, bf16[64,4096]{1,0:T(8,128)(2,1)S(1)}, u32[]{:S(2)}, u32[]{:S(2)}) %collective-permute-start) | collective-permute-done | bytes 524320 | tf_op jit(solution)/shard_map/ppermute | solution.py:589
  31.3 13.8 %backward_4.1 = (bf16[256,2176]{1,0:T(8,128)(2,1)S(1)}, f32[4,4,64,512]{3,2,1,0:T(8,128)S(1)}, f32[8,128]{1,0:T(8,128)S(1)}) custom-call(s32[2]{0:T(128)S(1)} %pad_add_fusion.idx, bf16[256,3584]{1,0:T(8,128)(2,1)S(1)} %copy-done, bf16[256,3584]{1,0:T(8,128)(2,1)} %collective-permute-done.3.refs_1_, bf16[4096,3584]{1,0:T(8,128)(2,1)} %refs_4_.5, ...), custom_call_target="tpu_custom_call" | custom-call | flops 10000000000 | bytes 20971520 | tf_op jit(solution)/shard_map/backward_4/pallas_call | solution.py:55
  45.1 1.7 %collective-permute-start.8 = (bf16[256,2176]{1,0:T(8,128)(2,1)S(1)}, bf16[256,2176]{1,0:T(8,128)(2,1)S(1)}, u32[]{:S(2)}, u32[]{:S(2)}) collective-permute-start(bf16[256,2176]{1,0:T(8,128)(2,1)S(1)} %get-tuple-element.67), channel_id=1, source_target_pairs={{0,4},{2,6},{4,0},{6,2},{8,12},{10,14},{12,8},{14,10},{1,5},{3,7},... | collective-permute-start | bytes 3342344 | tf_op jit(solution)/shard_map/ppermute | solution.py:589
  47.4 1.6 %collective-permute-start.5 = (bf16[192,4096]{1,0:T(8,128)(2,1)S(1)}, bf16[192,4096]{1,0:T(8,128)(2,1)S(1)}, u32[]{:S(2)}, u32[]{:S(2)}) collective-permute-start(bf16[192,4096]{1,0:T(8,128)(2,1)S(1)} %get-tuple-element.58), channel_id=1, source_target_pairs={{0,2},{2,0},{4,6},{6,4},{8,10},{10,8},{12,14},{14,12},{1,3},{3,1},... | collective-permute-start | bytes 4718600 | tf_op jit(solution)/shard_map/ppermute | solution.py:589
  49.0 4.4 %collective-permute-done.6.refs_1_ = bf16[272,2176]{1,0:T(8,128)(2,1)S(1)} collective-permute-done((bf16[272,2176]{1,0:T(8,128)(2,1)S(1)}, bf16[272,2176]{1,0:T(8,128)(2,1)S(1)}, u32[]{:S(2)}, u32[]{:S(2)}) %collective-permute-start.6) | collective-permute-done | bytes 1183776 | tf_op jit(solution)/shard_map/ppermute | solution.py:589
  53.4 2.4 %fold.4 = (bf16[144,2176]{1,0:T(8,128)(2,1)S(1)}, f32[4,2,64,512]{3,2,1,0:T(8,128)S(1)}, f32[128,128]{1,0:T(8,128)S(1)}, f32[8,128]{1,0:T(8,128)S(1)}) custom-call(s32[2]{0:T(128)S(1)} %pad_add_fusion.idx, f32[4,4,64,512]{3,2,1,0:T(8,128)S(1)} %get-tuple-element.59.refs_0_, bf16[272,2176]{1,0:T(8,128)(2,1)S(1)} %collective-permute-done.6.refs_1_, ...), custom_call_target="tpu_custom_call" | custom-call | bytes 6291456 | tf_op jit(solution)/shard_map/fold/pallas_call | solution.py:55
  56.4 12.4 %forward.3 = (f32[128,3584]{1,0:T(8,128)S(1)}, f32[128,3584]{1,0:T(8,128)S(1)}, f32[256,64]{1,0:T(8,128)S(1)}, f32[8,128]{1,0:T(8,128)S(1)}) custom-call(s32[2]{0:T(128)S(1)} %pad_add_fusion.idx, bf16[64,4096]{1,0:T(8,128)(2,1)S(1)} %copy-done.1, bf16[64,4096]{1,0:T(8,128)(2,1)S(1)} %get-tuple-element.54.refs_0_.refs_1_, ...), custom_call_target="tpu_custom_call" | custom-call | flops 17179869184 | bytes 33030144 | tf_op jit(solution)/shard_map/forward/pallas_call | solution.py:55
  68.9 3.8 %collective-permute-done.8.refs_1_ = bf16[256,2176]{1,0:T(8,128)(2,1)S(1)} collective-permute-done((bf16[256,2176]{1,0:T(8,128)(2,1)S(1)}, bf16[256,2176]{1,0:T(8,128)(2,1)S(1)}, u32[]{:S(2)}, u32[]{:S(2)}) %collective-permute-start.8) | collective-permute-done | bytes 1114144 | tf_op jit(solution)/shard_map/ppermute | solution.py:589
  72.6 2.4 %fold.5 = (bf16[128,2176]{1,0:T(8,128)(2,1)S(1)}, f32[4,2,64,512]{3,2,1,0:T(8,128)S(1)}, f32[8,128]{1,0:T(8,128)S(1)}) custom-call(s32[2]{0:T(128)S(1)} %pad_add_fusion.idx, f32[4,4,64,512]{3,2,1,0:T(8,128)S(1)} %get-tuple-element.66.refs_0_, bf16[256,2176]{1,0:T(8,128)(2,1)S(1)} %collective-permute-done.8.refs_1_, f32[8,128]{1,0:T(8,128)S(1)} %get-tuple-element.69.refs_2_), custom_call_target="tpu_custom_call" | custom-call | bytes 6291456 | tf_op jit(solution)/shard_map/fold/pallas_call | solution.py:55
  75.0 1.6 %collective-permute-start.11 = (bf16[128,2176]{1,0:T(8,128)(2,1)S(1)}, bf16[128,2176]{1,0:T(8,128)(2,1)S(1)}, u32[]{:S(2)}, u32[]{:S(2)}) collective-permute-start(bf16[128,2176]{1,0:T(8,128)(2,1)S(1)} %get-tuple-element.76), channel_id=1, source_target_pairs={{0,2},{2,0},{4,6},{6,4},{8,10},{10,8},{12,14},{14,12},{1,3},{3,1},... | collective-permute-start | bytes 1671176 | tf_op jit(solution)/shard_map/ppermute | solution.py:589
  76.6 7.7 %collective-permute-done.7.refs_1_ = bf16[144,2176]{1,0:T(8,128)(2,1)S(1)} collective-permute-done((bf16[144,2176]{1,0:T(8,128)(2,1)S(1)}, bf16[144,2176]{1,0:T(8,128)(2,1)S(1)}, u32[]{:S(2)}, u32[]{:S(2)}) %collective-permute-start.7) | collective-permute-done | bytes 626720 | tf_op jit(solution)/shard_map/ppermute | solution.py:589
  85.8 2.4 %collective-permute-start.9 = (bf16[80,2176]{1,0:T(8,128)(2,1)S(1)}, bf16[80,2176]{1,0:T(8,128)(2,1)S(1)}, u32[]{:S(2)}, u32[]{:S(2)}) collective-permute-start(bf16[80,2176]{1,0:T(8,128)(2,1)S(1)} %get-tuple-element.72), channel_id=1, source_target_pairs={{0,8},{2,10},{4,12},{6,14},{8,0},{10,2},{12,4},{14,6},{1,9},{3,11}... | collective-permute-start | bytes 1044488 | tf_op jit(solution)/shard_map/ppermute | solution.py:589
  88.2 8.4 %forward.4 = (f32[128,2048]{1,0:T(8,128)S(1)}, f32[128,2048]{1,0:T(8,128)S(1)}, f32[256,64]{1,0:T(8,128)S(1)}, f32[8,128]{1,0:T(8,128)S(1)}) custom-call(s32[2]{0:T(128)S(1)} %pad_add_fusion.idx, bf16[64,4096]{1,0:T(8,128)(2,1)S(1)} %get-tuple-element.53.refs_0_, bf16[192,4096]{1,0:T(8,128)(2,1)S(1)} %collective-permute-done.5.refs_1_.refs_2_.refs_3_, ...), custom_call_target="tpu_custom_call" | custom-call | flops 17179869184 | bytes 18874368 | tf_op jit(solution)/shard_map/forward/pallas_call | solution.py:55
  100.6 2.0 %combine.3 = (bf16[256,3584]{1,0:T(8,128)(2,1)}, f32[8,128]{1,0:T(8,128)S(1)}) custom-call(s32[2]{0:T(128)S(1)} %pad_add_fusion.idx, f32[128,3584]{1,0:T(8,128)S(1)} %get-tuple-element.73.refs_0_, f32[128,3584]{1,0:T(8,128)S(1)} %collective-permute-done.10.refs_1_, f32[8,128]{1,0:T(8,128)S(1)} %get-tuple-element.79.refs_2_), custom_call_target="tpu_custom_call" | custom-call | flops 17179869184 | bytes 4587520 | tf_op jit(solution)/shard_map/combine/pallas_call | solution.py:55
  102.6 5.6 %collective-permute-done.9.refs_1_.refs_2_ = bf16[80,2176]{1,0:T(8,128)(2,1)S(1)} collective-permute-done((bf16[80,2176]{1,0:T(8,128)(2,1)S(1)}, bf16[80,2176]{1,0:T(8,128)(2,1)S(1)}, u32[]{:S(2)}, u32[]{:S(2)}) %collective-permute-start.9) | collective-permute-done | bytes 348192 | tf_op jit(solution)/shard_map/ppermute | solution.py:589
  108.8 7.8 %forward.5 = (f32[128,1536]{1,0:T(8,128)}, f32[128,1536]{1,0:T(8,128)S(1)}, f32[8,128]{1,0:T(8,128)S(1)}) custom-call(s32[2]{0:T(128)S(1)} %pad_add_fusion.idx, bf16[64,4096]{1,0:T(8,128)(2,1)S(1)} %get-tuple-element.53.refs_0_, bf16[192,4096]{1,0:T(8,128)(2,1)S(1)} %collective-permute-done.5.refs_1_.refs_2_.refs_3_, ...), custom_call_target="tpu_custom_call" | custom-call | flops 17179869184 | bytes 14155776 | tf_op jit(solution)/shard_map/forward/pallas_call | solution.py:55
  118.3 1.6 %combine.4 = (bf16[256,3584]{1,0:T(8,128)(2,1)}, f32[8,128]{1,0:T(8,128)S(1)}) custom-call(s32[2]{0:T(128)S(1)} %pad_add_fusion.idx, f32[128,2048]{1,0:T(8,128)S(1)} %get-tuple-element.84.refs_0_, f32[128,2048]{1,0:T(8,128)S(1)} %collective-permute-done.13.refs_1_, bf16[256,3584]{1,0:T(8,128)(2,1)} %get-tuple-element.86.refs_2_, ...), custom_call_target="tpu_custom_call", output_to_operand_aliasing={{0}: (3, {})} | custom-call | flops 17179869184 | bytes 2621440 | tf_op jit(solution)/shard_map/combine/pallas_call | solution.py:55
  121.9 1.7 %combine.5 = (bf16[256,3584]{1,0:T(8,128)(2,1)}, f32[8,128]{1,0:T(8,128)S(1)}) custom-call(s32[2]{0:T(128)S(1)} %pad_add_fusion.idx, f32[128,1536]{1,0:T(8,128)S(1)} %copy-done.5, f32[128,1536]{1,0:T(8,128)S(1)} %collective-permute-done.12.refs_1_, bf16[256,3584]{1,0:T(8,128)(2,1)} %get-tuple-element.92.refs_2_, ...), custom_call_target="tpu_custom_call", output_to_operand_aliasing={{0}: (3, {})} | custom-call | flops 17179869184 | bytes 1966080 | tf_op jit(solution)/shard_map/combine/pallas_call | solution.py:55
  123.6 2.1 %finish.1 = (bf16[64,4096]{1,0:T(8,128)(2,1)}, f32[8,128]{1,0:T(8,128)}) custom-call(s32[2]{0:T(128)S(1)} %pad_add_fusion.idx, f32[4,1,64,512]{3,2,1,0:T(8,128)S(1)} %get-tuple-element.95.refs_0_, f32[4,1,64,512]{3,2,1,0:T(8,128)S(1)} %get-tuple-element.96.refs_1_, bf16[80,2176]{1,0:T(8,128)(2,1)S(1)} %collective-permute-done.9.refs_1_.refs_2_, ...), custom_call_target="tpu_custom_call" | custom-call | bytes 2097152 | tf_op jit(solution)/shard_map/finish/pallas_call | solution.py:55
  (42 shorter events, 15.7 us)
Async XLA Ops:
  0.6 7.4 %collective-permute-start.3 = (bf16[256,3584]{1,0:T(8,128)(2,1)}, bf16[256,3584]{1,0:T(8,128)(2,1)}, u32[]{:S(2)}, u32[]{:S(2)}) collective-permute-start(bf16[256,3584]{1,0:T(8,128)(2,1)} %refs_0_.4), channel_id=1, source_target_pairs={{0,1},{1,0},{2,3},{3,2},{4,5},{5,4},{6,7},{7,6},{8,9},{9,8},{10,11... | collective-permute-start | bytes 5505032 | tf_op jit(solution)/shard_map/ppermute | solution.py:592
  1.1 26.5 %collective-permute-start.1 = (bf16[64,4096]{1,0:T(8,128)(2,1)}, bf16[64,4096]{1,0:T(8,128)(2,1)S(1)}, u32[]{:S(2)}, u32[]{:S(2)}) collective-permute-start(bf16[64,4096]{1,0:T(8,128)(2,1)} %refs_0_.5), channel_id=1, source_target_pairs={{0,4},{2,6},{4,0},{6,2},{8,12},{10,14},{12,8},{14,10},{1,5},{3,7},... | collective-permute-start | bytes 1572872 | tf_op jit(solution)/shard_map/ppermute | solution.py:589
  3.8 26.4 %collective-permute-start = (bf16[64,4096]{1,0:T(8,128)(2,1)}, bf16[64,4096]{1,0:T(8,128)(2,1)S(1)}, u32[]{:S(2)}, u32[]{:S(2)}) collective-permute-start(bf16[64,4096]{1,0:T(8,128)(2,1)} %refs_0_.5), channel_id=1, source_target_pairs={{0,8},{2,10},{4,12},{6,14},{8,0},{10,2},{12,4},{14,6},{1,9},{3,11}... | collective-permute-start | bytes 1572872 | tf_op jit(solution)/shard_map/ppermute | solution.py:589
  6.4 23.8 %collective-permute-start.2 = (bf16[64,4096]{1,0:T(8,128)(2,1)}, bf16[64,4096]{1,0:T(8,128)(2,1)S(1)}, u32[]{:S(2)}, u32[]{:S(2)}) collective-permute-start(bf16[64,4096]{1,0:T(8,128)(2,1)} %refs_0_.5), channel_id=1, source_target_pairs={{0,2},{2,0},{4,6},{6,4},{8,10},{10,8},{12,14},{14,12},{1,3},{3,1},... | collective-permute-start | bytes 1572872 | tf_op jit(solution)/shard_map/ppermute | solution.py:589
  8.0 1.5 %copy-start = (bf16[256,3584]{1,0:T(8,128)(2,1)S(1)}, bf16[256,3584]{1,0:T(8,128)(2,1)}, u32[]{:S(2)}) copy-start(bf16[256,3584]{1,0:T(8,128)(2,1)} %refs_0_.4) | copy-start | bytes 5505028
  9.5 1.0 copy-start.3
  24.4 29.0 %collective-permute-start.6 = (bf16[272,2176]{1,0:T(8,128)(2,1)S(1)}, bf16[272,2176]{1,0:T(8,128)(2,1)S(1)}, u32[]{:S(2)}, u32[]{:S(2)}) collective-permute-start(bf16[272,2176]{1,0:T(8,128)(2,1)S(1)} %get-tuple-element.60), channel_id=1, source_target_pairs={{0,2},{2,0},{4,6},{6,4},{8,10},{10,8},{12,14},{14,12},{1,3},{3,1},... | collective-permute-start | bytes 3551240 | tf_op jit(solution)/shard_map/ppermute | solution.py:589
  30.8 16.0 %collective-permute-start.4 = (bf16[64,4096]{1,0:T(8,128)(2,1)S(1)}, bf16[64,4096]{1,0:T(8,128)(2,1)S(1)}, u32[]{:S(2)}, u32[]{:S(2)}) collective-permute-start(bf16[64,4096]{1,0:T(8,128)(2,1)S(1)} %get-tuple-element.55.refs_1_.refs_2_), channel_id=1, source_target_pairs={{0,4},{2,6},{4,0},{6,2},{8,12},{10,14},{12,8},{14,10},{1,5},{3,7},... | collective-permute-start | bytes 1572872 | tf_op jit(solution)/shard_map/ppermute | solution.py:589
  45.1 27.6 %collective-permute-start.8 = (bf16[256,2176]{1,0:T(8,128)(2,1)S(1)}, bf16[256,2176]{1,0:T(8,128)(2,1)S(1)}, u32[]{:S(2)}, u32[]{:S(2)}) collective-permute-start(bf16[256,2176]{1,0:T(8,128)(2,1)S(1)} %get-tuple-element.67), channel_id=1, source_target_pairs={{0,4},{2,6},{4,0},{6,2},{8,12},{10,14},{12,8},{14,10},{1,5},{3,7},... | collective-permute-start | bytes 3342344 | tf_op jit(solution)/shard_map/ppermute | solution.py:589
  47.4 9.0 %copy-start.1 = (bf16[64,4096]{1,0:T(8,128)(2,1)S(1)}, bf16[64,4096]{1,0:T(8,128)(2,1)}, u32[]{:S(2)}) copy-start(bf16[64,4096]{1,0:T(8,128)(2,1)} %refs_0_.5) | copy-start | bytes 1572868
  47.4 8.9 %copy-start.2 = (bf16[64,4096]{1,0:T(8,128)(2,1)S(1)}, bf16[64,4096]{1,0:T(8,128)(2,1)}, u32[]{:S(2)}) copy-start(bf16[64,4096]{1,0:T(8,128)(2,1)} %refs_5_.3) | copy-start | bytes 1572868
  47.4 40.8 %collective-permute-start.5 = (bf16[192,4096]{1,0:T(8,128)(2,1)S(1)}, bf16[192,4096]{1,0:T(8,128)(2,1)S(1)}, u32[]{:S(2)}, u32[]{:S(2)}) collective-permute-start(bf16[192,4096]{1,0:T(8,128)(2,1)S(1)} %get-tuple-element.58), channel_id=1, source_target_pairs={{0,2},{2,0},{4,6},{6,4},{8,10},{10,8},{12,14},{14,12},{1,3},{3,1},... | collective-permute-start | bytes 4718600 | tf_op jit(solution)/shard_map/ppermute | solution.py:589
  55.8 28.5 %collective-permute-start.7 = (bf16[144,2176]{1,0:T(8,128)(2,1)S(1)}, bf16[144,2176]{1,0:T(8,128)(2,1)S(1)}, u32[]{:S(2)}, u32[]{:S(2)}) collective-permute-start(bf16[144,2176]{1,0:T(8,128)(2,1)S(1)} %get-tuple-element.64), channel_id=1, source_target_pairs={{0,4},{2,6},{4,0},{6,2},{8,12},{10,14},{12,8},{14,10},{1,5},{3,7},... | collective-permute-start | bytes 1880072 | tf_op jit(solution)/shard_map/ppermute | solution.py:589
  68.8 31.8 %collective-permute-start.10 = (f32[128,3584]{1,0:T(8,128)S(1)}, f32[128,3584]{1,0:T(8,128)S(1)}, u32[]{:S(2)}, u32[]{:S(2)}) collective-permute-start(f32[128,3584]{1,0:T(8,128)S(1)} %get-tuple-element.74), channel_id=1, source_target_pairs={{0,1},{1,0},{2,3},{3,2},{4,5},{5,4},{6,7},{7,6},{8,9},{9,8},{10,11... | collective-permute-start | bytes 5505032 | tf_op jit(solution)/shard_map/ppermute | solution.py:592
  75.0 22.6 %collective-permute-start.11 = (bf16[128,2176]{1,0:T(8,128)(2,1)S(1)}, bf16[128,2176]{1,0:T(8,128)(2,1)S(1)}, u32[]{:S(2)}, u32[]{:S(2)}) collective-permute-start(bf16[128,2176]{1,0:T(8,128)(2,1)S(1)} %get-tuple-element.76), channel_id=1, source_target_pairs={{0,2},{2,0},{4,6},{6,4},{8,10},{10,8},{12,14},{14,12},{1,3},{3,1},... | collective-permute-start | bytes 1671176 | tf_op jit(solution)/shard_map/ppermute | solution.py:589
  85.8 22.4 %collective-permute-start.9 = (bf16[80,2176]{1,0:T(8,128)(2,1)S(1)}, bf16[80,2176]{1,0:T(8,128)(2,1)S(1)}, u32[]{:S(2)}, u32[]{:S(2)}) collective-permute-start(bf16[80,2176]{1,0:T(8,128)(2,1)S(1)} %get-tuple-element.72), channel_id=1, source_target_pairs={{0,8},{2,10},{4,12},{6,14},{8,0},{10,2},{12,4},{14,6},{1,9},{3,11}... | collective-permute-start | bytes 1044488 | tf_op jit(solution)/shard_map/ppermute | solution.py:589
  99.1 24.4 %collective-permute-start.15 = (bf16[64,2176]{1,0:T(8,128)(2,1)S(1)}, bf16[64,2176]{1,0:T(8,128)(2,1)S(1)}, u32[]{:S(2)}, u32[]{:S(2)}) collective-permute-start(bf16[64,2176]{1,0:T(8,128)(2,1)S(1)} %get-tuple-element.97), channel_id=1, source_target_pairs={{0,8},{2,10},{4,12},{6,14},{8,0},{10,2},{12,4},{14,6},{1,9},{3,11}... | collective-permute-start | bytes 835592 | tf_op jit(solution)/shard_map/ppermute | solution.py:589
  100.6 17.7 %collective-permute-start.13 = (f32[128,2048]{1,0:T(8,128)S(1)}, f32[128,2048]{1,0:T(8,128)S(1)}, u32[]{:S(2)}, u32[]{:S(2)}) collective-permute-start(f32[128,2048]{1,0:T(8,128)S(1)} %get-tuple-element.85), channel_id=1, source_target_pairs={{0,1},{1,0},{2,3},{3,2},{4,5},{5,4},{6,7},{7,6},{8,9},{9,8},{10,11... | collective-permute-start | bytes 3145736 | tf_op jit(solution)/shard_map/ppermute | solution.py:592
  108.8 8.5 %collective-permute-start.14 = (f32[128,128]{1,0:T(8,128)S(1)}, f32[128,128]{1,0:T(8,128)S(1)}, u32[]{:S(2)}, u32[]{:S(2)}) collective-permute-start(f32[128,128]{1,0:T(8,128)S(1)} %get-tuple-element.89.refs_2_), channel_id=1, source_target_pairs={{0,1},{1,0},{2,3},{3,2},{4,5},{5,4},{6,7},{7,6},{8,9},{9,8},{10,11... | collective-permute-start | bytes 196616 | tf_op jit(solution)/shard_map/ppermute | solution.py:592
  116.7 1.6 %copy-start.4 = (f32[128,1536]{1,0:T(8,128)}, f32[128,1536]{1,0:T(8,128)S(1)}, u32[]{:S(2)}) copy-start(f32[128,1536]{1,0:T(8,128)S(1)} %get-tuple-element.82.refs_0_) | copy-start | bytes 2359300
  116.7 4.1 %collective-permute-start.12 = (f32[128,1536]{1,0:T(8,128)}, f32[128,1536]{1,0:T(8,128)S(1)}, u32[]{:S(2)}, u32[]{:S(2)}) collective-permute-start(f32[128,1536]{1,0:T(8,128)} %get-tuple-element.83), channel_id=1, source_target_pairs={{0,1},{1,0},{2,3},{3,2},{4,5},{5,4},{6,7},{7,6},{8,9},{9,8},{10,11... | collective-permute-start | bytes 2359304 | tf_op jit(solution)/shard_map/ppermute | solution.py:592
  118.2 1.7 %collective-permute-start.16 = (f32[4,64,64]{2,1,0:T(8,128)S(1)}, f32[4,64,64]{2,1,0:T(8,128)S(1)}, u32[]{:S(2)}, u32[]{:S(2)}) collective-permute-start(f32[4,64,64]{2,1,0:T(8,128)S(1)} %get-tuple-element.100), channel_id=1, source_target_pairs={{0,1},{1,0},{2,3},{3,2},{4,5},{5,4},{6,7},{7,6},{8,9},{9,8},{10,11... | collective-permute-start | bytes 196616 | tf_op jit(solution)/shard_map/ppermute | solution.py:592
  120.8 1.1 copy-start.5

commit v13 on v11

--- a/solution.py
+++ b/solution.py
@@ -19,7 +19,7 @@
 SLOTS = 3
 RIGHT_ROWS = 16
 RIGHT_PARTS = 2
-TIMES = {"gate": 0, "backward_0": 19 * 10**9, "backward_4": 10 * 10**9, "forward": 1 << 34, "fold": 0, "combine": 1 << 34, "sketch_part": 1 << 34}
+TIMES = {"gate": 0, "backward_0": 19 * 10**9, "backward_4": 10 * 10**9, "forward": 1 << 34, "fold": 0, "combine": 1 << 34, "sketch_part": 1 << 36, "last_right": 1 << 34}
 ANY = pl.BlockSpec(memory_space=pl.ANY)
 HBM = pl.BlockSpec(memory_space=pltpu.HBM)
 
@@ -475,40 +475,43 @@
     )
 
 
-def combine(idx, keep, got, lo, total, batch, rows, before, after):
-    part, width = keep.shape
+def combine(idx, pieces, total, rows, batch, before, after):
+    part = pieces[0][0].shape[0]
     m = part // rows
 
-    def kernel(idx, keep, got, *refs):
-        out, x, sems = refs[-3:]
+    def kernel(idx, *refs):
+        out, sems = refs[-2 - len(pieces)], refs[-1]
         mine = (idx[0] & 1) ^ batch
-        x[...] = (keep[...] + got[...]).astype(jnp.bfloat16)
         copies = []
-        for i in range(m):
-            to = pl.ds(pl.multiple_of((2 * i + mine) * rows, BLK), rows)
-            copies.append(
-                pltpu.make_async_copy(
-                    x.at[pl.ds(i * rows, rows)], out.at[to, pl.ds(lo, width)], sems.at[i]
+        for k, (keep, _, lo) in enumerate(pieces):
+            x = refs[k - 1 - len(pieces)]
+            x[...] = (refs[2 * k][...] + refs[2 * k + 1][...]).astype(jnp.bfloat16)
+            for i in range(m):
+                to = pl.ds(pl.multiple_of((2 * i + mine) * rows, BLK), rows)
+                dst = out.at[to, pl.ds(lo, keep.shape[1])]
+                copies.append(
+                    pltpu.make_async_copy(x.at[pl.ds(i * rows, rows)], dst, sems.at[k, i])
                 )
-            )
-        for c in copies:
-            c.start()
+                copies[-1].start()
         for c in copies:
             c.wait()
 
+    flat = [a for keep, got, _ in pieces for a in (keep, got)]
+    width = sum(keep.shape[1] for keep, _, _ in pieces)
     (out,), token = call(
         kernel,
         idx,
-        [keep, got] + before,
-        [whole(keep.shape)] * 2 + [HBM] * len(before),
+        flat + before,
+        [whole(a.shape) for a in flat] + [HBM] * len(before),
         [jax.ShapeDtypeStruct((2 * part, total), jnp.bfloat16)],
         [HBM],
         "combine",
         (1,),
         (0, 10 * part * width),
         after,
-        [pltpu.VMEM((part, width), jnp.bfloat16), pltpu.SemaphoreType.DMA((m,))],
-        aliases={3: 0} if before else None,
+        [pltpu.VMEM(keep.shape, jnp.bfloat16) for keep, _, _ in pieces]
+        + [pltpu.SemaphoreType.DMA((len(pieces), m))],
+        aliases={1 + len(flat): 0} if before else None,
     )
     return out, [token]
 
@@ -645,7 +648,7 @@
             parts = [(m, chunks[m], 0) for m in [0] + evens]
         outs, t = forward(idx, parts, rows, weight, None if lo else in_sketch, lo, hi, after)
         start = lo * (hidden // tiles)
-        return (outs[1], swap(outs[0]), start, hidden, batch, rows), outs[-1], [t]
+        return (outs[1], swap(outs[0]), start), outs[-1], [t]
 
     cut = -(-tiles // 2)
     token = folded(0, 1, token)
@@ -654,15 +657,14 @@
     token = folded(0, 2, token)
     second, left2, token = batch_forward(1, 0, cut, token)
     token = folded(1, 2, token)
-    outputs, token = combine(idx, *first, [], token)
+    outputs, token = combine(idx, [first], hidden, rows, 0, [], token)
     third, _, token = batch_forward(1, cut, tiles, token)
     for step in range(3, bits):
         for p in range(PIECES):
             token = folded(p, step, token)
     right, token = last_right(idx, rights[0], msgs[0], token)
     right_got = swap(right)
-    outputs, token = combine(idx, *second, [outputs], token)
-    outputs, token = combine(idx, *third, [outputs], token)
+    outputs, token = combine(idx, [second, third], hidden, rows, 1, [outputs], token)
     part, token = sketch_part(idx, [left1, left2], right, right_got, rows, token)
     input_grad = finish(idx, keeps, msgs, token)
     part = (part + swap(part)) * (1.0 / LEN**0.5)

time: 118 us -> 118 us (level)
    pallas_call x17 -> x16, Pallas kernels: 72.1 us -> 71 us  [call(): pl.pallas_call(with_token, out_shape=list(out_shape) + [token], grid_spec...]
  transfers between devices with their start and end apart: 17 -> 17, of which waited for: 7 -> 7; matrix products, arithmetic and copies ran while one was open for 0% -> 0% of each run, Pallas kernels for 61% -> 60%
where the time goes in v13:
time: 118 us
  Pallas kernels  71 us (60%)
  waiting for transfers between devices  23.9 us (20%)
  starting transfers between devices  18.6 us (16%)
  local copies, waits for them, and re-layouts  3.27 us (3%)
    pallas_call x16, Pallas kernels, call(): pl.pallas_call(with_token, out_shape=list(out_shape) + [token], grid_spec...  71 us
    ppermute x11, waiting for transfers between devices, partner(): return lax.ppermute(x, 'outp', [(d, d ^ 1 << bit) for d in range(n)])  22.7 us
    ppermute x11, starting transfers between devices, partner(): return lax.ppermute(x, 'outp', [(d, d ^ 1 << bit) for d in range(n)])  16.9 us
    unnamed x8, local copies, waits for them, and re-layouts  2.53 us
  transfers between devices with their start and end apart: 17, of which 7 were waited for; matrix products, arithmetic and copies ran while one was open for 0% of the time, Pallas kernels for 60%

profile of v13, /device:TPU:0, one launch (start us, length us, event | category | flops | bytes accessed | tf_op | source)
XLA Modules:
  0.0 117.6 jit_solution(5385946907444288247)
XLA Ops:
  1.1 2.7 %collective-permute-start.1 = (bf16[64,4096]{1,0:T(8,128)(2,1)}, bf16[64,4096]{1,0:T(8,128)(2,1)S(1)}, u32[]{:S(2)}, u32[]{:S(2)}) collective-permute-start(bf16[64,4096]{1,0:T(8,128)(2,1)} %refs_0_.5), channel_id=1, source_target_pairs={{0,4},{2,6},{4,0},{6,2},{8,12},{10,14},{12,8},{14,10},{1,5},{3,7},... | collective-permute-start | bytes 1572872 | tf_op jit(solution)/shard_map/ppermute | solution.py:574
  3.8 2.6 %collective-permute-start = (bf16[64,4096]{1,0:T(8,128)(2,1)}, bf16[64,4096]{1,0:T(8,128)(2,1)S(1)}, u32[]{:S(2)}, u32[]{:S(2)}) collective-permute-start(bf16[64,4096]{1,0:T(8,128)(2,1)} %refs_0_.5), channel_id=1, source_target_pairs={{0,8},{2,10},{4,12},{6,14},{8,0},{10,2},{12,4},{14,6},{1,9},{3,11}... | collective-permute-start | bytes 1572872 | tf_op jit(solution)/shard_map/ppermute | solution.py:574
  6.4 1.5 %collective-permute-start.2 = (bf16[64,4096]{1,0:T(8,128)(2,1)}, bf16[64,4096]{1,0:T(8,128)(2,1)S(1)}, u32[]{:S(2)}, u32[]{:S(2)}) collective-permute-start(bf16[64,4096]{1,0:T(8,128)(2,1)} %refs_0_.5), channel_id=1, source_target_pairs={{0,2},{2,0},{4,6},{6,4},{8,10},{10,8},{12,14},{14,12},{1,3},{3,1},... | collective-permute-start | bytes 1572872 | tf_op jit(solution)/shard_map/ppermute | solution.py:574
  8.0 1.5 %copy-done = bf16[256,3584]{1,0:T(8,128)(2,1)S(1)} copy-done((bf16[256,3584]{1,0:T(8,128)(2,1)S(1)}, bf16[256,3584]{1,0:T(8,128)(2,1)}, u32[]{:S(2)}) %copy-start) | copy-done | bytes 1835032
  10.5 13.6 %backward_0.1 = (bf16[272,2176]{1,0:T(8,128)(2,1)S(1)}, f32[4,4,64,512]{3,2,1,0:T(8,128)S(1)}, f32[128,128]{1,0:T(8,128)S(1)}, f32[8,128]{1,0:T(8,128)S(1)}) custom-call(s32[2]{0:T(128)S(1)} %pad_add_fusion.idx, bf16[256,3584]{1,0:T(8,128)(2,1)S(1)} %copy-done, bf16[256,3584]{1,0:T(8,128)(2,1)S(1)} %collective-permute-done.3.refs_1_, ...), custom_call_target="tpu_custom_call" | custom-call | flops 19000000512 | bytes 20971520 | tf_op jit(solution)/shard_map/backward_0/pallas_call | solution.py:55
  24.7 2.9 %collective-permute-done.1.refs_1_ = bf16[64,4096]{1,0:T(8,128)(2,1)S(1)} collective-permute-done((bf16[64,4096]{1,0:T(8,128)(2,1)}, bf16[64,4096]{1,0:T(8,128)(2,1)S(1)}, u32[]{:S(2)}, u32[]{:S(2)}) %collective-permute-start.1) | collective-permute-done | bytes 524320 | tf_op jit(solution)/shard_map/ppermute | solution.py:574
  27.6 2.6 %collective-permute-done.refs_0_ = bf16[64,4096]{1,0:T(8,128)(2,1)S(1)} collective-permute-done((bf16[64,4096]{1,0:T(8,128)(2,1)}, bf16[64,4096]{1,0:T(8,128)(2,1)S(1)}, u32[]{:S(2)}, u32[]{:S(2)}) %collective-permute-start) | collective-permute-done | bytes 524320 | tf_op jit(solution)/shard_map/ppermute | solution.py:574
  31.3 13.4 %backward_4.1 = (bf16[256,2176]{1,0:T(8,128)(2,1)S(1)}, f32[4,4,64,512]{3,2,1,0:T(8,128)S(1)}, f32[8,128]{1,0:T(8,128)S(1)}) custom-call(s32[2]{0:T(128)S(1)} %pad_add_fusion.idx, bf16[256,3584]{1,0:T(8,128)(2,1)S(1)} %copy-done, bf16[256,3584]{1,0:T(8,128)(2,1)S(1)} %collective-permute-done.3.refs_1_, bf16[4096,3584]{1,0:T(8,128)(2,1)} %refs_4_.5, ...), custom_call_target="tpu_custom_call" | custom-call | flops 10000000000 | bytes 20971520 | tf_op jit(solution)/shard_map/backward_4/pallas_call | solution.py:55
  44.6 1.7 %collective-permute-start.8 = (bf16[256,2176]{1,0:T(8,128)(2,1)S(1)}, bf16[256,2176]{1,0:T(8,128)(2,1)S(1)}, u32[]{:S(2)}, u32[]{:S(2)}) collective-permute-start(bf16[256,2176]{1,0:T(8,128)(2,1)S(1)} %get-tuple-element.65), channel_id=1, source_target_pairs={{0,4},{2,6},{4,0},{6,2},{8,12},{10,14},{12,8},{14,10},{1,5},{3,7},... | collective-permute-start | bytes 3342344 | tf_op jit(solution)/shard_map/ppermute | solution.py:574
  47.0 1.6 %collective-permute-start.5 = (bf16[192,4096]{1,0:T(8,128)(2,1)S(1)}, bf16[192,4096]{1,0:T(8,128)(2,1)S(1)}, u32[]{:S(2)}, u32[]{:S(2)}) collective-permute-start(bf16[192,4096]{1,0:T(8,128)(2,1)S(1)} %get-tuple-element.56), channel_id=1, source_target_pairs={{0,2},{2,0},{4,6},{6,4},{8,10},{10,8},{12,14},{14,12},{1,3},{3,1},... | collective-permute-start | bytes 4718600 | tf_op jit(solution)/shard_map/ppermute | solution.py:574
  48.6 4.6 %collective-permute-done.6.refs_1_ = bf16[272,2176]{1,0:T(8,128)(2,1)S(1)} collective-permute-done((bf16[272,2176]{1,0:T(8,128)(2,1)S(1)}, bf16[272,2176]{1,0:T(8,128)(2,1)S(1)}, u32[]{:S(2)}, u32[]{:S(2)}) %collective-permute-start.6) | collective-permute-done | bytes 1183776 | tf_op jit(solution)/shard_map/ppermute | solution.py:574
  53.2 2.4 %fold.4 = (bf16[144,2176]{1,0:T(8,128)(2,1)S(1)}, f32[4,2,64,512]{3,2,1,0:T(8,128)S(1)}, f32[128,128]{1,0:T(8,128)S(1)}, f32[8,128]{1,0:T(8,128)S(1)}) custom-call(s32[2]{0:T(128)S(1)} %pad_add_fusion.idx, f32[4,4,64,512]{3,2,1,0:T(8,128)S(1)} %get-tuple-element.57.refs_0_, bf16[272,2176]{1,0:T(8,128)(2,1)S(1)} %collective-permute-done.6.refs_1_, ...), custom_call_target="tpu_custom_call" | custom-call | bytes 6291456 | tf_op jit(solution)/shard_map/fold/pallas_call | solution.py:55
  56.1 12.4 %forward.3 = (f32[128,3584]{1,0:T(8,128)S(1)}, f32[128,3584]{1,0:T(8,128)S(1)}, f32[256,64]{1,0:T(8,128)S(1)}, f32[8,128]{1,0:T(8,128)S(1)}) custom-call(s32[2]{0:T(128)S(1)} %pad_add_fusion.idx, bf16[64,4096]{1,0:T(8,128)(2,1)S(1)} %copy-done.1, bf16[64,4096]{1,0:T(8,128)(2,1)S(1)} %get-tuple-element.52.refs_0_.refs_1_, ...), custom_call_target="tpu_custom_call" | custom-call | flops 17179869184 | bytes 33030144 | tf_op jit(solution)/shard_map/forward/pallas_call | solution.py:55
  68.6 3.6 %collective-permute-done.8.refs_1_ = bf16[256,2176]{1,0:T(8,128)(2,1)S(1)} collective-permute-done((bf16[256,2176]{1,0:T(8,128)(2,1)S(1)}, bf16[256,2176]{1,0:T(8,128)(2,1)S(1)}, u32[]{:S(2)}, u32[]{:S(2)}) %collective-permute-start.8) | collective-permute-done | bytes 1114144 | tf_op jit(solution)/shard_map/ppermute | solution.py:574
  72.2 2.4 %fold.5 = (bf16[128,2176]{1,0:T(8,128)(2,1)S(1)}, f32[4,2,64,512]{3,2,1,0:T(8,128)S(1)}, f32[8,128]{1,0:T(8,128)S(1)}) custom-call(s32[2]{0:T(128)S(1)} %pad_add_fusion.idx, f32[4,4,64,512]{3,2,1,0:T(8,128)S(1)} %get-tuple-element.64.refs_0_, bf16[256,2176]{1,0:T(8,128)(2,1)S(1)} %collective-permute-done.8.refs_1_, f32[8,128]{1,0:T(8,128)S(1)} %get-tuple-element.67.refs_2_), custom_call_target="tpu_custom_call" | custom-call | bytes 6291456 | tf_op jit(solution)/shard_map/fold/pallas_call | solution.py:55
  74.6 1.6 %collective-permute-start.11 = (bf16[128,2176]{1,0:T(8,128)(2,1)S(1)}, bf16[128,2176]{1,0:T(8,128)(2,1)S(1)}, u32[]{:S(2)}, u32[]{:S(2)}) collective-permute-start(bf16[128,2176]{1,0:T(8,128)(2,1)S(1)} %get-tuple-element.75), channel_id=1, source_target_pairs={{0,2},{2,0},{4,6},{6,4},{8,10},{10,8},{12,14},{14,12},{1,3},{3,1},... | collective-permute-start | bytes 1671176 | tf_op jit(solution)/shard_map/ppermute | solution.py:574
  76.2 7.7 %collective-permute-done.7.refs_1_ = bf16[144,2176]{1,0:T(8,128)(2,1)S(1)} collective-permute-done((bf16[144,2176]{1,0:T(8,128)(2,1)S(1)}, bf16[144,2176]{1,0:T(8,128)(2,1)S(1)}, u32[]{:S(2)}, u32[]{:S(2)}) %collective-permute-start.7) | collective-permute-done | bytes 626720 | tf_op jit(solution)/shard_map/ppermute | solution.py:574
  83.9 1.5 %fold.6 = (bf16[80,2176]{1,0:T(8,128)(2,1)S(1)}, f32[4,1,64,512]{3,2,1,0:T(8,128)S(1)}, f32[128,128]{1,0:T(8,128)S(1)}, f32[8,128]{1,0:T(8,128)S(1)}) custom-call(s32[2]{0:T(128)S(1)} %pad_add_fusion.idx, f32[4,2,64,512]{3,2,1,0:T(8,128)S(1)} %get-tuple-element.61.refs_0_, bf16[144,2176]{1,0:T(8,128)(2,1)S(1)} %collective-permute-done.7.refs_1_, ...), custom_call_target="tpu_custom_call" | custom-call | bytes 3145728 | tf_op jit(solution)/shard_map/fold/pallas_call | solution.py:55
  85.4 2.4 %collective-permute-start.13 = (bf16[80,2176]{1,0:T(8,128)(2,1)S(1)}, bf16[80,2176]{1,0:T(8,128)(2,1)S(1)}, u32[]{:S(2)}, u32[]{:S(2)}) collective-permute-start(bf16[80,2176]{1,0:T(8,128)(2,1)S(1)} %get-tuple-element.83), channel_id=1, source_target_pairs={{0,8},{2,10},{4,12},{6,14},{8,0},{10,2},{12,4},{14,6},{1,9},{3,11}... | collective-permute-start | bytes 1044488 | tf_op jit(solution)/shard_map/ppermute | solution.py:574
  87.8 8.4 %forward.4 = (f32[128,2048]{1,0:T(8,128)S(1)}, f32[128,2048]{1,0:T(8,128)S(1)}, f32[256,64]{1,0:T(8,128)S(1)}, f32[8,128]{1,0:T(8,128)S(1)}) custom-call(s32[2]{0:T(128)S(1)} %pad_add_fusion.idx, bf16[64,4096]{1,0:T(8,128)(2,1)S(1)} %get-tuple-element.51.refs_0_, bf16[192,4096]{1,0:T(8,128)(2,1)S(1)} %collective-permute-done.5.refs_1_.refs_2_.refs_3_, ...), custom_call_target="tpu_custom_call" | custom-call | flops 17179869184 | bytes 18874368 | tf_op jit(solution)/shard_map/forward/pallas_call | solution.py:55
  100.3 1.8 %combine.2 = (bf16[256,3584]{1,0:T(8,128)(2,1)}, f32[8,128]{1,0:T(8,128)S(1)}) custom-call(s32[2]{0:T(128)S(1)} %pad_add_fusion.idx, f32[128,3584]{1,0:T(8,128)S(1)} %get-tuple-element.72.refs_0_, f32[128,3584]{1,0:T(8,128)S(1)} %collective-permute-done.10.refs_1_, f32[8,128]{1,0:T(8,128)S(1)} %get-tuple-element.77.refs_2_), custom_call_target="tpu_custom_call" | custom-call | flops 17179869184 | bytes 4587520 | tf_op jit(solution)/shard_map/combine/pallas_call | solution.py:55
  102.1 7.0 %forward.5 = (f32[128,1536]{1,0:T(8,128)S(1)}, f32[128,1536]{1,0:T(8,128)S(1)}, f32[8,128]{1,0:T(8,128)S(1)}) custom-call(s32[2]{0:T(128)S(1)} %pad_add_fusion.idx, bf16[64,4096]{1,0:T(8,128)(2,1)S(1)} %get-tuple-element.51.refs_0_, bf16[192,4096]{1,0:T(8,128)(2,1)S(1)} %collective-permute-done.5.refs_1_.refs_2_.refs_3_, ...), custom_call_target="tpu_custom_call" | custom-call | flops 17179869184 | bytes 14155776 | tf_op jit(solution)/shard_map/forward/pallas_call | solution.py:55
  111.6 1.7 %combine.3 = (bf16[256,3584]{1,0:T(8,128)(2,1)}, f32[8,128]{1,0:T(8,128)S(1)}) custom-call(s32[2]{0:T(128)S(1)} %pad_add_fusion.idx, f32[128,2048]{1,0:T(8,128)S(1)} %get-tuple-element.70.refs_0_, f32[128,2048]{1,0:T(8,128)S(1)} %collective-permute-done.9.refs_1_, f32[128,1536]{1,0:T(8,128)S(1)} %get-tuple-element.79.refs_2_, ...), custom_call_target="tpu_custom_call", output_to_operand_aliasing={{0}: (5, {})} | custom-call | flops 17179869184 | bytes 4587520 | tf_op jit(solution)/shard_map/combine/pallas_call | solution.py:55
  114.7 2.1 %finish.1 = (bf16[64,4096]{1,0:T(8,128)(2,1)}, f32[8,128]{1,0:T(8,128)}) custom-call(s32[2]{0:T(128)S(1)} %pad_add_fusion.idx, f32[4,1,64,512]{3,2,1,0:T(8,128)S(1)} %get-tuple-element.87.refs_0_, f32[4,1,64,512]{3,2,1,0:T(8,128)S(1)} %get-tuple-element.88.refs_1_, bf16[80,2176]{1,0:T(8,128)(2,1)S(1)} %collective-permute-done.13.refs_1_.refs_2_, ...), custom_call_target="tpu_custom_call" | custom-call | bytes 2097152 | tf_op jit(solution)/shard_map/finish/pallas_call | solution.py:55
  (37 shorter events, 13.3 us)
Async XLA Ops:
  0.6 7.4 %collective-permute-start.3 = (bf16[256,3584]{1,0:T(8,128)(2,1)}, bf16[256,3584]{1,0:T(8,128)(2,1)S(1)}, u32[]{:S(2)}, u32[]{:S(2)}) collective-permute-start(bf16[256,3584]{1,0:T(8,128)(2,1)} %refs_0_.4), channel_id=1, source_target_pairs={{0,1},{1,0},{2,3},{3,2},{4,5},{5,4},{6,7},{7,6},{8,9},{9,8},{10,11... | collective-permute-start | bytes 5505032 | tf_op jit(solution)/shard_map/ppermute | solution.py:577
  1.1 26.5 %collective-permute-start.1 = (bf16[64,4096]{1,0:T(8,128)(2,1)}, bf16[64,4096]{1,0:T(8,128)(2,1)S(1)}, u32[]{:S(2)}, u32[]{:S(2)}) collective-permute-start(bf16[64,4096]{1,0:T(8,128)(2,1)} %refs_0_.5), channel_id=1, source_target_pairs={{0,4},{2,6},{4,0},{6,2},{8,12},{10,14},{12,8},{14,10},{1,5},{3,7},... | collective-permute-start | bytes 1572872 | tf_op jit(solution)/shard_map/ppermute | solution.py:574
  3.8 26.4 %collective-permute-start = (bf16[64,4096]{1,0:T(8,128)(2,1)}, bf16[64,4096]{1,0:T(8,128)(2,1)S(1)}, u32[]{:S(2)}, u32[]{:S(2)}) collective-permute-start(bf16[64,4096]{1,0:T(8,128)(2,1)} %refs_0_.5), channel_id=1, source_target_pairs={{0,8},{2,10},{4,12},{6,14},{8,0},{10,2},{12,4},{14,6},{1,9},{3,11}... | collective-permute-start | bytes 1572872 | tf_op jit(solution)/shard_map/ppermute | solution.py:574
  6.4 23.8 %collective-permute-start.2 = (bf16[64,4096]{1,0:T(8,128)(2,1)}, bf16[64,4096]{1,0:T(8,128)(2,1)S(1)}, u32[]{:S(2)}, u32[]{:S(2)}) collective-permute-start(bf16[64,4096]{1,0:T(8,128)(2,1)} %refs_0_.5), channel_id=1, source_target_pairs={{0,2},{2,0},{4,6},{6,4},{8,10},{10,8},{12,14},{14,12},{1,3},{3,1},... | collective-permute-start | bytes 1572872 | tf_op jit(solution)/shard_map/ppermute | solution.py:574
  8.0 1.5 %copy-start = (bf16[256,3584]{1,0:T(8,128)(2,1)S(1)}, bf16[256,3584]{1,0:T(8,128)(2,1)}, u32[]{:S(2)}) copy-start(bf16[256,3584]{1,0:T(8,128)(2,1)} %refs_0_.4) | copy-start | bytes 5505028
  9.5 1.0 copy-start.3
  24.2 29.0 %collective-permute-start.6 = (bf16[272,2176]{1,0:T(8,128)(2,1)S(1)}, bf16[272,2176]{1,0:T(8,128)(2,1)S(1)}, u32[]{:S(2)}, u32[]{:S(2)}) collective-permute-start(bf16[272,2176]{1,0:T(8,128)(2,1)S(1)} %get-tuple-element.58), channel_id=1, source_target_pairs={{0,2},{2,0},{4,6},{6,4},{8,10},{10,8},{12,14},{14,12},{1,3},{3,1},... | collective-permute-start | bytes 3551240 | tf_op jit(solution)/shard_map/ppermute | solution.py:574
  30.8 15.5 %collective-permute-start.4 = (bf16[64,4096]{1,0:T(8,128)(2,1)S(1)}, bf16[64,4096]{1,0:T(8,128)(2,1)S(1)}, u32[]{:S(2)}, u32[]{:S(2)}) collective-permute-start(bf16[64,4096]{1,0:T(8,128)(2,1)S(1)} %get-tuple-element.53.refs_1_.refs_2_), channel_id=1, source_target_pairs={{0,4},{2,6},{4,0},{6,2},{8,12},{10,14},{12,8},{14,10},{1,5},{3,7},... | collective-permute-start | bytes 1572872 | tf_op jit(solution)/shard_map/ppermute | solution.py:574
  44.6 27.6 %collective-permute-start.8 = (bf16[256,2176]{1,0:T(8,128)(2,1)S(1)}, bf16[256,2176]{1,0:T(8,128)(2,1)S(1)}, u32[]{:S(2)}, u32[]{:S(2)}) collective-permute-start(bf16[256,2176]{1,0:T(8,128)(2,1)S(1)} %get-tuple-element.65), channel_id=1, source_target_pairs={{0,4},{2,6},{4,0},{6,2},{8,12},{10,14},{12,8},{14,10},{1,5},{3,7},... | collective-permute-start | bytes 3342344 | tf_op jit(solution)/shard_map/ppermute | solution.py:574
  47.0 9.2 %copy-start.1 = (bf16[64,4096]{1,0:T(8,128)(2,1)S(1)}, bf16[64,4096]{1,0:T(8,128)(2,1)}, u32[]{:S(2)}) copy-start(bf16[64,4096]{1,0:T(8,128)(2,1)} %refs_0_.5) | copy-start | bytes 1572868
  47.0 9.1 %copy-start.2 = (bf16[64,4096]{1,0:T(8,128)(2,1)S(1)}, bf16[64,4096]{1,0:T(8,128)(2,1)}, u32[]{:S(2)}) copy-start(bf16[64,4096]{1,0:T(8,128)(2,1)} %refs_5_.3) | copy-start | bytes 1572868
  47.0 40.8 %collective-permute-start.5 = (bf16[192,4096]{1,0:T(8,128)(2,1)S(1)}, bf16[192,4096]{1,0:T(8,128)(2,1)S(1)}, u32[]{:S(2)}, u32[]{:S(2)}) collective-permute-start(bf16[192,4096]{1,0:T(8,128)(2,1)S(1)} %get-tuple-element.56), channel_id=1, source_target_pairs={{0,2},{2,0},{4,6},{6,4},{8,10},{10,8},{12,14},{14,12},{1,3},{3,1},... | collective-permute-start | bytes 4718600 | tf_op jit(solution)/shard_map/ppermute | solution.py:574
  55.6 28.3 %collective-permute-start.7 = (bf16[144,2176]{1,0:T(8,128)(2,1)S(1)}, bf16[144,2176]{1,0:T(8,128)(2,1)S(1)}, u32[]{:S(2)}, u32[]{:S(2)}) collective-permute-start(bf16[144,2176]{1,0:T(8,128)(2,1)S(1)} %get-tuple-element.62), channel_id=1, source_target_pairs={{0,4},{2,6},{4,0},{6,2},{8,12},{10,14},{12,8},{14,10},{1,5},{3,7},... | collective-permute-start | bytes 1880072 | tf_op jit(solution)/shard_map/ppermute | solution.py:574
  68.5 31.7 %collective-permute-start.10 = (f32[128,3584]{1,0:T(8,128)S(1)}, f32[128,3584]{1,0:T(8,128)S(1)}, u32[]{:S(2)}, u32[]{:S(2)}) collective-permute-start(f32[128,3584]{1,0:T(8,128)S(1)} %get-tuple-element.73), channel_id=1, source_target_pairs={{0,1},{1,0},{2,3},{3,2},{4,5},{5,4},{6,7},{7,6},{8,9},{9,8},{10,11... | collective-permute-start | bytes 5505032 | tf_op jit(solution)/shard_map/ppermute | solution.py:577
  74.6 22.8 %collective-permute-start.11 = (bf16[128,2176]{1,0:T(8,128)(2,1)S(1)}, bf16[128,2176]{1,0:T(8,128)(2,1)S(1)}, u32[]{:S(2)}, u32[]{:S(2)}) collective-permute-start(bf16[128,2176]{1,0:T(8,128)(2,1)S(1)} %get-tuple-element.75), channel_id=1, source_target_pairs={{0,2},{2,0},{4,6},{6,4},{8,10},{10,8},{12,14},{14,12},{1,3},{3,1},... | collective-permute-start | bytes 1671176 | tf_op jit(solution)/shard_map/ppermute | solution.py:574
  85.4 24.3 %collective-permute-start.13 = (bf16[80,2176]{1,0:T(8,128)(2,1)S(1)}, bf16[80,2176]{1,0:T(8,128)(2,1)S(1)}, u32[]{:S(2)}, u32[]{:S(2)}) collective-permute-start(bf16[80,2176]{1,0:T(8,128)(2,1)S(1)} %get-tuple-element.83), channel_id=1, source_target_pairs={{0,8},{2,10},{4,12},{6,14},{8,0},{10,2},{12,4},{14,6},{1,9},{3,11}... | collective-permute-start | bytes 1044488 | tf_op jit(solution)/shard_map/ppermute | solution.py:574
  98.9 15.8 %collective-permute-start.14 = (bf16[64,2176]{1,0:T(8,128)(2,1)S(1)}, bf16[64,2176]{1,0:T(8,128)(2,1)S(1)}, u32[]{:S(2)}, u32[]{:S(2)}) collective-permute-start(bf16[64,2176]{1,0:T(8,128)(2,1)S(1)} %get-tuple-element.89), channel_id=1, source_target_pairs={{0,8},{2,10},{4,12},{6,14},{8,0},{10,2},{12,4},{14,6},{1,9},{3,11}... | collective-permute-start | bytes 835592 | tf_op jit(solution)/shard_map/ppermute | solution.py:574
  100.2 10.1 %collective-permute-start.9 = (f32[128,2048]{1,0:T(8,128)S(1)}, f32[128,2048]{1,0:T(8,128)S(1)}, u32[]{:S(2)}, u32[]{:S(2)}) collective-permute-start(f32[128,2048]{1,0:T(8,128)S(1)} %get-tuple-element.71), channel_id=1, source_target_pairs={{0,1},{1,0},{2,3},{3,2},{4,5},{5,4},{6,7},{7,6},{8,9},{9,8},{10,11... | collective-permute-start | bytes 3145736 | tf_op jit(solution)/shard_map/ppermute | solution.py:577
  109.1 2.5 %collective-permute-start.12 = (f32[128,1536]{1,0:T(8,128)S(1)}, f32[128,1536]{1,0:T(8,128)S(1)}, u32[]{:S(2)}, u32[]{:S(2)}) collective-permute-start(f32[128,1536]{1,0:T(8,128)S(1)} %get-tuple-element.80), channel_id=1, source_target_pairs={{0,1},{1,0},{2,3},{3,2},{4,5},{5,4},{6,7},{7,6},{8,9},{9,8},{10,11... | collective-permute-start | bytes 2359304 | tf_op jit(solution)/shard_map/ppermute | solution.py:577
  110.2 3.0 %collective-permute-start.15 = (f32[128,128]{1,0:T(8,128)S(1)}, f32[128,128]{1,0:T(8,128)S(1)}, u32[]{:S(2)}, u32[]{:S(2)}) collective-permute-start(f32[128,128]{1,0:T(8,128)S(1)} %get-tuple-element.92.refs_2_), channel_id=1, source_target_pairs={{0,1},{1,0},{2,3},{3,2},{4,5},{5,4},{6,7},{7,6},{8,9},{9,8},{10,11... | collective-permute-start | bytes 196616 | tf_op jit(solution)/shard_map/ppermute | solution.py:577
  114.3 2.6 %collective-permute-start.16 = (f32[4,64,64]{2,1,0:T(8,128)S(1)}, f32[4,64,64]{2,1,0:T(8,128)S(1)}, u32[]{:S(2)}, u32[]{:S(2)}) collective-permute-start(f32[4,64,64]{2,1,0:T(8,128)S(1)} %get-tuple-element.96), channel_id=1, source_target_pairs={{0,1},{1,0},{2,3},{3,2},{4,5},{5,4},{6,7},{7,6},{8,9},{9,8},{10,11... | collective-permute-start | bytes 196616 | tf_op jit(solution)/shard_map/ppermute | solution.py:577

commit v14 on v13

--- a/solution.py
+++ b/solution.py
@@ -19,7 +19,7 @@
 SLOTS = 3
 RIGHT_ROWS = 16
 RIGHT_PARTS = 2
-TIMES = {"gate": 0, "backward_0": 19 * 10**9, "backward_4": 10 * 10**9, "forward": 1 << 34, "fold": 0, "combine": 1 << 34, "sketch_part": 1 << 36, "last_right": 1 << 34}
+TIMES = {"gate": 6 * 10**9, "backward_0": 19 * 10**9, "backward_4": 8 * 10**9, "forward": 1 << 34, "fold": 0, "combine": 1 << 34, "sketch_part": 1 << 36, "last_right": 1 << 34}
 ANY = pl.BlockSpec(memory_space=pl.ANY)
 HBM = pl.BlockSpec(memory_space=pltpu.HBM)
 
@@ -618,7 +618,7 @@
         if p == 0:
             right = outs[2]
         if p == 0:
-            token = hold(singles, token)
+            token = hold([singles[0], 1], token)
             fetch([m for m in evens if m.bit_count() == 2])
     ready = [m for m in evens if m in chunks]
     while len(ready) < len(evens):

time: 118 us -> 119 us (level)
  waiting for transfers between devices: 23.9 us -> 26.7 us
  starting transfers between devices: 18.6 us -> 17.1 us
    ppermute x11, waiting for transfers between devices: 22.7 us -> 25.9 us  [partner(): return lax.ppermute(x, 'outp', [(d, d ^ 1 << bit) for d in range(n)])]
    ppermute x11, starting transfers between devices: 16.9 us -> 15.4 us  [partner(): return lax.ppermute(x, 'outp', [(d, d ^ 1 << bit) for d in range(n)])]
where the time goes in v14:
time: 119 us
  Pallas kernels  71 us (60%)
  waiting for transfers between devices  26.7 us (22%)
  starting transfers between devices  17.1 us (14%)
  local copies, waits for them, and re-layouts  3.27 us (3%)
    pallas_call x16, Pallas kernels, call(): pl.pallas_call(with_token, out_shape=list(out_shape) + [token], grid_spec...  71 us
    ppermute x11, waiting for transfers between devices, partner(): return lax.ppermute(x, 'outp', [(d, d ^ 1 << bit) for d in range(n)])  25.9 us
    ppermute x11, starting transfers between devices, partner(): return lax.ppermute(x, 'outp', [(d, d ^ 1 << bit) for d in range(n)])  15.4 us
    unnamed x8, local copies, waits for them, and re-layouts  2.53 us
  transfers between devices with their start and end apart: 17, of which 7 were waited for; matrix products, arithmetic and copies ran while one was open for 0% of the time, Pallas kernels for 60%

profile of v14, /device:TPU:0, one launch (start us, length us, event | category | flops | bytes accessed | tf_op | source)
XLA Modules:
  0.0 118.9 jit_solution(1787066459960209080)
XLA Ops:
  1.1 2.6 %collective-permute-start.1 = (bf16[64,4096]{1,0:T(8,128)(2,1)}, bf16[64,4096]{1,0:T(8,128)(2,1)S(1)}, u32[]{:S(2)}, u32[]{:S(2)}) collective-permute-start(bf16[64,4096]{1,0:T(8,128)(2,1)} %refs_0_.5), channel_id=1, source_target_pairs={{0,2},{2,0},{4,6},{6,4},{8,10},{10,8},{12,14},{14,12},{1,3},{3,1},... | collective-permute-start | bytes 1572872 | tf_op jit(solution)/shard_map/ppermute | solution.py:574
  3.7 2.6 %collective-permute-start = (bf16[64,4096]{1,0:T(8,128)(2,1)}, bf16[64,4096]{1,0:T(8,128)(2,1)S(1)}, u32[]{:S(2)}, u32[]{:S(2)}) collective-permute-start(bf16[64,4096]{1,0:T(8,128)(2,1)} %refs_0_.5), channel_id=1, source_target_pairs={{0,8},{2,10},{4,12},{6,14},{8,0},{10,2},{12,4},{14,6},{1,9},{3,11}... | collective-permute-start | bytes 1572872 | tf_op jit(solution)/shard_map/ppermute | solution.py:574
  6.3 1.6 %collective-permute-start.3 = (bf16[64,4096]{1,0:T(8,128)(2,1)}, bf16[64,4096]{1,0:T(8,128)(2,1)S(1)}, u32[]{:S(2)}, u32[]{:S(2)}) collective-permute-start(bf16[64,4096]{1,0:T(8,128)(2,1)} %refs_0_.5), channel_id=1, source_target_pairs={{0,4},{2,6},{4,0},{6,2},{8,12},{10,14},{12,8},{14,10},{1,5},{3,7},... | collective-permute-start | bytes 1572872 | tf_op jit(solution)/shard_map/ppermute | solution.py:574
  8.0 1.5 %copy-done = bf16[256,3584]{1,0:T(8,128)(2,1)S(1)} copy-done((bf16[256,3584]{1,0:T(8,128)(2,1)S(1)}, bf16[256,3584]{1,0:T(8,128)(2,1)}, u32[]{:S(2)}) %copy-start) | copy-done | bytes 1835032
  9.5 1.0 copy-done.3
  10.5 13.6 %backward_0.1 = (bf16[272,2176]{1,0:T(8,128)(2,1)S(1)}, f32[4,4,64,512]{3,2,1,0:T(8,128)S(1)}, f32[128,128]{1,0:T(8,128)S(1)}, f32[8,128]{1,0:T(8,128)S(1)}) custom-call(s32[2]{0:T(128)S(1)} %pad_add_fusion.idx, bf16[256,3584]{1,0:T(8,128)(2,1)S(1)} %copy-done, bf16[256,3584]{1,0:T(8,128)(2,1)S(1)} %collective-permute-done.2.refs_1_, ...), custom_call_target="tpu_custom_call" | custom-call | flops 19000000512 | bytes 20971520 | tf_op jit(solution)/shard_map/backward_0/pallas_call | solution.py:55
  24.7 5.5 %collective-permute-done.refs_0_ = bf16[64,4096]{1,0:T(8,128)(2,1)S(1)} collective-permute-done((bf16[64,4096]{1,0:T(8,128)(2,1)}, bf16[64,4096]{1,0:T(8,128)(2,1)S(1)}, u32[]{:S(2)}, u32[]{:S(2)}) %collective-permute-start) | collective-permute-done | bytes 524320 | tf_op jit(solution)/shard_map/ppermute | solution.py:574
  31.5 13.4 %backward_4.1 = (bf16[256,2176]{1,0:T(8,128)(2,1)S(1)}, f32[4,4,64,512]{3,2,1,0:T(8,128)S(1)}, f32[8,128]{1,0:T(8,128)S(1)}) custom-call(s32[2]{0:T(128)S(1)} %pad_add_fusion.idx, bf16[256,3584]{1,0:T(8,128)(2,1)S(1)} %copy-done, bf16[256,3584]{1,0:T(8,128)(2,1)S(1)} %collective-permute-done.2.refs_1_, bf16[4096,3584]{1,0:T(8,128)(2,1)} %refs_4_.5, ...), custom_call_target="tpu_custom_call" | custom-call | flops 8000000000 | bytes 20971520 | tf_op jit(solution)/shard_map/backward_4/pallas_call | solution.py:55
  44.9 1.4 %collective-permute-start.8 = (bf16[256,2176]{1,0:T(8,128)(2,1)S(1)}, bf16[256,2176]{1,0:T(8,128)(2,1)S(1)}, u32[]{:S(2)}, u32[]{:S(2)}) collective-permute-start(bf16[256,2176]{1,0:T(8,128)(2,1)S(1)} %get-tuple-element.63), channel_id=1, source_target_pairs={{0,4},{2,6},{4,0},{6,2},{8,12},{10,14},{12,8},{14,10},{1,5},{3,7},... | collective-permute-start | bytes 3342344 | tf_op jit(solution)/shard_map/ppermute | solution.py:574
  47.5 5.7 %collective-permute-done.6.refs_1_ = bf16[272,2176]{1,0:T(8,128)(2,1)S(1)} collective-permute-done((bf16[272,2176]{1,0:T(8,128)(2,1)S(1)}, bf16[272,2176]{1,0:T(8,128)(2,1)S(1)}, u32[]{:S(2)}, u32[]{:S(2)}) %collective-permute-start.6) | collective-permute-done | bytes 1183776 | tf_op jit(solution)/shard_map/ppermute | solution.py:574
  53.2 2.4 %fold.4 = (bf16[144,2176]{1,0:T(8,128)(2,1)S(1)}, f32[4,2,64,512]{3,2,1,0:T(8,128)S(1)}, f32[128,128]{1,0:T(8,128)S(1)}, f32[8,128]{1,0:T(8,128)S(1)}) custom-call(s32[2]{0:T(128)S(1)} %pad_add_fusion.idx, f32[4,4,64,512]{3,2,1,0:T(8,128)S(1)} %get-tuple-element.55.refs_0_, bf16[272,2176]{1,0:T(8,128)(2,1)S(1)} %collective-permute-done.6.refs_1_, ...), custom_call_target="tpu_custom_call" | custom-call | bytes 6291456 | tf_op jit(solution)/shard_map/fold/pallas_call | solution.py:55
  56.1 12.4 %forward.3 = (f32[128,3584]{1,0:T(8,128)S(1)}, f32[128,3584]{1,0:T(8,128)S(1)}, f32[256,64]{1,0:T(8,128)S(1)}, f32[8,128]{1,0:T(8,128)S(1)}) custom-call(s32[2]{0:T(128)S(1)} %pad_add_fusion.idx, bf16[64,4096]{1,0:T(8,128)(2,1)S(1)} %copy-done.1, bf16[64,4096]{1,0:T(8,128)(2,1)S(1)} %collective-permute-done.3.refs_0_.refs_1_, ...), custom_call_target="tpu_custom_call" | custom-call | flops 17179869184 | bytes 33030144 | tf_op jit(solution)/shard_map/forward/pallas_call | solution.py:55
  68.6 3.8 %collective-permute-done.8.refs_1_ = bf16[256,2176]{1,0:T(8,128)(2,1)S(1)} collective-permute-done((bf16[256,2176]{1,0:T(8,128)(2,1)S(1)}, bf16[256,2176]{1,0:T(8,128)(2,1)S(1)}, u32[]{:S(2)}, u32[]{:S(2)}) %collective-permute-start.8) | collective-permute-done | bytes 1114144 | tf_op jit(solution)/shard_map/ppermute | solution.py:574
  72.4 2.4 %fold.5 = (bf16[128,2176]{1,0:T(8,128)(2,1)S(1)}, f32[4,2,64,512]{3,2,1,0:T(8,128)S(1)}, f32[8,128]{1,0:T(8,128)S(1)}) custom-call(s32[2]{0:T(128)S(1)} %pad_add_fusion.idx, f32[4,4,64,512]{3,2,1,0:T(8,128)S(1)} %get-tuple-element.62.refs_0_, bf16[256,2176]{1,0:T(8,128)(2,1)S(1)} %collective-permute-done.8.refs_1_, f32[8,128]{1,0:T(8,128)S(1)} %get-tuple-element.65.refs_2_), custom_call_target="tpu_custom_call" | custom-call | bytes 6291456 | tf_op jit(solution)/shard_map/fold/pallas_call | solution.py:55
  75.3 9.2 %collective-permute-done.7.refs_1_ = bf16[144,2176]{1,0:T(8,128)(2,1)S(1)} collective-permute-done((bf16[144,2176]{1,0:T(8,128)(2,1)S(1)}, bf16[144,2176]{1,0:T(8,128)(2,1)S(1)}, u32[]{:S(2)}, u32[]{:S(2)}) %collective-permute-start.7) | collective-permute-done | bytes 626720 | tf_op jit(solution)/shard_map/ppermute | solution.py:574
  84.6 1.5 %fold.6 = (bf16[80,2176]{1,0:T(8,128)(2,1)S(1)}, f32[4,1,64,512]{3,2,1,0:T(8,128)S(1)}, f32[128,128]{1,0:T(8,128)S(1)}, f32[8,128]{1,0:T(8,128)S(1)}) custom-call(s32[2]{0:T(128)S(1)} %pad_add_fusion.idx, f32[4,2,64,512]{3,2,1,0:T(8,128)S(1)} %get-tuple-element.59.refs_0_, bf16[144,2176]{1,0:T(8,128)(2,1)S(1)} %collective-permute-done.7.refs_1_, ...), custom_call_target="tpu_custom_call" | custom-call | bytes 3145728 | tf_op jit(solution)/shard_map/fold/pallas_call | solution.py:55
  86.1 3.3 %collective-permute-start.13 = (bf16[80,2176]{1,0:T(8,128)(2,1)S(1)}, bf16[80,2176]{1,0:T(8,128)(2,1)S(1)}, u32[]{:S(2)}, u32[]{:S(2)}) collective-permute-start(bf16[80,2176]{1,0:T(8,128)(2,1)S(1)} %get-tuple-element.81), channel_id=1, source_target_pairs={{0,8},{2,10},{4,12},{6,14},{8,0},{10,2},{12,4},{14,6},{1,9},{3,11}... | collective-permute-start | bytes 1044488 | tf_op jit(solution)/shard_map/ppermute | solution.py:574
  89.4 8.4 %forward.4 = (f32[128,2048]{1,0:T(8,128)S(1)}, f32[128,2048]{1,0:T(8,128)S(1)}, f32[256,64]{1,0:T(8,128)S(1)}, f32[8,128]{1,0:T(8,128)S(1)}) custom-call(s32[2]{0:T(128)S(1)} %pad_add_fusion.idx, bf16[64,4096]{1,0:T(8,128)(2,1)S(1)} %get-tuple-element.50.refs_0_, bf16[192,4096]{1,0:T(8,128)(2,1)S(1)} %collective-permute-done.5.refs_1_.refs_2_.refs_3_, ...), custom_call_target="tpu_custom_call" | custom-call | flops 17179869184 | bytes 18874368 | tf_op jit(solution)/shard_map/forward/pallas_call | solution.py:55
  97.8 1.5 %fold.7 = (bf16[64,2176]{1,0:T(8,128)(2,1)S(1)}, f32[4,1,64,512]{3,2,1,0:T(8,128)S(1)}, f32[8,128]{1,0:T(8,128)S(1)}) custom-call(s32[2]{0:T(128)S(1)} %pad_add_fusion.idx, f32[4,2,64,512]{3,2,1,0:T(8,128)S(1)} %get-tuple-element.72.refs_0_, bf16[128,2176]{1,0:T(8,128)(2,1)S(1)} %collective-permute-done.11.refs_1_, f32[8,128]{1,0:T(8,128)S(1)} %get-tuple-element.74.refs_2_), custom_call_target="tpu_custom_call" | custom-call | bytes 3145728 | tf_op jit(solution)/shard_map/fold/pallas_call | solution.py:55
  100.3 1.8 %combine.2 = (bf16[256,3584]{1,0:T(8,128)(2,1)}, f32[8,128]{1,0:T(8,128)S(1)}) custom-call(s32[2]{0:T(128)S(1)} %pad_add_fusion.idx, f32[128,3584]{1,0:T(8,128)S(1)} %get-tuple-element.70.refs_0_, f32[128,3584]{1,0:T(8,128)S(1)} %collective-permute-done.10.refs_1_, f32[8,128]{1,0:T(8,128)S(1)} %get-tuple-element.75.refs_2_), custom_call_target="tpu_custom_call" | custom-call | flops 17179869184 | bytes 4587520 | tf_op jit(solution)/shard_map/combine/pallas_call | solution.py:55
  102.1 7.0 %forward.5 = (f32[128,1536]{1,0:T(8,128)S(1)}, f32[128,1536]{1,0:T(8,128)S(1)}, f32[8,128]{1,0:T(8,128)S(1)}) custom-call(s32[2]{0:T(128)S(1)} %pad_add_fusion.idx, bf16[64,4096]{1,0:T(8,128)(2,1)S(1)} %get-tuple-element.50.refs_0_, bf16[192,4096]{1,0:T(8,128)(2,1)S(1)} %collective-permute-done.5.refs_1_.refs_2_.refs_3_, ...), custom_call_target="tpu_custom_call" | custom-call | flops 17179869184 | bytes 14155776 | tf_op jit(solution)/shard_map/forward/pallas_call | solution.py:55
  111.6 1.7 %combine.3 = (bf16[256,3584]{1,0:T(8,128)(2,1)}, f32[8,128]{1,0:T(8,128)S(1)}) custom-call(s32[2]{0:T(128)S(1)} %pad_add_fusion.idx, f32[128,2048]{1,0:T(8,128)S(1)} %get-tuple-element.68.refs_0_, f32[128,2048]{1,0:T(8,128)S(1)} %collective-permute-done.9.refs_1_, f32[128,1536]{1,0:T(8,128)S(1)} %get-tuple-element.77.refs_2_, ...), custom_call_target="tpu_custom_call", output_to_operand_aliasing={{0}: (5, {})} | custom-call | flops 17179869184 | bytes 4587520 | tf_op jit(solution)/shard_map/combine/pallas_call | solution.py:55
  114.7 1.3 %collective-permute-done.14.refs_3_ = bf16[64,2176]{1,0:T(8,128)(2,1)S(1)} collective-permute-done((bf16[64,2176]{1,0:T(8,128)(2,1)S(1)}, bf16[64,2176]{1,0:T(8,128)(2,1)S(1)}, u32[]{:S(2)}, u32[]{:S(2)}) %collective-permute-start.14) | collective-permute-done | bytes 278560 | tf_op jit(solution)/shard_map/ppermute | solution.py:574
  116.0 2.1 %finish.1 = (bf16[64,4096]{1,0:T(8,128)(2,1)}, f32[8,128]{1,0:T(8,128)}) custom-call(s32[2]{0:T(128)S(1)} %pad_add_fusion.idx, f32[4,1,64,512]{3,2,1,0:T(8,128)S(1)} %get-tuple-element.85.refs_0_, f32[4,1,64,512]{3,2,1,0:T(8,128)S(1)} %get-tuple-element.86.refs_1_, bf16[80,2176]{1,0:T(8,128)(2,1)S(1)} %collective-permute-done.13.refs_1_.refs_2_, ...), custom_call_target="tpu_custom_call" | custom-call | bytes 2097152 | tf_op jit(solution)/shard_map/finish/pallas_call | solution.py:55
  (37 shorter events, 10.5 us)
Async XLA Ops:
  0.6 7.4 %collective-permute-start.2 = (bf16[256,3584]{1,0:T(8,128)(2,1)}, bf16[256,3584]{1,0:T(8,128)(2,1)S(1)}, u32[]{:S(2)}, u32[]{:S(2)}) collective-permute-start(bf16[256,3584]{1,0:T(8,128)(2,1)} %refs_0_.4), channel_id=1, source_target_pairs={{0,1},{1,0},{2,3},{3,2},{4,5},{5,4},{6,7},{7,6},{8,9},{9,8},{10,11... | collective-permute-start | bytes 5505032 | tf_op jit(solution)/shard_map/ppermute | solution.py:577
  1.1 23.6 %collective-permute-start.1 = (bf16[64,4096]{1,0:T(8,128)(2,1)}, bf16[64,4096]{1,0:T(8,128)(2,1)S(1)}, u32[]{:S(2)}, u32[]{:S(2)}) collective-permute-start(bf16[64,4096]{1,0:T(8,128)(2,1)} %refs_0_.5), channel_id=1, source_target_pairs={{0,2},{2,0},{4,6},{6,4},{8,10},{10,8},{12,14},{14,12},{1,3},{3,1},... | collective-permute-start | bytes 1572872 | tf_op jit(solution)/shard_map/ppermute | solution.py:574
  3.7 26.5 %collective-permute-start = (bf16[64,4096]{1,0:T(8,128)(2,1)}, bf16[64,4096]{1,0:T(8,128)(2,1)S(1)}, u32[]{:S(2)}, u32[]{:S(2)}) collective-permute-start(bf16[64,4096]{1,0:T(8,128)(2,1)} %refs_0_.5), channel_id=1, source_target_pairs={{0,8},{2,10},{4,12},{6,14},{8,0},{10,2},{12,4},{14,6},{1,9},{3,11}... | collective-permute-start | bytes 1572872 | tf_op jit(solution)/shard_map/ppermute | solution.py:574
  6.3 40.0 %collective-permute-start.3 = (bf16[64,4096]{1,0:T(8,128)(2,1)}, bf16[64,4096]{1,0:T(8,128)(2,1)S(1)}, u32[]{:S(2)}, u32[]{:S(2)}) collective-permute-start(bf16[64,4096]{1,0:T(8,128)(2,1)} %refs_0_.5), channel_id=1, source_target_pairs={{0,4},{2,6},{4,0},{6,2},{8,12},{10,14},{12,8},{14,10},{1,5},{3,7},... | collective-permute-start | bytes 1572872 | tf_op jit(solution)/shard_map/ppermute | solution.py:574
  8.0 1.5 %copy-start = (bf16[256,3584]{1,0:T(8,128)(2,1)S(1)}, bf16[256,3584]{1,0:T(8,128)(2,1)}, u32[]{:S(2)}) copy-start(bf16[256,3584]{1,0:T(8,128)(2,1)} %refs_0_.4) | copy-start | bytes 5505028
  9.5 1.0 copy-start.3
  24.2 29.0 %collective-permute-start.6 = (bf16[272,2176]{1,0:T(8,128)(2,1)S(1)}, bf16[272,2176]{1,0:T(8,128)(2,1)S(1)}, u32[]{:S(2)}, u32[]{:S(2)}) collective-permute-start(bf16[272,2176]{1,0:T(8,128)(2,1)S(1)} %get-tuple-element.56), channel_id=1, source_target_pairs={{0,2},{2,0},{4,6},{6,4},{8,10},{10,8},{12,14},{14,12},{1,3},{3,1},... | collective-permute-start | bytes 3551240 | tf_op jit(solution)/shard_map/ppermute | solution.py:574
  30.8 15.5 %collective-permute-start.4 = (bf16[64,4096]{1,0:T(8,128)(2,1)S(1)}, bf16[64,4096]{1,0:T(8,128)(2,1)S(1)}, u32[]{:S(2)}, u32[]{:S(2)}) collective-permute-start(bf16[64,4096]{1,0:T(8,128)(2,1)S(1)} %get-tuple-element.51.refs_1_.refs_2_), channel_id=1, source_target_pairs={{0,4},{2,6},{4,0},{6,2},{8,12},{10,14},{12,8},{14,10},{1,5},{3,7},... | collective-permute-start | bytes 1572872 | tf_op jit(solution)/shard_map/ppermute | solution.py:574
  44.9 27.5 %collective-permute-start.8 = (bf16[256,2176]{1,0:T(8,128)(2,1)S(1)}, bf16[256,2176]{1,0:T(8,128)(2,1)S(1)}, u32[]{:S(2)}, u32[]{:S(2)}) collective-permute-start(bf16[256,2176]{1,0:T(8,128)(2,1)S(1)} %get-tuple-element.63), channel_id=1, source_target_pairs={{0,4},{2,6},{4,0},{6,2},{8,12},{10,14},{12,8},{14,10},{1,5},{3,7},... | collective-permute-start | bytes 3342344 | tf_op jit(solution)/shard_map/ppermute | solution.py:574
  47.0 9.1 %copy-start.1 = (bf16[64,4096]{1,0:T(8,128)(2,1)S(1)}, bf16[64,4096]{1,0:T(8,128)(2,1)}, u32[]{:S(2)}) copy-start(bf16[64,4096]{1,0:T(8,128)(2,1)} %refs_0_.5) | copy-start | bytes 1572868
  47.0 9.1 %copy-start.2 = (bf16[64,4096]{1,0:T(8,128)(2,1)S(1)}, bf16[64,4096]{1,0:T(8,128)(2,1)}, u32[]{:S(2)}) copy-start(bf16[64,4096]{1,0:T(8,128)(2,1)} %refs_5_.3) | copy-start | bytes 1572868
  47.0 42.4 %collective-permute-start.5 = (bf16[192,4096]{1,0:T(8,128)(2,1)S(1)}, bf16[192,4096]{1,0:T(8,128)(2,1)S(1)}, u32[]{:S(2)}, u32[]{:S(2)}) collective-permute-start(bf16[192,4096]{1,0:T(8,128)(2,1)S(1)} %get-tuple-element.54), channel_id=1, source_target_pairs={{0,2},{2,0},{4,6},{6,4},{8,10},{10,8},{12,14},{14,12},{1,3},{3,1},... | collective-permute-start | bytes 4718600 | tf_op jit(solution)/shard_map/ppermute | solution.py:574
  55.6 29.0 %collective-permute-start.7 = (bf16[144,2176]{1,0:T(8,128)(2,1)S(1)}, bf16[144,2176]{1,0:T(8,128)(2,1)S(1)}, u32[]{:S(2)}, u32[]{:S(2)}) collective-permute-start(bf16[144,2176]{1,0:T(8,128)(2,1)S(1)} %get-tuple-element.60), channel_id=1, source_target_pairs={{0,4},{2,6},{4,0},{6,2},{8,12},{10,14},{12,8},{14,10},{1,5},{3,7},... | collective-permute-start | bytes 1880072 | tf_op jit(solution)/shard_map/ppermute | solution.py:574
  68.5 31.7 %collective-permute-start.10 = (f32[128,3584]{1,0:T(8,128)S(1)}, f32[128,3584]{1,0:T(8,128)S(1)}, u32[]{:S(2)}, u32[]{:S(2)}) collective-permute-start(f32[128,3584]{1,0:T(8,128)S(1)} %get-tuple-element.71), channel_id=1, source_target_pairs={{0,1},{1,0},{2,3},{3,2},{4,5},{5,4},{6,7},{7,6},{8,9},{9,8},{10,11... | collective-permute-start | bytes 5505032 | tf_op jit(solution)/shard_map/ppermute | solution.py:577
  74.8 23.0 %collective-permute-start.11 = (bf16[128,2176]{1,0:T(8,128)(2,1)S(1)}, bf16[128,2176]{1,0:T(8,128)(2,1)S(1)}, u32[]{:S(2)}, u32[]{:S(2)}) collective-permute-start(bf16[128,2176]{1,0:T(8,128)(2,1)S(1)} %get-tuple-element.73), channel_id=1, source_target_pairs={{0,2},{2,0},{4,6},{6,4},{8,10},{10,8},{12,14},{14,12},{1,3},{3,1},... | collective-permute-start | bytes 1671176 | tf_op jit(solution)/shard_map/ppermute | solution.py:574
  86.1 24.1 %collective-permute-start.13 = (bf16[80,2176]{1,0:T(8,128)(2,1)S(1)}, bf16[80,2176]{1,0:T(8,128)(2,1)S(1)}, u32[]{:S(2)}, u32[]{:S(2)}) collective-permute-start(bf16[80,2176]{1,0:T(8,128)(2,1)S(1)} %get-tuple-element.81), channel_id=1, source_target_pairs={{0,8},{2,10},{4,12},{6,14},{8,0},{10,2},{12,4},{14,6},{1,9},{3,11}... | collective-permute-start | bytes 1044488 | tf_op jit(solution)/shard_map/ppermute | solution.py:574
  99.3 16.7 %collective-permute-start.14 = (bf16[64,2176]{1,0:T(8,128)(2,1)S(1)}, bf16[64,2176]{1,0:T(8,128)(2,1)S(1)}, u32[]{:S(2)}, u32[]{:S(2)}) collective-permute-start(bf16[64,2176]{1,0:T(8,128)(2,1)S(1)} %get-tuple-element.87), channel_id=1, source_target_pairs={{0,8},{2,10},{4,12},{6,14},{8,0},{10,2},{12,4},{14,6},{1,9},{3,11}... | collective-permute-start | bytes 835592 | tf_op jit(solution)/shard_map/ppermute | solution.py:574
  100.2 10.6 %collective-permute-start.9 = (f32[128,2048]{1,0:T(8,128)S(1)}, f32[128,2048]{1,0:T(8,128)S(1)}, u32[]{:S(2)}, u32[]{:S(2)}) collective-permute-start(f32[128,2048]{1,0:T(8,128)S(1)} %get-tuple-element.69), channel_id=1, source_target_pairs={{0,1},{1,0},{2,3},{3,2},{4,5},{5,4},{6,7},{7,6},{8,9},{9,8},{10,11... | collective-permute-start | bytes 3145736 | tf_op jit(solution)/shard_map/ppermute | solution.py:577
  109.1 2.5 %collective-permute-start.12 = (f32[128,1536]{1,0:T(8,128)S(1)}, f32[128,1536]{1,0:T(8,128)S(1)}, u32[]{:S(2)}, u32[]{:S(2)}) collective-permute-start(f32[128,1536]{1,0:T(8,128)S(1)} %get-tuple-element.78), channel_id=1, source_target_pairs={{0,1},{1,0},{2,3},{3,2},{4,5},{5,4},{6,7},{7,6},{8,9},{9,8},{10,11... | collective-permute-start | bytes 2359304 | tf_op jit(solution)/shard_map/ppermute | solution.py:577
  110.7 2.5 %collective-permute-start.15 = (f32[128,128]{1,0:T(8,128)S(1)}, f32[128,128]{1,0:T(8,128)S(1)}, u32[]{:S(2)}, u32[]{:S(2)}) collective-permute-start(f32[128,128]{1,0:T(8,128)S(1)} %get-tuple-element.90.refs_2_), channel_id=1, source_target_pairs={{0,1},{1,0},{2,3},{3,2},{4,5},{5,4},{6,7},{7,6},{8,9},{9,8},{10,11... | collective-permute-start | bytes 196616 | tf_op jit(solution)/shard_map/ppermute | solution.py:577
  114.3 3.8 %collective-permute-start.16 = (f32[4,64,64]{2,1,0:T(8,128)S(1)}, f32[4,64,64]{2,1,0:T(8,128)S(1)}, u32[]{:S(2)}, u32[]{:S(2)}) collective-permute-start(f32[4,64,64]{2,1,0:T(8,128)S(1)} %get-tuple-element.94), channel_id=1, source_target_pairs={{0,1},{1,0},{2,3},{3,2},{4,5},{5,4},{6,7},{7,6},{8,9},{9,8},{10,11... | collective-permute-start | bytes 196616 | tf_op jit(solution)/shard_map/ppermute | solution.py:577
